TPU v7x, 32 devices: a whole 2x2x4 slice. The times are simulated.
32 devices in a mesh: dp: 2 (over y), row: 4 (over z), col: 4 (over x, core).
Axes of the slice: x: 2, y: 2, z: 4, core: 2. Of those that a mesh axis runs over, the one named last changes fastest.
Arguments:
- hidden_in: bfloat16 [16384, 1088], P(('dp', 'row', 'col')), may hold values from -6 to 6
- cotangent: bfloat16 [16384, 1088], P(('dp', 'row', 'col')), may hold values from -6 to 6
- segments: int32 [16, 1024], P(('dp', 'row')), may hold values from 0 to 3, never falling along the last dimension, each value on 1 to 800 neighbouring positions
- qkv_weight: float32 [1088, 3, 1088], P(('dp', 'row'), None, 'col'), may hold values from -0.1875 to 0.1875
- out_weight: float32 [1088, 1088], P('col', ('dp', 'row')), may hold values from -1.5 to 1.5
- up_weight: float32 [1088, 4352], P(('dp', 'row'), 'col'), may hold values from -0.1875 to 0.1875
- down_weight: float32 [4352, 1088], P('col', ('dp', 'row')), may hold values from -0.09375 to 0.09375
- vectors: float32 [12, 1088], P('col', ('dp', 'row')), may hold values from -1.2 to 1.4, as said below
- qkv_first: float32 [1088, 3, 1088], P(('dp', 'row'), None, 'col'), may hold values from -128 to 128
- out_first: float32 [1088, 1088], P('col', ('dp', 'row')), may hold values from -20 to 20
- up_first: float32 [1088, 4352], P(('dp', 'row'), 'col'), may hold values from -24 to 24
- down_first: float32 [4352, 1088], P('col', ('dp', 'row')), may hold values from -56 to 56
- vectors_first: float32 [12, 1088], P('col', ('dp', 'row')), may hold values from -64 to 64
- qkv_second: float32 [1088, 3, 1088], P(('dp', 'row'), None, 'col'), may hold values from 18.0224 to 294.912
- out_second: float32 [1088, 1088], P('col', ('dp', 'row')), may hold values from 0.49152 to 8.192
- up_second: float32 [1088, 4352], P(('dp', 'row'), 'col'), may hold values from 0.73728 to 11.79648
- down_second: float32 [4352, 1088], P('col', ('dp', 'row')), may hold values from 3.2768 to 55.7056
- vectors_second: float32 [12, 1088], P('col', ('dp', 'row')), may hold values from 4.096 to 65.536
Outputs:
- layer_out: bfloat16 [16384, 1088], P(('dp', 'row', 'col'))
- input_grad: float32 [16384, 1088], P(('dp', 'row', 'col'))
- qkv_first_new: float32 [1088, 3, 1088], P(('dp', 'row'), None, 'col')
- qkv_second_new: float32 [1088, 3, 1088], P(('dp', 'row'), None, 'col')
- qkv_weight_new: float32 [1088, 3, 1088], P(('dp', 'row'), None, 'col')
- out_first_new: float32 [1088, 1088], P('col', ('dp', 'row'))
- out_second_new: float32 [1088, 1088], P('col', ('dp', 'row'))
- out_weight_new: float32 [1088, 1088], P('col', ('dp', 'row'))
- up_first_new: float32 [1088, 4352], P(('dp', 'row'), 'col')
- up_second_new: float32 [1088, 4352], P(('dp', 'row'), 'col')
- up_weight_new: float32 [1088, 4352], P(('dp', 'row'), 'col')
- down_first_new: float32 [4352, 1088], P('col', ('dp', 'row'))
- down_second_new: float32 [4352, 1088], P('col', ('dp', 'row'))
- down_weight_new: float32 [4352, 1088], P('col', ('dp', 'row'))
- vectors_first_new: float32 [12, 1088], P('col', ('dp', 'row'))
- vectors_second_new: float32 [12, 1088], P('col', ('dp', 'row'))
- vectors_new: float32 [12, 1088], P('col', ('dp', 'row'))
Inputs may be any that keep to these rules, and one draw needn't show every extreme that they name: `segments`: within each sequence the numbers start at 0 and never fall; each number covers 1 to 800 consecutive tokens, one of them exactly 800. `vectors`: rows 0 and 5 lie within 0.6 to 1.4; the other rows within -1.2 to 1.2.
All inputs are finite; a program needn't handle non-finite values.
Results may differ from a plain program's by a relative error of at most 0.015.
Values may be sent and summed in bfloat16 or wider, within the bound.
No kernel may reach another device: no remote copies, remote signals or barrier semaphores. Data moves between devices by JAX's collectives and lax.ppermute only.
A program may use at most 256 MiB of HBM per device.

v0:
```python
import jax
import jax.numpy as jnp
from jax import lax
from jax.sharding import PartitionSpec as P

D = 1088
HEAD_DIM = 64
FF = 4352
SEQ = 1024
STEP = 5


beta_one = 0.9
beta_two = 0.999
epsilon = 1e-08
decay_rate = 0.1
masked_score = -1000000000.0


def contract_first(left, right):
    return lax.dot_general(
        left, right, (((0,), (0,)), ((), ())), preferred_element_type=jnp.float32
    )


def contract_last(left, right):
    return lax.dot_general(
        left, right, (((1,), (1,)), ((), ())), preferred_element_type=jnp.float32
    )


def normalize(rows, gain, shift):
    row_mean = jnp.mean(rows, -1, keepdims=True)
    centred = rows - row_mean
    inverse = lax.rsqrt(jnp.mean(centred * centred, -1, keepdims=True) + 1e-05)
    scaled = centred * inverse
    return (scaled * gain + shift, scaled, inverse)


def norm_back(grad_out, scaled, inverse, gain):
    grad_scaled = grad_out * gain
    return inverse * (
        grad_scaled
        - jnp.mean(grad_scaled, -1, keepdims=True)
        - scaled * jnp.mean(grad_scaled * scaled, -1, keepdims=True)
    )


def gelu_tanh(values):
    return jax.nn.gelu(values, approximate=True)


def adamw(weight, gradient, moment_one, moment_two, step_rate, shrink):
    moment_one = beta_one * moment_one + (1.0 - beta_one) * gradient
    moment_two = beta_two * moment_two + (1.0 - beta_two) * gradient * gradient
    update = (
        moment_one
        / (1.0 - beta_one**STEP)
        / (jnp.sqrt(moment_two / (1.0 - beta_two**STEP)) + epsilon)
    )
    return (moment_one, moment_two, weight - step_rate * (update + shrink * weight))


def placed(block, start_at, length):
    return lax.dynamic_update_slice_in_dim(jnp.zeros((length,), jnp.float32), block, start_at, 0)


def local(
    hidden_in,
    cotangent,
    segments,
    qkv_weight,
    out_weight,
    up_weight,
    down_weight,
    vectors,
    qkv_first,
    out_first,
    up_first,
    down_first,
    vectors_first,
    qkv_second,
    out_second,
    up_second,
    down_second,
    vectors_second,
):
    column = lax.axis_index("col")
    col_count = lax.axis_size("col")
    rows_here = hidden_in.shape[0]
    model_width = hidden_in.shape[1]
    group_rows = rows_here * col_count
    own_start = column * rows_here
    head_count = model_width // HEAD_DIM
    score_scale = HEAD_DIM ** (-0.5)
    qkv_local, out_local, up_local, down_local, vector_piece = (
        lax.all_gather(qkv_weight.astype(jnp.bfloat16), ("dp", "row"), axis=0, tiled=True),
        lax.all_gather(out_weight.astype(jnp.bfloat16), ("dp", "row"), axis=1, tiled=True),
        lax.all_gather(up_weight.astype(jnp.bfloat16), ("dp", "row"), axis=0, tiled=True),
        lax.all_gather(down_weight.astype(jnp.bfloat16), ("dp", "row"), axis=1, tiled=True),
        lax.all_gather(vectors.astype(jnp.bfloat16), ("dp", "row"), axis=1, tiled=True),
    )
    inputs_all, cotangent_all, vector_half = (
        lax.all_gather(hidden_in, "col", axis=0, tiled=True),
        lax.all_gather(cotangent, "col", axis=0, tiled=True),
        lax.all_gather(vector_piece, "col", axis=0, tiled=True),
    )
    vector_rows = vector_half.astype(jnp.float32)

    def own_rows(array):
        return lax.dynamic_slice_in_dim(array, own_start, rows_here, 0)

    inputs_wide = inputs_all.astype(jnp.float32)
    normed_one, scaled_one, inverse_one = normalize(inputs_wide, vector_rows[0], vector_rows[1])
    normed_low = normed_one.astype(jnp.bfloat16)
    col_width = qkv_local.shape[2]
    qkv_flat = qkv_local.reshape(model_width, 3 * col_width)
    linear = jnp.dot(normed_low, qkv_flat, preferred_element_type=jnp.float32).reshape(
        group_rows, 3, col_width
    )
    bias_rows = jnp.stack([vector_rows[2], jnp.zeros_like(vector_rows[2]), vector_rows[3]])
    projected = (
        linear + lax.dynamic_slice_in_dim(bias_rows, column * col_width, col_width, 1)
    ).astype(jnp.bfloat16)
    projected_all = lax.all_gather(projected, "col", axis=2, tiled=True)
    queries = own_rows(projected_all)[:, 0]
    key_rows = projected_all[:, 1]
    values = projected_all[:, 2]
    labels = segments.reshape(group_rows)
    query_place = own_start + jnp.arange(rows_here)
    key_place = jnp.arange(group_rows)
    allowed = (
        (key_place[None, :] <= query_place[:, None])
        & (key_place[None, :] // SEQ == query_place[:, None] // SEQ)
        & (labels[None, :] == own_rows(labels)[:, None])
    )

    def head_slice(array, head_index):
        return lax.dynamic_slice_in_dim(array, head_index * HEAD_DIM, HEAD_DIM, 1)

    def head_scores(head_index):
        raw_scores = (
            contract_last(head_slice(queries, head_index), head_slice(key_rows, head_index))
            * score_scale
        )
        return jnp.where(allowed, raw_scores, masked_score)

    def head_forward(head_index):
        scores = head_scores(head_index)
        row_max = jnp.max(scores, -1, keepdims=True)
        row_total = jnp.sum(jnp.exp(scores - row_max), -1, keepdims=True)
        log_total = row_max + jnp.log(row_total)
        attn_probs = jnp.exp(scores - log_total).astype(jnp.bfloat16)
        return (
            jnp.dot(attn_probs, head_slice(values, head_index), preferred_element_type=jnp.float32),
            log_total,
        )

    heads_mixed, log_totals = lax.map(head_forward, jnp.arange(head_count))
    attn_mixed = heads_mixed.transpose(1, 0, 2).reshape(rows_here, model_width).astype(jnp.bfloat16)
    mixed_cols = lax.all_to_all(attn_mixed, "col", split_axis=1, concat_axis=0, tiled=True)
    attention = lax.psum(
        jnp.dot(mixed_cols, out_local, preferred_element_type=jnp.float32).astype(jnp.bfloat16),
        "col",
    ).astype(jnp.float32)
    residual = inputs_wide + attention + vector_rows[4]
    normed_two, scaled_two, inverse_two = normalize(residual, vector_rows[5], vector_rows[6])
    normed_two_low = normed_two.astype(jnp.bfloat16)
    ff_width = up_local.shape[1]
    bias_up = lax.dynamic_slice_in_dim(vector_rows[8:].reshape(-1), column * ff_width, ff_width, 0)
    up_linear = jnp.dot(normed_two_low, up_local, preferred_element_type=jnp.float32) + bias_up
    active, gelu_pullback = jax.vjp(gelu_tanh, up_linear)
    active_low = active.astype(jnp.bfloat16)
    branch = lax.psum_scatter(
        jnp.dot(active_low, down_local, preferred_element_type=jnp.float32).astype(jnp.bfloat16),
        "col",
        scatter_dimension=0,
        tiled=True,
    ).astype(jnp.float32)
    layer_out = (own_rows(residual) + branch + vector_rows[7]).astype(jnp.bfloat16)
    grad_down = contract_first(active_low, cotangent_all)
    grad_active = contract_last(cotangent_all, down_local)
    grad_up_linear = gelu_pullback(grad_active)[0]
    grad_up_low = grad_up_linear.astype(jnp.bfloat16)
    grad_up = contract_first(normed_two_low, grad_up_low)
    grad_normed_two = lax.psum(
        contract_last(grad_up_low, up_local).astype(jnp.bfloat16), "col"
    ).astype(jnp.float32)
    grad_residual = cotangent_all.astype(jnp.float32) + norm_back(
        grad_normed_two, scaled_two, inverse_two, vector_rows[5]
    )
    grad_residual_low = grad_residual.astype(jnp.bfloat16)
    grad_out = contract_first(mixed_cols, grad_residual_low)
    grad_mixed_cols = contract_last(grad_residual_low, out_local).astype(jnp.bfloat16)
    grad_mixed = lax.all_to_all(grad_mixed_cols, "col", split_axis=0, concat_axis=1, tiled=True)

    def head_backward(packed):
        head_index, log_total = packed
        attn_probs = jnp.exp(head_scores(head_index) - log_total)
        grad_head = head_slice(grad_mixed, head_index)
        grad_probs = contract_last(grad_head, head_slice(values, head_index))
        row_delta = jnp.sum(attn_probs * grad_probs, -1, keepdims=True)
        grad_scores = (attn_probs * (grad_probs - row_delta)).astype(jnp.bfloat16)
        grad_query = (
            jnp.dot(
                grad_scores, head_slice(key_rows, head_index), preferred_element_type=jnp.float32
            )
            * score_scale
        )
        grad_key = contract_first(grad_scores, head_slice(queries, head_index)) * score_scale
        grad_value = contract_first(attn_probs.astype(jnp.bfloat16), grad_head)
        return (grad_query, grad_key, grad_value)

    grads_query, grads_key, grads_value = lax.map(
        head_backward, (jnp.arange(head_count), log_totals)
    )
    query_own = grads_query.transpose(1, 0, 2).reshape(rows_here, model_width)
    key_part = grads_key.transpose(1, 0, 2).reshape(group_rows, model_width)
    value_part = grads_value.transpose(1, 0, 2).reshape(group_rows, model_width)
    query_part = lax.dynamic_update_slice_in_dim(
        jnp.zeros((group_rows, model_width), jnp.float32), query_own, own_start, 0
    )
    grad_projected = lax.psum_scatter(
        jnp.stack([query_part, key_part, value_part], 1).astype(jnp.bfloat16),
        "col",
        scatter_dimension=2,
        tiled=True,
    ).astype(jnp.float32)
    grad_projected_low = grad_projected.astype(jnp.bfloat16).reshape(group_rows, 3 * col_width)
    grad_qkv = contract_first(normed_low, grad_projected_low).reshape(model_width, 3, col_width)
    grad_normed_one = contract_last(grad_projected_low, qkv_flat)
    grad_vector = jnp.concatenate(
        [
            jnp.stack(
                [
                    jnp.sum(grad_normed_one * scaled_one, 0),
                    jnp.sum(grad_normed_one, 0),
                    placed(jnp.sum(grad_projected[:, 0], 0), column * col_width, model_width),
                    placed(jnp.sum(grad_projected[:, 2], 0), column * col_width, model_width),
                    jnp.sum(own_rows(grad_residual), 0),
                    jnp.sum(own_rows(grad_normed_two * scaled_two), 0),
                    jnp.sum(own_rows(grad_normed_two), 0),
                    jnp.sum(cotangent.astype(jnp.float32), 0),
                ]
            ),
            placed(jnp.sum(grad_up_linear, 0), column * ff_width, ff_width * col_count).reshape(
                -1, model_width
            ),
        ],
        0,
    )
    grad_normed_own, grad_vector_part = (
        lax.psum_scatter(
            grad_normed_one.astype(jnp.bfloat16), "col", scatter_dimension=0, tiled=True
        ).astype(jnp.float32),
        lax.psum_scatter(
            grad_vector.astype(jnp.bfloat16), "col", scatter_dimension=0, tiled=True
        ).astype(jnp.float32),
    )
    input_grad = own_rows(grad_residual) + norm_back(
        grad_normed_own, own_rows(scaled_one), own_rows(inverse_one), vector_rows[0]
    )
    sum_qkv, sum_out, sum_up, sum_down, sum_vector = (
        lax.psum_scatter(grad_qkv, ("dp", "row"), scatter_dimension=0, tiled=True),
        lax.psum_scatter(grad_out, ("dp", "row"), scatter_dimension=1, tiled=True),
        lax.psum_scatter(grad_up, ("dp", "row"), scatter_dimension=0, tiled=True),
        lax.psum_scatter(grad_down, ("dp", "row"), scatter_dimension=1, tiled=True),
        lax.psum_scatter(grad_vector_part, ("dp", "row"), scatter_dimension=1, tiled=True),
    )
    qkv_m, qkv_v, qkv_w = adamw(
        qkv_weight, sum_qkv, qkv_first, qkv_second, 1.5 * D ** (-0.5), decay_rate
    )
    out_m, out_v, out_w = adamw(
        out_weight, sum_out, out_first, out_second, 1.5 * (D // 64) ** (-0.5), decay_rate
    )
    up_m, up_v, up_w = adamw(up_weight, sum_up, up_first, up_second, 1.5 * D ** (-0.5), decay_rate)
    down_m, down_v, down_w = adamw(
        down_weight, sum_down, down_first, down_second, 1.5 * FF ** (-0.5), decay_rate
    )
    vec_m, vec_v, vec_w = adamw(vectors, sum_vector, vectors_first, vectors_second, 0.5, 0.0)
    return (
        layer_out,
        input_grad,
        qkv_m,
        qkv_v,
        qkv_w,
        out_m,
        out_v,
        out_w,
        up_m,
        up_v,
        up_w,
        down_m,
        down_v,
        down_w,
        vec_m,
        vec_v,
        vec_w,
    )


def solution(mesh):
    return jax.shard_map(
        local,
        mesh=mesh,
        in_specs=(
            P(("dp", "row", "col"), None),
            P(("dp", "row", "col"), None),
            P(("dp", "row"), None),
            P(("dp", "row"), None, "col"),
            P("col", ("dp", "row")),
            P(("dp", "row"), "col"),
            P("col", ("dp", "row")),
            P("col", ("dp", "row")),
            P(("dp", "row"), None, "col"),
            P("col", ("dp", "row")),
            P(("dp", "row"), "col"),
            P("col", ("dp", "row")),
            P("col", ("dp", "row")),
            P(("dp", "row"), None, "col"),
            P("col", ("dp", "row")),
            P(("dp", "row"), "col"),
            P("col", ("dp", "row")),
            P("col", ("dp", "row")),
        ),
        out_specs=(
            P(("dp", "row", "col"), None),
            P(("dp", "row", "col"), None),
            P(("dp", "row"), None, "col"),
            P(("dp", "row"), None, "col"),
            P(("dp", "row"), None, "col"),
            P("col", ("dp", "row")),
            P("col", ("dp", "row")),
            P("col", ("dp", "row")),
            P(("dp", "row"), "col"),
            P(("dp", "row"), "col"),
            P(("dp", "row"), "col"),
            P("col", ("dp", "row")),
            P("col", ("dp", "row")),
            P("col", ("dp", "row")),
            P("col", ("dp", "row")),
            P("col", ("dp", "row")),
            P("col", ("dp", "row")),
        ),
        check_vma=False,
    )
```

profile of v0, /device:TPU:0, one launch (start us, length us, event | category | flops | bytes accessed | tf_op | source)
XLA Modules:
  0.0 1658.2 jit_solution(13977244099936303672)
XLA Ops:
  10.6 28.7 %all-gather = bf16[8,136,3]{1,2,0:T(4,128)(2,1)S(1)} all-gather(bf16[1,136,3]{1,2,0:T(4,128)(2,1)S(1)} %convert_bitcast_fusion), channel_id=1, replica_groups=mesh['dp'=2,'row'=4,'col'=4] {'dp','row'}, dimensions={0}, use_global_device_ids=true | all-gather | bytes 7344 | tf_op jit(solution)/shard_map/all_gather | solution.py:101
  39.4 5.2 all-gather.1
  45.4 21.8 %all-gather.11.cloned.1.call-done = bf16[1088,3,272]{2,0,1:T(8,128)(2,1)} async-done(((bf16[136,3,272]{2,0,1:T(8,128)(2,1)}), bf16[1088,3,272]{2,0,1:T(8,128)(2,1)}) %all-gather.11.cloned.1.call-update) | async-done | bytes 1775632 | tf_op jit(solution)/shard_map/all_gather | solution.py:97
  70.2 33.1 %all-gather.9.cloned.1.call-done = bf16[2048,1088]{0,1:T(8,128)(2,1)} async-done(((bf16[512,1088]{0,1:T(8,128)(2,1)}), bf16[2048,1088]{0,1:T(8,128)(2,1)}) %all-gather.9.cloned.1.call-update) | async-done | bytes 4456464 | tf_op jit(solution)/shard_map/all_gather | solution.py:104
  108.2 6.5 add_convert_fusion.2
  114.9 86.6 %all-gather.13.cloned.1.call-done = bf16[2048,3,1088]{0,2,1:T(8,128)(2,1)} async-done(((bf16[2048,3,272]{0,2,1:T(8,128)(2,1)}), bf16[2048,3,1088]{0,2,1:T(8,128)(2,1)}) %all-gather.13.cloned.1.call-update) | async-done | bytes 13369360 | tf_op jit(solution)/shard_map/all_gather | solution.py:125
  203.5 8.8 slice_bitcast_fusion
  212.3 6.5 copy.56
  218.9 6.6 copy.57
  226.6 125.3 %while.28 = (s32[]{:T(128)}, bf16[17,512,64]{1,2,0:T(8,128)(2,1)}, f32[17,512,1]{1,2,0:T(1,128)S(1)}, s32[17]{0:T(128)S(1)}, bf16[512,1088]{1,0:T(8,128)(2,1)S(1...) while((s32[]{:T(128)}, bf16[17,512,64]{1,2,0:T(8,128)(2,1)}, ...), condition=%wide.region_5.6_spmd.clone, body=%wide.region_2.5_spmd.clone.sunk | while | flops 281017856 | bytes 13935843 | solution.py:159
  351.8 3.5 all-to-all-start
  355.4 34.3 %all_gather.32 = bf16[272,1088]{0,1:T(8,128)(2,1)S(1)} all-gather(bf16[272,136]{0,1:T(8,128)(2,1)S(1)} %convert_element_type.112), channel_id=1, replica_groups=mesh['dp'=2,'row'=4,'col'=4] {'dp','row'}, dimensions={1}, use_global_device_ids=true | all-gather | bytes 665856 | tf_op jit(solution)/shard_map/all_gather | solution.py:98
  390.9 4.5 convolution_convert_fusion.2
  398.1 88.5 %all-reduce.8.cloned.1.call-done = bf16[2048,1088]{0,1:T(8,128)(2,1)} async-done(((bf16[2048,1088]{0,1:T(8,128)(2,1)}), bf16[2048,1088]{0,1:T(8,128)(2,1)}) %all-reduce.8.cloned.1.call-update) | async-done | bytes 4456464 | tf_op jit(solution)/shard_map/psum | solution.py:162
  486.6 6.1 fusion.82
  496.1 4.5 subtract_multiply_fusion
  500.6 42.2 %all-gather.15.cloned.1.call-done = bf16[1088,1088]{1,0:T(8,128)(2,1)} async-done(((bf16[136,1088]{1,0:T(8,128)(2,1)}), bf16[1088,1088]{1,0:T(8,128)(2,1)}) %all-gather.15.cloned.1.call-update) | async-done | bytes 2367504 | tf_op jit(solution)/shard_map/all_gather | solution.py:99
  542.9 11.9 convolution_add_fusion
  554.8 24.1 %all-gather.19.cloned.1.call-done = bf16[2048,1088]{0,1:T(8,128)(2,1)} async-done(((bf16[512,1088]{0,1:T(8,128)(2,1)}), bf16[2048,1088]{0,1:T(8,128)(2,1)}) %all-gather.19.cloned.1.call-update) | async-done | bytes 4456464 | tf_op jit(solution)/shard_map/all_gather | solution.py:105
  578.8 13.2 fusion.74
  592.1 100.0 %reduce-scatter.27.cloned.1.call-done = f32[1088,136]{0,1:T(8,128)} async-done(((f32[1088,1088]{0,1:T(8,128)}), f32[1088,136]{0,1:T(8,128)}) %reduce-scatter.27.cloned.1.call-update) | async-done | bytes 591888
  695.2 52.7 %all-gather.17.cloned.1.call-done = bf16[1088,1088]{0,1:T(8,128)(2,1)} async-done(((bf16[1088,136]{0,1:T(8,128)(2,1)}), bf16[1088,1088]{0,1:T(8,128)(2,1)}) %all-gather.17.cloned.1.call-update) | async-done | bytes 2367504 | tf_op jit(solution)/shard_map/all_gather | solution.py:100
  748.0 16.8 %fusion.76 = (bf16[1088]{0:T(1024)(128)(2,1)}, bf16[2048,1088]{0,1:T(8,128)(2,1)S(1)}) fusion(f32[2048,1088]{0,1:T(8,128)} %convolution_add_fusion, bf16[2048,1088]{0,1:T(8,128)(2,1)} %all-gather.19.cloned.1.call-done, bf16[1088,1088]{0,1:T(8,128)(2,1)} %all-gather.17.cloned.1.call-done), kind=kOutput, calls=%fused_computation.167 | convolution fusion | flops 4895407104 | bytes 20195456 | tf_op jit(solution)/shard_map/dot_general | solution.py:27
  766.8 7.6 convolution_convert_fusion
  774.4 88.5 %all-reduce.10.cloned.1.call-done = bf16[2048,1088]{0,1:T(8,128)(2,1)} async-done(((bf16[2048,1088]{0,1:T(8,128)(2,1)}), bf16[2048,1088]{0,1:T(8,128)(2,1)}) %all-reduce.10.cloned.1.call-update) | async-done | bytes 4456464 | tf_op jit(solution)/shard_map/psum | solution.py:186
  862.9 6.2 multiply_reduce_fusion.3
  869.1 6.9 multiply_add_fusion
  880.6 3.5 all-to-all-start.1
  884.2 15.1 all-to-all-done.1
  900.4 208.5 %while.29 = (s32[]{:T(128)}, bf16[17,512,64]{1,2,0:T(8,128)(2,1)S(1)}, bf16[17,2048,64]{1,2,0:T(8,128)(2,1)}, bf16[17,2048,64]{1,2,0:T(8,128)(2,1)}, s32[17]{0:T...) while((s32[]{:T(128)}, ...), condition=%wide.region_15.16_spmd.clone, body=%wide.region_13.15_spmd.clone.sunk | while | flops 685932032 | bytes 34638088 | solution.py:214
  903.5 3.3 multiply_reduce_fusion.6
  915.8 3.3 multiply_reduce_fusion.6
  928.0 3.3 multiply_reduce_fusion.6
  940.3 3.3 multiply_reduce_fusion.6
  952.6 3.3 multiply_reduce_fusion.6
  964.8 3.3 multiply_reduce_fusion.6
  977.1 3.3 multiply_reduce_fusion.6
  989.4 3.3 multiply_reduce_fusion.6
  1001.6 3.3 multiply_reduce_fusion.6
  1013.9 3.3 multiply_reduce_fusion.6
  1026.1 3.3 multiply_reduce_fusion.6
  1038.4 3.3 multiply_reduce_fusion.6
  1050.7 3.3 multiply_reduce_fusion.6
  1063.0 3.3 multiply_reduce_fusion.6
  1075.2 3.3 multiply_reduce_fusion.6
  1087.5 3.3 multiply_reduce_fusion.6
  1099.8 3.3 multiply_reduce_fusion.6
  1111.2 8.3 pad_maximum_fusion
  1120.7 7.2 fusion.52
  1128.0 12.9 convolution_convert_fusion.1
  1141.7 11.5 fusion.55
  1153.3 70.7 %reduce-scatter.17.cloned.1.call-done = bf16[2048,3,272]{0,2,1:T(8,128)(2,1)} async-done(((bf16[2048,3,1088]{0,2,1:T(8,128)(2,1)}), bf16[2048,3,272]{0,2,1:T(8,128)(2,1)}) %reduce-scatter.17.cloned.1.call-update) | async-done | bytes 3342352 | tf_op jit(solution)/shard_map/reduce_scatter | solution.py:223
  1223.9 10.8 fusion.48
  1236.8 9.7 bitcast_convert_fusion
  1251.0 3.3 convert_element_type.125
  1256.8 37.0 %reduce-scatter.23.cloned.1.call-done = f32[272,136]{0,1:T(8,128)} async-done(((f32[272,1088]{0,1:T(8,128)}), f32[272,136]{0,1:T(8,128)}) %reduce-scatter.23.cloned.1.call-update) | async-done | bytes 147984
  1295.6 45.5 %reduce-scatter.15.cloned.1.call-done = bf16[512,1088]{0,1:T(8,128)(2,1)} async-done(((bf16[2048,1088]{0,1:T(8,128)(2,1)}), bf16[512,1088]{0,1:T(8,128)(2,1)}) %reduce-scatter.15.cloned.1.call-update) | async-done | bytes 1114128 | tf_op jit(solution)/shard_map/reduce_scatter | solution.py:174
  1344.4 100.7 %reduce-scatter.25.cloned.1.call-done = f32[136,1088]{1,0:T(8,128)} async-done(((f32[1088,1088]{1,0:T(8,128)}), f32[136,1088]{1,0:T(8,128)}) %reduce-scatter.25.cloned.1.call-update) | async-done | bytes 591888
  1447.8 10.3 bitcast_reduce_fusion
  1459.8 87.6 %reduce-scatter.21.cloned.1.call-done = f32[136,3,272]{2,0,1:T(8,128)} async-done(((f32[1088,3,272]{2,0,1:T(8,128)}), f32[136,3,272]{2,0,1:T(8,128)}) %reduce-scatter.21.cloned.1.call-update) | async-done | bytes 443920 | tf_op jit(solution)/shard_map/reduce_scatter | solution.py:264
  1550.0 45.2 %reduce-scatter.19.cloned.1.call-done = bf16[512,1088]{0,1:T(8,128)(2,1)} async-done(((bf16[2048,1088]{0,1:T(8,128)(2,1)}), bf16[512,1088]{0,1:T(8,128)(2,1)}) %reduce-scatter.19.cloned.1.call-update) | async-done | bytes 1114128 | tf_op jit(solution)/shard_map/reduce_scatter | solution.py:253
  1597.7 4.8 dynamic-slice_reduce_fusion.1
  1602.5 10.5 all-reduce.3
  1613.1 37.5 %all-reduce.4 = f32[3,1088]{1,0:T(4,128)S(1)} all-reduce(f32[3,1088]{1,0:T(4,128)S(1)} %dynamic-slice_convert_fusion), channel_id=10, replica_groups=mesh['dp'=2,'row'=4,'col'=4] {'dp','row'}, use_global_device_ids=true, to_apply=%region_34.35.clone | all-reduce | flops 3264 | bytes 26112
  (414 shorter events, 315.0 us)
Async XLA Ops:
  7.2 60.0 %all-gather.11.cloned.1.call-start = ((), (), s32[]{:S(2)}) async-start(), calls=%async_computation.10 | async-start | bytes 2820096 | tf_op jit(solution)/shard_map/all_gather | solution.py:97
  9.1 94.2 %all-gather.9.cloned.1.call-start = ((), (), s32[]{:S(2)}) async-start(), calls=%async_computation.9 | async-start | bytes 5570560 | tf_op jit(solution)/shard_map/all_gather | solution.py:104
  9.8 191.6 %all-gather.13.cloned.1.call-start = ((), (), s32[]{:S(2)}) async-start(), calls=%async_computation.11 | async-start | bytes 16711680 | tf_op jit(solution)/shard_map/all_gather | solution.py:125
  45.3 62.8 %copy-start.23 = (f32[1088]{0:T(1024)}, f32[1088]{0:T(1024)S(1)}, u32[]{:S(2)}) copy-start(f32[1088]{0:T(1024)S(1)} %get-tuple-element.374) | copy-start | bytes 13060
  45.3 62.8 %copy-start.31 = (f32[1088]{0:T(1024)}, f32[1088]{0:T(1024)S(1)}, u32[]{:S(2)}) copy-start(f32[1088]{0:T(1024)S(1)} %get-tuple-element.375) | copy-start | bytes 13060
  45.3 497.6 %copy-start.33 = (f32[1088]{0:T(1024)}, f32[1088]{0:T(1024)S(1)}, u32[]{:S(2)}) copy-start(f32[1088]{0:T(1024)S(1)} %get-tuple-element.378) | copy-start | bytes 13060
  103.3 3.6 copy-start.2
  106.9 7.8 copy-start.25
  108.1 6.6 copy-start.27
  108.2 6.6 copy-start.35
  226.5 128.8 %copy-start.14 = (f32[272,136]{0,1:T(8,128)S(1)}, f32[272,136]{0,1:T(8,128)}, u32[]{:S(2)}) copy-start(f32[272,136]{0,1:T(8,128)} %param.26) | copy-start | bytes 443908
  351.8 37.9 %all-to-all-start = ((bf16[512,4,272]{0,2,1:T(8,128)(2,1)}), bf16[512,4,272]{0,2,1:T(8,128)(2,1)S(1)}, u32[]{:S(2)}, u32[]{:S(2)}) async-start(bf16[512,4,272]{0,2,1:T(8,128)(2,1)} %bitcast.12), calls=%async_computation | async-start | bytes 2228224 | tf_op jit(solution)/shard_map/all_to_all | solution.py:161
  355.3 131.2 %all-reduce.8.cloned.1.call-start = ((), (), s32[]{:S(2)}) async-start(), calls=%async_computation.12 | async-start | bytes 8912896 | tf_op jit(solution)/shard_map/psum | solution.py:162
  389.9 1.0 copy-start.4
  395.4 1.1 copy-start.11
  395.4 147.4 %all-gather.15.cloned.1.call-start = ((), (), s32[]{:S(2)}) async-start(), calls=%async_computation.13 | async-start | bytes 2820096 | tf_op jit(solution)/shard_map/all_gather | solution.py:99
  397.3 181.6 %all-gather.19.cloned.1.call-start = ((), (), s32[]{:S(2)}) async-start(), calls=%async_computation.16 | async-start | bytes 5570560 | tf_op jit(solution)/shard_map/all_gather | solution.py:105
  397.9 294.2 %reduce-scatter.27.cloned.1.call-start = ((), (), s32[]{:S(2)}) async-start(), calls=%async_computation.23 | async-start | bytes 5640192
  492.7 3.4 copy-start
  592.0 100.1 %copy-start.16 = (f32[1088,136]{0,1:T(8,128)S(1)}, f32[1088,136]{0,1:T(8,128)}, u32[]{:S(2)}) copy-start(f32[1088,136]{0,1:T(8,128)} %param.28) | copy-start | bytes 1775620
  592.0 156.0 %all-gather.17.cloned.1.call-start = ((), (), s32[]{:S(2)}) async-start(), calls=%async_computation.14 | async-start | bytes 2820096 | tf_op jit(solution)/shard_map/all_gather | solution.py:100
  695.2 167.7 %all-reduce.10.cloned.1.call-start = ((), (), s32[]{:S(2)}) async-start(), calls=%async_computation.17 | async-start | bytes 8912896 | tf_op jit(solution)/shard_map/psum | solution.py:186
  748.0 18.8 %copy-start.39 = (bf16[1088,1088]{1,0:T(8,128)(2,1)S(1)}, bf16[1088,1088]{1,0:T(8,128)(2,1)}, u32[]{:S(2)}) copy-start(bf16[1088,1088]{1,0:T(8,128)(2,1)} %all-gather.15.cloned.1.call-done) | copy-start | bytes 7102468
  764.8 2.0 copy-start.42
  862.9 6.2 copy-start.3
  876.0 3.5 copy-start.1
  880.6 18.7 %all-to-all-start.1 = ((bf16[4,512,272]{1,2,0:T(8,128)(2,1)}), bf16[4,512,272]{1,2,0:T(8,128)(2,1)S(1)}, u32[]{:S(2)}, u32[]{:S(2)}) async-start(bf16[4,512,272]{1,2,0:T(8,128)(2,1)} %bitcast.103), calls=%async_computation.2 | async-start | bytes 2228224 | tf_op jit(solution)/shard_map/all_to_all | solution.py:195
  884.1 339.8 %reduce-scatter.17.cloned.1.call-start = ((), (), s32[]{:S(2)}) async-start(), calls=%async_computation.18 | async-start | bytes 16711680 | tf_op jit(solution)/shard_map/reduce_scatter | solution.py:223
  899.3 1.0 copy-start.10
  1108.9 2.3 copy-start.6
  1119.5 1.2 copy-start.5
  1119.5 174.3 %reduce-scatter.23.cloned.1.call-start = ((), (), s32[]{:S(2)}) async-start(), calls=%async_computation.21 | async-start | bytes 1880064
  1128.0 213.2 %reduce-scatter.15.cloned.1.call-start = ((), (), s32[]{:S(2)}) async-start(), calls=%async_computation.15 | async-start | bytes 5570560 | tf_op jit(solution)/shard_map/reduce_scatter | solution.py:174
  1141.0 0.7 copy-start.34
  1141.0 304.2 %reduce-scatter.25.cloned.1.call-start = ((), (), s32[]{:S(2)}) async-start(), calls=%async_computation.22 | async-start | bytes 5640192
  1153.2 70.8 %copy-start.24 = (f32[1088]{0:T(1024)S(1)}, f32[1088]{0:T(1024)}, u32[]{:S(2)}) copy-start(f32[1088]{0:T(1024)} %copy-done.23) | copy-start | bytes 13060
  1153.2 70.8 %copy-start.26 = (f32[2048]{0:T(1024)S(1)}, f32[2048]{0:T(1024)}, u32[]{:S(2)}) copy-start(f32[2048]{0:T(1024)} %copy-done.25) | copy-start | bytes 24580
  1153.2 70.8 %copy-start.28 = (f32[2048]{0:T(1024)S(1)}, f32[2048]{0:T(1024)}, u32[]{:S(2)}) copy-start(f32[2048]{0:T(1024)} %copy-done.27) | copy-start | bytes 24580
  1153.2 70.7 %copy-start.32 = (f32[1088]{0:T(1024)S(1)}, f32[1088]{0:T(1024)}, u32[]{:S(2)}) copy-start(f32[1088]{0:T(1024)} %copy-done.31) | copy-start | bytes 13060
  1153.2 394.2 %reduce-scatter.21.cloned.1.call-start = ((), (), s32[]{:S(2)}) async-start(), calls=%async_computation.20 | async-start | bytes 5640192 | tf_op jit(solution)/shard_map/reduce_scatter | solution.py:264
  1234.8 2.1 copy-start.8
  1234.8 360.4 %reduce-scatter.19.cloned.1.call-start = ((), (), s32[]{:S(2)}) async-start(), calls=%async_computation.19 | async-start | bytes 5570560 | tf_op jit(solution)/shard_map/reduce_scatter | solution.py:253
  1246.6 1.2 copy-start.7
  1246.6 1.5 copy-start.41
  1246.6 2.1 copy-start.40
  1246.6 4.1 copy-start.38
  1254.4 39.4 %copy-start.15 = (f32[272,136]{0,1:T(8,128)S(1)}, f32[272,136]{0,1:T(8,128)}, u32[]{:S(2)}) copy-start(f32[272,136]{0,1:T(8,128)} %param.26) | copy-start | bytes 443908
  1254.4 39.4 %copy-start.21 = (f32[272,136]{0,1:T(8,128)S(1)}, f32[272,136]{0,1:T(8,128)}, u32[]{:S(2)}) copy-start(f32[272,136]{0,1:T(8,128)} %param.36) | copy-start | bytes 443908
  1254.4 39.4 %copy-start.22 = (f32[272,136]{0,1:T(8,128)S(1)}, f32[272,136]{0,1:T(8,128)}, u32[]{:S(2)}) copy-start(f32[272,136]{0,1:T(8,128)} %param.31) | copy-start | bytes 443908
  1254.4 86.7 %copy-start.29 = (f32[1088]{0:T(1024)S(1)}, f32[1088]{0:T(1024)}, u32[]{:S(2)}) copy-start(f32[1088]{0:T(1024)} %get-tuple-element.379) | copy-start | bytes 13060
  1254.4 190.7 %copy-start.12 = (f32[136,1088]{1,0:T(8,128)S(1)}, f32[136,1088]{1,0:T(8,128)}, u32[]{:S(2)}) copy-start(f32[136,1088]{1,0:T(8,128)} %param.27) | copy-start | bytes 1775620
  1254.4 190.7 %copy-start.17 = (f32[136,1088]{1,0:T(8,128)S(1)}, f32[136,1088]{1,0:T(8,128)}, u32[]{:S(2)}) copy-start(f32[136,1088]{1,0:T(8,128)} %param.37) | copy-start | bytes 1775620
  1254.4 190.7 %copy-start.18 = (f32[136,1088]{1,0:T(8,128)S(1)}, f32[136,1088]{1,0:T(8,128)}, u32[]{:S(2)}) copy-start(f32[136,1088]{1,0:T(8,128)} %param.32) | copy-start | bytes 1775620
  1447.8 10.4 copy-start.9
  1459.0 88.4 %copy-start.13 = (f32[136,3,272]{2,0,1:T(8,128)S(1)}, f32[136,3,272]{2,0,1:T(8,128)}, u32[]{:S(2)}) copy-start(f32[136,3,272]{2,0,1:T(8,128)} %param.25) | copy-start | bytes 1331716
  1459.0 88.3 %copy-start.19 = (f32[136,3,272]{2,0,1:T(8,128)S(1)}, f32[136,3,272]{2,0,1:T(8,128)}, u32[]{:S(2)}) copy-start(f32[136,3,272]{2,0,1:T(8,128)} %param.35) | copy-start | bytes 1331716
  1459.0 88.3 %copy-start.20 = (f32[136,3,272]{2,0,1:T(8,128)S(1)}, f32[136,3,272]{2,0,1:T(8,128)}, u32[]{:S(2)}) copy-start(f32[136,3,272]{2,0,1:T(8,128)} %param.30) | copy-start | bytes 1331716
  1597.6 53.0 %copy-start.30 = (f32[3,136]{1,0:T(4,128)S(1)}, f32[3,136]{1,0:T(4,128)}, u32[]{:S(2)}) copy-start(f32[3,136]{1,0:T(4,128)} %param.29) | copy-start | bytes 4900
  1597.6 52.9 %copy-start.36 = (f32[3,136]{1,0:T(4,128)S(1)}, f32[3,136]{1,0:T(4,128)}, u32[]{:S(2)}) copy-start(f32[3,136]{1,0:T(4,128)} %param.39) | copy-start | bytes 4900
  1597.6 52.9 %copy-start.37 = (f32[3,136]{1,0:T(4,128)S(1)}, f32[3,136]{1,0:T(4,128)}, u32[]{:S(2)}) copy-start(f32[3,136]{1,0:T(4,128)} %param.34) | copy-start | bytes 4900
Sparse Core Ops, SparseCore 0:
  10.7 56.4 all-gather.10
  68.8 34.4 all-gather.8
  114.8 86.5 all-gather.12
  395.6 90.9 all-reduce.7
  489.1 53.7 all-gather.14
  544.3 34.5 all-gather.18
  592.1 99.8 reduce-scatter.26
  695.3 52.6 all-gather.16
  774.6 88.2 all-reduce.9
  1119.6 104.2 reduce-scatter.16
  1228.4 65.3 reduce-scatter.22
  1296.2 44.9 reduce-scatter.14
  1345.2 99.8 reduce-scatter.24
  1448.6 98.6 reduce-scatter.20
  1549.9 45.2 reduce-scatter.18
where the time goes:
time: 1670 us; the launch traced here: 1660 us
  waiting for transfers between devices  941 us (56%)
  matrix products  386 us (23%)
  blocking collectives  116 us (7%)
  other arithmetic  99.1 us (6%)
  local copies, waits for them, and re-layouts  69.7 us (4%)
  loops' own time  22.8 us (1%)
    unnamed x18, waiting for transfers between devices  239 us
    dot_general x55, matrix products, contract_last(): lax.dot_general(left, right, (((1,), (1,)), ((), ())), preferred_element_...  170 us
    dot_general x38, matrix products, contract_first(): lax.dot_general(left, right, (((0,), (0,)), ((), ())), preferred_element_...  99.7 us
    psum x1, waiting for transfers between devices, local(): lax.psum(jnp.dot(mixed_cols, out_local, preferred_element_type=jnp.float3...  88.5 us
    psum x1, waiting for transfers between devices, local(): lax.psum(contract_last(grad_up_low, up_local).astype(jnp.bfloat16), 'col')  88.5 us
    reduce_scatter x1, waiting for transfers between devices, local(): lax.psum_scatter(grad_qkv, ('dp', 'row'), scatter_dimension=0, tiled=True)  87.6 us
    all_gather x1, waiting for transfers between devices, local(): projected_all = lax.all_gather(projected, 'col', axis=2, tiled=True)  86.6 us
    reduce_scatter x1, waiting for transfers between devices, local(): lax.psum_scatter(jnp.stack([query_part, key_part, value_part], 1).astype(...  70.7 us
  transfers between devices with their start and end apart: 17, of which 16 were waited for; matrix products, arithmetic and copies ran while one was open for 7% of the time, Pallas kernels for 0%

commit v1 on v0

v1 whole, which is shorter than its diff:
```python
import functools

import jax
import jax.numpy as jnp
from jax import lax
from jax.experimental import pallas as pl
from jax.experimental.pallas import tpu as pltpu
from jax.sharding import PartitionSpec as P

D = 1088
HEAD_DIM = 64
FF = 4352
SEQ = 1024
STEP = 5

LANES = 128
VEC_ROWS = 8


beta_one = 0.9
beta_two = 0.999
epsilon = 1e-08
decay_rate = 0.1
masked_score = -1000000000.0

f32 = jnp.float32
bf16 = jnp.bfloat16


def contract(left, right, left_dim, right_dim):
    return lax.dot_general(
        left, right, (((left_dim,), (right_dim,)), ((), ())), preferred_element_type=f32
    )


def contract_first(left, right):
    return contract(left, right, 0, 0)


def contract_last(left, right):
    return contract(left, right, 1, 1)


def normalize(rows, gain, shift):
    row_mean = jnp.mean(rows, -1, keepdims=True)
    centred = rows - row_mean
    inverse = lax.rsqrt(jnp.mean(centred * centred, -1, keepdims=True) + 1e-05)
    scaled = centred * inverse
    return (scaled * gain + shift, scaled, inverse)


def norm_back(grad_out, scaled, inverse, gain):
    grad_scaled = grad_out * gain
    return inverse * (
        grad_scaled
        - jnp.mean(grad_scaled, -1, keepdims=True)
        - scaled * jnp.mean(grad_scaled * scaled, -1, keepdims=True)
    )


def gelu_tanh(values):
    return jax.nn.gelu(values, approximate=True)


def adamw(weight, gradient, moment_one, moment_two, step_rate, shrink):
    moment_one = beta_one * moment_one + (1.0 - beta_one) * gradient
    moment_two = beta_two * moment_two + (1.0 - beta_two) * gradient * gradient
    update = (
        moment_one
        / (1.0 - beta_one**STEP)
        / (jnp.sqrt(moment_two / (1.0 - beta_two**STEP)) + epsilon)
    )
    return (moment_one, moment_two, weight - step_rate * (update + shrink * weight))


def mask_tables(kseg_own, kseg_oth, qseg, bias_own, bias_oth):
    count = bias_own.shape[0]
    key_place = lax.broadcasted_iota(jnp.int32, (count, count), 0)
    query_place = lax.broadcasted_iota(jnp.int32, (count, count), 1)
    same = kseg_own[...] == qseg[...]
    bias_own[...] = jnp.where(same & (key_place <= query_place), 0.0, masked_score)
    bias_oth[...] = jnp.where(kseg_oth[...] == qseg[...], 0.0, masked_score)


def head_lanes(block, half):
    lane = lax.broadcasted_iota(jnp.int32, block.shape, 1)
    return jnp.where((lane // HEAD_DIM) == half, block, jnp.zeros_like(block))


def attention_forward(
    later, qseg, kseg_own, kseg_oth, q, k_own, v_own, k_oth, v_oth, out, lse, bias_own, bias_oth
):
    pair = pl.program_id(0)
    count = q.shape[0]
    step = count // 2

    @pl.when(pair == 0)
    def _():
        mask_tables(kseg_own, kseg_oth, qseg, bias_own, bias_oth)

    def body(with_other):
        queries = q[...] * jnp.asarray(HEAD_DIM**-0.5, bf16)
        values_own = v_own[...].astype(f32).T.astype(bf16)
        values_oth = v_oth[...].astype(f32).T.astype(bf16) if with_other else None
        for part in range(2):
            cols = slice(part * step, (part + 1) * step)
            seen = (part + 1) * step
            pieces = []
            for half in range(2):
                q_head = head_lanes(queries[cols], half)
                rows = slice(half * HEAD_DIM, (half + 1) * HEAD_DIM)
                s_own = contract_last(k_own[:seen], q_head) + bias_own[:seen, cols]
                top = jnp.max(s_own, 0, keepdims=True)
                if with_other:
                    s_oth = contract_last(k_oth[...], q_head) + bias_oth[:, cols]
                    top = jnp.maximum(top, jnp.max(s_oth, 0, keepdims=True))
                e_own = jnp.exp(s_own - top)
                total = jnp.sum(e_own, 0, keepdims=True)
                mixed = jnp.dot(
                    values_own[rows, :seen], e_own.astype(bf16), preferred_element_type=f32
                )
                if with_other:
                    e_oth = jnp.exp(s_oth - top)
                    total = total + jnp.sum(e_oth, 0, keepdims=True)
                    mixed = mixed + jnp.dot(
                        values_oth[rows], e_oth.astype(bf16), preferred_element_type=f32
                    )
                lse[0, half : half + 1, cols] = top + jnp.log(total)
                pieces.append(mixed / total)
            out[cols] = jnp.concatenate(pieces, 0).T.astype(bf16)

    @pl.when(later[0] == 1)
    def _():
        body(True)

    @pl.when(later[0] == 0)
    def _():
        body(False)


def attention_backward(
    later, qseg, kseg_own, kseg_oth, q, k_own, v_own, k_oth, v_oth, grad, out, lse,
    dq, dk_own, dv_own, dk_oth, dv_oth, bias_own, bias_oth,
):
    pair = pl.program_id(0)
    count = q.shape[0]
    step = count // 2

    @pl.when(pair == 0)
    def _():
        mask_tables(kseg_own, kseg_oth, qseg, bias_own, bias_oth)

    def body(with_other):
        scale = jnp.asarray(HEAD_DIM**-0.5, bf16)
        queries = q[...] * scale
        keys_own = k_own[...].astype(f32).T.astype(bf16)
        keys_oth = k_oth[...].astype(f32).T.astype(bf16) if with_other else None
        products = (grad[...].astype(f32) * out[...].astype(f32)).T
        dk_a = [jnp.zeros((step, LANES), f32) for _ in range(2)]
        dv_a = [jnp.zeros((step, LANES), f32) for _ in range(2)]
        dk_b = jnp.zeros((count, LANES), f32)
        dv_b = jnp.zeros((count, LANES), f32)
        for part in range(2):
            cols = slice(part * step, (part + 1) * step)
            pieces = []
            for half in range(2):
                q_head = head_lanes(queries[cols], half)
                g_head = head_lanes(grad[cols], half)
                rows = slice(half * HEAD_DIM, (half + 1) * HEAD_DIM)
                delta = jnp.sum(products[rows, cols], 0, keepdims=True)
                log_total = lse[0, half : half + 1, cols]

                def block(keys, values, bias):
                    probs = jnp.exp(contract_last(keys, q_head) + bias - log_total)
                    d_probs = contract_last(values, g_head)
                    d_scores = (probs * (d_probs - delta)).astype(bf16)
                    dk = jnp.dot(d_scores, q_head, preferred_element_type=f32)
                    dv = jnp.dot(probs.astype(bf16), g_head, preferred_element_type=f32)
                    return (d_scores, dk, dv)

                d_query = jnp.zeros((HEAD_DIM, step), f32)
                for chunk in range(part + 1):
                    span = slice(chunk * step, (chunk + 1) * step)
                    d_scores, dk, dv = block(k_own[span], v_own[span], bias_own[span, cols])
                    dk_a[chunk] = dk_a[chunk] + dk
                    dv_a[chunk] = dv_a[chunk] + dv
                    d_query = d_query + jnp.dot(
                        keys_own[rows, span], d_scores, preferred_element_type=f32
                    )
                if with_other:
                    d_scores, dk, dv = block(k_oth[...], v_oth[...], bias_oth[:, cols])
                    dk_b = dk_b + dk
                    dv_b = dv_b + dv
                    d_query = d_query + jnp.dot(
                        keys_oth[rows], d_scores, preferred_element_type=f32
                    )
                pieces.append(d_query)
            dq[cols] = (jnp.concatenate(pieces, 0).T * HEAD_DIM**-0.5).astype(bf16)
        for chunk in range(2):
            span = slice(chunk * step, (chunk + 1) * step)
            dk_own[span] = dk_a[chunk].astype(bf16)
            dv_own[span] = dv_a[chunk].astype(bf16)
        dk_oth[...] = dk_b.astype(bf16)
        dv_oth[...] = dv_b.astype(bf16)

    @pl.when(later[0] == 1)
    def _():
        body(True)

    @pl.when(later[0] == 0)
    def _():
        body(False)


def attention_specs(count, pairs):
    def whole(shape):
        return pl.BlockSpec(shape, lambda p, later: (0,) * len(shape))

    def lanes(start):
        return pl.BlockSpec((count, LANES), lambda p, later: (0, start + p))

    segments = [whole((1, count)), whole((count, 1)), whole((count, 1))]
    projected = [lanes(0), lanes(pairs), lanes(2 * pairs), lanes(0), lanes(pairs)]
    totals = pl.BlockSpec((1, 2, count), lambda p, later: (p, 0, 0))
    return segments, projected, lanes(0), totals


def attend(later, labels, projected, others):
    count = projected.shape[0]
    pairs = projected.shape[1] // (3 * LANES)
    segments, blocks, wide, totals = attention_specs(count, pairs)
    work = count * count * LANES * pairs * 2
    return pl.pallas_call(
        attention_forward,
        grid_spec=pltpu.PrefetchScalarGridSpec(
            num_scalar_prefetch=1,
            grid=(pairs,),
            in_specs=segments + blocks,
            out_specs=[wide, totals],
            scratch_shapes=[pltpu.VMEM((count, count), f32), pltpu.VMEM((count, count), f32)],
        ),
        out_shape=[
            jax.ShapeDtypeStruct((count, pairs * LANES), bf16),
            jax.ShapeDtypeStruct((pairs, 2, count), f32),
        ],
        compiler_params=pltpu.CompilerParams(vmem_limit_bytes=48 << 20),
        cost_estimate=pl.CostEstimate(
            flops=4 * work, bytes_accessed=6 * count * pairs * LANES * 2, transcendentals=0
        ),
        name="attention_forward",
    )(later, *labels, projected, projected, projected, others, others)


def attend_back(later, labels, projected, others, grad, mixed, log_totals):
    count = projected.shape[0]
    pairs = projected.shape[1] // (3 * LANES)
    segments, blocks, wide, totals = attention_specs(count, pairs)
    work = count * count * LANES * pairs * 2
    return pl.pallas_call(
        attention_backward,
        grid_spec=pltpu.PrefetchScalarGridSpec(
            num_scalar_prefetch=1,
            grid=(pairs,),
            in_specs=segments + blocks + [wide, wide, totals],
            out_specs=[wide] * 5,
            scratch_shapes=[pltpu.VMEM((count, count), f32), pltpu.VMEM((count, count), f32)],
        ),
        out_shape=[jax.ShapeDtypeStruct((count, pairs * LANES), bf16)] * 5,
        compiler_params=pltpu.CompilerParams(vmem_limit_bytes=48 << 20),
        cost_estimate=pl.CostEstimate(
            flops=10 * work, bytes_accessed=12 * count * pairs * LANES * 2, transcendentals=0
        ),
        name="attention_backward",
    )(later, *labels, projected, projected, projected, others, others, grad, mixed, log_totals)


AXES = ("col", "dp", "row")


def gather_blocks(block):
    cols = lax.axis_size("col")
    whole = lax.all_gather(block, AXES, axis=0, tiled=False)
    return whole.reshape(cols, -1, *block.shape)


def scatter_blocks(blocks):
    flat = blocks.reshape(-1, blocks.shape[-1])
    return lax.psum_scatter(flat, AXES, scatter_dimension=0, tiled=True)


def local(
    hidden_in,
    cotangent,
    segments,
    qkv_weight,
    out_weight,
    up_weight,
    down_weight,
    vectors,
    qkv_first,
    out_first,
    up_first,
    down_first,
    vectors_first,
    qkv_second,
    out_second,
    up_second,
    down_second,
    vectors_second,
):
    column = lax.axis_index("col")
    cols = lax.axis_size("col")
    here, width = hidden_in.shape
    rows_own = qkv_weight.shape[0]
    owners = lax.axis_size("dp") * lax.axis_size("row")
    piece = qkv_weight.shape[2]
    halves = SEQ // here
    later = lax.rem(column, halves).reshape(1).astype(jnp.int32)
    padded = -(-width // LANES) * LANES

    vec_shape = vectors.shape
    vec_count = vec_shape[0] * vec_shape[1]
    attn_block = jnp.concatenate(
        [
            jnp.concatenate(
                [qkv_weight.reshape(rows_own, 3 * piece), out_weight.T], 1
            ).astype(bf16),
            jnp.pad(
                vectors.reshape(1, vec_count).astype(bf16),
                ((0, VEC_ROWS - 1), (0, 4 * piece - vec_count)),
            ),
        ],
        0,
    )
    attn_all = gather_blocks(attn_block)
    up_all = gather_blocks(up_weight.astype(bf16)).reshape(cols, width, -1)
    down_all = gather_blocks(down_weight.T.astype(bf16)).reshape(cols, width, -1)

    vec = (
        attn_all[:, :, rows_own, :vec_count]
        .reshape(cols, owners, *vec_shape)
        .transpose(0, 2, 1, 3)
        .reshape(cols * vec_shape[0], width)
        .astype(f32)
    )
    attn_weights = (
        attn_all[:, :, :rows_own]
        .reshape(cols, width, 4, piece)
        .transpose(1, 2, 0, 3)
        .reshape(width, 4, width)
    )
    attn_weights = jnp.pad(attn_weights, ((0, 0), (0, 0), (0, padded - width)))
    qkv_flat = attn_weights[:, :3].reshape(width, 3 * padded)
    out_turned = attn_weights[:, 3]

    def widen(row):
        return jnp.pad(row, (0, padded - width))

    inputs = hidden_in.astype(f32)
    normed_one, scaled_one, inverse_one = normalize(inputs, vec[0], vec[1])
    normed_low = normed_one.astype(bf16)
    bias = jnp.concatenate([widen(vec[2]), jnp.zeros((padded,), f32), widen(vec[3])])
    projected = (jnp.dot(normed_low, qkv_flat, preferred_element_type=f32) + bias).astype(bf16)
    ahead = [(c, c + 1) for c in range(cols - 1) if c % halves + 1 < halves]
    behind = [(b, a) for a, b in ahead]
    others = lax.ppermute(projected[:, padded:], "col", ahead)

    own_half = lax.dynamic_slice_in_dim(segments.reshape(-1), column * here, here, 0)
    first_half = lax.dynamic_slice_in_dim(
        segments.reshape(-1), (column - lax.rem(column, halves)) * here, here, 0
    )
    labels = (own_half.reshape(1, here), own_half.reshape(here, 1), first_half.reshape(here, 1))
    mixed, log_totals = attend(later, labels, projected, others)
    residual = inputs + contract_last(mixed, out_turned) + vec[4]
    normed_two, scaled_two, inverse_two = normalize(residual, vec[5], vec[6])
    normed_two_low = normed_two.astype(bf16)

    branch = jnp.zeros((here, width), f32)
    grad_normed_two = jnp.zeros((here, width), f32)
    grad_up, grad_down, grad_up_bias = [], [], []
    for c in range(cols):
        up_linear = jnp.dot(normed_two_low, up_all[c], preferred_element_type=f32) + vec[8 + c]
        active, gelu_pullback = jax.vjp(gelu_tanh, up_linear)
        active_low = active.astype(bf16)
        branch = branch + contract_last(active_low, down_all[c])
        grad_active = jnp.dot(cotangent, down_all[c], preferred_element_type=f32)
        grad_up_linear = gelu_pullback(grad_active)[0]
        grad_up_low = grad_up_linear.astype(bf16)
        grad_down.append(contract_first(cotangent, active_low).astype(bf16))
        grad_up.append(contract_first(normed_two_low, grad_up_low).astype(bf16))
        grad_up_bias.append(jnp.sum(grad_up_linear, 0))
        grad_normed_two = grad_normed_two + contract_last(grad_up_low, up_all[c])
    layer_out = (residual + branch + vec[7]).astype(bf16)
    sum_down = scatter_blocks(jnp.stack(grad_down)).astype(f32)
    sum_up = scatter_blocks(jnp.stack(grad_up)).astype(f32)

    grad_residual = cotangent.astype(f32) + norm_back(
        grad_normed_two, scaled_two, inverse_two, vec[5]
    )
    grad_residual_low = grad_residual.astype(bf16)
    grad_mixed = jnp.dot(grad_residual_low, out_turned, preferred_element_type=f32).astype(bf16)
    grad_out = contract_first(grad_residual_low, mixed)
    dq, dk_own, dv_own, dk_oth, dv_oth = attend_back(
        later, labels, projected, others, grad_mixed, mixed, log_totals
    )
    back = lax.ppermute(jnp.concatenate([dk_oth, dv_oth], 1), "col", behind)
    grad_kv = jnp.concatenate([dk_own, dv_own], 1).astype(f32) + back.astype(f32)
    grad_projected = jnp.concatenate([dq, grad_kv.astype(bf16)], 1)
    grad_qkv = contract_first(normed_low, grad_projected)
    grad_normed_one = contract_last(grad_projected, qkv_flat)
    input_grad = grad_residual + norm_back(grad_normed_one, scaled_one, inverse_one, vec[0])

    grad_vector = jnp.concatenate(
        [
            jnp.stack(
                [
                    jnp.sum(grad_normed_one * scaled_one, 0),
                    jnp.sum(grad_normed_one, 0),
                    jnp.sum(dq.astype(f32), 0)[:width],
                    jnp.sum(grad_kv[:, padded:], 0)[:width],
                    jnp.sum(grad_residual, 0),
                    jnp.sum(grad_normed_two * scaled_two, 0),
                    jnp.sum(grad_normed_two, 0),
                    jnp.sum(cotangent.astype(f32), 0),
                ]
            ),
            jnp.stack(grad_up_bias),
        ],
        0,
    ).astype(bf16)
    vec_part = (
        grad_vector.reshape(cols, vec_shape[0], owners, vec_shape[1])
        .transpose(0, 2, 1, 3)
        .reshape(cols, owners, 1, vec_count)
    )
    vec_part = jnp.pad(vec_part, ((0, 0), (0, 0), (0, VEC_ROWS - 1), (0, 4 * piece - vec_count)))
    grad_attn = jnp.concatenate(
        [
            grad_qkv.astype(bf16).reshape(width, 3, padded),
            grad_out.astype(bf16).reshape(width, 1, padded),
        ],
        1,
    )[:, :, :width]
    grad_attn = (
        grad_attn.reshape(owners, rows_own, 4, cols, piece)
        .transpose(3, 0, 1, 2, 4)
        .reshape(cols, owners, rows_own, 4 * piece)
    )
    sum_attn = scatter_blocks(jnp.concatenate([grad_attn, vec_part], 2)).astype(f32)
    sum_qkv = sum_attn[:rows_own, : 3 * piece].reshape(rows_own, 3, piece)
    sum_out = sum_attn[:rows_own, 3 * piece :].T
    sum_vector = sum_attn[rows_own, :vec_count].reshape(vec_shape)

    qkv_m, qkv_v, qkv_w = adamw(
        qkv_weight, sum_qkv, qkv_first, qkv_second, 1.5 * D ** (-0.5), decay_rate
    )
    out_m, out_v, out_w = adamw(
        out_weight, sum_out, out_first, out_second, 1.5 * (D // 64) ** (-0.5), decay_rate
    )
    up_m, up_v, up_w = adamw(up_weight, sum_up, up_first, up_second, 1.5 * D ** (-0.5), decay_rate)
    down_m, down_v, down_w = adamw(
        down_weight, sum_down.T, down_first, down_second, 1.5 * FF ** (-0.5), decay_rate
    )
    vec_m, vec_v, vec_w = adamw(vectors, sum_vector, vectors_first, vectors_second, 0.5, 0.0)
    return (
        layer_out,
        input_grad,
        qkv_m,
        qkv_v,
        qkv_w,
        out_m,
        out_v,
        out_w,
        up_m,
        up_v,
        up_w,
        down_m,
        down_v,
        down_w,
        vec_m,
        vec_v,
        vec_w,
    )


def solution(mesh):
    tokens = P(("dp", "row", "col"), None)
    qkv = P(("dp", "row"), None, "col")
    tall = P("col", ("dp", "row"))
    up = P(("dp", "row"), "col")
    state = (qkv, tall, up, tall, tall)
    return jax.shard_map(
        local,
        mesh=mesh,
        in_specs=(tokens, tokens, P(("dp", "row"), None)) + state * 3,
        out_specs=(tokens, tokens)
        + (qkv,) * 3
        + (tall,) * 3
        + (up,) * 3
        + (tall,) * 3
        + (tall,) * 3,
        check_vma=False,
    )
```

time: 1670 us -> 863 us (0.52)
  waiting for transfers between devices: 941 us -> 445 us
  matrix products: 386 us -> 104 us
  blocking collectives: 116 us -> 0 us
  local copies, waits for them, and re-layouts: 69.7 us -> 179 us
  other arithmetic: 99.1 us -> 58.5 us
  Pallas kernels: 0 us -> 37.5 us
  loops' own time: 22.8 us -> 0 us
    dot_general x131 -> x30, matrix products: 386 us -> 104 us  [the longest x20 65.8 us: contract(): lax.dot_general(left, right, (((left_dim,), (right_dim,)), ((), ())), pre...]
    psum x2 -> x0, waiting for transfers between devices: 177 us -> none  [the longest x1 88.5 us: local(): lax.psum(jnp.dot(mixed_cols, out_local, preferred_element_type=jnp.float3...]
    reduce_scatter x4 -> x1, waiting for transfers between devices: 249 us -> 135 us  [scatter_blocks(): return lax.psum_scatter(flat, AXES, scatter_dimension=0, tiled=True)]
    unnamed x18 -> x8, waiting for transfers between devices: 239 us -> 137 us
    all_gather x6 -> x3, waiting for transfers between devices: 261 us -> 173 us  [gather_blocks(): whole = lax.all_gather(block, AXES, axis=0, tiled=False)]
    reshape x2 -> x9, local copies, waits for them, and re-layouts: 0.18 us -> 77.5 us  [the longest x1 25.1 us: local(): attn_weights = attn_all[:, :, :rows_own].reshape(cols, width, 4, piece).t...]
    all_gather x3 -> x0, blocking collectives: 68.2 us -> none  [the longest x1 34.3 us: local(): lax.all_gather(out_weight.astype(jnp.bfloat16), ('dp', 'row'), axis=1, ti...]
    unnamed x2 -> x0, blocking collectives: 48 us -> none
  transfers between devices with their start and end apart: 17 -> 8, of which waited for: 16 -> 4; matrix products, arithmetic and copies ran while one was open for 7% -> 32% of each run, Pallas kernels for 0% -> 4%
where the time goes in v1:
time: 863 us; the launch traced here: 855 us
  waiting for transfers between devices  445 us (52%)
  local copies, waits for them, and re-layouts  179 us (21%)
  matrix products  104 us (12%)
  other arithmetic  58.5 us (7%)
  Pallas kernels  37.5 us (4%)
  between operations  15.5 us (2%)
  starting transfers between devices  15.2 us (2%)
    all_gather x3, waiting for transfers between devices, gather_blocks(): whole = lax.all_gather(block, AXES, axis=0, tiled=False)  173 us
    unnamed x8, waiting for transfers between devices  137 us
    reduce_scatter x1, waiting for transfers between devices, scatter_blocks(): return lax.psum_scatter(flat, AXES, scatter_dimension=0, tiled=True)  135 us
    dot_general x20, matrix products, contract(): lax.dot_general(left, right, (((left_dim,), (right_dim,)), ((), ())), pre...  65.8 us
    reshape x1, local copies, waits for them, and re-layouts, local(): attn_weights = attn_all[:, :, :rows_own].reshape(cols, width, 4, piece).t...  25.1 us
    reshape x1, local copies, waits for them, and re-layouts, local(): grad_attn.reshape(owners, rows_own, 4, cols, piece).transpose(3, 0, 1, 2, 4)  25.1 us
    transpose x1, local copies, waits for them, and re-layouts, local(): attn_weights = attn_all[:, :, :rows_own].reshape(cols, width, 4, piece).t...  21.7 us
    reshape x1, local copies, waits for them, and re-layouts, local(): grad_attn = grad_attn.reshape(owners, rows_own, 4, cols, piece).transpose...  21.1 us
  transfers between devices with their start and end apart: 8, of which 4 were waited for; matrix products, arithmetic and copies ran while one was open for 32% of the time, Pallas kernels for 4%

profile of v1, /device:TPU:0, one launch (start us, length us, event | category | flops | bytes accessed | tf_op | source)
XLA Modules:
  0.0 855.3 jit_solution(16318117487886182999)
XLA Ops:
  13.0 88.8 %all-gather.7.cloned.1.call-done = bf16[4608,1088]{1,0:T(8,128)(2,1)} async-done(((bf16[144,1088]{1,0:T(8,128)(2,1)}), bf16[4608,1088]{1,0:T(8,128)(2,1)}) %all-gather.7.cloned.1.call-update) | async-done | bytes 10027024 | tf_op jit(solution)/shard_map/all_gather | solution.py:282
  101.8 8.4 slice.159
  111.6 25.1 %reshape.179 = bf16[4,1088,4,272]{3,2,1,0:T(4,128)(2,1)} reshape(bf16[4,8,136,1088]{3,2,1,0:T(8,128)(2,1)} %slice.159) | data formatting | bytes 18939904 | tf_op jit(solution)/shard_map/reshape | solution.py:348
  136.6 21.7 %copy.103 = bf16[1088,4,4,272]{0,3,2,1:T(8,128)(2,1)} copy(bf16[1088,4,4,272]{3,1,0,2:T(4,128)(2,1)} %bitcast.117) | data formatting | bytes 18939904 | tf_op jit(solution)/shard_map/transpose | solution.py:349
  159.0 7.0 pad_slice_fusion.1
  166.0 9.4 %add_convert_fusion.q.k_own.v_own = bf16[512,3456]{1,0:T(8,128)(2,1)S(1)} fusion(bf16[1088,3456]{0,1:T(8,128)(2,1)} %bitcast.125, f32[3456]{0:T(1024)S(1)} %select_maximum_fusion, bf16[512,1088]{0,1:T(8,128)(2,1)S(1)} %copy-done.10, f32[1088]{0:T(1024)S(1)} %get-tuple-element.100, f32[1088]{0:T(1024)S(1)} %get-tuple-element.101, ...), kind=kOutput, calls=%fused_computation.18 | convolution fusion | flops 3857252352 | bytes 12199936 | tf_op jit(solution)/shard_map/dot_general | solution.py:363
  175.5 1.7 slice.162
  178.0 13.1 %collective-permute-start = (bf16[512,2304]{1,0:T(8,128)(2,1)}, bf16[512,2304]{1,0:T(8,128)(2,1)S(1)}, u32[]{:S(2)}, u32[]{:S(2)}) collective-permute-start(bf16[512,2304]{1,0:T(8,128)(2,1)} %slice.162), channel_id=1, source_target_pairs={{0,1},{2,3},{4,5},{6,7},{8,9},{10,11},{12,13},{14,15},{16,17},{18,... | collective-permute-start | bytes 7077896 | tf_op jit(solution)/shard_map/ppermute | solution.py:366
  191.6 17.6 %attention_forward.1 = (bf16[512,1152]{1,0:T(8,128)(2,1)S(1)}, f32[9,2,512]{2,1,0:T(2,128)S(1)}) custom-call(s32[1]{0:T(128)} %bitcast.later, s32[1,512]{1,0:T(1,128)S(1)} %bitcast.110, s32[512,1]{1,0:T(8,128)S(1)} %copy.104.kseg_own, s32[512,1]{1,0:T(8,128)S(1)} %copy.105.kseg_oth, bf16[512,3456]{1,0:T(8,128)(2,1)} %copy-done.5, ...), custom_call_target="tpu_custom_call" | custom-call | flops 2415919104 | bytes 7077888 | tf_op jit(solution)/shard_map/attention_forward/pallas_call | solution.py:233
  209.3 3.9 fusion.123
  213.5 1.4 add_convert_fusion.1
  214.9 3.9 convolution_add_fusion.6
  218.8 1.8 fusion.10
  221.6 1.7 convolution_add_fusion.7
  223.3 1.8 fusion.9
  225.1 1.7 convolution_add_fusion.8
  226.7 2.2 fusion.8
  228.9 1.7 convolution_add_fusion.9
  230.6 1.8 fusion.7
  232.4 5.3 pad_maximum_fusion.2
  237.8 137.3 %reduce-scatter.12.cloned.1.call-done = bf16[136,1088]{1,0:T(8,128)(2,1)} async-done(((bf16[4352,1088]{1,0:T(8,128)(2,1)}), bf16[136,1088]{1,0:T(8,128)(2,1)}) %reduce-scatter.12.cloned.1.call-update) | async-done | bytes 295952
  375.1 3.0 multiply_subtract_fusion
  378.2 84.0 %all-gather.11.cloned.1.call-done = bf16[4352,1088]{1,0:T(8,128)(2,1)} async-done(((bf16[136,1088]{1,0:T(8,128)(2,1)}), bf16[4352,1088]{1,0:T(8,128)(2,1)}) %all-gather.11.cloned.1.call-update) | async-done | bytes 9469968 | tf_op jit(solution)/shard_map/all_gather | solution.py:282
  462.2 6.5 fusion.127
  469.7 1.6 fusion.6
  472.1 3.6 fusion.126
  475.8 1.6 fusion.5
  477.8 3.6 fusion.125
  481.4 1.8 fusion.4
  483.5 3.6 fusion.124
  487.1 1.6 fusion.3
  488.8 5.3 pad_maximum_fusion.1
  494.2 3.8 fusion.77
  498.0 3.6 convolution_add_fusion.2
  501.7 1.6 convolution_add_fusion.1
  503.4 2.9 multiply_reduce_fusion
  508.4 2.9 convolution_convert_fusion.10.grad
  511.4 19.8 %attention_backward.1 = (bf16[512,1152]{1,0:T(8,128)(2,1)S(1)}, bf16[512,1152]{1,0:T(8,128)(2,1)S(1)}, bf16[512,1152]{1,0:T(8,128)(2,1)S(1)}, bf16[512,1152]{1,0:T(8,128)(2,1)S(1)}, bf16[512,1152]{1,0:T(8,128)(2,1)}) custom-call(s32[1]{0:T(128)} %bitcast.later, s32[1,512]{1,0:T(1,128)S(1)} %bitcast.111, s32[512,1]{1,0:T(8,128)S(1)} %copy.104.kseg_own, ...), custom_call_target="tpu_custom_call" | custom-call | flops 6039797760 | bytes 14155776 | tf_op jit(solution)/shard_map/attention_backward/pallas_call | solution.py:259
  531.2 3.3 pad_maximum_fusion.4
  534.5 1.8 collective-permute-start.1
  536.3 1.5 reduce.1
  537.8 1.5 reduce
  540.5 1.3 stack.83
  548.2 4.7 fusion.2
  552.9 5.2 copy.110
  558.1 2.5 convert_add_fusion
  560.7 10.4 %fusion.29 = (bf16[1088]{0:T(1024)(128)(2,1)S(1)}, f32[512]{0:T(512)S(1)}, f32[512]{0:T(512)S(1)}, bf16[1088]{0:T(1024)(128)(2,1)S(1)}, f32[512,1088]{0,1:T(8,128)}) fusion(bf16[512,1088]{0,1:T(8,128)(2,1)S(1)} %copy-done.12, f32[512]{0:T(512)S(1)} %copy-done.53, f32[512]{0:T(512)S(1)} %copy-done.44, f32[1088]{0:T(1024)S(1)} %copy-done.34, ...), kind=kOutput, calls=%fused_computation.72 | convolution fusion | flops 3863016448 | bytes 14418432 | tf_op jit(solution)/shard_map/dot_general | solution.py:31
  572.5 8.3 convolution_convert_fusion
  580.8 11.3 %copy.109 = bf16[1088,3456]{0,1:T(8,128)(2,1)} copy(bf16[1088,3456]{1,0:T(8,128)(2,1)} %convolution_convert_fusion) | data formatting | bytes 15040512 | tf_op jit(solution)/shard_map/convert_element_type | solution.py:439
  592.1 8.5 pad_maximum_fusion
  600.6 14.4 %copy.111 = bf16[1088,4,1088]{2,0,1:T(8,128)(2,1)} copy(bf16[1088,4,1088]{0,2,1:T(8,128)(2,1)} %pad_maximum_fusion) | data formatting | bytes 18939904 | tf_op jit(solution)/shard_map/slice | solution.py:437
  615.0 25.1 %reshape.184 = bf16[8,136,4,4,272]{4,3,1,0,2:T(4,128)(2,1)} reshape(bf16[1088,4,1088]{2,0,1:T(8,128)(2,1)} %copy.111) | data formatting | bytes 18939904 | tf_op jit(solution)/shard_map/reshape | solution.py:445
  640.1 18.3 %copy.112 = bf16[4,8,136,4,272]{4,3,2,1,0:T(4,128)(2,1)} copy(bf16[4,8,136,4,272]{4,0,2,1,3:T(4,128)(2,1)} %bitcast.118) | data formatting | bytes 18939904 | tf_op jit(solution)/shard_map/transpose | solution.py:446
  658.4 21.1 %reshape.185 = bf16[4,8,136,1088]{3,2,1,0:T(8,128)(2,1)} reshape(bf16[4,8,136,4,272]{4,3,2,1,0:T(4,128)(2,1)} %copy.112) | data formatting | bytes 18939904 | tf_op jit(solution)/shard_map/reshape | solution.py:447
  679.5 8.7 %fusion.1 = bf16[4,8,144,1088]{3,2,1,0:T(8,128)(2,1)} fusion(bf16[4,8,1,408]{3,2,1,0:T(2,128)(2,1)S(1)} %reshape.213, bf16[4,8,136,1088]{3,2,1,0:T(8,128)(2,1)} %reshape.185), kind=kLoop, calls=%fused_computation.3 | loop fusion | flops 30081024 | bytes 19523072 | tf_op jit(solution)/shard_map/concatenate | solution.py:449
  688.2 4.3 fusion.79
  692.6 3.6 convolution_add_fusion.5
  696.3 1.8 convolution_add_fusion.4
  698.6 2.8 fusion.14
  701.4 2.0 fusion.28
  703.5 2.6 multiply_subtract_fusion.1
  706.0 135.3 %reduce-scatter.8.cloned.1.call-done = bf16[144,1088]{1,0:T(8,128)(2,1)} async-done(((bf16[4608,1088]{1,0:T(8,128)(2,1)}), bf16[144,1088]{1,0:T(8,128)(2,1)}) %reduce-scatter.8.cloned.1.call-update) | async-done | bytes 313360 | tf_op jit(solution)/shard_map/reduce_scatter | solution.py:288
  843.0 2.0 multiply_subtract_fusion.3
  845.0 2.6 multiply_subtract_fusion.2
  (253 shorter events, 27.0 us)
Async XLA Ops:
  7.2 4.4 copy-start.17
  7.2 94.6 %all-gather.7.cloned.1.call-start = ((), (), s32[]{:S(2)}) async-start(), calls=%async_computation.4 | async-start | bytes 10948608 | tf_op jit(solution)/shard_map/all_gather | solution.py:282
  9.0 3.4 copy-start.10
  11.5 203.4 %all-gather.9.cloned.1.call-start = ((), (), s32[]{:S(2)}) async-start(), calls=%async_computation.5 | async-start | bytes 10340352 | tf_op jit(solution)/shard_map/all_gather | solution.py:282
  12.4 362.7 %reduce-scatter.12.cloned.1.call-start = ((), (), s32[]{:S(2)}) async-start(), calls=%async_computation.8 | async-start | bytes 10340352
  12.6 153.4 %copy-start.43 = (f32[512]{0:T(512)}, f32[512]{0:T(512)S(1)}, u32[]{:S(2)}) copy-start(f32[512]{0:T(512)S(1)} %broadcast_multiply_fusion.5) | copy-start | bytes 6148
  13.0 153.0 %copy-start.52 = (f32[512]{0:T(512)}, f32[512]{0:T(512)S(1)}, u32[]{:S(2)}) copy-start(f32[512]{0:T(512)S(1)} %add_rsqrt_fusion.1) | copy-start | bytes 6148
  159.0 7.0 copy-start.33
  159.0 7.0 copy-start.49
  159.0 54.5 %copy-start.31 = (f32[1088]{0:T(1024)}, f32[1088]{0:T(1024)S(1)}, u32[]{:S(2)}) copy-start(f32[1088]{0:T(1024)S(1)} %get-tuple-element.96) | copy-start | bytes 13060
  175.4 2.6 copy-start.5
  175.4 15.7 %copy-start.51 = (s32[2,1024]{1,0:T(2,128)S(1)}, s32[2,1024]{1,0:T(2,128)}, u32[]{:S(2)}) copy-start(s32[2,1024]{1,0:T(2,128)} %param.20) | copy-start | bytes 24580
  178.0 13.6 %collective-permute-start = (bf16[512,2304]{1,0:T(8,128)(2,1)}, bf16[512,2304]{1,0:T(8,128)(2,1)S(1)}, u32[]{:S(2)}, u32[]{:S(2)}) collective-permute-start(bf16[512,2304]{1,0:T(8,128)(2,1)} %slice.162), channel_id=1, source_target_pairs={{0,1},{2,3},{4,5},{6,7},{8,9},{10,11},{12,13},{14,15},{16,17},{18,... | collective-permute-start | bytes 7077896 | tf_op jit(solution)/shard_map/ppermute | solution.py:366
  191.6 17.7 %copy-start = (bf16[512,2304]{1,0:T(8,128)(2,1)}, bf16[512,2304]{1,0:T(8,128)(2,1)S(1)}, u32[]{:S(2)}) copy-start(bf16[512,2304]{1,0:T(8,128)(2,1)S(1)} %collective-permute-done.k_oth.v_oth) | copy-start | bytes 7077892
  191.6 17.7 %copy-start.11 = (bf16[512,1088]{0,1:T(8,128)(2,1)S(1)}, bf16[512,1088]{0,1:T(8,128)(2,1)}, u32[]{:S(2)}) copy-start(bf16[512,1088]{0,1:T(8,128)(2,1)} %param.18) | copy-start | bytes 3342340
  209.3 3.9 copy-start.1
  213.2 293.1 %copy-start.6 = (f32[512,1088]{0,1:T(8,128)}, f32[512,1088]{0,1:T(8,128)S(1)}, u32[]{:S(2)}) copy-start(f32[512,1088]{0,1:T(8,128)S(1)} %get-tuple-element.125) | copy-start | bytes 6684676
  214.9 3.9 copy-start.14
  214.9 5.7 slice-start.3
  214.9 5.7 slice-start.4
  218.8 2.8 slice-start.5
  237.7 137.4 %copy-start.26 = (f32[1088,136]{0,1:T(8,128)S(1)}, f32[1088,136]{0,1:T(8,128)}, u32[]{:S(2)}) copy-start(f32[1088,136]{0,1:T(8,128)} %param.24) | copy-start | bytes 1775620
  237.7 224.4 %all-gather.11.cloned.1.call-start = ((), (), s32[]{:S(2)}) async-start(), calls=%async_computation.6 | async-start | bytes 10340352 | tf_op jit(solution)/shard_map/all_gather | solution.py:282
  378.1 325.3 %reduce-scatter.10.cloned.1.call-start = ((), (), s32[]{:S(2)}) async-start(), calls=%async_computation.7 | async-start | bytes 10340352
  462.2 7.5 copy-start.24
  462.2 9.1 %slice-start.9 = ((s8[10027008]{0:T(1024)(128)(4,1)}), s8[4194304]{0:T(1024)(128)(4,1)S(1)}, s32[]{:S(2)}) async-start(s8[10027008]{0:T(1024)(128)(4,1)} %bitcast.138), calls=%async_computation.18 | async-start | bytes 8388608
  462.2 9.2 %slice-start.10 = ((s8[10027008]{0:T(1024)(128)(4,1)}), s8[4194304]{0:T(1024)(128)(4,1)S(1)}, s32[]{:S(2)}) async-start(s8[10027008]{0:T(1024)(128)(4,1)} %bitcast.138), calls=%async_computation.19 | async-start | bytes 8388608
  469.6 2.5 copy-start.63
  494.1 347.2 %reduce-scatter.8.cloned.1.call-start = ((), (), s32[]{:S(2)}) async-start(), calls=%async_computation.3 | async-start | bytes 10948608 | tf_op jit(solution)/shard_map/reduce_scatter | solution.py:288
  494.2 3.8 copy-start.61
  494.2 7.4 slice-start.6
  494.2 7.4 slice-start.7
  498.0 3.7 slice-start.8
  498.0 3.7 copy-start.59
  503.3 2.9 copy-start.16
  503.3 3.9 slice-start
  503.3 4.3 slice-start.1
  507.2 4.2 copy-start.8
  531.2 3.3 copy-start.3
  534.5 13.7 %copy-start.2 = (bf16[512,1152]{1,0:T(8,128)(2,1)S(1)}, bf16[512,1152]{1,0:T(8,128)(2,1)}, u32[]{:S(2)}) copy-start(bf16[512,1152]{1,0:T(8,128)(2,1)} %copy-done.1) | copy-start | bytes 3538948
  534.5 23.6 %collective-permute-start.1 = (bf16[512,2304]{1,0:T(8,128)(2,1)}, bf16[512,2304]{1,0:T(8,128)(2,1)}, u32[]{:S(2)}, u32[]{:S(2)}) collective-permute-start(bf16[512,2304]{1,0:T(8,128)(2,1)} %pad_maximum_fusion.4), channel_id=1, source_target_pairs={{1,0},{3,2},{5,4},{7,6},{9,8},{11,10},{13,12},{15,14},{17,16},{19,... | collective-permute-start | bytes 7077896 | tf_op jit(solution)/shard_map/ppermute | solution.py:406
  558.1 2.5 copy-start.4
  558.1 2.5 copy-start.12
  558.1 2.5 copy-start.34
  558.1 2.5 copy-start.44
  558.1 2.5 copy-start.53
  560.6 10.5 %copy-start.20 = (bf16[512,2304]{1,0:T(8,128)(2,1)}, bf16[512,2304]{1,0:T(8,128)(2,1)S(1)}, u32[]{:S(2)}) copy-start(bf16[512,2304]{1,0:T(8,128)(2,1)S(1)} %get-tuple-element.120) | copy-start | bytes 7077892
  688.2 4.3 copy-start.67
  688.2 8.0 slice-start.12
  688.2 8.0 slice-start.13
  692.5 3.7 slice-start.14
  692.5 3.7 copy-start.64
  696.3 2.3 copy-start.69
  698.6 2.8 copy-start.9
  698.6 2.8 copy-start.21
  698.6 2.8 copy-start.46
  698.6 2.8 copy-start.55
  706.0 137.0 %copy-start.25 = (f32[272,136]{0,1:T(8,128)S(1)}, f32[272,136]{0,1:T(8,128)}, u32[]{:S(2)}) copy-start(f32[272,136]{0,1:T(8,128)} %param.22) | copy-start | bytes 443908
  706.0 137.0 %copy-start.30 = (f32[272,136]{0,1:T(8,128)S(1)}, f32[272,136]{0,1:T(8,128)}, u32[]{:S(2)}) copy-start(f32[272,136]{0,1:T(8,128)} %param.32) | copy-start | bytes 443908
  706.0 138.9 %copy-start.19 = (f32[136,3,272]{2,0,1:T(8,128)S(1)}, f32[136,3,272]{2,0,1:T(8,128)}, u32[]{:S(2)}) copy-start(f32[136,3,272]{2,0,1:T(8,128)} %param.21) | copy-start | bytes 1331716
  706.0 138.9 %copy-start.29 = (f32[136,3,272]{2,0,1:T(8,128)S(1)}, f32[136,3,272]{2,0,1:T(8,128)}, u32[]{:S(2)}) copy-start(f32[136,3,272]{2,0,1:T(8,128)} %param.31) | copy-start | bytes 1331716
  845.0 2.7 copy-start.47
  845.0 2.7 copy-start.56
  845.0 2.7 copy-start.57
  (34 other events, 51.4 us)
Sparse Core Ops, SparseCore 0:
  11.6 90.0 all-gather.6
  105.2 83.1 all-gather.8
  237.9 137.1 reduce-scatter.11
  378.4 83.7 all-gather.10
  494.2 131.7 reduce-scatter.9
  688.3 152.9 reduce-scatter.7

commit v2 on v1

--- a/solution.py
+++ b/solution.py
@@ -14,7 +14,6 @@
 STEP = 5
 
 LANES = 128
-VEC_ROWS = 8
 
 
 beta_one = 0.9
@@ -274,18 +273,221 @@
     )(later, *labels, projected, projected, projected, others, others, grad, mixed, log_totals)
 
 
+def place_kernel(spans, piece, sources, biased, continued, places, x, *refs):
+    weights, refs = refs[:sources], refs[sources:]
+    bias, refs = (refs[0], refs[1:]) if biased else (None, refs)
+    before, refs = (refs[0], refs[1:]) if continued else (None, refs)
+    out, whole, product = refs
+    step = pl.program_id(0)
+    each = pl.num_programs(0) // sources
+
+    @pl.when(step == 0)
+    def _():
+        whole[...] = before[...].astype(f32) if continued else jnp.zeros_like(whole)
+
+    for k, weight in enumerate(weights):
+
+        @pl.when(step // each == k)
+        def _(weight=weight):
+            product[...] = jnp.dot(x[...], weight[0], preferred_element_type=f32)
+
+    for place in range(x.shape[1] // piece):
+
+        @pl.when(places[step] == place)
+        def _(place=place):
+            for source, target in spans:
+                start = target + place * piece
+                block = product[:, source : source + piece]
+                if biased:
+                    block = block + bias[:, start : start + piece]
+                whole[:, start : start + piece] = block
+
+    @pl.when(step == pl.num_programs(0) - 1)
+    def _():
+        out[...] = whole[...].astype(bf16)
+
+
+def multiply_and_place(places, x, weights, lanes, lane_block, spans, piece, out_lanes, bias, before):
+    count, depth = x.shape
+    each = weights[0].shape[0]
+    sources = len(weights)
+
+    def fixed(shape):
+        return pl.BlockSpec(shape, lambda j, places: (0, 0))
+
+    in_specs = [fixed((count, depth))]
+    for k in range(sources):
+        in_specs.append(
+            pl.BlockSpec(
+                (1, depth, lanes),
+                lambda j, places, k=k: (jnp.clip(j - k * each, 0, each - 1), 0, lane_block),
+            )
+        )
+    operands = [x, *weights]
+    if bias is not None:
+        in_specs.append(fixed(bias.shape))
+        operands.append(bias)
+    if before is not None:
+        in_specs.append(fixed(before.shape))
+        operands.append(before)
+    return pl.pallas_call(
+        functools.partial(
+            place_kernel, spans, piece, sources, bias is not None, before is not None
+        ),
+        grid_spec=pltpu.PrefetchScalarGridSpec(
+            num_scalar_prefetch=1,
+            grid=(each * sources,),
+            in_specs=in_specs,
+            out_specs=fixed((count, out_lanes)),
+            scratch_shapes=[pltpu.VMEM((count, out_lanes), f32), pltpu.VMEM((count, lanes), f32)],
+        ),
+        out_shape=jax.ShapeDtypeStruct((count, out_lanes), bf16),
+        compiler_params=pltpu.CompilerParams(vmem_limit_bytes=48 << 20),
+        cost_estimate=pl.CostEstimate(
+            flops=2 * count * depth * lanes * each * sources,
+            bytes_accessed=2 * (each * sources * depth * lanes + count * (depth + out_lanes)),
+            transcendentals=0,
+        ),
+        name="multiply_and_place",
+    )(places, *operands)
+
+
+def split_both(parity, cols, write):
+    for p in range(2):
+
+        @pl.when(parity[0] == p)
+        def _(p=p):
+            for i in range(cols // 2):
+                write(0, i, p + 2 * i)
+                write(1, i, 1 - p + 2 * i)
+
+
+def split_mixed_kernel(piece, cols, lead, parity, mixed, own, oth):
+    count, lanes = own.shape[1:]
+    values = mixed[...].astype(f32)
+    before = jnp.zeros((count, lead), f32)
+    after = jnp.zeros((count, lanes - lead - piece), f32)
+
+    def write(which, i, c):
+        block = values[:, c * piece : (c + 1) * piece]
+        (own, oth)[which][i] = jnp.concatenate([before, block, after], 1).astype(bf16)
+
+    split_both(parity, cols, write)
+
+
+def split_grads_kernel(piece, cols, parity, dq, dk, dv, back, own, oth, sums):
+    count, lanes = own.shape[1:]
+    wide = dq.shape[1]
+    grads = [
+        dq[...].astype(f32),
+        dk[...].astype(f32) + back[:, :wide].astype(f32),
+        dv[...].astype(f32) + back[:, wide:].astype(f32),
+    ]
+    sums[0:1] = jnp.sum(grads[0], 0, keepdims=True)
+    sums[1:2] = jnp.sum(grads[2], 0, keepdims=True)
+    after = jnp.zeros((count, lanes - 3 * piece), f32)
+
+    def write(which, i, c):
+        blocks = [g[:, c * piece : (c + 1) * piece] for g in grads]
+        (own, oth)[which][i] = jnp.concatenate([*blocks, after], 1).astype(bf16)
+
+    split_both(parity, cols, write)
+
+
+def whole_specs(shapes):
+    return [pl.BlockSpec(s, lambda i, p, n=len(s): (0,) * n) for s in shapes]
+
+
+def split_call(kernel, parity, operands, out_shapes, name):
+    moved = sum(x.size * x.dtype.itemsize for x in operands) * 2
+    return pl.pallas_call(
+        kernel,
+        grid_spec=pltpu.PrefetchScalarGridSpec(
+            num_scalar_prefetch=1,
+            grid=(1,),
+            in_specs=whole_specs([x.shape for x in operands]),
+            out_specs=whole_specs([s.shape for s in out_shapes]),
+        ),
+        out_shape=out_shapes,
+        compiler_params=pltpu.CompilerParams(vmem_limit_bytes=48 << 20),
+        cost_estimate=pl.CostEstimate(flops=moved, bytes_accessed=moved, transcendentals=0),
+        name=name,
+    )(parity, *operands)
+
+
+def block_grads_kernel(lane_lead, joined, left_one, left_two, grads, mixed, vec_part, *refs):
+    received, out, total = refs if joined else (None, *refs)
+    lanes_one = grads.shape[2]
+    total[:, :lanes_one] = jnp.dot(left_one[...], grads[0], preferred_element_type=f32)
+    total[:, lanes_one:] = jnp.zeros_like(total[:, lanes_one:])
+    total[:, lane_lead:] += jnp.dot(left_two[...], mixed[0], preferred_element_type=f32)
+    total[:, -LANES:] += vec_part[0].astype(f32)
+    whole = total[...]
+    if joined:
+        whole = whole + received[0].astype(f32)
+    out[0] = whole.astype(bf16)
+
+
+def block_grads(left_one, left_two, grads, mixed, vec_part, received, lane_lead):
+    each, count, _ = grads.shape
+    width = left_one.shape[0]
+    lanes = lane_lead + mixed.shape[2]
+
+    def fixed(shape):
+        return pl.BlockSpec(shape, lambda i: (0, 0))
+
+    def step(shape):
+        return pl.BlockSpec((1, *shape[1:]), lambda i: (i, 0, 0))
+
+    operands = [left_one, left_two, grads, mixed, vec_part]
+    in_specs = [fixed(left_one.shape), fixed(left_two.shape)]
+    in_specs += [step(x.shape) for x in operands[2:]]
+    if received is not None:
+        operands.append(received)
+        in_specs.append(step(received.shape))
+    return pl.pallas_call(
+        functools.partial(block_grads_kernel, lane_lead, received is not None),
+        grid=(each,),
+        in_specs=in_specs,
+        out_specs=step((each, width, lanes)),
+        out_shape=jax.ShapeDtypeStruct((each, width, lanes), bf16),
+        scratch_shapes=[pltpu.VMEM((width, lanes), f32)],
+        compiler_params=pltpu.CompilerParams(vmem_limit_bytes=48 << 20),
+        cost_estimate=pl.CostEstimate(
+            flops=2 * each * count * width * (grads.shape[2] + mixed.shape[2]),
+            bytes_accessed=2 * each * width * lanes * 2,
+            transcendentals=0,
+        ),
+        name="block_grads",
+    )(*operands)
+
+
 AXES = ("col", "dp", "row")
 
 
-def gather_blocks(block):
+def planes():
+    owners = lax.axis_size("dp") * lax.axis_size("row")
     cols = lax.axis_size("col")
-    whole = lax.all_gather(block, AXES, axis=0, tiled=False)
-    return whole.reshape(cols, -1, *block.shape)
-
-
-def scatter_blocks(blocks):
+    return [
+        [c * owners + k for c in range(p, cols, 2) for k in range(owners)] for p in range(2)
+    ]
+
+
+def partner(block):
+    pairs = [(c, c ^ 1) for c in range(lax.axis_size("col"))]
+    return lax.ppermute(block, "col", pairs)
+
+
+def gather_plane(block):
+    whole = lax.all_gather(block, AXES, axis=0, tiled=False, axis_index_groups=planes())
+    return whole.reshape(lax.axis_size("col") // 2, -1, block.shape[-1])
+
+
+def scatter_plane(blocks):
     flat = blocks.reshape(-1, blocks.shape[-1])
-    return lax.psum_scatter(flat, AXES, scatter_dimension=0, tiled=True)
+    return lax.psum_scatter(
+        flat, AXES, scatter_dimension=0, tiled=True, axis_index_groups=planes()
+    )
 
 
 def local(
@@ -315,52 +517,64 @@
     owners = lax.axis_size("dp") * lax.axis_size("row")
     piece = qkv_weight.shape[2]
     halves = SEQ // here
+    each = cols // 2
+    odd = lax.rem(column, 2)
+    even_here = odd == 0
+    parity = odd.reshape(1).astype(jnp.int32)
+    places_own = (odd + 2 * jnp.arange(each)).astype(jnp.int32)
+    places_oth = (1 - odd + 2 * jnp.arange(each)).astype(jnp.int32)
     later = lax.rem(column, halves).reshape(1).astype(jnp.int32)
     padded = -(-width // LANES) * LANES
+    spare = padded - width
+    lanes_qkv = -(-3 * piece // LANES) * LANES
+    lead_out = 3 * piece // LANES * LANES
+    lanes_out = padded - lead_out
+
+    def by_parity(own, oth):
+        return jnp.where(even_here, own, oth), jnp.where(even_here, oth, own)
 
     vec_shape = vectors.shape
     vec_count = vec_shape[0] * vec_shape[1]
+    vec_lines = -(-vec_count // spare)
+    vec_fill = vec_lines * spare - vec_count
+    vec_lanes = jnp.pad(vectors.reshape(vec_count).astype(bf16), (0, vec_fill))
     attn_block = jnp.concatenate(
         [
-            jnp.concatenate(
-                [qkv_weight.reshape(rows_own, 3 * piece), out_weight.T], 1
-            ).astype(bf16),
-            jnp.pad(
-                vectors.reshape(1, vec_count).astype(bf16),
-                ((0, VEC_ROWS - 1), (0, 4 * piece - vec_count)),
-            ),
+            qkv_weight.reshape(rows_own, 3 * piece).astype(bf16),
+            out_weight.T.astype(bf16),
+            jnp.pad(vec_lanes.reshape(vec_lines, spare), ((0, rows_own - vec_lines), (0, 0))),
         ],
-        0,
-    )
-    attn_all = gather_blocks(attn_block)
-    up_all = gather_blocks(up_weight.astype(bf16)).reshape(cols, width, -1)
-    down_all = gather_blocks(down_weight.T.astype(bf16)).reshape(cols, width, -1)
-
-    vec = (
-        attn_all[:, :, rows_own, :vec_count]
-        .reshape(cols, owners, *vec_shape)
-        .transpose(0, 2, 1, 3)
-        .reshape(cols * vec_shape[0], width)
-        .astype(f32)
-    )
-    attn_weights = (
-        attn_all[:, :, :rows_own]
-        .reshape(cols, width, 4, piece)
-        .transpose(1, 2, 0, 3)
-        .reshape(width, 4, width)
-    )
-    attn_weights = jnp.pad(attn_weights, ((0, 0), (0, 0), (0, padded - width)))
-    qkv_flat = attn_weights[:, :3].reshape(width, 3 * padded)
-    out_turned = attn_weights[:, 3]
+        1,
+    )
+    attn_own = gather_plane(attn_block)
+    vec_own = attn_own.reshape(each, owners, rows_own, padded)[:, :, :vec_lines, width:]
+    vec_oth = partner(vec_own)
+    attn_oth = partner(attn_own)
+    up_own = gather_plane(up_weight.astype(bf16))
+    up_oth = partner(up_own)
+    down_own = gather_plane(down_weight.T.astype(bf16))
+    down_oth = partner(down_own)
+
+    def vec_rows(lines):
+        lines = lines.reshape(each, owners, vec_lines * spare)[:, :, :vec_count]
+        lines = lines.reshape(each, owners, *vec_shape).transpose(0, 2, 1, 3)
+        return lines.reshape(each, vec_shape[0], width).astype(f32)
+
+    vec = jnp.stack(by_parity(vec_rows(vec_own), vec_rows(vec_oth)), 1).reshape(-1, width)
 
     def widen(row):
-        return jnp.pad(row, (0, padded - width))
+        return jnp.pad(row, (0, spare))
 
     inputs = hidden_in.astype(f32)
     normed_one, scaled_one, inverse_one = normalize(inputs, vec[0], vec[1])
     normed_low = normed_one.astype(bf16)
-    bias = jnp.concatenate([widen(vec[2]), jnp.zeros((padded,), f32), widen(vec[3])])
-    projected = (jnp.dot(normed_low, qkv_flat, preferred_element_type=f32) + bias).astype(bf16)
+    bias = jnp.concatenate([widen(vec[2]), jnp.zeros((padded,), f32), widen(vec[3])]).reshape(1, -1)
+    spans = tuple((part * piece, part * padded) for part in range(3))
+    projected = None
+    for places, weights in ((places_own, attn_own), (places_oth, attn_oth)):
+        projected = multiply_and_place(
+            places, normed_low, [weights], lanes_qkv, 0, spans, piece, 3 * padded, bias, projected
+        )
     ahead = [(c, c + 1) for c in range(cols - 1) if c % halves + 1 < halves]
     behind = [(b, a) for a, b in ahead]
     others = lax.ppermute(projected[:, padded:], "col", ahead)
@@ -371,85 +585,154 @@
     )
     labels = (own_half.reshape(1, here), own_half.reshape(here, 1), first_half.reshape(here, 1))
     mixed, log_totals = attend(later, labels, projected, others)
-    residual = inputs + contract_last(mixed, out_turned) + vec[4]
+    mixed_shape = jax.ShapeDtypeStruct((each, here, lanes_out), bf16)
+    lead = 3 * piece - lead_out
+    mixed_own, mixed_oth = split_call(
+        functools.partial(split_mixed_kernel, piece, cols, lead),
+        parity,
+        [mixed],
+        [mixed_shape] * 2,
+        "split_mixed",
+    )
+    residual = inputs + vec[4]
+    for blocks, weights in ((mixed_own, attn_own), (mixed_oth, attn_oth)):
+        for i in range(each):
+            residual = residual + contract_last(blocks[i], weights[i][:, lead_out:])
     normed_two, scaled_two, inverse_two = normalize(residual, vec[5], vec[6])
     normed_two_low = normed_two.astype(bf16)
 
+    bias_even, bias_odd = vec[8::2], vec[9::2]
+    bias_own, bias_oth = by_parity(bias_even, bias_odd)
+
+    def up_part(ups, biases):
+        return [
+            jnp.dot(normed_two_low, ups[i], preferred_element_type=f32) + biases[i]
+            for i in range(each)
+        ]
+
+    linear_own = up_part(up_own, bias_own)
+    linear_oth = up_part(up_oth, bias_oth)
+    (linear_own, linear_oth, down_own) = lax.optimization_barrier(
+        (linear_own, linear_oth, down_own)
+    )
     branch = jnp.zeros((here, width), f32)
+
+    def forward_part(linears, downs, branch):
+        lows, pullbacks = [], []
+        for i in range(each):
+            active, pullback = jax.vjp(gelu_tanh, linears[i])
+            lows.append(active.astype(bf16))
+            pullbacks.append(pullback)
+            branch = branch + contract_last(lows[i], downs[i])
+        return lows, pullbacks, branch
+
+    lows_own, pull_own, branch = forward_part(linear_own, down_own, branch)
+    lows_oth, pull_oth, branch = forward_part(linear_oth, down_oth, branch)
+    layer_out = (residual + branch + vec[7]).astype(bf16)
+
+    def paired_sum(left, rights_own, rights_oth):
+        send = jnp.stack([contract_first(left, r).astype(bf16) for r in rights_oth])
+        received = partner(send)
+        total = jnp.stack(
+            [
+                (contract_first(left, r) + received[i].astype(f32)).astype(bf16)
+                for i, r in enumerate(rights_own)
+            ]
+        )
+        return scatter_plane(total).astype(f32)
+
+    sum_down = paired_sum(cotangent, lows_own, lows_oth)
+
     grad_normed_two = jnp.zeros((here, width), f32)
-    grad_up, grad_down, grad_up_bias = [], [], []
-    for c in range(cols):
-        up_linear = jnp.dot(normed_two_low, up_all[c], preferred_element_type=f32) + vec[8 + c]
-        active, gelu_pullback = jax.vjp(gelu_tanh, up_linear)
-        active_low = active.astype(bf16)
-        branch = branch + contract_last(active_low, down_all[c])
-        grad_active = jnp.dot(cotangent, down_all[c], preferred_element_type=f32)
-        grad_up_linear = gelu_pullback(grad_active)[0]
-        grad_up_low = grad_up_linear.astype(bf16)
-        grad_down.append(contract_first(cotangent, active_low).astype(bf16))
-        grad_up.append(contract_first(normed_two_low, grad_up_low).astype(bf16))
-        grad_up_bias.append(jnp.sum(grad_up_linear, 0))
-        grad_normed_two = grad_normed_two + contract_last(grad_up_low, up_all[c])
-    layer_out = (residual + branch + vec[7]).astype(bf16)
-    sum_down = scatter_blocks(jnp.stack(grad_down)).astype(f32)
-    sum_up = scatter_blocks(jnp.stack(grad_up)).astype(f32)
+
+    def backward_part(ups, downs, pullbacks, grad_normed_two):
+        lows, sums = [], []
+        for i in range(each):
+            grad_active = jnp.dot(cotangent, downs[i], preferred_element_type=f32)
+            grad_linear = pullbacks[i](grad_active)[0]
+            lows.append(grad_linear.astype(bf16))
+            sums.append(jnp.sum(grad_linear, 0))
+            grad_normed_two = grad_normed_two + contract_last(lows[i], ups[i])
+        return lows, sums, grad_normed_two
+
+    dups_oth, dbias_oth, grad_normed_two = backward_part(
+        up_oth, down_oth, pull_oth, grad_normed_two
+    )
+    dups_own, dbias_own, grad_normed_two = backward_part(
+        up_own, down_own, pull_own, grad_normed_two
+    )
+    sum_up = paired_sum(normed_two_low, dups_own, dups_oth)
 
     grad_residual = cotangent.astype(f32) + norm_back(
         grad_normed_two, scaled_two, inverse_two, vec[5]
     )
     grad_residual_low = grad_residual.astype(bf16)
-    grad_mixed = jnp.dot(grad_residual_low, out_turned, preferred_element_type=f32).astype(bf16)
-    grad_out = contract_first(grad_residual_low, mixed)
+    grad_mixed = multiply_and_place(
+        jnp.concatenate([places_own, places_oth]),
+        grad_residual_low,
+        [attn_own, attn_oth],
+        lanes_out,
+        lead_out // lanes_out,
+        ((lead, 0),),
+        piece,
+        padded,
+        None,
+        None,
+    )
     dq, dk_own, dv_own, dk_oth, dv_oth = attend_back(
         later, labels, projected, others, grad_mixed, mixed, log_totals
     )
     back = lax.ppermute(jnp.concatenate([dk_oth, dv_oth], 1), "col", behind)
-    grad_kv = jnp.concatenate([dk_own, dv_own], 1).astype(f32) + back.astype(f32)
-    grad_projected = jnp.concatenate([dq, grad_kv.astype(bf16)], 1)
-    grad_qkv = contract_first(normed_low, grad_projected)
-    grad_normed_one = contract_last(grad_projected, qkv_flat)
+    grads_shape = jax.ShapeDtypeStruct((each, here, lanes_qkv), bf16)
+    grads_own, grads_oth, grad_sums = split_call(
+        functools.partial(split_grads_kernel, piece, cols),
+        parity,
+        [dq, dk_own, dv_own, back],
+        [grads_shape, grads_shape, jax.ShapeDtypeStruct((8, padded), f32)],
+        "split_grads",
+    )
+    grad_normed_one = jnp.zeros((here, width), f32)
+    for blocks, weights in ((grads_own, attn_own), (grads_oth, attn_oth)):
+        for i in range(each):
+            grad_normed_one = grad_normed_one + contract_last(blocks[i], weights[i][:, :lanes_qkv])
     input_grad = grad_residual + norm_back(grad_normed_one, scaled_one, inverse_one, vec[0])
 
+    dbias_even, dbias_odd = by_parity(jnp.stack(dbias_own), jnp.stack(dbias_oth))
     grad_vector = jnp.concatenate(
         [
             jnp.stack(
                 [
                     jnp.sum(grad_normed_one * scaled_one, 0),
                     jnp.sum(grad_normed_one, 0),
-                    jnp.sum(dq.astype(f32), 0)[:width],
-                    jnp.sum(grad_kv[:, padded:], 0)[:width],
+                    grad_sums[0, :width],
+                    grad_sums[1, :width],
                     jnp.sum(grad_residual, 0),
                     jnp.sum(grad_normed_two * scaled_two, 0),
                     jnp.sum(grad_normed_two, 0),
                     jnp.sum(cotangent.astype(f32), 0),
                 ]
             ),
-            jnp.stack(grad_up_bias),
+            jnp.stack([dbias_even, dbias_odd], 1).reshape(cols, width),
         ],
         0,
     ).astype(bf16)
-    vec_part = (
-        grad_vector.reshape(cols, vec_shape[0], owners, vec_shape[1])
-        .transpose(0, 2, 1, 3)
-        .reshape(cols, owners, 1, vec_count)
-    )
-    vec_part = jnp.pad(vec_part, ((0, 0), (0, 0), (0, VEC_ROWS - 1), (0, 4 * piece - vec_count)))
-    grad_attn = jnp.concatenate(
-        [
-            grad_qkv.astype(bf16).reshape(width, 3, padded),
-            grad_out.astype(bf16).reshape(width, 1, padded),
-        ],
-        1,
-    )[:, :, :width]
-    grad_attn = (
-        grad_attn.reshape(owners, rows_own, 4, cols, piece)
-        .transpose(3, 0, 1, 2, 4)
-        .reshape(cols, owners, rows_own, 4 * piece)
-    )
-    sum_attn = scatter_blocks(jnp.concatenate([grad_attn, vec_part], 2)).astype(f32)
-    sum_qkv = sum_attn[:rows_own, : 3 * piece].reshape(rows_own, 3, piece)
-    sum_out = sum_attn[:rows_own, 3 * piece :].T
-    sum_vector = sum_attn[rows_own, :vec_count].reshape(vec_shape)
+    vec_part = grad_vector.reshape(cols, vec_shape[0], owners, vec_shape[1]).transpose(0, 2, 1, 3)
+    vec_part = jnp.pad(vec_part.reshape(cols, owners, vec_count), ((0, 0), (0, 0), (0, vec_fill)))
+    vec_part = jnp.pad(
+        vec_part.reshape(cols, owners, vec_lines, spare),
+        ((0, 0), (0, 0), (0, rows_own - vec_lines), (LANES - spare, 0)),
+    ).reshape(cols, width, LANES)
+    vec_here, vec_there = by_parity(vec_part[0::2], vec_part[1::2])
+    left_one, left_two = normed_low.T, grad_residual_low.T
+    received = partner(
+        block_grads(left_one, left_two, grads_oth, mixed_oth, vec_there, None, lead_out)
+    )
+    sum_attn = scatter_plane(
+        block_grads(left_one, left_two, grads_own, mixed_own, vec_here, received, lead_out)
+    ).astype(f32)
+    sum_qkv = sum_attn[:, : 3 * piece].reshape(rows_own, 3, piece)
+    sum_out = sum_attn[:, 3 * piece : width].T
+    sum_vector = sum_attn[:vec_lines, width:].reshape(-1)[:vec_count].reshape(vec_shape)
 
     qkv_m, qkv_v, qkv_w = adamw(
         qkv_weight, sum_qkv, qkv_first, qkv_second, 1.5 * D ** (-0.5), decay_rate

time: 863 us -> 783 us (0.907)
  local copies, waits for them, and re-layouts: 179 us -> 34.6 us
  Pallas kernels: 37.5 us -> 77.8 us
  waiting for transfers between devices: 445 us -> 482 us
  other arithmetic: 58.5 us -> 39 us
  starting transfers between devices: 15.2 us -> 34.4 us
  matrix products: 104 us -> 90.6 us
    reduce_scatter x1 -> x0, waiting for transfers between devices: 135 us -> none  [scatter_blocks(): return lax.psum_scatter(flat, AXES, scatter_dimension=0, tiled=True)]
    unnamed x8 -> x9, waiting for transfers between devices: 137 us -> 257 us
    reshape x7 -> x11, local copies, waits for them, and re-layouts: 77.2 us -> 1.14 us  [the longest x1 0.41 us: local(): sum_qkv = sum_attn[:, :3 * piece].reshape(rows_own, 3, piece)]
    pallas_call x0 -> x7, Pallas kernels: none -> 40.7 us  [the longest x3 22.3 us: multiply_and_place(): pl.pallas_call(functools.partial(place_kernel, spans, piece, sources, bia...]
    transpose x3 -> x1, local copies, waits for them, and re-layouts: 40 us -> 0.03 us  [local(): grad_vector.reshape(cols, vec_shape[0], owners, vec_shape[1])]
    all_gather x3, waiting for transfers between devices: 173 us -> 206 us  [gather_plane(): lax.all_gather(block, AXES, axis=0, tiled=False, axis_index_groups=planes())]
    slice x6 -> x9, local copies, waits for them, and re-layouts: 31.6 us -> 4.3 us  [the longest x2 1.57 us: local(): bias_even, bias_odd = (vec[8::2], vec[9::2])]
    concatenate x3 -> x1, other arithmetic: 18 us -> 0.07 us  [local(): jnp.concatenate([places_own, places_oth])]
  transfers between devices with their start and end apart: 8 -> 15, of which waited for: 4 -> 9; matrix products, arithmetic and copies ran while one was open for 32% -> 15% of each run, Pallas kernels for 4% -> 10%
where the time goes in v2:
time: 783 us; the launch traced here: 774 us
  waiting for transfers between devices  482 us (62%)
  matrix products  90.6 us (12%)
  Pallas kernels  77.8 us (10%)
  other arithmetic  39 us (5%)
  local copies, waits for them, and re-layouts  34.6 us (4%)
  starting transfers between devices  34.4 us (4%)
  between operations  15.9 us (2%)
    unnamed x9, waiting for transfers between devices  257 us
    all_gather x3, waiting for transfers between devices, gather_plane(): lax.all_gather(block, AXES, axis=0, tiled=False, axis_index_groups=planes())  206 us
    dot_general x24, matrix products, contract(): lax.dot_general(left, right, (((left_dim,), (right_dim,)), ((), ())), pre...  62.1 us
    pallas_call x3, Pallas kernels, multiply_and_place(): pl.pallas_call(functools.partial(place_kernel, spans, piece, sources, bia...  22.3 us
    pallas_call x1, Pallas kernels, attend_back(): pl.pallas_call(attention_backward, grid_spec=pltpu.PrefetchScalarGridSpec...  19.7 us
    unnamed x185, local copies, waits for them, and re-layouts  19.4 us
    pallas_call x1, Pallas kernels, attend(): pl.pallas_call(attention_forward, grid_spec=pltpu.PrefetchScalarGridSpec(...  17.5 us
    ppermute x7, starting transfers between devices, partner(): return lax.ppermute(block, 'col', pairs)  17.3 us
  transfers between devices with their start and end apart: 15, of which 9 were waited for; matrix products, arithmetic and copies ran while one was open for 15% of the time, Pallas kernels for 10%

profile of v2, /device:TPU:0, one launch (start us, length us, event | category | flops | bytes accessed | tf_op | source)
XLA Modules:
  0.0 774.1 jit_solution(11741773610952137815)
XLA Ops:
  11.8 85.2 %all-gather.7.cloned.1.call-done = bf16[2176,1152]{1,0:T(8,128)(2,1)} async-done(((bf16[136,1152]{1,0:T(8,128)(2,1)}), bf16[2176,1152]{1,0:T(8,128)(2,1)}) %all-gather.7.cloned.1.call-update) | async-done | bytes 5013520 | tf_op jit(solution)/shard_map/all_gather | solution.py:482
  99.1 6.2 collective-permute-done
  108.5 7.2 multiply_and_place.3.refs_2_
  115.8 1.8 copy-done.1
  118.8 8.5 %multiply_and_place.4.q.k_own.v_own = bf16[512,3456]{1,0:T(8,128)(2,1)S(1)} custom-call(s32[2]{0:T(128)S(1)} %fusion.130.places, bf16[512,1088]{1,0:T(8,128)(2,1)S(1)} %copy-done.3, bf16[2,1088,1152]{2,1,0:T(8,128)(2,1)} %collective-permute-done.1.refs_0_.refs_1_, f32[1,3456]{1,0:T(1,128)S(1)} %reshape.347.refs_1_, bf16[512,3456]{1,0:T(8,128)(2,1)} %copy-done.1), custom_call_target="tpu_custom_call" | custom-call | flops 1996488704 | bytes 8552448 | tf_op jit(solution)/shard_map/multiply_and_place/pallas_call | solution.py:333
  127.4 1.7 slice.265
  129.8 15.1 %collective-permute-start.2 = (bf16[512,2304]{1,0:T(8,128)(2,1)}, bf16[512,2304]{1,0:T(8,128)(2,1)}, u32[]{:S(2)}, u32[]{:S(2)}) collective-permute-start(bf16[512,2304]{1,0:T(8,128)(2,1)} %slice.265), channel_id=1, source_target_pairs={{0,1},{2,3},{4,5},{6,7},{8,9},{10,11},{12,13},{14,15},{16,17},{18,... | collective-permute-start | bytes 7077896 | tf_op jit(solution)/shard_map/ppermute | solution.py:580
  146.0 35.8 %all-gather.11.cloned.1.call-done = bf16[2176,1088]{1,0:T(8,128)(2,1)} async-done(((bf16[136,1088]{1,0:T(8,128)(2,1)}), bf16[2176,1088]{1,0:T(8,128)(2,1)}) %all-gather.11.cloned.1.call-update) | async-done | bytes 4734992 | tf_op jit(solution)/shard_map/all_gather | solution.py:482
  181.8 84.8 %all-gather.9.cloned.1.call-done = bf16[2176,1088]{1,0:T(8,128)(2,1)} async-done(((bf16[136,1088]{1,0:T(8,128)(2,1)}), bf16[2176,1088]{1,0:T(8,128)(2,1)}) %all-gather.9.cloned.1.call-update) | async-done | bytes 4734992 | tf_op jit(solution)/shard_map/all_gather | solution.py:482
  268.3 2.8 slice_bitcast_fusion.9
  271.2 17.5 %attention_forward.1 = (bf16[512,1152]{1,0:T(8,128)(2,1)S(1)}, f32[9,2,512]{2,1,0:T(2,128)S(1)}) custom-call(s32[1]{0:T(128)} %bitcast.4.later.parity, s32[1,512]{1,0:T(1,128)S(1)} %bitcast.207, s32[512,1]{1,0:T(8,128)S(1)} %copy.91.kseg_own, s32[512,1]{1,0:T(8,128)S(1)} %copy.92.kseg_oth, bf16[512,3456]{1,0:T(8,128)(2,1)} %copy-done, ...), custom_call_target="tpu_custom_call" | custom-call | flops 2415919104 | bytes 7077888 | tf_op jit(solution)/shard_map/attention_forward/pallas_call | solution.py:232
  290.6 1.9 convolution_add_fusion.2
  292.6 2.1 convolution_add_fusion.1
  296.8 1.7 convolution_add_fusion.12
  298.5 1.7 convolution_add_fusion.11
  300.2 4.2 convolution_add_fusion.10
  304.4 4.2 convolution_add_fusion.9
  308.6 5.9 fusion.144
  315.6 1.6 fusion.1
  317.3 4.9 fusion.143
  324.4 7.1 collective-permute-start.7
  331.5 3.0 fusion.141
  334.6 3.0 fusion.142
  337.6 1.9 collective-permute-done.7
  339.5 1.8 fusion.22
  341.3 1.6 fusion.21
  343.0 2.8 pad_maximum_fusion.1
  346.2 3.5 fusion.3
  349.7 1.8 fusion.2
  351.5 2.8 pad_maximum_fusion.2
  357.2 3.4 fusion.66
  360.7 3.6 fusion.9
  364.3 2.3 multiply_reduce_fusion
  366.6 2.2 fusion.138
  368.8 2.8 convert_element_type.205
  371.6 1.9 copy.93.x
  373.4 6.6 multiply_and_place.5.grad
  381.1 19.7 %attention_backward.1 = (bf16[512,1152]{1,0:T(8,128)(2,1)S(1)}, bf16[512,1152]{1,0:T(8,128)(2,1)S(1)}, bf16[512,1152]{1,0:T(8,128)(2,1)S(1)}, bf16[512,1152]{1,0:T(8,128)(2,1)S(1)}, bf16[512,1152]{1,0:T(8,128)(2,1)}) custom-call(s32[1]{0:T(128)} %bitcast.4.later.parity, s32[1,512]{1,0:T(1,128)S(1)} %bitcast.208, s32[512,1]{1,0:T(8,128)S(1)} %copy.91.kseg_own, ...), custom_call_target="tpu_custom_call" | custom-call | flops 6039797760 | bytes 14155776 | tf_op jit(solution)/shard_map/attention_backward/pallas_call | solution.py:258
  400.8 4.0 pad_maximum_fusion.4
  406.2 3.7 fusion.24
  410.0 3.6 fusion.23
  413.6 2.9 pad_maximum_fusion.3
  417.1 1.8 convert_bitcast_fusion.2.left_two
  418.9 2.5 collective-permute-done.5.back
  425.2 5.5 split_grads.1
  430.7 3.2 fusion.79
  433.9 2.9 fusion.82
  436.9 3.1 convolution_add_fusion.4
  440.5 3.4 fusion.36
  446.2 5.2 block_grads.2
  451.5 9.2 %collective-permute-start.6 = (bf16[2,1088,1152]{2,1,0:T(8,128)(2,1)}, bf16[2,1088,1152]{2,1,0:T(8,128)(2,1)S(1)}, u32[]{:S(2)}, u32[]{:S(2)}) collective-permute-start(bf16[2,1088,1152]{2,1,0:T(8,128)(2,1)} %block_grads.2), channel_id=1, source_target_pairs={{0,1},{1,0},{2,3},{3,2},{4,5},{5,4},{6,7},{7,6},{8,9},{9,8},{10,11... | collective-permute-start | bytes 15040520 | tf_op jit(solution)/shard_map/ppermute | solution.py:478
  460.7 8.2 %collective-permute-done.6.refs_0_ = bf16[2,1088,1152]{2,1,0:T(8,128)(2,1)S(1)} collective-permute-done((bf16[2,1088,1152]{2,1,0:T(8,128)(2,1)}, bf16[2,1088,1152]{2,1,0:T(8,128)(2,1)S(1)}, u32[]{:S(2)}, u32[]{:S(2)}) %collective-permute-start.6) | collective-permute-done | bytes 5013536 | tf_op jit(solution)/shard_map/ppermute | solution.py:478
  468.9 2.3 copy-done.27
  471.2 7.1 block_grads.3
  480.0 3.6 fusion.28
  483.6 3.6 fusion.69
  487.3 1.8 convolution_add_fusion.8
  489.6 4.7 fusion.14
  494.4 3.8 fusion.35
  498.2 2.6 multiply_subtract_fusion.1
  500.9 120.1 %reduce-scatter.14.cloned.1.call-done = bf16[136,1088]{1,0:T(8,128)(2,1)} async-done(((bf16[2176,1088]{1,0:T(8,128)(2,1)}), bf16[136,1088]{1,0:T(8,128)(2,1)}) %reduce-scatter.14.cloned.1.call-update) | async-done | bytes 295952
  621.0 2.7 multiply_subtract_fusion
  623.7 137.0 %reduce-scatter.10.cloned.1.call-done = bf16[136,1152]{1,0:T(8,128)(2,1)} async-done(((bf16[2176,1152]{1,0:T(8,128)(2,1)}), bf16[136,1152]{1,0:T(8,128)(2,1)}) %reduce-scatter.10.cloned.1.call-update) | async-done | bytes 313360
  762.4 2.9 multiply_subtract_fusion.2
  (300 shorter events, 40.3 us)
Async XLA Ops:
  7.2 89.7 %all-gather.7.cloned.1.call-start = ((), (), s32[]{:S(2)}) async-start(), calls=%async_computation.3 | async-start | bytes 5326848 | tf_op jit(solution)/shard_map/all_gather | solution.py:482
  8.7 88.3 %copy-start.20 = (bf16[512,1088]{0,1:T(8,128)(2,1)S(1)}, bf16[512,1088]{0,1:T(8,128)(2,1)}, u32[]{:S(2)}) copy-start(bf16[512,1088]{0,1:T(8,128)(2,1)} %param.18) | copy-start | bytes 3342340
  10.1 171.8 %all-gather.11.cloned.1.call-start = ((), (), s32[]{:S(2)}) async-start(), calls=%async_computation.5 | async-start | bytes 5326848 | tf_op jit(solution)/shard_map/all_gather | solution.py:482
  10.9 255.7 %all-gather.9.cloned.1.call-start = ((), (), s32[]{:S(2)}) async-start(), calls=%async_computation.4 | async-start | bytes 5326848 | tf_op jit(solution)/shard_map/all_gather | solution.py:482
  11.7 486.5 %reduce-scatter.12.cloned.1.call-start = ((), (), s32[]{:S(2)}) async-start(), calls=%async_computation.7 | async-start | bytes 5326848
  96.9 20.6 %collective-permute-start.1 = (bf16[2,1088,1152]{2,1,0:T(8,128)(2,1)}, bf16[2,1088,1152]{2,1,0:T(8,128)(2,1)}, u32[]{:S(2)}, u32[]{:S(2)}) collective-permute-start(bf16[2,1088,1152]{2,1,0:T(8,128)(2,1)} %bitcast.209), channel_id=1, source_target_pairs={{0,1},{1,0},{2,3},{3,2},{4,5},{5,4},{6,7},{7,6},{8,9},{9,8},{10,11... | collective-permute-start | bytes 15040520 | tf_op jit(solution)/shard_map/ppermute | solution.py:478
  97.2 10.6 %copy-start.53 = (f32[512]{0:T(512)}, f32[512]{0:T(512)S(1)}, u32[]{:S(2)}) copy-start(f32[512]{0:T(512)S(1)} %broadcast_multiply_fusion.5) | copy-start | bytes 6148
  97.6 10.9 %copy-start.57 = (f32[512]{0:T(512)}, f32[512]{0:T(512)S(1)}, u32[]{:S(2)}) copy-start(f32[512]{0:T(512)S(1)} %add_rsqrt_fusion.1) | copy-start | bytes 6148
  98.4 6.9 collective-permute-start
  108.5 7.3 copy-start.2
  129.8 141.4 %collective-permute-start.2 = (bf16[512,2304]{1,0:T(8,128)(2,1)}, bf16[512,2304]{1,0:T(8,128)(2,1)}, u32[]{:S(2)}, u32[]{:S(2)}) collective-permute-start(bf16[512,2304]{1,0:T(8,128)(2,1)} %slice.265), channel_id=1, source_target_pairs={{0,1},{2,3},{4,5},{6,7},{8,9},{10,11},{12,13},{14,15},{16,17},{18,... | collective-permute-start | bytes 7077896 | tf_op jit(solution)/shard_map/ppermute | solution.py:580
  146.0 125.1 %copy-start.14 = (s32[512,1]{1,0:T(8,128)}, s32[512,1]{1,0:T(8,128)S(1)}, u32[]{:S(2)}) copy-start(s32[512,1]{1,0:T(8,128)S(1)} %copy.92.kseg_oth) | copy-start | bytes 6148
  181.8 126.8 %collective-permute-start.4 = (bf16[2,1088,1088]{2,1,0:T(8,128)(2,1)}, bf16[2,1088,1088]{2,1,0:T(8,128)(2,1)}, u32[]{:S(2)}, u32[]{:S(2)}) collective-permute-start(bf16[2,1088,1088]{2,1,0:T(8,128)(2,1)} %bitcast.224), channel_id=1, source_target_pairs={{0,1},{1,0},{2,3},{3,2},{4,5},{5,4},{6,7},{7,6},{8,9},{9,8},{10,11... | collective-permute-start | bytes 14204936 | tf_op jit(solution)/shard_map/ppermute | solution.py:478
  266.6 33.6 %collective-permute-start.3 = (bf16[2,1088,1088]{2,1,0:T(8,128)(2,1)}, bf16[2,1088,1088]{2,1,0:T(8,128)(2,1)}, u32[]{:S(2)}, u32[]{:S(2)}) collective-permute-start(bf16[2,1088,1088]{2,1,0:T(8,128)(2,1)} %bitcast.233), channel_id=1, source_target_pairs={{0,1},{1,0},{2,3},{3,2},{4,5},{5,4},{6,7},{7,6},{8,9},{9,8},{10,11... | collective-permute-start | bytes 14204936 | tf_op jit(solution)/shard_map/ppermute | solution.py:478
  271.1 18.1 %copy-start.33 = (bf16[1088,1152]{1,0:T(8,128)(2,1)}, bf16[1088,1152]{1,0:T(8,128)(2,1)S(1)}, u32[]{:S(2)}) copy-start(bf16[1088,1152]{1,0:T(8,128)(2,1)S(1)} %get-tuple-element.123) | copy-start | bytes 7520260
  271.1 23.5 %copy-start.31 = (bf16[1088,1152]{1,0:T(8,128)(2,1)}, bf16[1088,1152]{1,0:T(8,128)(2,1)S(1)}, u32[]{:S(2)}) copy-start(bf16[1088,1152]{1,0:T(8,128)(2,1)S(1)} %get-tuple-element.122) | copy-start | bytes 7520260
  289.3 5.4 copy-start.16
  292.5 4.3 slice-start.4
  298.5 33.0 %copy-start.76 = (f32[512,1088]{0,1:T(8,128)}, f32[512,1088]{0,1:T(8,128)S(1)}, u32[]{:S(2)}) copy-start(f32[512,1088]{0,1:T(8,128)S(1)} %convolution_add_fusion.12) | copy-start | bytes 6684676
  300.2 34.4 %copy-start.73 = (f32[512,1088]{0,1:T(8,128)}, f32[512,1088]{0,1:T(8,128)S(1)}, u32[]{:S(2)}) copy-start(f32[512,1088]{0,1:T(8,128)S(1)} %convolution_add_fusion.11) | copy-start | bytes 6684676
  304.4 12.9 %copy-start.70 = (f32[512,1088]{0,1:T(8,128)}, f32[512,1088]{0,1:T(8,128)S(1)}, u32[]{:S(2)}) copy-start(f32[512,1088]{0,1:T(8,128)S(1)} %convolution_add_fusion.10) | copy-start | bytes 6684676
  304.4 4.2 copy-start.28
  308.6 6.0 copy-start.79
  317.2 14.3 %slice-start = ((s8[5013504]{0:T(1024)(128)(4,1)}), s8[4194304]{0:T(1024)(128)(4,1)S(1)}, s32[]{:S(2)}) async-start(s8[5013504]{0:T(1024)(128)(4,1)} %bitcast.226), calls=%async_computation.9 | async-start | bytes 8388608
  322.1 9.4 %slice-start.1 = ((s8[5013504]{0:T(1024)(128)(4,1)}), s8[819200]{0:T(1024)(128)(4,1)S(1)}, s32[]{:S(2)}) async-start(s8[5013504]{0:T(1024)(128)(4,1)} %bitcast.226), calls=%async_computation.10 | async-start | bytes 1638400
  324.4 15.1 %collective-permute-start.7 = (bf16[2,1088,1088]{2,1,0:T(8,128)(2,1)S(1)}, bf16[2,1088,1088]{2,1,0:T(8,128)(2,1)S(1)}, u32[]{:S(2)}, u32[]{:S(2)}) collective-permute-start(bf16[2,1088,1088]{2,1,0:T(8,128)(2,1)S(1)} %pad_maximum_fusion), channel_id=1, source_target_pairs={{0,1},{1,0},{2,3},{3,2},{4,5},{5,4},{6,7},{7,6},{8,9},{9,8},{10,11... | collective-permute-start | bytes 14204936 | tf_op jit(solution)/shard_map/ppermute | solution.py:478
  334.5 6.8 copy-start.68
  337.6 3.8 copy-start.66
  345.8 275.2 %reduce-scatter.14.cloned.1.call-start = ((), (), s32[]{:S(2)}) async-start(), calls=%async_computation.8 | async-start | bytes 5326848
  346.2 3.6 copy-start.71
  346.2 9.0 %slice-start.6 = ((s8[5013504]{0:T(1024)(128)(4,1)}), s8[4194304]{0:T(1024)(128)(4,1)S(1)}, s32[]{:S(2)}) async-start(s8[5013504]{0:T(1024)(128)(4,1)} %bitcast.236), calls=%async_computation.15 | async-start | bytes 8388608
  349.7 5.4 slice-start.7
  351.5 3.2 copy-start.52
  351.5 3.2 copy-start.54
  354.3 51.9 %collective-permute-start.8 = (bf16[2,1088,1088]{2,1,0:T(8,128)(2,1)}, bf16[2,1088,1088]{2,1,0:T(8,128)(2,1)}, u32[]{:S(2)}, u32[]{:S(2)}) collective-permute-start(bf16[2,1088,1088]{2,1,0:T(8,128)(2,1)} %pad_maximum_fusion.2), channel_id=1, source_target_pairs={{0,1},{1,0},{2,3},{3,2},{4,5},{5,4},{6,7},{7,6},{8,9},{9,8},{10,11... | collective-permute-start | bytes 14204936 | tf_op jit(solution)/shard_map/ppermute | solution.py:478
  357.2 3.4 copy-start.65
  360.6 3.6 copy-start.25
  360.7 3.6 copy-start.67
  373.4 7.7 copy-start.15
  400.8 4.1 copy-start.8
  400.8 4.1 copy-start.10
  400.8 4.1 copy-start.12
  400.8 5.4 copy-start.30
  400.8 5.4 copy-start.74
  404.9 16.5 %collective-permute-start.5 = (bf16[512,2304]{1,0:T(8,128)(2,1)}, bf16[512,2304]{1,0:T(8,128)(2,1)}, u32[]{:S(2)}, u32[]{:S(2)}) collective-permute-start(bf16[512,2304]{1,0:T(8,128)(2,1)} %pad_maximum_fusion.4), channel_id=1, source_target_pairs={{1,0},{3,2},{5,4},{7,6},{9,8},{11,10},{13,12},{15,14},{17,16},{19,... | collective-permute-start | bytes 7077896 | tf_op jit(solution)/shard_map/ppermute | solution.py:685
  406.2 3.8 copy-start.77
  416.5 344.2 %reduce-scatter.10.cloned.1.call-start = ((), (), s32[]{:S(2)}) async-start(), calls=%async_computation.6 | async-start | bytes 5326848
  425.2 5.5 copy-start.34
  430.7 6.1 copy-start.4
  436.9 3.7 copy-start.32
  446.2 25.0 %copy-start.5 = (bf16[2,512,896]{2,1,0:T(8,128)(2,1)S(1)}, bf16[2,512,896]{2,1,0:T(8,128)(2,1)}, u32[]{:S(2)}) copy-start(bf16[2,512,896]{2,1,0:T(8,128)(2,1)} %copy-done.4) | copy-start | bytes 5505028
  451.5 17.4 %collective-permute-start.6 = (bf16[2,1088,1152]{2,1,0:T(8,128)(2,1)}, bf16[2,1088,1152]{2,1,0:T(8,128)(2,1)S(1)}, u32[]{:S(2)}, u32[]{:S(2)}) collective-permute-start(bf16[2,1088,1152]{2,1,0:T(8,128)(2,1)} %block_grads.2), channel_id=1, source_target_pairs={{0,1},{1,0},{2,3},{3,2},{4,5},{5,4},{6,7},{7,6},{8,9},{9,8},{10,11... | collective-permute-start | bytes 15040520 | tf_op jit(solution)/shard_map/ppermute | solution.py:478
  480.0 3.6 copy-start.80
  480.0 7.3 slice-start.2
  483.6 3.7 slice-start.3
  483.6 3.7 copy-start.75
  489.6 4.7 copy-start.23
  489.6 4.7 copy-start.40
  494.4 3.8 copy-start.36
  494.4 3.8 copy-start.44
  494.4 3.8 copy-start.45
  498.2 122.8 %copy-start.38 = (f32[1088,136]{0,1:T(8,128)S(1)}, f32[1088,136]{0,1:T(8,128)}, u32[]{:S(2)}) copy-start(f32[1088,136]{0,1:T(8,128)} %param.24) | copy-start | bytes 1775620
  498.2 122.8 %copy-start.46 = (f32[1088,136]{0,1:T(8,128)S(1)}, f32[1088,136]{0,1:T(8,128)}, u32[]{:S(2)}) copy-start(f32[1088,136]{0,1:T(8,128)} %param.34) | copy-start | bytes 1775620
  500.9 261.5 %copy-start.39 = (f32[136,3,272]{2,0,1:T(8,128)S(1)}, f32[136,3,272]{2,0,1:T(8,128)}, u32[]{:S(2)}) copy-start(f32[136,3,272]{2,0,1:T(8,128)} %param.21) | copy-start | bytes 1331716
  (42 other events, 74.8 us)
Sparse Core Ops, SparseCore 0:
  11.3 85.5 all-gather.6
  100.2 81.5 all-gather.10
  185.1 81.4 all-gather.8
  345.9 133.7 reduce-scatter.11
  485.8 135.1 reduce-scatter.13
  626.2 134.4 reduce-scatter.9

commit v3 on v2

--- a/solution.py
+++ b/solution.py
@@ -352,17 +352,16 @@
     )(places, *operands)
 
 
-def split_both(parity, cols, write):
-    for p in range(2):
-
-        @pl.when(parity[0] == p)
-        def _(p=p):
-            for i in range(cols // 2):
-                write(0, i, p + 2 * i)
-                write(1, i, 1 - p + 2 * i)
-
-
-def split_mixed_kernel(piece, cols, lead, parity, mixed, own, oth):
+def split_all(column, cols, write):
+    for here in range(cols):
+
+        @pl.when(column[0] == here)
+        def _(here=here):
+            for k in range(cols):
+                write(k % 2, k // 2, here ^ k)
+
+
+def split_mixed_kernel(piece, cols, lead, column, mixed, own, oth):
     count, lanes = own.shape[1:]
     values = mixed[...].astype(f32)
     before = jnp.zeros((count, lead), f32)
@@ -372,10 +371,10 @@
         block = values[:, c * piece : (c + 1) * piece]
         (own, oth)[which][i] = jnp.concatenate([before, block, after], 1).astype(bf16)
 
-    split_both(parity, cols, write)
-
-
-def split_grads_kernel(piece, cols, parity, dq, dk, dv, back, own, oth, sums):
+    split_all(column, cols, write)
+
+
+def split_grads_kernel(piece, cols, column, dq, dk, dv, back, own, oth, sums):
     count, lanes = own.shape[1:]
     wide = dq.shape[1]
     grads = [
@@ -391,14 +390,14 @@
         blocks = [g[:, c * piece : (c + 1) * piece] for g in grads]
         (own, oth)[which][i] = jnp.concatenate([*blocks, after], 1).astype(bf16)
 
-    split_both(parity, cols, write)
+    split_all(column, cols, write)
 
 
 def whole_specs(shapes):
     return [pl.BlockSpec(s, lambda i, p, n=len(s): (0,) * n) for s in shapes]
 
 
-def split_call(kernel, parity, operands, out_shapes, name):
+def split_call(kernel, column, operands, out_shapes, name):
     moved = sum(x.size * x.dtype.itemsize for x in operands) * 2
     return pl.pallas_call(
         kernel,
@@ -412,26 +411,27 @@
         compiler_params=pltpu.CompilerParams(vmem_limit_bytes=48 << 20),
         cost_estimate=pl.CostEstimate(flops=moved, bytes_accessed=moved, transcendentals=0),
         name=name,
-    )(parity, *operands)
-
-
-def block_grads_kernel(lane_lead, joined, left_one, left_two, grads, mixed, vec_part, *refs):
-    received, out, total = refs if joined else (None, *refs)
+    )(column, *operands)
+
+
+def block_grads_kernel(joined, left_one, left_two, grads, mixed, *refs):
+    vec_part, received, out, total = refs if joined else (None, None, *refs)
     lanes_one = grads.shape[2]
+    lane_lead = total.shape[1] - mixed.shape[2]
     total[:, :lanes_one] = jnp.dot(left_one[...], grads[0], preferred_element_type=f32)
     total[:, lanes_one:] = jnp.zeros_like(total[:, lanes_one:])
     total[:, lane_lead:] += jnp.dot(left_two[...], mixed[0], preferred_element_type=f32)
-    total[:, -LANES:] += vec_part[0].astype(f32)
-    whole = total[...]
     if joined:
-        whole = whole + received[0].astype(f32)
-    out[0] = whole.astype(bf16)
-
-
-def block_grads(left_one, left_two, grads, mixed, vec_part, received, lane_lead):
+        total[:, -LANES:] += vec_part[0].astype(f32)
+        out[0] = (total[...] + received[0].astype(f32)).astype(bf16)
+    else:
+        out[0] = total[...].astype(bf16)
+
+
+def block_grads(left_one, left_two, grads, mixed, more):
     each, count, _ = grads.shape
     width = left_one.shape[0]
-    lanes = lane_lead + mixed.shape[2]
+    lanes = -(-width // LANES) * LANES
 
     def fixed(shape):
         return pl.BlockSpec(shape, lambda i: (0, 0))
@@ -439,14 +439,11 @@
     def step(shape):
         return pl.BlockSpec((1, *shape[1:]), lambda i: (i, 0, 0))
 
-    operands = [left_one, left_two, grads, mixed, vec_part]
+    operands = [left_one, left_two, grads, mixed, *(more or ())]
     in_specs = [fixed(left_one.shape), fixed(left_two.shape)]
     in_specs += [step(x.shape) for x in operands[2:]]
-    if received is not None:
-        operands.append(received)
-        in_specs.append(step(received.shape))
     return pl.pallas_call(
-        functools.partial(block_grads_kernel, lane_lead, received is not None),
+        functools.partial(block_grads_kernel, more is not None),
         grid=(each,),
         in_specs=in_specs,
         out_specs=step((each, width, lanes)),
@@ -473,21 +470,146 @@
     ]
 
 
+def flip_col(block, bit):
+    return lax.ppermute(block, "col", [(c, c ^ bit) for c in range(lax.axis_size("col"))])
+
+
 def partner(block):
-    pairs = [(c, c ^ 1) for c in range(lax.axis_size("col"))]
-    return lax.ppermute(block, "col", pairs)
-
-
-def gather_plane(block):
+    return flip_col(block, 1)
+
+
+def flip_dp(block):
+    return lax.ppermute(block, "dp", [(0, 1), (1, 0)])
+
+
+def shift_row(block, by):
+    count = lax.axis_size("row")
+    return lax.ppermute(block, "row", [(i, (i + by) % count) for i in range(count)])
+
+
+def by_place(blocks):
+    column = lax.axis_index("col")
+    pairs = blocks.reshape(-1, 2, *blocks.shape[1:])
+    pairs = jnp.where(column % 2 == 1, pairs[:, ::-1], pairs)
+    return upper_bit(pairs).reshape(blocks.shape)
+
+
+def upper_bit(blocks):
+    return jnp.where(lax.axis_index("col") // 2 == 1, blocks[::-1], blocks)
+
+
+def short_rows():
+    return lax.axis_size("row") == 4 and lax.axis_size("dp") == 2 and lax.axis_size("col") == 4
+
+
+def assemble_kernel(place, first, first_x, second, second_y, first_y, second_x, out, sems):
+    dp, row = place[0], place[1]
+    copies = []
+    for m in range(2):
+        for source, dx, dy, at in (
+            (first.at[m], 0, 0, m),
+            (first_x.at[m], 1, 0, m),
+            (second.at[m], 0, 0, m + 2),
+            (second_y.at[m], 0, 1, m + 2),
+            (first_y.at[0, m], 0, 1, m),
+            (first_y.at[1, m], 1, 1, m),
+            (second_x.at[0, m], 1, 0, m + 2),
+            (second_x.at[1, m], 1, 1, m + 2),
+        ):
+            target = out.at[dx, 1 - dp if dy else dp, lax.rem(row + 4 - at, 4)]
+            copies.append(pltpu.make_async_copy(source, target, sems.at[len(copies)]))
+    for copy in copies:
+        copy.start()
+    for copy in copies:
+        copy.wait()
+
+
+def assemble(pieces):
+    block = pieces[0].shape[1:]
+    place = jnp.stack([lax.axis_index("dp"), lax.axis_index("row")]).astype(jnp.int32)
+    out = pl.pallas_call(
+        assemble_kernel,
+        grid_spec=pltpu.PrefetchScalarGridSpec(
+            num_scalar_prefetch=1,
+            grid=(1,),
+            in_specs=[pl.BlockSpec(memory_space=pl.ANY)] * 6,
+            out_specs=pl.BlockSpec(memory_space=pl.ANY),
+            scratch_shapes=[pltpu.SemaphoreType.DMA((16,))],
+        ),
+        out_shape=jax.ShapeDtypeStruct((2, 2, 4, *block), bf16),
+        cost_estimate=pl.CostEstimate(
+            flops=0, bytes_accessed=64 * block[0] * block[1], transcendentals=0
+        ),
+        name="assemble",
+    )(place, *pieces)
+    return out.reshape(2, -1, block[1])
+
+
+def spread_rows(block):
+    return [block] + [shift_row(block, m) for m in range(1, 4)]
+
+
+def spread_one(pieces):
+    first, second = jnp.stack(pieces[:2]), jnp.stack(pieces[2:])
+    return [first, flip_col(first, 2), second, flip_dp(second)]
+
+
+def spread_two(pieces):
+    first_y = flip_dp(jnp.stack(pieces[:2]))
+    return [*pieces, first_y, flip_col(jnp.stack(pieces[2:]), 2)]
+
+
+def gather_groups(block):
     whole = lax.all_gather(block, AXES, axis=0, tiled=False, axis_index_groups=planes())
-    return whole.reshape(lax.axis_size("col") // 2, -1, block.shape[-1])
-
-
-def scatter_plane(blocks):
-    flat = blocks.reshape(-1, blocks.shape[-1])
-    return lax.psum_scatter(
-        flat, AXES, scatter_dimension=0, tiled=True, axis_index_groups=planes()
-    )
+    return upper_bit(whole.reshape(lax.axis_size("col") // 2, -1, block.shape[-1]))
+
+
+def together(*arrays):
+    return lax.optimization_barrier(arrays)
+
+
+def added(one, other):
+    return (one.astype(f32) + other.astype(f32)).astype(bf16)
+
+
+def at_place(array, which, axis):
+    return lax.dynamic_index_in_dim(array, which, axis, keepdims=False)
+
+
+def scatter_one(blocks):
+    if not short_rows():
+        return blocks
+    dp = lax.axis_index("dp")
+    parts = blocks.reshape(2, 2, 4, -1, blocks.shape[-1])
+    first, second = parts[:, :, :2], parts[:, :, 2:]
+    first_y = flip_dp(at_place(first, 1 - dp, 1))
+    second_x = flip_col(second[1], 2)
+    return added(at_place(first, dp, 1), first_y), added(second[0], second_x)
+
+
+def scatter_two(halves):
+    if not short_rows():
+        return halves
+    dp = lax.axis_index("dp")
+    first, second = halves
+    first_x = flip_col(first[1], 2)
+    second_y = flip_dp(at_place(second, 1 - dp, 0))
+    return jnp.concatenate(
+        [added(first[0], first_x), added(at_place(second, dp, 0), second_y)], 0
+    )
+
+
+def scatter_three(rows):
+    if not short_rows():
+        flat = upper_bit(rows).reshape(-1, rows.shape[-1])
+        return lax.psum_scatter(
+            flat, AXES, scatter_dimension=0, tiled=True, axis_index_groups=planes()
+        ).astype(f32)
+    row = lax.axis_index("row")
+    total = at_place(rows, row, 0).astype(f32)
+    for m in range(1, 4):
+        total = total + shift_row(at_place(rows, (row + m) % 4, 0), m).astype(f32)
+    return total
 
 
 def local(
@@ -518,20 +640,15 @@
     piece = qkv_weight.shape[2]
     halves = SEQ // here
     each = cols // 2
-    odd = lax.rem(column, 2)
-    even_here = odd == 0
-    parity = odd.reshape(1).astype(jnp.int32)
-    places_own = (odd + 2 * jnp.arange(each)).astype(jnp.int32)
-    places_oth = (1 - odd + 2 * jnp.arange(each)).astype(jnp.int32)
+    column_word = column.reshape(1).astype(jnp.int32)
+    places_own = (column ^ (2 * jnp.arange(each))).astype(jnp.int32)
+    places_oth = (column ^ (2 * jnp.arange(each) + 1)).astype(jnp.int32)
     later = lax.rem(column, halves).reshape(1).astype(jnp.int32)
     padded = -(-width // LANES) * LANES
     spare = padded - width
     lanes_qkv = -(-3 * piece // LANES) * LANES
     lead_out = 3 * piece // LANES * LANES
     lanes_out = padded - lead_out
-
-    def by_parity(own, oth):
-        return jnp.where(even_here, own, oth), jnp.where(even_here, oth, own)
 
     vec_shape = vectors.shape
     vec_count = vec_shape[0] * vec_shape[1]
@@ -546,21 +663,31 @@
         ],
         1,
     )
-    attn_own = gather_plane(attn_block)
+    up_block, down_block = up_weight.astype(bf16), down_weight.T.astype(bf16)
+    staged = short_rows()
+    if staged:
+        attn_one = spread_one(spread_rows(attn_block))
+        up_block, attn_one = together(up_block, attn_one)
+        up_rows = spread_rows(up_block)
+        down_block, up_rows = together(down_block, up_rows)
+        down_rows = spread_rows(down_block)
+        attn_own = assemble(spread_two(attn_one))
+        up_one, down_one = spread_one(up_rows), spread_one(down_rows)
+    else:
+        attn_own, up_own, down_own = [
+            gather_groups(b) for b in (attn_block, up_block, down_block)
+        ]
     vec_own = attn_own.reshape(each, owners, rows_own, padded)[:, :, :vec_lines, width:]
     vec_oth = partner(vec_own)
     attn_oth = partner(attn_own)
-    up_own = gather_plane(up_weight.astype(bf16))
-    up_oth = partner(up_own)
-    down_own = gather_plane(down_weight.T.astype(bf16))
-    down_oth = partner(down_own)
 
     def vec_rows(lines):
         lines = lines.reshape(each, owners, vec_lines * spare)[:, :, :vec_count]
         lines = lines.reshape(each, owners, *vec_shape).transpose(0, 2, 1, 3)
         return lines.reshape(each, vec_shape[0], width).astype(f32)
 
-    vec = jnp.stack(by_parity(vec_rows(vec_own), vec_rows(vec_oth)), 1).reshape(-1, width)
+    vec = jnp.stack([vec_rows(vec_own), vec_rows(vec_oth)], 1).reshape(cols, -1, width)
+    vec = by_place(vec).reshape(-1, width)
 
     def widen(row):
         return jnp.pad(row, (0, spare))
@@ -568,6 +695,9 @@
     inputs = hidden_in.astype(f32)
     normed_one, scaled_one, inverse_one = normalize(inputs, vec[0], vec[1])
     normed_low = normed_one.astype(bf16)
+    if staged:
+        normed_low, up_one = together(normed_low, up_one)
+        up_two = spread_two(up_one)
     bias = jnp.concatenate([widen(vec[2]), jnp.zeros((padded,), f32), widen(vec[3])]).reshape(1, -1)
     spans = tuple((part * piece, part * padded) for part in range(3))
     projected = None
@@ -575,6 +705,9 @@
         projected = multiply_and_place(
             places, normed_low, [weights], lanes_qkv, 0, spans, piece, 3 * padded, bias, projected
         )
+    if staged:
+        projected, down_one = together(projected, down_one)
+        down_two = spread_two(down_one)
     ahead = [(c, c + 1) for c in range(cols - 1) if c % halves + 1 < halves]
     behind = [(b, a) for a, b in ahead]
     others = lax.ppermute(projected[:, padded:], "col", ahead)
@@ -585,11 +718,15 @@
     )
     labels = (own_half.reshape(1, here), own_half.reshape(here, 1), first_half.reshape(here, 1))
     mixed, log_totals = attend(later, labels, projected, others)
+    if staged:
+        mixed, up_two = together(mixed, up_two)
+        up_own = assemble(up_two)
+    up_oth = partner(up_own)
     mixed_shape = jax.ShapeDtypeStruct((each, here, lanes_out), bf16)
     lead = 3 * piece - lead_out
     mixed_own, mixed_oth = split_call(
         functools.partial(split_mixed_kernel, piece, cols, lead),
-        parity,
+        column_word,
         [mixed],
         [mixed_shape] * 2,
         "split_mixed",
@@ -601,8 +738,8 @@
     normed_two, scaled_two, inverse_two = normalize(residual, vec[5], vec[6])
     normed_two_low = normed_two.astype(bf16)
 
-    bias_even, bias_odd = vec[8::2], vec[9::2]
-    bias_own, bias_oth = by_parity(bias_even, bias_odd)
+    bias_up = by_place(vec[8:])
+    bias_own, bias_oth = bias_up[0::2], bias_up[1::2]
 
     def up_part(ups, biases):
         return [
@@ -611,10 +748,12 @@
         ]
 
     linear_own = up_part(up_own, bias_own)
+    if staged:
+        linear_own, down_two = together(linear_own, down_two)
+        down_own = assemble(down_two)
+    down_oth = partner(down_own)
     linear_oth = up_part(up_oth, bias_oth)
-    (linear_own, linear_oth, down_own) = lax.optimization_barrier(
-        (linear_own, linear_oth, down_own)
-    )
+
     branch = jnp.zeros((here, width), f32)
 
     def forward_part(linears, downs, branch):
@@ -630,18 +769,20 @@
     lows_oth, pull_oth, branch = forward_part(linear_oth, down_oth, branch)
     layer_out = (residual + branch + vec[7]).astype(bf16)
 
-    def paired_sum(left, rights_own, rights_oth):
-        send = jnp.stack([contract_first(left, r).astype(bf16) for r in rights_oth])
-        received = partner(send)
-        total = jnp.stack(
+    def partner_grads(left, rights):
+        return jnp.stack([contract_first(left, r).astype(bf16) for r in rights])
+
+    def plane_grads(left, rights, received):
+        return jnp.stack(
             [
                 (contract_first(left, r) + received[i].astype(f32)).astype(bf16)
-                for i, r in enumerate(rights_own)
+                for i, r in enumerate(rights)
             ]
         )
-        return scatter_plane(total).astype(f32)
-
-    sum_down = paired_sum(cotangent, lows_own, lows_oth)
+
+    sent_down = partner_grads(cotangent, lows_oth)
+    down_oth, sent_down = together(down_oth, sent_down)
+    received_down = partner(sent_down)
 
     grad_normed_two = jnp.zeros((here, width), f32)
 
@@ -658,10 +799,15 @@
     dups_oth, dbias_oth, grad_normed_two = backward_part(
         up_oth, down_oth, pull_oth, grad_normed_two
     )
+    lows_own, dups_oth = together(lows_own, dups_oth)
+    total_down = plane_grads(cotangent, lows_own, received_down)
+    sent_up = partner_grads(normed_two_low, dups_oth)
+    down_own, total_down, sent_up = together(down_own, total_down, sent_up)
+    received_up = partner(sent_up)
+    one_down = scatter_one(total_down)
     dups_own, dbias_own, grad_normed_two = backward_part(
         up_own, down_own, pull_own, grad_normed_two
     )
-    sum_up = paired_sum(normed_two_low, dups_own, dups_oth)
 
     grad_residual = cotangent.astype(f32) + norm_back(
         grad_normed_two, scaled_two, inverse_two, vec[5]
@@ -679,25 +825,33 @@
         None,
         None,
     )
+    total_up = plane_grads(normed_two_low, dups_own, received_up)
+    grad_mixed, total_up, one_down = together(grad_mixed, total_up, one_down)
     dq, dk_own, dv_own, dk_oth, dv_oth = attend_back(
         later, labels, projected, others, grad_mixed, mixed, log_totals
     )
     back = lax.ppermute(jnp.concatenate([dk_oth, dv_oth], 1), "col", behind)
+    two_down = scatter_two(one_down)
+    one_up = scatter_one(total_up)
+    dq, dk_own, dv_own, two_down, one_up = together(dq, dk_own, dv_own, two_down, one_up)
     grads_shape = jax.ShapeDtypeStruct((each, here, lanes_qkv), bf16)
     grads_own, grads_oth, grad_sums = split_call(
         functools.partial(split_grads_kernel, piece, cols),
-        parity,
+        column_word,
         [dq, dk_own, dv_own, back],
         [grads_shape, grads_shape, jax.ShapeDtypeStruct((8, padded), f32)],
         "split_grads",
     )
+    two_up = scatter_two(one_up)
+    left_one, left_two = normed_low.T, grad_residual_low.T
+    received = partner(block_grads(left_one, left_two, grads_oth, mixed_oth, None))
     grad_normed_one = jnp.zeros((here, width), f32)
     for blocks, weights in ((grads_own, attn_own), (grads_oth, attn_oth)):
         for i in range(each):
             grad_normed_one = grad_normed_one + contract_last(blocks[i], weights[i][:, :lanes_qkv])
     input_grad = grad_residual + norm_back(grad_normed_one, scaled_one, inverse_one, vec[0])
 
-    dbias_even, dbias_odd = by_parity(jnp.stack(dbias_own), jnp.stack(dbias_oth))
+    dbias = jnp.stack([jnp.stack(dbias_own), jnp.stack(dbias_oth)], 1).reshape(cols, width)
     grad_vector = jnp.concatenate(
         [
             jnp.stack(
@@ -712,24 +866,22 @@
                     jnp.sum(cotangent.astype(f32), 0),
                 ]
             ),
-            jnp.stack([dbias_even, dbias_odd], 1).reshape(cols, width),
+            by_place(dbias),
         ],
         0,
     ).astype(bf16)
     vec_part = grad_vector.reshape(cols, vec_shape[0], owners, vec_shape[1]).transpose(0, 2, 1, 3)
     vec_part = jnp.pad(vec_part.reshape(cols, owners, vec_count), ((0, 0), (0, 0), (0, vec_fill)))
-    vec_part = jnp.pad(
-        vec_part.reshape(cols, owners, vec_lines, spare),
-        ((0, 0), (0, 0), (0, rows_own - vec_lines), (LANES - spare, 0)),
-    ).reshape(cols, width, LANES)
-    vec_here, vec_there = by_parity(vec_part[0::2], vec_part[1::2])
-    left_one, left_two = normed_low.T, grad_residual_low.T
-    received = partner(
-        block_grads(left_one, left_two, grads_oth, mixed_oth, vec_there, None, lead_out)
-    )
-    sum_attn = scatter_plane(
-        block_grads(left_one, left_two, grads_own, mixed_own, vec_here, received, lead_out)
-    ).astype(f32)
+    vec_part = by_place(vec_part.reshape(cols, owners, vec_lines, spare))
+    vec_here = (vec_part[0::2].astype(f32) + partner(vec_part[1::2]).astype(f32)).astype(bf16)
+    vec_here = jnp.pad(
+        vec_here, ((0, 0), (0, 0), (0, rows_own - vec_lines), (LANES - spare, 0))
+    ).reshape(each, width, LANES)
+    total_attn = block_grads(
+        left_one, left_two, grads_own, mixed_own, (vec_here, received)
+    )
+    sum_down, sum_up = scatter_three(two_down), scatter_three(two_up)
+    sum_attn = scatter_three(scatter_two(scatter_one(total_attn)))
     sum_qkv = sum_attn[:, : 3 * piece].reshape(rows_own, 3, piece)
     sum_out = sum_attn[:, 3 * piece : width].T
     sum_vector = sum_attn[:vec_lines, width:].reshape(-1)[:vec_count].reshape(vec_shape)

time: 783 us -> 1010 us (1.29)
  Pallas kernels: 77.8 us -> 540 us
  waiting for transfers between devices: 482 us -> 181 us
  starting transfers between devices: 34.4 us -> 69.2 us
  other arithmetic: 39 us -> 69.9 us
  local copies, waits for them, and re-layouts: 34.6 us -> 50.5 us
  between operations: 15.9 us -> 2.72 us
    pallas_call x2 -> x5, Pallas kernels: 12.4 us -> 474 us  [the longest x3 461 us: assemble(): pl.pallas_call(assemble_kernel, grid_spec=pltpu.PrefetchScalarGridSpec(nu...]
    unnamed x9 -> x0, waiting for transfers between devices: 257 us -> none
    all_gather x3 -> x0, waiting for transfers between devices: 206 us -> none  [gather_plane(): lax.all_gather(block, AXES, axis=0, tiled=False, axis_index_groups=planes())]
    ppermute x7 -> x50, waiting for transfers between devices: 16.3 us -> 181 us  [the longest x18 89.5 us: shift_row(): lax.ppermute(block, 'row', [(i, (i + by) % count) for i in range(count)])]
    ppermute x7 -> x50, starting transfers between devices: 17.3 us -> 66 us  [the longest x18 35.9 us: shift_row(): lax.ppermute(block, 'row', [(i, (i + by) % count) for i in range(count)])]
    another operation x7 -> x22, other arithmetic: 9.09 us -> 26.2 us  [the longest x3 7.16 us: spread_two(): first_y = flip_dp(jnp.stack(pieces[:2]))]
    ppermute x1, starting transfers between devices: 15.1 us -> 1.83 us  [local(): others = lax.ppermute(projected[:, padded:], 'col', ahead)]
    convert_element_type x3 -> x17, other arithmetic: 1.55 us -> 14.5 us  [the longest x12 12.3 us: added(): return (one.astype(f32) + other.astype(f32)).astype(bf16)]
  transfers between devices with their start and end apart: 15 -> 52, of which waited for: 9 -> 22; matrix products, arithmetic and copies ran while one was open for 15% -> 16% of each run, Pallas kernels for 10% -> 54%
where the time goes in v3:
time: 1010 us; the launch traced here: 995 us
  Pallas kernels  540 us (53%)
  waiting for transfers between devices  181 us (18%)
  matrix products  81.9 us (8%)
  other arithmetic  69.9 us (7%)
  starting transfers between devices  69.2 us (7%)
  local copies, waits for them, and re-layouts  50.5 us (5%)
    pallas_call x3, Pallas kernels, assemble(): pl.pallas_call(assemble_kernel, grid_spec=pltpu.PrefetchScalarGridSpec(nu...  461 us
    ppermute x18, waiting for transfers between devices, shift_row(): lax.ppermute(block, 'row', [(i, (i + by) % count) for i in range(count)])  89.5 us
    dot_general x24, matrix products, contract(): lax.dot_general(left, right, (((left_dim,), (right_dim,)), ((), ())), pre...  56.8 us
    ppermute x12, waiting for transfers between devices, flip_dp(): return lax.ppermute(block, 'dp', [(0, 1), (1, 0)])  53.8 us
    ppermute x20, waiting for transfers between devices, flip_col(): lax.ppermute(block, 'col', [(c, c ^ bit) for c in range(lax.axis_size('co...  37.9 us
    ppermute x18, starting transfers between devices, shift_row(): lax.ppermute(block, 'row', [(i, (i + by) % count) for i in range(count)])  35.9 us
    pallas_call x3, Pallas kernels, multiply_and_place(): pl.pallas_call(functools.partial(place_kernel, spans, piece, sources, bia...  22.2 us
  transfers between devices with their start and end apart: 52, of which 22 were waited for; matrix products, arithmetic and copies ran while one was open for 16% of the time, Pallas kernels for 54%

profile of v3, /device:TPU:0, one launch (start us, length us, event | category | flops | bytes accessed | tf_op | source)
XLA Modules:
  0.0 995.0 jit_solution(17581689897304507854)
XLA Ops:
  2.7 3.1 collective-permute-start
  8.8 7.3 collective-permute-done
  18.0 3.4 collective-permute-done.3
  21.4 14.0 %collective-permute-done.2 = bf16[136,1152]{1,0:T(8,128)(2,1)S(1)} collective-permute-done((bf16[136,1152]{1,0:T(8,128)(2,1)S(1)}, bf16[136,1152]{1,0:T(8,128)(2,1)S(1)}, u32[]{:S(2)}, u32[]{:S(2)}) %collective-permute-start.2) | collective-permute-done | bytes 313376 | tf_op jit(solution)/shard_map/ppermute | solution.py:487
  38.1 13.5 %collective-permute-done.4.second_y = bf16[2,136,1152]{2,1,0:T(8,128)(2,1)} collective-permute-done((bf16[2,136,1152]{2,1,0:T(8,128)(2,1)S(1)}, bf16[2,136,1152]{2,1,0:T(8,128)(2,1)}, u32[]{:S(2)}, u32[]{:S(2)}) %collective-permute-start.4) | collective-permute-done | bytes 626720 | tf_op jit(solution)/shard_map/ppermute | solution.py:482
  51.6 2.4 pad_maximum_fusion.5
  62.8 2.7 collective-permute-start.10
  66.1 8.0 collective-permute-done.8
  74.1 11.1 %collective-permute-done.9 = bf16[136,1088]{1,0:T(8,128)(2,1)S(1)} collective-permute-done((bf16[136,1088]{1,0:T(8,128)(2,1)}, bf16[136,1088]{1,0:T(8,128)(2,1)S(1)}, u32[]{:S(2)}, u32[]{:S(2)}) %collective-permute-start.9) | collective-permute-done | bytes 295968 | tf_op jit(solution)/shard_map/ppermute | solution.py:487
  85.2 13.0 %collective-permute-start.14 = (bf16[136,1088]{1,0:T(8,128)(2,1)S(1)}, bf16[136,1088]{1,0:T(8,128)(2,1)}, u32[]{:S(2)}, u32[]{:S(2)}) collective-permute-start(bf16[136,1088]{1,0:T(8,128)(2,1)S(1)} %convert_bitcast_fusion), channel_id=1, source_target_pairs={{0,4},{4,8},{8,12},{12,0},{1,5},{5,9},{9,13},{13,1},{2,6},{6,10},{... | collective-permute-start | bytes 887816 | tf_op jit(solution)/shard_map/ppermute | solution.py:487
  99.8 153.8 %assemble.3 = bf16[2,2,4,136,1152]{4,3,2,1,0:T(8,128)(2,1)} custom-call(s32[2]{0:T(128)} %pad_add_fusion.place, bf16[2,136,1152]{2,1,0:T(8,128)(2,1)} %copy-done.27, bf16[2,136,1152]{2,1,0:T(8,128)(2,1)} %collective-permute-done.1.first_x, bf16[2,136,1152]{2,1,0:T(8,128)(2,1)} %copy-done.28, bf16[2,136,1152]{2,1,0:T(8,128)(2,1)} %collective-permute-done.4.second_y, ...), custom_call_target="tpu_custom_call" | custom-call | bytes 10027008 | tf_op jit(solution)/shard_map/assemble/pallas_call | solution.py:530
  261.3 2.6 fusion.163
  268.9 3.0 collective-permute-done.11.first_x
  274.1 2.5 pad_maximum_fusion.7
  277.1 7.2 multiply_and_place.3.refs_2_
  286.1 8.5 multiply_and_place.4.q.k_own.v_own
  305.1 2.5 pad_maximum_fusion.10
  308.2 2.8 slice_bitcast_fusion.11
  311.1 17.4 %attention_forward.1 = (bf16[512,1152]{1,0:T(8,128)(2,1)S(1)}, f32[9,2,512]{2,1,0:T(2,128)S(1)}) custom-call(s32[1]{0:T(128)} %bitcast.15.later, s32[1,512]{1,0:T(1,128)S(1)} %bitcast.376, s32[512,1]{1,0:T(8,128)S(1)} %copy.72.kseg_own, s32[512,1]{1,0:T(8,128)S(1)} %copy.73.kseg_oth, bf16[512,3456]{1,0:T(8,128)(2,1)} %copy-done, bf16[512,3456]{1,0:T(8,128)(2,1)} %copy-done, ...), custom_call_target="tpu_custom_call" | custom-call | flops 2415919104 | bytes 7077888 | tf_op jit(solution)/shard_map/attention_forward/pallas_call | solution.py:232
  338.3 153.8 %assemble.4 = bf16[2,2,4,136,1088]{4,3,2,1,0:T(8,128)(2,1)} custom-call(s32[2]{0:T(128)} %pad_add_fusion.place, bf16[2,136,1088]{2,1,0:T(8,128)(2,1)} %pad_maximum_fusion.14.first, bf16[2,136,1088]{2,1,0:T(8,128)(2,1)} %collective-permute-done.11.first_x, bf16[2,136,1088]{2,1,0:T(8,128)(2,1)} %pad_maximum_fusion.15.second, ...), custom_call_target="tpu_custom_call" | custom-call | bytes 9469952 | tf_op jit(solution)/shard_map/assemble/pallas_call | solution.py:530
  492.1 3.0 fusion.162
  495.1 2.4 collective-permute-start.24
  498.3 3.1 convolution_add_fusion.12
  501.4 3.0 convolution_add_fusion.11
  504.4 153.8 %assemble.5 = bf16[2,2,4,136,1088]{4,3,2,1,0:T(8,128)(2,1)} custom-call(s32[2]{0:T(128)} %pad_add_fusion.place, bf16[2,136,1088]{2,1,0:T(8,128)(2,1)} %copy-done.30, bf16[2,136,1088]{2,1,0:T(8,128)(2,1)} %collective-permute-done.15.first_x, bf16[2,136,1088]{2,1,0:T(8,128)(2,1)} %pad_maximum_fusion.17.second, ...), custom_call_target="tpu_custom_call" | custom-call | bytes 9469952 | tf_op jit(solution)/shard_map/assemble/pallas_call | solution.py:530
  658.9 2.8 fusion.161
  664.8 3.0 convolution_add_fusion.8
  667.8 3.5 convolution_add_fusion.9
  673.6 3.4 convolution_add_fusion.10
  679.9 3.0 fusion.164
  682.9 3.0 fusion.165
  691.3 4.9 fusion.80
  699.2 2.8 fusion.14
  702.1 3.1 pad_maximum_fusion.2
  705.1 4.5 fusion.21
  709.6 2.9 pad_maximum_fusion.1
  712.6 3.0 fusion.169
  715.6 3.2 fusion.168
  721.1 3.5 fusion.9
  729.2 2.8 convert_element_type.412
  733.6 8.4 copy.75
  745.7 2.4 slice_bitcast_fusion.20
  750.0 6.5 multiply_and_place.5.grad
  760.2 15.0 %collective-permute-done.28 = bf16[2,2,136,1088]{3,2,1,0:T(8,128)(2,1)} collective-permute-done((bf16[2,2,136,1088]{3,2,1,0:T(8,128)(2,1)}, bf16[2,2,136,1088]{3,2,1,0:T(8,128)(2,1)}, u32[]{:S(2)}, u32[]{:S(2)}) %collective-permute-start.28) | collective-permute-done | bytes 1183776 | tf_op jit(solution)/shard_map/ppermute | solution.py:482
  779.9 3.5 fusion.24
  783.4 3.4 fusion.23
  795.1 19.9 %attention_backward.1 = (bf16[512,1152]{1,0:T(8,128)(2,1)S(1)}, bf16[512,1152]{1,0:T(8,128)(2,1)S(1)}, bf16[512,1152]{1,0:T(8,128)(2,1)S(1)}, bf16[512,1152]{1,0:T(8,128)(2,1)S(1)}, bf16[512,1152]{1,0:T(8,128)(2,1)}) custom-call(s32[1]{0:T(128)} %bitcast.15.later, s32[1,512]{1,0:T(1,128)S(1)} %bitcast.377, s32[512,1]{1,0:T(8,128)S(1)} %copy.72.kseg_own, ...), custom_call_target="tpu_custom_call" | custom-call | flops 6039797760 | bytes 14155776 | tf_op jit(solution)/shard_map/attention_backward/pallas_call | solution.py:258
  820.6 10.6 %collective-permute-done.32 = bf16[2,2,136,1088]{3,2,1,0:T(8,128)(2,1)} collective-permute-done((bf16[2,2,136,1088]{3,2,1,0:T(8,128)(2,1)}, bf16[2,2,136,1088]{3,2,1,0:T(8,128)(2,1)}, u32[]{:S(2)}, u32[]{:S(2)}) %collective-permute-start.32) | collective-permute-done | bytes 1183776 | tf_op jit(solution)/shard_map/ppermute | solution.py:482
  835.2 3.0 collective-permute-start.51
  838.8 5.2 split_grads.1
  846.2 5.7 block_grads.2
  854.5 9.4 collective-permute-done.50
  863.8 2.7 multiply_subtract_fusion
  866.5 3.4 collective-permute-done.45
  877.3 3.5 fusion.46
  883.2 3.3 collective-permute-start.48
  887.8 7.2 block_grads.3
  898.1 17.2 %collective-permute-done.47 = bf16[136,1088]{1,0:T(8,128)(2,1)S(1)} collective-permute-done((bf16[136,1088]{1,0:T(8,128)(2,1)S(1)}, bf16[136,1088]{1,0:T(8,128)(2,1)S(1)}, u32[]{:S(2)}, u32[]{:S(2)}) %collective-permute-start.47) | collective-permute-done | bytes 295968 | tf_op jit(solution)/shard_map/ppermute | solution.py:487
  918.3 8.2 collective-permute-done.37
  927.5 20.7 %collective-permute-done.39 = bf16[2,2,136,1152]{3,2,1,0:T(8,128)(2,1)S(1)} collective-permute-done((bf16[2,2,136,1152]{3,2,1,0:T(8,128)(2,1)S(1)}, bf16[2,2,136,1152]{3,2,1,0:T(8,128)(2,1)S(1)}, u32[]{:S(2)}, u32[]{:S(2)}) %collective-permute-start.39) | collective-permute-done | bytes 1253408 | tf_op jit(solution)/shard_map/ppermute | solution.py:474
  949.4 10.7 %collective-permute-done.38 = bf16[2,136,1152]{2,1,0:T(8,128)(2,1)S(1)} collective-permute-done((bf16[2,136,1152]{2,1,0:T(8,128)(2,1)S(1)}, bf16[2,136,1152]{2,1,0:T(8,128)(2,1)S(1)}, u32[]{:S(2)}, u32[]{:S(2)}) %collective-permute-start.38) | collective-permute-done | bytes 626720 | tf_op jit(solution)/shard_map/ppermute | solution.py:474
  965.6 3.7 fusion.45
  970.6 17.9 %collective-permute-done.42 = bf16[136,1152]{1,0:T(8,128)(2,1)S(1)} collective-permute-done((bf16[136,1152]{1,0:T(8,128)(2,1)S(1)}, bf16[136,1152]{1,0:T(8,128)(2,1)S(1)}, u32[]{:S(2)}, u32[]{:S(2)}) %collective-permute-start.42) | collective-permute-done | bytes 313376 | tf_op jit(solution)/shard_map/ppermute | solution.py:487
  991.6 2.7 multiply_subtract_fusion.2
  (438 shorter events, 151.1 us)
Async XLA Ops:
  2.0 35.0 %copy-start.44 = (f32[136,1088]{1,0:T(8,128)S(1)}, f32[136,1088]{1,0:T(8,128)}, u32[]{:S(2)}) copy-start(f32[136,1088]{1,0:T(8,128)} %param.23) | copy-start | bytes 1775620
  2.3 35.5 %copy-start.74 = (s32[2,1024]{1,0:T(2,128)S(1)}, s32[2,1024]{1,0:T(2,128)}, u32[]{:S(2)}) copy-start(s32[2,1024]{1,0:T(2,128)} %param.20) | copy-start | bytes 24580
  2.3 35.6 %copy-start.15 = (bf16[512,1088]{0,1:T(8,128)(2,1)S(1)}, bf16[512,1088]{0,1:T(8,128)(2,1)}, u32[]{:S(2)}) copy-start(bf16[512,1088]{0,1:T(8,128)(2,1)} %param.18) | copy-start | bytes 3342340
  2.7 13.4 %collective-permute-start = (bf16[136,1152]{1,0:T(8,128)(2,1)S(1)}, bf16[136,1152]{1,0:T(8,128)(2,1)S(1)}, u32[]{:S(2)}, u32[]{:S(2)}) collective-permute-start(bf16[136,1152]{1,0:T(8,128)(2,1)S(1)} %concatenate.26), channel_id=1, source_target_pairs={{0,4},{4,8},{8,12},{12,0},{1,5},{5,9},{9,13},{13,1},{2,6},{6,10},{... | collective-permute-start | bytes 940040 | tf_op jit(solution)/shard_map/ppermute | solution.py:487
  5.8 15.6 %collective-permute-start.3 = (bf16[136,1152]{1,0:T(8,128)(2,1)S(1)}, bf16[136,1152]{1,0:T(8,128)(2,1)S(1)}, u32[]{:S(2)}, u32[]{:S(2)}) collective-permute-start(bf16[136,1152]{1,0:T(8,128)(2,1)S(1)} %concatenate.26), channel_id=1, source_target_pairs={{0,12},{4,0},{8,4},{12,8},{1,13},{5,1},{9,5},{13,9},{2,14},{6,2},{... | collective-permute-start | bytes 940040 | tf_op jit(solution)/shard_map/ppermute | solution.py:487
  7.9 27.5 %collective-permute-start.2 = (bf16[136,1152]{1,0:T(8,128)(2,1)S(1)}, bf16[136,1152]{1,0:T(8,128)(2,1)S(1)}, u32[]{:S(2)}, u32[]{:S(2)}) collective-permute-start(bf16[136,1152]{1,0:T(8,128)(2,1)S(1)} %concatenate.26), channel_id=1, source_target_pairs={{0,8},{4,12},{8,0},{12,4},{1,9},{5,13},{9,1},{13,5},{2,10},{6,14},... | collective-permute-start | bytes 940040 | tf_op jit(solution)/shard_map/ppermute | solution.py:487
  16.1 37.9 %copy-start.27 = (bf16[2,136,1152]{2,1,0:T(8,128)(2,1)}, bf16[2,136,1152]{2,1,0:T(8,128)(2,1)S(1)}, u32[]{:S(2)}) copy-start(bf16[2,136,1152]{2,1,0:T(8,128)(2,1)S(1)} %pad_maximum_fusion.12.first) | copy-start | bytes 1880068
  16.2 21.9 %collective-permute-start.1 = (bf16[2,136,1152]{2,1,0:T(8,128)(2,1)S(1)}, bf16[2,136,1152]{2,1,0:T(8,128)(2,1)}, u32[]{:S(2)}, u32[]{:S(2)}) collective-permute-start(bf16[2,136,1152]{2,1,0:T(8,128)(2,1)S(1)} %pad_maximum_fusion.12.first), channel_id=1, source_target_pairs={{0,2},{1,3},{2,0},{3,1},{4,6},{5,7},{6,4},{7,5},{8,10},{9,11},{10,... | collective-permute-start | bytes 1880072 | tf_op jit(solution)/shard_map/ppermute | solution.py:474
  35.4 16.2 %collective-permute-start.4 = (bf16[2,136,1152]{2,1,0:T(8,128)(2,1)S(1)}, bf16[2,136,1152]{2,1,0:T(8,128)(2,1)}, u32[]{:S(2)}, u32[]{:S(2)}) collective-permute-start(bf16[2,136,1152]{2,1,0:T(8,128)(2,1)S(1)} %pad_maximum_fusion.13.second), channel_id=1, source_target_pairs={{0,16},{16,0},{1,17},{17,1},{2,18},{18,2},{3,19},{19,3},{4,20},{20... | collective-permute-start | bytes 1880072 | tf_op jit(solution)/shard_map/ppermute | solution.py:482
  54.0 45.8 %collective-permute-start.5 = (bf16[2,2,136,1152]{3,2,1,0:T(8,128)(2,1)}, bf16[2,2,136,1152]{3,2,1,0:T(8,128)(2,1)}, u32[]{:S(2)}, u32[]{:S(2)}) collective-permute-start(bf16[2,2,136,1152]{3,2,1,0:T(8,128)(2,1)} %pad_maximum_fusion.5), channel_id=1, source_target_pairs={{0,16},{16,0},{1,17},{17,1},{2,18},{18,2},{3,19},{19,3},{4,20},{20... | collective-permute-start | bytes 3760136 | tf_op jit(solution)/shard_map/ppermute | solution.py:482
  57.9 41.9 %collective-permute-start.6 = (bf16[2,2,136,1152]{3,2,1,0:T(8,128)(2,1)}, bf16[2,2,136,1152]{3,2,1,0:T(8,128)(2,1)}, u32[]{:S(2)}, u32[]{:S(2)}) collective-permute-start(bf16[2,2,136,1152]{3,2,1,0:T(8,128)(2,1)} %pad_maximum_fusion.6), channel_id=1, source_target_pairs={{0,2},{1,3},{2,0},{3,1},{4,6},{5,7},{6,4},{7,5},{8,10},{9,11},{10,... | collective-permute-start | bytes 3760136 | tf_op jit(solution)/shard_map/ppermute | solution.py:474
  61.6 12.5 %collective-permute-start.8 = (bf16[136,1088]{1,0:T(8,128)(2,1)}, bf16[136,1088]{1,0:T(8,128)(2,1)S(1)}, u32[]{:S(2)}, u32[]{:S(2)}) collective-permute-start(bf16[136,1088]{1,0:T(8,128)(2,1)} %convert_element_type.373), channel_id=1, source_target_pairs={{0,4},{4,8},{8,12},{12,0},{1,5},{5,9},{9,13},{13,1},{2,6},{6,10},{... | collective-permute-start | bytes 887816 | tf_op jit(solution)/shard_map/ppermute | solution.py:487
  61.6 23.5 %collective-permute-start.9 = (bf16[136,1088]{1,0:T(8,128)(2,1)}, bf16[136,1088]{1,0:T(8,128)(2,1)S(1)}, u32[]{:S(2)}, u32[]{:S(2)}) collective-permute-start(bf16[136,1088]{1,0:T(8,128)(2,1)} %convert_element_type.373), channel_id=1, source_target_pairs={{0,8},{4,12},{8,0},{12,4},{1,9},{5,13},{9,1},{13,5},{2,10},{6,14},... | collective-permute-start | bytes 887816 | tf_op jit(solution)/shard_map/ppermute | solution.py:487
  62.8 22.4 %collective-permute-start.10 = (bf16[136,1088]{1,0:T(8,128)(2,1)}, bf16[136,1088]{1,0:T(8,128)(2,1)S(1)}, u32[]{:S(2)}, u32[]{:S(2)}) collective-permute-start(bf16[136,1088]{1,0:T(8,128)(2,1)} %convert_element_type.373), channel_id=1, source_target_pairs={{0,12},{4,0},{8,4},{12,8},{1,13},{5,1},{9,5},{13,9},{2,14},{6,2},{... | collective-permute-start | bytes 887816 | tf_op jit(solution)/shard_map/ppermute | solution.py:487
  66.1 187.6 %copy-start.53 = (bf16[136,1088]{1,0:T(8,128)(2,1)S(1)}, bf16[136,1088]{1,0:T(8,128)(2,1)}, u32[]{:S(2)}) copy-start(bf16[136,1088]{1,0:T(8,128)(2,1)} %convert_element_type.373) | copy-start | bytes 887812
  85.2 170.9 %collective-permute-start.14 = (bf16[136,1088]{1,0:T(8,128)(2,1)S(1)}, bf16[136,1088]{1,0:T(8,128)(2,1)}, u32[]{:S(2)}, u32[]{:S(2)}) collective-permute-start(bf16[136,1088]{1,0:T(8,128)(2,1)S(1)} %convert_bitcast_fusion), channel_id=1, source_target_pairs={{0,4},{4,8},{8,12},{12,0},{1,5},{5,9},{9,13},{13,1},{2,6},{6,10},{... | collective-permute-start | bytes 887816 | tf_op jit(solution)/shard_map/ppermute | solution.py:487
  98.2 159.4 %collective-permute-start.17 = (bf16[136,1088]{1,0:T(8,128)(2,1)S(1)}, bf16[136,1088]{1,0:T(8,128)(2,1)}, u32[]{:S(2)}, u32[]{:S(2)}) collective-permute-start(bf16[136,1088]{1,0:T(8,128)(2,1)S(1)} %convert_bitcast_fusion), channel_id=1, source_target_pairs={{0,12},{4,0},{8,4},{12,8},{1,13},{5,1},{9,5},{13,9},{2,14},{6,2},{... | collective-permute-start | bytes 887816 | tf_op jit(solution)/shard_map/ppermute | solution.py:487
  98.4 160.8 %collective-permute-start.16 = (bf16[136,1088]{1,0:T(8,128)(2,1)S(1)}, bf16[136,1088]{1,0:T(8,128)(2,1)}, u32[]{:S(2)}, u32[]{:S(2)}) collective-permute-start(bf16[136,1088]{1,0:T(8,128)(2,1)S(1)} %convert_bitcast_fusion), channel_id=1, source_target_pairs={{0,8},{4,12},{8,0},{12,4},{1,9},{5,13},{9,1},{13,5},{2,10},{6,14},... | collective-permute-start | bytes 887816 | tf_op jit(solution)/shard_map/ppermute | solution.py:487
  253.6 32.5 %collective-permute-start.13 = (bf16[2,1088,1152]{2,1,0:T(8,128)(2,1)}, bf16[2,1088,1152]{2,1,0:T(8,128)(2,1)}, u32[]{:S(2)}, u32[]{:S(2)}) collective-permute-start(bf16[2,1088,1152]{2,1,0:T(8,128)(2,1)} %bitcast.378), channel_id=1, source_target_pairs={{0,1},{1,0},{2,3},{3,2},{4,5},{5,4},{6,7},{7,6},{8,9},{9,8},{10,11... | collective-permute-start | bytes 15040520 | tf_op jit(solution)/shard_map/ppermute | solution.py:474
  254.6 17.2 %collective-permute-start.11 = (bf16[2,136,1088]{2,1,0:T(8,128)(2,1)}, bf16[2,136,1088]{2,1,0:T(8,128)(2,1)}, u32[]{:S(2)}, u32[]{:S(2)}) collective-permute-start(bf16[2,136,1088]{2,1,0:T(8,128)(2,1)} %pad_maximum_fusion.14.first), channel_id=1, source_target_pairs={{0,2},{1,3},{2,0},{3,1},{4,6},{5,7},{6,4},{7,5},{8,10},{9,11},{10,... | collective-permute-start | bytes 1775624 | tf_op jit(solution)/shard_map/ppermute | solution.py:474
  256.1 17.3 %collective-permute-start.12 = (bf16[2,136,1088]{2,1,0:T(8,128)(2,1)}, bf16[2,136,1088]{2,1,0:T(8,128)(2,1)}, u32[]{:S(2)}, u32[]{:S(2)}) collective-permute-start(bf16[2,136,1088]{2,1,0:T(8,128)(2,1)} %pad_maximum_fusion.15.second), channel_id=1, source_target_pairs={{0,16},{16,0},{1,17},{17,1},{2,18},{18,2},{3,19},{19,3},{4,20},{20... | collective-permute-start | bytes 1775624 | tf_op jit(solution)/shard_map/ppermute | solution.py:482
  257.6 43.7 %copy-start.30 = (bf16[2,136,1088]{2,1,0:T(8,128)(2,1)}, bf16[2,136,1088]{2,1,0:T(8,128)(2,1)S(1)}, u32[]{:S(2)}) copy-start(bf16[2,136,1088]{2,1,0:T(8,128)(2,1)S(1)} %pad_maximum_fusion.16.first) | copy-start | bytes 1775620
  257.6 37.0 %collective-permute-start.15 = (bf16[2,136,1088]{2,1,0:T(8,128)(2,1)S(1)}, bf16[2,136,1088]{2,1,0:T(8,128)(2,1)}, u32[]{:S(2)}, u32[]{:S(2)}) collective-permute-start(bf16[2,136,1088]{2,1,0:T(8,128)(2,1)S(1)} %pad_maximum_fusion.16.first), channel_id=1, source_target_pairs={{0,2},{1,3},{2,0},{3,1},{4,6},{5,7},{6,4},{7,5},{8,10},{9,11},{10,... | collective-permute-start | bytes 1775624 | tf_op jit(solution)/shard_map/ppermute | solution.py:474
  261.2 2.9 collective-permute-start.7
  264.2 30.5 %collective-permute-start.18 = (bf16[2,136,1088]{2,1,0:T(8,128)(2,1)}, bf16[2,136,1088]{2,1,0:T(8,128)(2,1)}, u32[]{:S(2)}, u32[]{:S(2)}) collective-permute-start(bf16[2,136,1088]{2,1,0:T(8,128)(2,1)} %pad_maximum_fusion.17.second), channel_id=1, source_target_pairs={{0,16},{16,0},{1,17},{17,1},{2,18},{18,2},{3,19},{19,3},{4,20},{20... | collective-permute-start | bytes 1775624 | tf_op jit(solution)/shard_map/ppermute | solution.py:482
  276.6 52.0 %collective-permute-start.20 = (bf16[2,2,136,1088]{3,2,1,0:T(8,128)(2,1)}, bf16[2,2,136,1088]{3,2,1,0:T(8,128)(2,1)}, u32[]{:S(2)}, u32[]{:S(2)}) collective-permute-start(bf16[2,2,136,1088]{3,2,1,0:T(8,128)(2,1)} %pad_maximum_fusion.7), channel_id=1, source_target_pairs={{0,16},{16,0},{1,17},{17,1},{2,18},{18,2},{3,19},{19,3},{4,20},{20... | collective-permute-start | bytes 3551240 | tf_op jit(solution)/shard_map/ppermute | solution.py:482
  296.4 14.7 %collective-permute-start.19 = (bf16[512,2304]{1,0:T(8,128)(2,1)S(1)}, bf16[512,2304]{1,0:T(8,128)(2,1)S(1)}, u32[]{:S(2)}, u32[]{:S(2)}) collective-permute-start(bf16[512,2304]{1,0:T(8,128)(2,1)S(1)} %slice.267), channel_id=1, source_target_pairs={{0,1},{2,3},{4,5},{6,7},{8,9},{10,11},{12,13},{14,15},{16,17},{18,... | collective-permute-start | bytes 7077896 | tf_op jit(solution)/shard_map/ppermute | solution.py:713
  299.6 30.6 %collective-permute-start.21 = (bf16[2,2,136,1088]{3,2,1,0:T(8,128)(2,1)S(1)}, bf16[2,2,136,1088]{3,2,1,0:T(8,128)(2,1)S(1)}, u32[]{:S(2)}, u32[]{:S(2)}) collective-permute-start(bf16[2,2,136,1088]{3,2,1,0:T(8,128)(2,1)S(1)} %pad_maximum_fusion.8), channel_id=1, source_target_pairs={{0,2},{1,3},{2,0},{3,1},{4,6},{5,7},{6,4},{7,5},{8,10},{9,11},{10,... | collective-permute-start | bytes 3551240 | tf_op jit(solution)/shard_map/ppermute | solution.py:474
  303.6 200.8 %collective-permute-start.22 = (bf16[2,2,136,1088]{3,2,1,0:T(8,128)(2,1)}, bf16[2,2,136,1088]{3,2,1,0:T(8,128)(2,1)}, u32[]{:S(2)}, u32[]{:S(2)}) collective-permute-start(bf16[2,2,136,1088]{3,2,1,0:T(8,128)(2,1)} %pad_maximum_fusion.9), channel_id=1, source_target_pairs={{0,16},{16,0},{1,17},{17,1},{2,18},{18,2},{3,19},{19,3},{4,20},{20... | collective-permute-start | bytes 3551240 | tf_op jit(solution)/shard_map/ppermute | solution.py:482
  307.6 196.8 %collective-permute-start.23 = (bf16[2,2,136,1088]{3,2,1,0:T(8,128)(2,1)}, bf16[2,2,136,1088]{3,2,1,0:T(8,128)(2,1)}, u32[]{:S(2)}, u32[]{:S(2)}) collective-permute-start(bf16[2,2,136,1088]{3,2,1,0:T(8,128)(2,1)} %pad_maximum_fusion.10), channel_id=1, source_target_pairs={{0,2},{1,3},{2,0},{3,1},{4,6},{5,7},{6,4},{7,5},{8,10},{9,11},{10,... | collective-permute-start | bytes 3551240 | tf_op jit(solution)/shard_map/ppermute | solution.py:474
  311.0 25.1 %copy-start.32 = (bf16[1088,1152]{1,0:T(8,128)(2,1)}, bf16[1088,1152]{1,0:T(8,128)(2,1)S(1)}, u32[]{:S(2)}) copy-start(bf16[1088,1152]{1,0:T(8,128)(2,1)S(1)} %get-tuple-element.209) | copy-start | bytes 7520260
  495.1 172.7 %collective-permute-start.24 = (bf16[2,1088,1088]{2,1,0:T(8,128)(2,1)}, bf16[2,1088,1088]{2,1,0:T(8,128)(2,1)}, u32[]{:S(2)}, u32[]{:S(2)}) collective-permute-start(bf16[2,1088,1088]{2,1,0:T(8,128)(2,1)} %bitcast.49), channel_id=1, source_target_pairs={{0,1},{1,0},{2,3},{3,2},{4,5},{5,4},{6,7},{7,6},{8,9},{9,8},{10,11... | collective-permute-start | bytes 14204936 | tf_op jit(solution)/shard_map/ppermute | solution.py:474
  658.2 21.4 %collective-permute-start.25 = (bf16[2,1088,1088]{2,1,0:T(8,128)(2,1)}, bf16[2,1088,1088]{2,1,0:T(8,128)(2,1)S(1)}, u32[]{:S(2)}, u32[]{:S(2)}) collective-permute-start(bf16[2,1088,1088]{2,1,0:T(8,128)(2,1)} %bitcast.382), channel_id=1, source_target_pairs={{0,1},{1,0},{2,3},{3,2},{4,5},{5,4},{6,7},{7,6},{8,9},{9,8},{10,11... | collective-permute-start | bytes 14204936 | tf_op jit(solution)/shard_map/ppermute | solution.py:474
  679.6 25.5 %collective-permute-start.26 = (bf16[2,1088,1088]{1,2,0:T(8,128)(2,1)S(1)}, bf16[2,1088,1088]{1,2,0:T(8,128)(2,1)}, u32[]{:S(2)}, u32[]{:S(2)}) collective-permute-start(bf16[2,1088,1088]{1,2,0:T(8,128)(2,1)S(1)} %pad_maximum_fusion), channel_id=1, source_target_pairs={{0,1},{1,0},{2,3},{3,2},{4,5},{5,4},{6,7},{7,6},{8,9},{9,8},{10,11... | collective-permute-start | bytes 14204936 | tf_op jit(solution)/shard_map/ppermute | solution.py:474
  720.4 59.4 %collective-permute-start.27 = (bf16[2,1088,1088]{2,1,0:T(8,128)(2,1)}, bf16[2,1088,1088]{2,1,0:T(8,128)(2,1)}, u32[]{:S(2)}, u32[]{:S(2)}) collective-permute-start(bf16[2,1088,1088]{2,1,0:T(8,128)(2,1)} %pad_maximum_fusion.2), channel_id=1, source_target_pairs={{0,1},{1,0},{2,3},{3,2},{4,5},{5,4},{6,7},{7,6},{8,9},{9,8},{10,11... | collective-permute-start | bytes 14204936 | tf_op jit(solution)/shard_map/ppermute | solution.py:474
  745.2 30.1 %collective-permute-start.28 = (bf16[2,2,136,1088]{3,2,1,0:T(8,128)(2,1)}, bf16[2,2,136,1088]{3,2,1,0:T(8,128)(2,1)}, u32[]{:S(2)}, u32[]{:S(2)}) collective-permute-start(bf16[2,2,136,1088]{3,2,1,0:T(8,128)(2,1)} %dynamic-slice_bitcast_fusion.2), channel_id=1, source_target_pairs={{0,16},{16,0},{1,17},{17,1},{2,18},{18,2},{3,19},{19,3},{4,20},{20... | collective-permute-start | bytes 3551240 | tf_op jit(solution)/shard_map/ppermute | solution.py:482
  748.1 29.8 %collective-permute-start.29 = (bf16[2,2,136,1088]{3,2,1,0:T(8,128)(2,1)}, bf16[2,2,136,1088]{3,2,1,0:T(8,128)(2,1)}, u32[]{:S(2)}, u32[]{:S(2)}) collective-permute-start(bf16[2,2,136,1088]{3,2,1,0:T(8,128)(2,1)} %slice_bitcast_fusion.20), channel_id=1, source_target_pairs={{0,2},{1,3},{2,0},{3,1},{4,6},{5,7},{6,4},{7,5},{8,10},{9,11},{10,... | collective-permute-start | bytes 3551240 | tf_op jit(solution)/shard_map/ppermute | solution.py:474
  788.9 30.1 %collective-permute-start.31 = (bf16[2,136,1088]{2,1,0:T(8,128)(2,1)S(1)}, bf16[2,136,1088]{2,1,0:T(8,128)(2,1)}, u32[]{:S(2)}, u32[]{:S(2)}) collective-permute-start(bf16[2,136,1088]{2,1,0:T(8,128)(2,1)S(1)} %dynamic-slice_bitcast_fusion.5), channel_id=1, source_target_pairs={{0,16},{16,0},{1,17},{17,1},{2,18},{18,2},{3,19},{19,3},{4,20},{20... | collective-permute-start | bytes 1775624 | tf_op jit(solution)/shard_map/ppermute | solution.py:482
  791.4 26.4 %collective-permute-start.30 = (bf16[2,136,1088]{2,1,0:T(8,128)(2,1)}, bf16[2,136,1088]{2,1,0:T(8,128)(2,1)}, u32[]{:S(2)}, u32[]{:S(2)}) collective-permute-start(bf16[2,136,1088]{2,1,0:T(8,128)(2,1)} %slice_bitcast_fusion.25), channel_id=1, source_target_pairs={{0,2},{1,3},{2,0},{3,1},{4,6},{5,7},{6,4},{7,5},{8,10},{9,11},{10,... | collective-permute-start | bytes 1775624 | tf_op jit(solution)/shard_map/ppermute | solution.py:474
  794.0 37.1 %collective-permute-start.32 = (bf16[2,2,136,1088]{3,2,1,0:T(8,128)(2,1)}, bf16[2,2,136,1088]{3,2,1,0:T(8,128)(2,1)}, u32[]{:S(2)}, u32[]{:S(2)}) collective-permute-start(bf16[2,2,136,1088]{3,2,1,0:T(8,128)(2,1)} %dynamic-slice_bitcast_fusion.1), channel_id=1, source_target_pairs={{0,16},{16,0},{1,17},{17,1},{2,18},{18,2},{3,19},{19,3},{4,20},{20... | collective-permute-start | bytes 3551240 | tf_op jit(solution)/shard_map/ppermute | solution.py:482
  794.5 38.9 %collective-permute-start.33 = (bf16[2,2,136,1088]{3,2,1,0:T(8,128)(2,1)}, bf16[2,2,136,1088]{3,2,1,0:T(8,128)(2,1)}, u32[]{:S(2)}, u32[]{:S(2)}) collective-permute-start(bf16[2,2,136,1088]{3,2,1,0:T(8,128)(2,1)} %slice_bitcast_fusion.18), channel_id=1, source_target_pairs={{0,2},{1,3},{2,0},{3,1},{4,6},{5,7},{6,4},{7,5},{8,10},{9,11},{10,... | collective-permute-start | bytes 3551240 | tf_op jit(solution)/shard_map/ppermute | solution.py:474
  816.4 22.4 %collective-permute-start.34 = (bf16[512,2304]{1,0:T(8,128)(2,1)S(1)}, bf16[512,2304]{1,0:T(8,128)(2,1)}, u32[]{:S(2)}, u32[]{:S(2)}) collective-permute-start(bf16[512,2304]{1,0:T(8,128)(2,1)S(1)} %pad_maximum_fusion.4), channel_id=1, source_target_pairs={{1,0},{3,2},{5,4},{7,6},{9,8},{11,10},{13,12},{15,14},{17,16},{19,... | collective-permute-start | bytes 7077896 | tf_op jit(solution)/shard_map/ppermute | solution.py:833
  835.2 18.4 %collective-permute-start.51 = (bf16[136,1088]{1,0:T(8,128)(2,1)S(1)}, bf16[136,1088]{1,0:T(8,128)(2,1)S(1)}, u32[]{:S(2)}, u32[]{:S(2)}) collective-permute-start(bf16[136,1088]{1,0:T(8,128)(2,1)S(1)} %get-tuple-element.218), channel_id=1, source_target_pairs={{0,12},{4,0},{8,4},{12,8},{1,13},{5,1},{9,5},{13,9},{2,14},{6,2},{... | collective-permute-start | bytes 887816 | tf_op jit(solution)/shard_map/ppermute | solution.py:487
  838.2 25.6 %collective-permute-start.50 = (bf16[136,1088]{1,0:T(8,128)(2,1)S(1)}, bf16[136,1088]{1,0:T(8,128)(2,1)S(1)}, u32[]{:S(2)}, u32[]{:S(2)}) collective-permute-start(bf16[136,1088]{1,0:T(8,128)(2,1)S(1)} %get-tuple-element.219), channel_id=1, source_target_pairs={{0,8},{4,12},{8,0},{12,4},{1,9},{5,13},{9,1},{13,5},{2,10},{6,14},... | collective-permute-start | bytes 887816 | tf_op jit(solution)/shard_map/ppermute | solution.py:487
  838.2 25.6 %collective-permute-start.49 = (bf16[136,1088]{1,0:T(8,128)(2,1)S(1)}, bf16[136,1088]{1,0:T(8,128)(2,1)S(1)}, u32[]{:S(2)}, u32[]{:S(2)}) collective-permute-start(bf16[136,1088]{1,0:T(8,128)(2,1)S(1)} %get-tuple-element.217), channel_id=1, source_target_pairs={{0,4},{4,8},{8,12},{12,0},{1,5},{5,9},{9,13},{13,1},{2,6},{6,10},{... | collective-permute-start | bytes 887816 | tf_op jit(solution)/shard_map/ppermute | solution.py:487
  844.0 30.9 %copy-start.5 = (bf16[2,512,896]{2,1,0:T(8,128)(2,1)}, bf16[2,512,896]{2,1,0:T(8,128)(2,1)S(1)}, u32[]{:S(2)}) copy-start(bf16[2,512,896]{2,1,0:T(8,128)(2,1)S(1)} %get-tuple-element.143.grads) | copy-start | bytes 5505028
  851.9 35.9 %collective-permute-start.36 = (bf16[2,1088,1152]{2,1,0:T(8,128)(2,1)}, bf16[2,1088,1152]{2,1,0:T(8,128)(2,1)}, u32[]{:S(2)}, u32[]{:S(2)}) collective-permute-start(bf16[2,1088,1152]{2,1,0:T(8,128)(2,1)} %block_grads.2), channel_id=1, source_target_pairs={{0,1},{1,0},{2,3},{3,2},{4,5},{5,4},{6,7},{7,6},{8,9},{9,8},{10,11... | collective-permute-start | bytes 15040520 | tf_op jit(solution)/shard_map/ppermute | solution.py:474
  852.0 18.9 %collective-permute-start.44 = (bf16[2,136,1088]{2,1,0:T(8,128)(2,1)S(1)}, bf16[2,136,1088]{2,1,0:T(8,128)(2,1)S(1)}, u32[]{:S(2)}, u32[]{:S(2)}) collective-permute-start(bf16[2,136,1088]{2,1,0:T(8,128)(2,1)S(1)} %slice_bitcast_fusion.24), channel_id=1, source_target_pairs={{0,2},{1,3},{2,0},{3,1},{4,6},{5,7},{6,4},{7,5},{8,10},{9,11},{10,... | collective-permute-start | bytes 1775624 | tf_op jit(solution)/shard_map/ppermute | solution.py:474
  853.6 16.3 %collective-permute-start.45 = (bf16[2,136,1088]{2,1,0:T(8,128)(2,1)S(1)}, bf16[2,136,1088]{2,1,0:T(8,128)(2,1)S(1)}, u32[]{:S(2)}, u32[]{:S(2)}) collective-permute-start(bf16[2,136,1088]{2,1,0:T(8,128)(2,1)S(1)} %dynamic-slice_bitcast_fusion.3), channel_id=1, source_target_pairs={{0,16},{16,0},{1,17},{17,1},{2,18},{18,2},{3,19},{19,3},{4,20},{20... | collective-permute-start | bytes 1775624 | tf_op jit(solution)/shard_map/ppermute | solution.py:482
  881.5 6.2 collective-permute-start.35
  883.2 14.9 %collective-permute-start.48 = (bf16[136,1088]{1,0:T(8,128)(2,1)S(1)}, bf16[136,1088]{1,0:T(8,128)(2,1)S(1)}, u32[]{:S(2)}, u32[]{:S(2)}) collective-permute-start(bf16[136,1088]{1,0:T(8,128)(2,1)S(1)} %get-tuple-element.222), channel_id=1, source_target_pairs={{0,12},{4,0},{8,4},{12,8},{1,13},{5,1},{9,5},{13,9},{2,14},{6,2},{... | collective-permute-start | bytes 887816 | tf_op jit(solution)/shard_map/ppermute | solution.py:487
  886.5 28.9 %collective-permute-start.47 = (bf16[136,1088]{1,0:T(8,128)(2,1)S(1)}, bf16[136,1088]{1,0:T(8,128)(2,1)S(1)}, u32[]{:S(2)}, u32[]{:S(2)}) collective-permute-start(bf16[136,1088]{1,0:T(8,128)(2,1)S(1)} %get-tuple-element.221), channel_id=1, source_target_pairs={{0,8},{4,12},{8,0},{12,4},{1,9},{5,13},{9,1},{13,5},{2,10},{6,14},... | collective-permute-start | bytes 887816 | tf_op jit(solution)/shard_map/ppermute | solution.py:487
  887.6 27.8 %collective-permute-start.46 = (bf16[136,1088]{1,0:T(8,128)(2,1)S(1)}, bf16[136,1088]{1,0:T(8,128)(2,1)S(1)}, u32[]{:S(2)}, u32[]{:S(2)}) collective-permute-start(bf16[136,1088]{1,0:T(8,128)(2,1)S(1)} %get-tuple-element.220), channel_id=1, source_target_pairs={{0,4},{4,8},{8,12},{12,0},{1,5},{5,9},{9,13},{13,1},{2,6},{6,10},{... | collective-permute-start | bytes 887816 | tf_op jit(solution)/shard_map/ppermute | solution.py:487
  895.0 20.4 %copy-start.61 = (f32[136,1088]{1,0:T(8,128)S(1)}, f32[136,1088]{1,0:T(8,128)}, u32[]{:S(2)}) copy-start(f32[136,1088]{1,0:T(8,128)} %param.33) | copy-start | bytes 1775620
  895.1 20.4 %copy-start.62 = (f32[136,1088]{1,0:T(8,128)S(1)}, f32[136,1088]{1,0:T(8,128)}, u32[]{:S(2)}) copy-start(f32[136,1088]{1,0:T(8,128)} %param.28) | copy-start | bytes 1775620
  895.1 22.5 %slice-start.2 = ((s8[5013504]{0:T(1024)(128)(4,1)}), s8[819200]{0:T(1024)(128)(4,1)S(1)}, s32[]{:S(2)}) async-start(s8[5013504]{0:T(1024)(128)(4,1)} %bitcast.394), calls=%async_computation.2 | async-start | bytes 1638400
  897.1 20.4 %slice-start.3 = ((s8[5013504]{0:T(1024)(128)(4,1)}), s8[4194304]{0:T(1024)(128)(4,1)S(1)}, s32[]{:S(2)}) async-start(s8[5013504]{0:T(1024)(128)(4,1)} %bitcast.394), calls=%async_computation.3 | async-start | bytes 8388608
  897.3 29.2 %collective-permute-start.37 = (bf16[2,2,136,1152]{3,2,1,0:T(8,128)(2,1)S(1)}, bf16[2,2,136,1152]{3,2,1,0:T(8,128)(2,1)S(1)}, u32[]{:S(2)}, u32[]{:S(2)}) collective-permute-start(bf16[2,2,136,1152]{3,2,1,0:T(8,128)(2,1)S(1)} %dynamic-slice_bitcast_fusion), channel_id=1, source_target_pairs={{0,16},{16,0},{1,17},{17,1},{2,18},{18,2},{3,19},{19,3},{4,20},{20... | collective-permute-start | bytes 3760136 | tf_op jit(solution)/shard_map/ppermute | solution.py:482
  917.6 30.5 %collective-permute-start.39 = (bf16[2,2,136,1152]{3,2,1,0:T(8,128)(2,1)S(1)}, bf16[2,2,136,1152]{3,2,1,0:T(8,128)(2,1)S(1)}, u32[]{:S(2)}, u32[]{:S(2)}) collective-permute-start(bf16[2,2,136,1152]{3,2,1,0:T(8,128)(2,1)S(1)} %slice_bitcast_fusion.16), channel_id=1, source_target_pairs={{0,2},{1,3},{2,0},{3,1},{4,6},{5,7},{6,4},{7,5},{8,10},{9,11},{10,... | collective-permute-start | bytes 3760136 | tf_op jit(solution)/shard_map/ppermute | solution.py:474
  926.9 33.3 %collective-permute-start.38 = (bf16[2,136,1152]{2,1,0:T(8,128)(2,1)S(1)}, bf16[2,136,1152]{2,1,0:T(8,128)(2,1)S(1)}, u32[]{:S(2)}, u32[]{:S(2)}) collective-permute-start(bf16[2,136,1152]{2,1,0:T(8,128)(2,1)S(1)} %slice_bitcast_fusion.22), channel_id=1, source_target_pairs={{0,2},{1,3},{2,0},{3,1},{4,6},{5,7},{6,4},{7,5},{8,10},{9,11},{10,... | collective-permute-start | bytes 1880072 | tf_op jit(solution)/shard_map/ppermute | solution.py:474
  948.6 13.3 %collective-permute-start.40 = (bf16[2,136,1152]{2,1,0:T(8,128)(2,1)S(1)}, bf16[2,136,1152]{2,1,0:T(8,128)(2,1)S(1)}, u32[]{:S(2)}, u32[]{:S(2)}) collective-permute-start(bf16[2,136,1152]{2,1,0:T(8,128)(2,1)S(1)} %dynamic-slice_bitcast_fusion.4), channel_id=1, source_target_pairs={{0,16},{16,0},{1,17},{17,1},{2,18},{18,2},{3,19},{19,3},{4,20},{20... | collective-permute-start | bytes 1880072 | tf_op jit(solution)/shard_map/ppermute | solution.py:482
  962.4 8.2 collective-permute-start.43
  962.4 26.0 %collective-permute-start.42 = (bf16[136,1152]{1,0:T(8,128)(2,1)S(1)}, bf16[136,1152]{1,0:T(8,128)(2,1)S(1)}, u32[]{:S(2)}, u32[]{:S(2)}) collective-permute-start(bf16[136,1152]{1,0:T(8,128)(2,1)S(1)} %get-tuple-element.224), channel_id=1, source_target_pairs={{0,8},{4,12},{8,0},{12,4},{1,9},{5,13},{9,1},{13,5},{2,10},{6,14},... | collective-permute-start | bytes 940040 | tf_op jit(solution)/shard_map/ppermute | solution.py:487
  963.7 24.8 %collective-permute-start.41 = (bf16[136,1152]{1,0:T(8,128)(2,1)S(1)}, bf16[136,1152]{1,0:T(8,128)(2,1)S(1)}, u32[]{:S(2)}, u32[]{:S(2)}) collective-permute-start(bf16[136,1152]{1,0:T(8,128)(2,1)S(1)} %get-tuple-element.223), channel_id=1, source_target_pairs={{0,4},{4,8},{8,12},{12,0},{1,5},{5,9},{9,13},{13,1},{2,6},{6,10},{... | collective-permute-start | bytes 940040 | tf_op jit(solution)/shard_map/ppermute | solution.py:487
  (81 other events, 468.6 us)

commit v4 on v3

--- a/solution.py
+++ b/solution.py
@@ -414,49 +414,106 @@
     )(column, *operands)
 
 
-def block_grads_kernel(joined, left_one, left_two, grads, mixed, *refs):
-    vec_part, received, out, total = refs if joined else (None, None, *refs)
-    lanes_one = grads.shape[2]
-    lane_lead = total.shape[1] - mixed.shape[2]
-    total[:, :lanes_one] = jnp.dot(left_one[...], grads[0], preferred_element_type=f32)
-    total[:, lanes_one:] = jnp.zeros_like(total[:, lanes_one:])
-    total[:, lane_lead:] += jnp.dot(left_two[...], mixed[0], preferred_element_type=f32)
-    if joined:
+def block_grads_kernel(counts, has_vec, has_received, split, place, *refs):
+    refs = list(refs)
+    step = pl.program_id(0)
+    lefts = [refs.pop(0) for _ in counts]
+    rights = [[refs.pop(0) for _ in range(count)] for count in counts]
+    vec_part = refs.pop(0) if has_vec else None
+    received = refs.pop(0) if has_received else None
+    total = refs.pop()
+
+    def product(left, right):
+        right = right[0] if len(right.shape) == 3 else right[...]
+        return jnp.dot(left[...], right, preferred_element_type=f32)
+
+    if counts[0] > 1:
+        for i, right in enumerate(rights[0]):
+
+            @pl.when(step == i)
+            def _(right=right):
+                total[...] = product(lefts[0], right)
+
+    else:
+        lanes_one = rights[0][0].shape[-1]
+        total[:, :lanes_one] = product(lefts[0], rights[0][0])
+        total[:, lanes_one:] = jnp.zeros_like(total[:, lanes_one:])
+    for left, right in zip(lefts[1:], rights[1:]):
+        total[:, -right[0].shape[-1] :] += product(left, right[0])
+    if has_vec:
         total[:, -LANES:] += vec_part[0].astype(f32)
-        out[0] = (total[...] + received[0].astype(f32)).astype(bf16)
+    if has_received:
+        total[...] += received[0].astype(f32)
+    if not split:
+        refs[0][0] = total[...].astype(bf16)
+        return
+    first_keep, first_send, second_keep, second_send = refs
+    half = total.shape[0] // 2
+    quarter = half // 2
+
+    def rows(start):
+        return total[pl.ds(pl.multiple_of(start, 8), quarter)].astype(bf16)
+
+    first_keep[0] = rows(place[0] * half)
+    first_send[0] = rows((1 - place[0]) * half)
+    for i, second in enumerate((second_keep, second_send)):
+
+        @pl.when(step == i)
+        def _(second=second):
+            for dp in range(2):
+                second[dp] = total[dp * half + quarter : (dp + 1) * half].astype(bf16)
+
+
+def block_grads(pairs, vec_part, received, split):
+    lefts, rights = zip(*pairs)
+    rights = [r if isinstance(r, list) else [r] for r in rights]
+    width, count = lefts[0].shape
+    each = 2
+    lanes = rights[0][0].shape[-1] if len(pairs) == 1 else -(-width // LANES) * LANES
+    place = lax.axis_index("dp").reshape(1).astype(jnp.int32)
+
+    def fixed(shape):
+        return pl.BlockSpec(shape, lambda i, place: (0,) * len(shape))
+
+    def step(shape):
+        return pl.BlockSpec((1, *shape[1:]), lambda i, place: (i, 0, 0))
+
+    flat = [r for right in rights for r in right]
+    more = [x for x in (vec_part, received) if x is not None]
+    in_specs = [fixed(x.shape) for x in lefts]
+    in_specs += [step(x.shape) if x.ndim == 3 else fixed(x.shape) for x in flat]
+    in_specs += [step(x.shape) for x in more]
+    if split:
+        part = (each, width // 4, lanes)
+        out_specs = [step(part), step(part), fixed(part), fixed(part)]
+        out_shape = [jax.ShapeDtypeStruct(part, bf16)] * 4
     else:
-        out[0] = total[...].astype(bf16)
-
-
-def block_grads(left_one, left_two, grads, mixed, more):
-    each, count, _ = grads.shape
-    width = left_one.shape[0]
-    lanes = -(-width // LANES) * LANES
-
-    def fixed(shape):
-        return pl.BlockSpec(shape, lambda i: (0, 0))
-
-    def step(shape):
-        return pl.BlockSpec((1, *shape[1:]), lambda i: (i, 0, 0))
-
-    operands = [left_one, left_two, grads, mixed, *(more or ())]
-    in_specs = [fixed(left_one.shape), fixed(left_two.shape)]
-    in_specs += [step(x.shape) for x in operands[2:]]
+        out_specs = step((each, width, lanes))
+        out_shape = jax.ShapeDtypeStruct((each, width, lanes), bf16)
     return pl.pallas_call(
-        functools.partial(block_grads_kernel, more is not None),
-        grid=(each,),
-        in_specs=in_specs,
-        out_specs=step((each, width, lanes)),
-        out_shape=jax.ShapeDtypeStruct((each, width, lanes), bf16),
-        scratch_shapes=[pltpu.VMEM((width, lanes), f32)],
-        compiler_params=pltpu.CompilerParams(vmem_limit_bytes=48 << 20),
+        functools.partial(
+            block_grads_kernel,
+            [len(r) for r in rights],
+            vec_part is not None,
+            received is not None,
+            split,
+        ),
+        grid_spec=pltpu.PrefetchScalarGridSpec(
+            num_scalar_prefetch=1,
+            grid=(each,),
+            in_specs=in_specs,
+            out_specs=out_specs,
+            scratch_shapes=[pltpu.VMEM((width, lanes), f32)],
+        ),
+        out_shape=out_shape,
+        compiler_params=pltpu.CompilerParams(vmem_limit_bytes=56 << 20),
         cost_estimate=pl.CostEstimate(
-            flops=2 * each * count * width * (grads.shape[2] + mixed.shape[2]),
+            flops=2 * each * count * width * lanes,
             bytes_accessed=2 * each * width * lanes * 2,
             transcendentals=0,
         ),
         name="block_grads",
-    )(*operands)
+    )(place, *lefts, *flat, *more)
 
 
 AXES = ("col", "dp", "row")
@@ -502,47 +559,48 @@
     return lax.axis_size("row") == 4 and lax.axis_size("dp") == 2 and lax.axis_size("col") == 4
 
 
-def assemble_kernel(place, first, first_x, second, second_y, first_y, second_x, out, sems):
-    dp, row = place[0], place[1]
-    copies = []
-    for m in range(2):
-        for source, dx, dy, at in (
-            (first.at[m], 0, 0, m),
-            (first_x.at[m], 1, 0, m),
-            (second.at[m], 0, 0, m + 2),
-            (second_y.at[m], 0, 1, m + 2),
-            (first_y.at[0, m], 0, 1, m),
-            (first_y.at[1, m], 1, 1, m),
-            (second_x.at[0, m], 1, 0, m + 2),
-            (second_x.at[1, m], 1, 1, m + 2),
-        ):
-            target = out.at[dx, 1 - dp if dy else dp, lax.rem(row + 4 - at, 4)]
-            copies.append(pltpu.make_async_copy(source, target, sems.at[len(copies)]))
-    for copy in copies:
-        copy.start()
-    for copy in copies:
-        copy.wait()
+def assemble_kernel(ranges, targets, *refs):
+    sources, out = refs[:-1], refs[-1]
+    step = pl.program_id(0)
+    for (start, end), source in zip(ranges, sources):
+
+        @pl.when((step >= start) & (step < end))
+        def _(source=source):
+            out[...] = source[...]
 
 
 def assemble(pieces):
-    block = pieces[0].shape[1:]
-    place = jnp.stack([lax.axis_index("dp"), lax.axis_index("row")]).astype(jnp.int32)
+    rows, lanes = pieces[0].shape[-2:]
+    pieces = [p.reshape(-1, rows, lanes) for p in pieces]
+    starts = [sum(p.shape[0] for p in pieces[:k]) for k in range(len(pieces))]
+    ends = [start + p.shape[0] for start, p in zip(starts, pieces)]
+    over_x = jnp.array([0, 0, 1, 1, 0, 0, 0, 0, 0, 0, 1, 1, 1, 1, 1, 1], jnp.int32)
+    over_y = jnp.array([0, 0, 0, 0, 0, 0, 1, 1, 1, 1, 1, 1, 0, 0, 1, 1], jnp.int32)
+    behind = jnp.array([0, 1, 0, 1, 2, 3, 2, 3, 0, 1, 0, 1, 2, 3, 2, 3], jnp.int32)
+    dp, row = lax.axis_index("dp"), lax.axis_index("row")
+    targets = (over_x * 8 + (dp ^ over_y) * 4 + (row + 4 - behind) % 4).astype(jnp.int32)
+
+    def from_piece(start, end):
+        return pl.BlockSpec(
+            (1, rows, lanes), lambda i, targets: (jnp.clip(i - start, 0, end - start - 1), 0, 0)
+        )
+
     out = pl.pallas_call(
-        assemble_kernel,
+        functools.partial(assemble_kernel, tuple(zip(starts, ends))),
         grid_spec=pltpu.PrefetchScalarGridSpec(
             num_scalar_prefetch=1,
-            grid=(1,),
-            in_specs=[pl.BlockSpec(memory_space=pl.ANY)] * 6,
-            out_specs=pl.BlockSpec(memory_space=pl.ANY),
-            scratch_shapes=[pltpu.SemaphoreType.DMA((16,))],
-        ),
-        out_shape=jax.ShapeDtypeStruct((2, 2, 4, *block), bf16),
+            grid=(ends[-1],),
+            in_specs=[from_piece(start, end) for start, end in zip(starts, ends)],
+            out_specs=pl.BlockSpec((1, rows, lanes), lambda i, targets: (targets[i], 0, 0)),
+        ),
+        out_shape=jax.ShapeDtypeStruct((ends[-1], rows, lanes), bf16),
+        compiler_params=pltpu.CompilerParams(vmem_limit_bytes=32 << 20),
         cost_estimate=pl.CostEstimate(
-            flops=0, bytes_accessed=64 * block[0] * block[1], transcendentals=0
+            flops=0, bytes_accessed=64 * rows * lanes, transcendentals=0
         ),
         name="assemble",
-    )(place, *pieces)
-    return out.reshape(2, -1, block[1])
+    )(targets, *pieces)
+    return out.reshape(2, -1, lanes)
 
 
 def spread_rows(block):
@@ -579,12 +637,9 @@
 def scatter_one(blocks):
     if not short_rows():
         return blocks
-    dp = lax.axis_index("dp")
-    parts = blocks.reshape(2, 2, 4, -1, blocks.shape[-1])
-    first, second = parts[:, :, :2], parts[:, :, 2:]
-    first_y = flip_dp(at_place(first, 1 - dp, 1))
-    second_x = flip_col(second[1], 2)
-    return added(at_place(first, dp, 1), first_y), added(second[0], second_x)
+    first_keep, first_send, second_keep, second_send = blocks
+    first_y, second_x = flip_dp(first_send), flip_col(second_send, 2)
+    return added(first_keep, first_y), added(second_keep, second_x)
 
 
 def scatter_two(halves):
@@ -594,9 +649,10 @@
     first, second = halves
     first_x = flip_col(first[1], 2)
     second_y = flip_dp(at_place(second, 1 - dp, 0))
-    return jnp.concatenate(
+    both = jnp.concatenate(
         [added(first[0], first_x), added(at_place(second, dp, 0), second_y)], 0
     )
+    return both.reshape(4, -1, both.shape[-1])
 
 
 def scatter_three(rows):
@@ -769,18 +825,8 @@
     lows_oth, pull_oth, branch = forward_part(linear_oth, down_oth, branch)
     layer_out = (residual + branch + vec[7]).astype(bf16)
 
-    def partner_grads(left, rights):
-        return jnp.stack([contract_first(left, r).astype(bf16) for r in rights])
-
-    def plane_grads(left, rights, received):
-        return jnp.stack(
-            [
-                (contract_first(left, r) + received[i].astype(f32)).astype(bf16)
-                for i, r in enumerate(rights)
-            ]
-        )
-
-    sent_down = partner_grads(cotangent, lows_oth)
+    left_down, left_up = cotangent.T, normed_two_low.T
+    sent_down = block_grads([(left_down, lows_oth)], None, None, False)
     down_oth, sent_down = together(down_oth, sent_down)
     received_down = partner(sent_down)
 
@@ -800,8 +846,8 @@
         up_oth, down_oth, pull_oth, grad_normed_two
     )
     lows_own, dups_oth = together(lows_own, dups_oth)
-    total_down = plane_grads(cotangent, lows_own, received_down)
-    sent_up = partner_grads(normed_two_low, dups_oth)
+    total_down = block_grads([(left_down, lows_own)], None, received_down, staged)
+    sent_up = block_grads([(left_up, dups_oth)], None, None, False)
     down_own, total_down, sent_up = together(down_own, total_down, sent_up)
     received_up = partner(sent_up)
     one_down = scatter_one(total_down)
@@ -825,7 +871,7 @@
         None,
         None,
     )
-    total_up = plane_grads(normed_two_low, dups_own, received_up)
+    total_up = block_grads([(left_up, dups_own)], None, received_up, staged)
     grad_mixed, total_up, one_down = together(grad_mixed, total_up, one_down)
     dq, dk_own, dv_own, dk_oth, dv_oth = attend_back(
         later, labels, projected, others, grad_mixed, mixed, log_totals
@@ -844,7 +890,9 @@
     )
     two_up = scatter_two(one_up)
     left_one, left_two = normed_low.T, grad_residual_low.T
-    received = partner(block_grads(left_one, left_two, grads_oth, mixed_oth, None))
+    pairs_oth = [(left_one, grads_oth), (left_two, mixed_oth)]
+    pairs_own = [(left_one, grads_own), (left_two, mixed_own)]
+    received = partner(block_grads(pairs_oth, None, None, False))
     grad_normed_one = jnp.zeros((here, width), f32)
     for blocks, weights in ((grads_own, attn_own), (grads_oth, attn_oth)):
         for i in range(each):
@@ -877,9 +925,7 @@
     vec_here = jnp.pad(
         vec_here, ((0, 0), (0, 0), (0, rows_own - vec_lines), (LANES - spare, 0))
     ).reshape(each, width, LANES)
-    total_attn = block_grads(
-        left_one, left_two, grads_own, mixed_own, (vec_here, received)
-    )
+    total_attn = block_grads(pairs_own, vec_here, received, staged)
     sum_down, sum_up = scatter_three(two_down), scatter_three(two_up)
     sum_attn = scatter_three(scatter_two(scatter_one(total_attn)))
     sum_qkv = sum_attn[:, : 3 * piece].reshape(rows_own, 3, piece)

time: 1010 us -> 583 us (0.58)
  Pallas kernels: 540 us -> 148 us
  other arithmetic: 69.9 us -> 58.2 us
    pallas_call x5 -> x9, Pallas kernels: 474 us -> 83.1 us  [the longest x6 51.8 us: block_grads(): pl.pallas_call(functools.partial(block_grads_kernel, [len(r) for r in rig...]
    ppermute x12, waiting for transfers between devices: 53.8 us -> 85.4 us  [flip_dp(): return lax.ppermute(block, 'dp', [(0, 1), (1, 0)])]
    ppermute x20, waiting for transfers between devices: 37.9 us -> 17.3 us  [flip_col(): lax.ppermute(block, 'col', [(c, c ^ bit) for c in range(lax.axis_size('co...]
    dot_general x24 -> x16, matrix products: 56.8 us -> 40.9 us  [contract(): lax.dot_general(left, right, (((left_dim,), (right_dim,)), ((), ())), pre...]
    ppermute x18, waiting for transfers between devices: 89.5 us -> 76.9 us  [shift_row(): lax.ppermute(block, 'row', [(i, (i + by) % count) for i in range(count)])]
    ppermute x18, starting transfers between devices: 35.9 us -> 24.1 us  [shift_row(): lax.ppermute(block, 'row', [(i, (i + by) % count) for i in range(count)])]
    dot_general x4, matrix products: 12.2 us -> 23 us  [backward_part(): grad_active = jnp.dot(cotangent, downs[i], preferred_element_type=f32)]
  transfers between devices with their start and end apart: 52 -> 52, of which waited for: 22 -> 22; matrix products, arithmetic and copies ran while one was open for 16% -> 26% of each run, Pallas kernels for 54% -> 20%
where the time goes in v4:
time: 583 us; the launch traced here: 578 us
  waiting for transfers between devices  180 us (31%)
  Pallas kernels  148 us (25%)
  matrix products  82.4 us (14%)
  starting transfers between devices  61.5 us (11%)
  other arithmetic  58.2 us (10%)
  local copies, waits for them, and re-layouts  45.1 us (8%)
    ppermute x12, waiting for transfers between devices, flip_dp(): return lax.ppermute(block, 'dp', [(0, 1), (1, 0)])  85.4 us
    ppermute x18, waiting for transfers between devices, shift_row(): lax.ppermute(block, 'row', [(i, (i + by) % count) for i in range(count)])  76.9 us
    pallas_call x6, Pallas kernels, block_grads(): pl.pallas_call(functools.partial(block_grads_kernel, [len(r) for r in rig...  51.8 us
    dot_general x16, matrix products, contract(): lax.dot_general(left, right, (((left_dim,), (right_dim,)), ((), ())), pre...  40.9 us
    pallas_call x3, Pallas kernels, assemble(): pl.pallas_call(functools.partial(assemble_kernel, tuple(zip(starts, ends)...  31.3 us
    ppermute x18, starting transfers between devices, shift_row(): lax.ppermute(block, 'row', [(i, (i + by) % count) for i in range(count)])  24.1 us
    dot_general x4, matrix products, backward_part(): grad_active = jnp.dot(cotangent, downs[i], preferred_element_type=f32)  23 us
    pallas_call x3, Pallas kernels, multiply_and_place(): pl.pallas_call(functools.partial(place_kernel, spans, piece, sources, bia...  22.3 us
  transfers between devices with their start and end apart: 52, of which 22 were waited for; matrix products, arithmetic and copies ran while one was open for 26% of the time, Pallas kernels for 20%

profile of v4, /device:TPU:0, one launch (start us, length us, event | category | flops | bytes accessed | tf_op | source)
XLA Modules:
  0.0 578.1 jit_solution(2375018987832815197)
XLA Ops:
  2.7 3.1 collective-permute-start
  8.8 7.3 %collective-permute-done = bf16[136,1152]{1,0:T(8,128)(2,1)S(1)} collective-permute-done((bf16[136,1152]{1,0:T(8,128)(2,1)S(1)}, bf16[136,1152]{1,0:T(8,128)(2,1)S(1)}, u32[]{:S(2)}, u32[]{:S(2)}) %collective-permute-start) | collective-permute-done | bytes 313376 | tf_op jit(solution)/shard_map/ppermute | solution.py:544
  17.9 3.4 collective-permute-done.3
  21.3 14.0 %collective-permute-done.2 = bf16[136,1152]{1,0:T(8,128)(2,1)S(1)} collective-permute-done((bf16[136,1152]{1,0:T(8,128)(2,1)S(1)}, bf16[136,1152]{1,0:T(8,128)(2,1)S(1)}, u32[]{:S(2)}, u32[]{:S(2)}) %collective-permute-start.2) | collective-permute-done | bytes 313376 | tf_op jit(solution)/shard_map/ppermute | solution.py:544
  39.6 11.9 %collective-permute-done.4.refs_3_ = bf16[2,136,1152]{2,1,0:T(8,128)(2,1)S(1)} collective-permute-done((bf16[2,136,1152]{2,1,0:T(8,128)(2,1)S(1)}, bf16[2,136,1152]{2,1,0:T(8,128)(2,1)S(1)}, u32[]{:S(2)}, u32[]{:S(2)}) %collective-permute-start.4) | collective-permute-done | bytes 626720 | tf_op jit(solution)/shard_map/ppermute | solution.py:539
  63.1 2.7 collective-permute-start.10
  65.8 15.8 %collective-permute-done.5 = bf16[2,2,136,1152]{3,2,1,0:T(8,128)(2,1)} collective-permute-done((bf16[2,2,136,1152]{3,2,1,0:T(8,128)(2,1)}, bf16[2,2,136,1152]{3,2,1,0:T(8,128)(2,1)}, u32[]{:S(2)}, u32[]{:S(2)}) %collective-permute-start.5) | collective-permute-done | bytes 1253408 | tf_op jit(solution)/shard_map/ppermute | solution.py:539
  84.0 10.1 %assemble.3 = bf16[16,136,1152]{2,1,0:T(8,128)(2,1)} custom-call(s32[16]{0:T(128)S(1)} %fusion.109.targets, bf16[2,136,1152]{2,1,0:T(8,128)(2,1)S(1)} %pad_maximum_fusion.10.refs_0_, bf16[2,136,1152]{2,1,0:T(8,128)(2,1)S(1)} %collective-permute-done.1.refs_1_, bf16[2,136,1152]{2,1,0:T(8,128)(2,1)S(1)} %pad_maximum_fusion.11.refs_2_, ...), custom_call_target="tpu_custom_call" | custom-call | bytes 10027008 | tf_op jit(solution)/shard_map/assemble/pallas_call | solution.py:588
  94.3 4.0 collective-permute-start.17
  100.1 6.3 %collective-permute-done.14 = bf16[136,1088]{1,0:T(8,128)(2,1)S(1)} collective-permute-done((bf16[136,1088]{1,0:T(8,128)(2,1)S(1)}, bf16[136,1088]{1,0:T(8,128)(2,1)S(1)}, u32[]{:S(2)}, u32[]{:S(2)}) %collective-permute-start.14) | collective-permute-done | bytes 295968 | tf_op jit(solution)/shard_map/ppermute | solution.py:544
  107.8 5.7 collective-permute-done.17
  115.0 8.7 %collective-permute-done.16 = bf16[136,1088]{1,0:T(8,128)(2,1)S(1)} collective-permute-done((bf16[136,1088]{1,0:T(8,128)(2,1)S(1)}, bf16[136,1088]{1,0:T(8,128)(2,1)S(1)}, u32[]{:S(2)}, u32[]{:S(2)}) %collective-permute-start.16) | collective-permute-done | bytes 295968 | tf_op jit(solution)/shard_map/ppermute | solution.py:544
  125.6 5.1 fusion.120
  143.7 7.2 %multiply_and_place.3.refs_2_ = bf16[512,3456]{1,0:T(8,128)(2,1)S(1)} custom-call(s32[2]{0:T(128)S(1)} %fusion.111.places, bf16[512,1088]{1,0:T(8,128)(2,1)S(1)} %copy.91.x, bf16[2,1088,1152]{2,1,0:T(8,128)(2,1)} %bitcast.24.refs_0_, f32[1,3456]{1,0:T(1,128)S(1)} %reshape.258.refs_1_), custom_call_target="tpu_custom_call" | custom-call | flops 1996488704 | bytes 8552448 | tf_op jit(solution)/shard_map/multiply_and_place/pallas_call | solution.py:333
  154.0 8.5 %multiply_and_place.4.q.k_own.v_own = bf16[512,3456]{1,0:T(8,128)(2,1)S(1)} custom-call(s32[2]{0:T(128)S(1)} %copy-done.21, bf16[512,1088]{1,0:T(8,128)(2,1)S(1)} %copy-done.3, bf16[2,1088,1152]{2,1,0:T(8,128)(2,1)} %collective-permute-done.13.refs_0_.refs_1_, f32[1,3456]{1,0:T(1,128)S(1)} %reshape.258.refs_1_, bf16[512,3456]{1,0:T(8,128)(2,1)} %copy-done.1), custom_call_target="tpu_custom_call" | custom-call | flops 1996488704 | bytes 8552448 | tf_op jit(solution)/shard_map/multiply_and_place/pallas_call | solution.py:333
  165.1 3.1 collective-permute-start.19
  168.4 2.5 pad_maximum_fusion.5
  171.4 2.5 pad_maximum_fusion.6
  174.4 4.3 slice_bitcast_fusion.7
  178.7 17.5 %attention_forward.1 = (bf16[512,1152]{1,0:T(8,128)(2,1)S(1)}, f32[9,2,512]{2,1,0:T(2,128)S(1)}) custom-call(s32[1]{0:T(128)} %bitcast.15.later, s32[1,512]{1,0:T(1,128)S(1)} %bitcast.292, s32[512,1]{1,0:T(8,128)S(1)} %copy-done.15, s32[512,1]{1,0:T(8,128)S(1)} %copy-done.16, bf16[512,3456]{1,0:T(8,128)(2,1)} %copy-done, bf16[512,3456]{1,0:T(8,128)(2,1)} %copy-done, ...), custom_call_target="tpu_custom_call" | custom-call | flops 2415919104 | bytes 7077888 | tf_op jit(solution)/shard_map/attention_forward/pallas_call | solution.py:232
  206.2 11.2 %assemble.4 = bf16[16,136,1088]{2,1,0:T(8,128)(2,1)} custom-call(s32[16]{0:T(128)S(1)} %copy-done.20, bf16[2,136,1088]{2,1,0:T(8,128)(2,1)S(1)} %copy-done.5, bf16[2,136,1088]{2,1,0:T(8,128)(2,1)S(1)} %copy-done.11, bf16[2,136,1088]{2,1,0:T(8,128)(2,1)S(1)} %copy-done.7, bf16[2,136,1088]{2,1,0:T(8,128)(2,1)} %collective-permute-done.12.refs_3_, ...), custom_call_target="tpu_custom_call" | custom-call | bytes 9469952 | tf_op jit(solution)/shard_map/assemble/pallas_call | solution.py:588
  217.4 2.9 fusion.119
  220.3 4.1 collective-permute-start.24
  224.8 3.3 convolution_add_fusion.12
  228.1 3.3 convolution_add_fusion.11
  231.4 9.9 %assemble.5 = bf16[16,136,1088]{2,1,0:T(8,128)(2,1)} custom-call(s32[16]{0:T(128)S(1)} %copy-done.20, bf16[2,136,1088]{2,1,0:T(8,128)(2,1)} %pad_maximum_fusion.14.refs_0_, bf16[2,136,1088]{2,1,0:T(8,128)(2,1)} %collective-permute-done.15.refs_1_, bf16[2,136,1088]{2,1,0:T(8,128)(2,1)} %pad_maximum_fusion.15.refs_2_, ...), custom_call_target="tpu_custom_call" | custom-call | bytes 9469952 | tf_op jit(solution)/shard_map/assemble/pallas_call | solution.py:588
  243.1 2.6 multiply_convert_fusion.3.refs_1_
  247.4 4.3 fusion.118
  251.7 6.0 %multiply_convert_fusion = (bf16[512,1088]{1,0:T(8,128)(2,1)}, f32[512,1088]{1,0:T(8,128)}) fusion(f32[1088]{0:T(1024)S(1)} %get-tuple-element.219, bf16[512,1088]{0,1:T(8,128)(2,1)S(1)} %add_convert_fusion.6, bf16[2,1088,1088]{2,1,0:T(8,128)(2,1)} %collective-permute-done.24), kind=kOutput, calls=%fused_computation.87 | convolution fusion | flops 1217724416 | bytes 6967552 | tf_op jit(solution)/shard_map/dot_general | solution.py:802
  257.7 5.9 %multiply_convert_fusion.1 = (bf16[512,1088]{1,0:T(8,128)(2,1)}, f32[512,1088]{1,0:T(8,128)}) fusion(f32[1088]{0:T(1024)S(1)} %get-tuple-element.218, bf16[512,1088]{0,1:T(8,128)(2,1)S(1)} %add_convert_fusion.6, bf16[2,1088,1088]{2,1,0:T(8,128)(2,1)} %collective-permute-done.24), kind=kOutput, calls=%fused_computation.88 | convolution fusion | flops 1217724416 | bytes 6967552 | tf_op jit(solution)/shard_map/dot_general | solution.py:802
  263.7 7.3 %block_grads.6 = bf16[2,1088,1088]{2,1,0:T(8,128)(2,1)} custom-call(s32[1]{0:T(128)} %bitcast.59.place, bf16[1088,512]{1,0:T(8,128)(2,1)} %bitcast.306, bf16[512,1088]{1,0:T(8,128)(2,1)} %get-tuple-element.268.refs_1_, bf16[512,1088]{1,0:T(8,128)(2,1)} %get-tuple-element.270.refs_2_), custom_call_target="tpu_custom_call" | custom-call | flops 2424307712 | bytes 9469952 | tf_op jit(solution)/shard_map/block_grads/pallas_call | solution.py:493
  271.5 3.4 fusion.127
  274.9 3.0 convolution_add_fusion.8
  279.4 6.2 %fusion.123 = (bf16[1088]{0:T(1024)(128)(2,1)S(1)}, bf16[512,1088]{1,0:T(8,128)(2,1)}) fusion(f32[512,1088]{1,0:T(8,128)S(1)} %copy-done.96, bf16[512,1088]{0,1:T(8,128)(2,1)S(1)} %copy-done.40, bf16[2,1088,1088]{2,1,0:T(8,128)(2,1)} %collective-permute-done.25), kind=kOutput, calls=%fused_computation.266 | convolution fusion | flops 1223851008 | bytes 6965376 | tf_op jit(solution)/shard_map/dot_general | solution.py:838
  285.6 6.0 %fusion.124 = (bf16[1088]{0:T(1024)(128)(2,1)S(1)}, bf16[512,1088]{1,0:T(8,128)(2,1)}) fusion(f32[512,1088]{1,0:T(8,128)S(1)} %copy-done.95, bf16[512,1088]{0,1:T(8,128)(2,1)S(1)} %copy-done.40, bf16[2,1088,1088]{2,1,0:T(8,128)(2,1)} %collective-permute-done.25), kind=kOutput, calls=%fused_computation.267 | convolution fusion | flops 1223851008 | bytes 6965376 | tf_op jit(solution)/shard_map/dot_general | solution.py:838
  291.7 7.6 %block_grads.8 = bf16[2,1088,1088]{2,1,0:T(8,128)(2,1)} custom-call(s32[1]{0:T(128)} %bitcast.59.place, bf16[1088,512]{1,0:T(8,128)(2,1)} %fusion.151.refs_0_, bf16[512,1088]{1,0:T(8,128)(2,1)} %get-tuple-element.147.refs_1_, bf16[512,1088]{1,0:T(8,128)(2,1)} %get-tuple-element.148.refs_2_), custom_call_target="tpu_custom_call" | custom-call | flops 2424307712 | bytes 9469952 | tf_op jit(solution)/shard_map/block_grads/pallas_call | solution.py:493
  299.3 3.4 fusion.13
  302.8 4.9 fusion.62
  307.7 4.6 fusion.6
  312.3 10.1 %block_grads.7 = (bf16[2,272,1088]{2,1,0:T(8,128)(2,1)}, bf16[2,272,1088]{2,1,0:T(8,128)(2,1)}, bf16[2,272,1088]{2,1,0:T(8,128)(2,1)}, bf16[2,272,1088]{2,1,0:T(8,128)(2,1)}) custom-call(s32[1]{0:T(128)} %bitcast.59.place, bf16[1088,512]{1,0:T(8,128)(2,1)} %bitcast.307, bf16[512,1088]{1,0:T(8,128)(2,1)} %copy-done.59, ...), custom_call_target="tpu_custom_call" | custom-call | flops 2424307712 | bytes 9469952 | tf_op jit(solution)/shard_map/block_grads/pallas_call | solution.py:493
  322.4 5.2 fusion.121
  327.7 5.5 fusion.122
  335.6 3.5 fusion.1
  350.1 6.6 %multiply_and_place.5.grad = bf16[512,1152]{1,0:T(8,128)(2,1)S(1)} custom-call(s32[4]{0:T(128)S(1)} %pad_add_fusion.places, bf16[512,1088]{1,0:T(8,128)(2,1)S(1)} %copy.102.x, bf16[2,1088,1152]{2,1,0:T(8,128)(2,1)} %bitcast.24.refs_0_, bf16[2,1088,1152]{2,1,0:T(8,128)(2,1)} %collective-permute-done.13.refs_0_.refs_1_), custom_call_target="tpu_custom_call" | custom-call | flops 1711276032 | bytes 5636096 | tf_op jit(solution)/shard_map/multiply_and_place/pallas_call | solution.py:333
  357.9 18.5 %collective-permute-done.28 = bf16[2,272,1088]{2,1,0:T(8,128)(2,1)} collective-permute-done((bf16[2,272,1088]{2,1,0:T(8,128)(2,1)}, bf16[2,272,1088]{2,1,0:T(8,128)(2,1)}, u32[]{:S(2)}, u32[]{:S(2)}) %collective-permute-start.28) | collective-permute-done | bytes 1183776 | tf_op jit(solution)/shard_map/ppermute | solution.py:539
  379.6 9.5 %block_grads.9 = (bf16[2,272,1088]{2,1,0:T(8,128)(2,1)}, bf16[2,272,1088]{2,1,0:T(8,128)(2,1)}, bf16[2,272,1088]{2,1,0:T(8,128)(2,1)}, bf16[2,272,1088]{2,1,0:T(8,128)(2,1)}) custom-call(s32[1]{0:T(128)} %bitcast.59.place, bf16[1088,512]{1,0:T(8,128)(2,1)} %fusion.151.refs_0_, bf16[512,1088]{1,0:T(8,128)(2,1)} %copy-done.89, bf16[512,1088]{1,0:T(8,128)(2,1)} %copy-done.90, ...), custom_call_target="tpu_custom_call" | custom-call | flops 2424307712 | bytes 9469952 | tf_op jit(solution)/shard_map/block_grads/pallas_call | solution.py:493
  394.2 19.7 %attention_backward.1 = (bf16[512,1152]{1,0:T(8,128)(2,1)S(1)}, bf16[512,1152]{1,0:T(8,128)(2,1)S(1)}, bf16[512,1152]{1,0:T(8,128)(2,1)S(1)}, bf16[512,1152]{1,0:T(8,128)(2,1)S(1)}, bf16[512,1152]{1,0:T(8,128)(2,1)}) custom-call(s32[1]{0:T(128)} %bitcast.15.later, s32[1,512]{1,0:T(1,128)S(1)} %bitcast.293, s32[512,1]{1,0:T(8,128)S(1)} %copy-done.15, ...), custom_call_target="tpu_custom_call" | custom-call | flops 6039797760 | bytes 14155776 | tf_op jit(solution)/shard_map/attention_backward/pallas_call | solution.py:258
  419.5 11.9 %collective-permute-done.32 = bf16[2,272,1088]{2,1,0:T(8,128)(2,1)} collective-permute-done((bf16[2,272,1088]{2,1,0:T(8,128)(2,1)}, bf16[2,272,1088]{2,1,0:T(8,128)(2,1)}, u32[]{:S(2)}, u32[]{:S(2)}) %collective-permute-start.32) | collective-permute-done | bytes 1183776 | tf_op jit(solution)/shard_map/ppermute | solution.py:539
  436.7 5.3 split_grads.1
  441.9 8.0 %block_grads.10 = bf16[2,1088,1152]{2,1,0:T(8,128)(2,1)} custom-call(s32[1]{0:T(128)} %bitcast.59.place, bf16[1088,512]{1,0:T(8,128)(2,1)} %bitcast.294, bf16[1088,512]{1,0:T(8,128)(2,1)} %convert_bitcast_fusion.2.refs_1_, bf16[2,512,896]{2,1,0:T(8,128)(2,1)} %get-tuple-element.176.refs_2_, bf16[2,512,384]{2,1,0:T(8,128)(2,1)} %copy-done.8), custom_call_target="tpu_custom_call" | custom-call | flops 2566914048 | bytes 10027008 | tf_op jit(solution)/shard_map/block_grads/pallas_call | solution.py:493
  454.4 12.2 %collective-permute-done.45 = bf16[272,1088]{1,0:T(8,128)(2,1)S(1)} collective-permute-done((bf16[272,1088]{1,0:T(8,128)(2,1)S(1)}, bf16[272,1088]{1,0:T(8,128)(2,1)S(1)}, u32[]{:S(2)}, u32[]{:S(2)}) %collective-permute-start.45) | collective-permute-done | bytes 591904 | tf_op jit(solution)/shard_map/ppermute | solution.py:539
  474.4 3.5 fusion.60
  479.7 3.8 collective-permute-start.48
  484.4 9.4 %block_grads.11 = (bf16[2,272,1152]{2,1,0:T(8,128)(2,1)}, bf16[2,272,1152]{2,1,0:T(8,128)(2,1)}, bf16[2,272,1152]{2,1,0:T(8,128)(2,1)}, bf16[2,272,1152]{2,1,0:T(8,128)(2,1)}) custom-call(s32[1]{0:T(128)} %bitcast.59.place, bf16[1088,512]{1,0:T(8,128)(2,1)} %bitcast.295, bf16[1088,512]{1,0:T(8,128)(2,1)} %convert_bitcast_fusion.2.refs_1_, ...), custom_call_target="tpu_custom_call" | custom-call | flops 2566914048 | bytes 10027008 | tf_op jit(solution)/shard_map/block_grads/pallas_call | solution.py:493
  496.0 2.9 multiply_subtract_fusion
  499.7 9.6 %collective-permute-done.47 = bf16[136,1088]{1,0:T(8,128)(2,1)} collective-permute-done((bf16[136,1088]{1,0:T(8,128)(2,1)S(1)}, bf16[136,1088]{1,0:T(8,128)(2,1)}, u32[]{:S(2)}, u32[]{:S(2)}) %collective-permute-start.47) | collective-permute-done | bytes 295968 | tf_op jit(solution)/shard_map/ppermute | solution.py:544
  509.3 2.7 multiply_subtract_fusion.1
  512.0 11.7 %collective-permute-done.39 = bf16[2,272,1152]{2,1,0:T(8,128)(2,1)S(1)} collective-permute-done((bf16[2,272,1152]{2,1,0:T(8,128)(2,1)}, bf16[2,272,1152]{2,1,0:T(8,128)(2,1)S(1)}, u32[]{:S(2)}, u32[]{:S(2)}) %collective-permute-start.39) | collective-permute-done | bytes 1253408 | tf_op jit(solution)/shard_map/ppermute | solution.py:531
  525.0 4.4 collective-permute-done.37
  530.3 10.8 %collective-permute-done.40 = bf16[272,1152]{1,0:T(8,128)(2,1)S(1)} collective-permute-done((bf16[272,1152]{1,0:T(8,128)(2,1)S(1)}, bf16[272,1152]{1,0:T(8,128)(2,1)S(1)}, u32[]{:S(2)}, u32[]{:S(2)}) %collective-permute-start.40) | collective-permute-done | bytes 626720 | tf_op jit(solution)/shard_map/ppermute | solution.py:539
  542.9 3.3 collective-permute-start.43
  549.4 4.6 collective-permute-done.43
  554.1 17.3 %collective-permute-done.42 = bf16[136,1152]{1,0:T(8,128)(2,1)S(1)} collective-permute-done((bf16[136,1152]{1,0:T(8,128)(2,1)S(1)}, bf16[136,1152]{1,0:T(8,128)(2,1)S(1)}, u32[]{:S(2)}, u32[]{:S(2)}) %collective-permute-start.42) | collective-permute-done | bytes 313376 | tf_op jit(solution)/shard_map/ppermute | solution.py:544
  574.4 2.7 multiply_subtract_fusion.2
  (430 shorter events, 129.1 us)
Async XLA Ops:
  2.3 35.8 %copy-start.80 = (s32[2,1024]{1,0:T(2,128)S(1)}, s32[2,1024]{1,0:T(2,128)}, u32[]{:S(2)}) copy-start(s32[2,1024]{1,0:T(2,128)} %param.29) | copy-start | bytes 24580
  2.7 13.4 %collective-permute-start = (bf16[136,1152]{1,0:T(8,128)(2,1)S(1)}, bf16[136,1152]{1,0:T(8,128)(2,1)S(1)}, u32[]{:S(2)}, u32[]{:S(2)}) collective-permute-start(bf16[136,1152]{1,0:T(8,128)(2,1)S(1)} %concatenate.26), channel_id=1, source_target_pairs={{0,4},{4,8},{8,12},{12,0},{1,5},{5,9},{9,13},{13,1},{2,6},{6,10},{... | collective-permute-start | bytes 940040 | tf_op jit(solution)/shard_map/ppermute | solution.py:544
  5.8 15.6 %collective-permute-start.3 = (bf16[136,1152]{1,0:T(8,128)(2,1)S(1)}, bf16[136,1152]{1,0:T(8,128)(2,1)S(1)}, u32[]{:S(2)}, u32[]{:S(2)}) collective-permute-start(bf16[136,1152]{1,0:T(8,128)(2,1)S(1)} %concatenate.26), channel_id=1, source_target_pairs={{0,12},{4,0},{8,4},{12,8},{1,13},{5,1},{9,5},{13,9},{2,14},{6,2},{... | collective-permute-start | bytes 940040 | tf_op jit(solution)/shard_map/ppermute | solution.py:544
  7.8 27.5 %collective-permute-start.2 = (bf16[136,1152]{1,0:T(8,128)(2,1)S(1)}, bf16[136,1152]{1,0:T(8,128)(2,1)S(1)}, u32[]{:S(2)}, u32[]{:S(2)}) collective-permute-start(bf16[136,1152]{1,0:T(8,128)(2,1)S(1)} %concatenate.26), channel_id=1, source_target_pairs={{0,8},{4,12},{8,0},{12,4},{1,9},{5,13},{9,1},{13,5},{2,10},{6,14},... | collective-permute-start | bytes 940040 | tf_op jit(solution)/shard_map/ppermute | solution.py:544
  16.1 23.5 %collective-permute-start.1 = (bf16[2,136,1152]{2,1,0:T(8,128)(2,1)S(1)}, bf16[2,136,1152]{2,1,0:T(8,128)(2,1)S(1)}, u32[]{:S(2)}, u32[]{:S(2)}) collective-permute-start(bf16[2,136,1152]{2,1,0:T(8,128)(2,1)S(1)} %pad_maximum_fusion.10.refs_0_), channel_id=1, source_target_pairs={{0,2},{1,3},{2,0},{3,1},{4,6},{5,7},{6,4},{7,5},{8,10},{9,11},{10,... | collective-permute-start | bytes 1880072 | tf_op jit(solution)/shard_map/ppermute | solution.py:531
  35.4 16.1 %collective-permute-start.4 = (bf16[2,136,1152]{2,1,0:T(8,128)(2,1)S(1)}, bf16[2,136,1152]{2,1,0:T(8,128)(2,1)S(1)}, u32[]{:S(2)}, u32[]{:S(2)}) collective-permute-start(bf16[2,136,1152]{2,1,0:T(8,128)(2,1)S(1)} %pad_maximum_fusion.11.refs_2_), channel_id=1, source_target_pairs={{0,16},{16,0},{1,17},{17,1},{2,18},{18,2},{3,19},{19,3},{4,20},{20... | collective-permute-start | bytes 1880072 | tf_op jit(solution)/shard_map/ppermute | solution.py:539
  39.6 93.7 %copy-start.73 = (f32[512]{0:T(512)}, f32[512]{0:T(512)S(1)}, u32[]{:S(2)}) copy-start(f32[512]{0:T(512)S(1)} %broadcast_multiply_fusion.5) | copy-start | bytes 6148
  52.7 28.9 %collective-permute-start.5 = (bf16[2,2,136,1152]{3,2,1,0:T(8,128)(2,1)}, bf16[2,2,136,1152]{3,2,1,0:T(8,128)(2,1)}, u32[]{:S(2)}, u32[]{:S(2)}) collective-permute-start(bf16[2,2,136,1152]{3,2,1,0:T(8,128)(2,1)} %pad_maximum_fusion.1), channel_id=1, source_target_pairs={{0,16},{16,0},{1,17},{17,1},{2,18},{18,2},{3,19},{19,3},{4,20},{20... | collective-permute-start | bytes 3760136 | tf_op jit(solution)/shard_map/ppermute | solution.py:539
  55.4 28.7 %collective-permute-start.6 = (bf16[2,2,136,1152]{3,2,1,0:T(8,128)(2,1)}, bf16[2,2,136,1152]{3,2,1,0:T(8,128)(2,1)}, u32[]{:S(2)}, u32[]{:S(2)}) collective-permute-start(bf16[2,2,136,1152]{3,2,1,0:T(8,128)(2,1)} %pad_maximum_fusion.2), channel_id=1, source_target_pairs={{0,2},{1,3},{2,0},{3,1},{4,6},{5,7},{6,4},{7,5},{8,10},{9,11},{10,... | collective-permute-start | bytes 3760136 | tf_op jit(solution)/shard_map/ppermute | solution.py:531
  56.9 37.2 %copy-start.17 = (s32[512]{0:T(512)}, s32[512]{0:T(512)S(1)}, u32[]{:S(2)}) copy-start(s32[512]{0:T(512)S(1)} %get-tuple-element.265) | copy-start | bytes 6148
  60.8 72.5 %copy-start.75 = (f32[512]{0:T(512)}, f32[512]{0:T(512)S(1)}, u32[]{:S(2)}) copy-start(f32[512]{0:T(512)S(1)} %add_rsqrt_fusion.1) | copy-start | bytes 6148
  61.9 32.3 %collective-permute-start.8 = (bf16[136,1088]{1,0:T(8,128)(2,1)S(1)}, bf16[136,1088]{1,0:T(8,128)(2,1)S(1)}, u32[]{:S(2)}, u32[]{:S(2)}) collective-permute-start(bf16[136,1088]{1,0:T(8,128)(2,1)S(1)} %convert_element_type.301), channel_id=1, source_target_pairs={{0,4},{4,8},{8,12},{12,0},{1,5},{5,9},{9,13},{13,1},{2,6},{6,10},{... | collective-permute-start | bytes 887816 | tf_op jit(solution)/shard_map/ppermute | solution.py:544
  62.0 32.3 %collective-permute-start.9 = (bf16[136,1088]{1,0:T(8,128)(2,1)S(1)}, bf16[136,1088]{1,0:T(8,128)(2,1)S(1)}, u32[]{:S(2)}, u32[]{:S(2)}) collective-permute-start(bf16[136,1088]{1,0:T(8,128)(2,1)S(1)} %convert_element_type.301), channel_id=1, source_target_pairs={{0,8},{4,12},{8,0},{12,4},{1,9},{5,13},{9,1},{13,5},{2,10},{6,14},... | collective-permute-start | bytes 887816 | tf_op jit(solution)/shard_map/ppermute | solution.py:544
  63.1 31.2 %collective-permute-start.10 = (bf16[136,1088]{1,0:T(8,128)(2,1)S(1)}, bf16[136,1088]{1,0:T(8,128)(2,1)S(1)}, u32[]{:S(2)}, u32[]{:S(2)}) collective-permute-start(bf16[136,1088]{1,0:T(8,128)(2,1)S(1)} %convert_element_type.301), channel_id=1, source_target_pairs={{0,12},{4,0},{8,4},{12,8},{1,13},{5,1},{9,5},{13,9},{2,14},{6,2},{... | collective-permute-start | bytes 887816 | tf_op jit(solution)/shard_map/ppermute | solution.py:544
  65.8 28.3 %copy-start.19 = (s32[16]{0:T(128)}, s32[16]{0:T(128)S(1)}, u32[]{:S(2)}) copy-start(s32[16]{0:T(128)S(1)} %fusion.109.targets) | copy-start | bytes 196
  94.1 58.6 %collective-permute-start.13 = (bf16[2,1088,1152]{2,1,0:T(8,128)(2,1)}, bf16[2,1088,1152]{2,1,0:T(8,128)(2,1)}, u32[]{:S(2)}, u32[]{:S(2)}) collective-permute-start(bf16[2,1088,1152]{2,1,0:T(8,128)(2,1)} %bitcast.24.refs_0_), channel_id=1, source_target_pairs={{0,1},{1,0},{2,3},{3,2},{4,5},{5,4},{6,7},{7,6},{8,9},{9,8},{10,11... | collective-permute-start | bytes 15040520 | tf_op jit(solution)/shard_map/ppermute | solution.py:531
  94.2 49.4 %copy-start.23 = (s32[2]{0:T(128)}, s32[2]{0:T(128)S(1)}, u32[]{:S(2)}) copy-start(s32[2]{0:T(128)S(1)} %fusion.111.places) | copy-start | bytes 28
  94.3 12.1 %collective-permute-start.14 = (bf16[136,1088]{1,0:T(8,128)(2,1)S(1)}, bf16[136,1088]{1,0:T(8,128)(2,1)S(1)}, u32[]{:S(2)}, u32[]{:S(2)}) collective-permute-start(bf16[136,1088]{1,0:T(8,128)(2,1)S(1)} %convert_bitcast_fusion), channel_id=1, source_target_pairs={{0,4},{4,8},{8,12},{12,0},{1,5},{5,9},{9,13},{13,1},{2,6},{6,10},{... | collective-permute-start | bytes 887816 | tf_op jit(solution)/shard_map/ppermute | solution.py:544
  94.3 19.2 %collective-permute-start.17 = (bf16[136,1088]{1,0:T(8,128)(2,1)S(1)}, bf16[136,1088]{1,0:T(8,128)(2,1)S(1)}, u32[]{:S(2)}, u32[]{:S(2)}) collective-permute-start(bf16[136,1088]{1,0:T(8,128)(2,1)S(1)} %convert_bitcast_fusion), channel_id=1, source_target_pairs={{0,12},{4,0},{8,4},{12,8},{1,13},{5,1},{9,5},{13,9},{2,14},{6,2},{... | collective-permute-start | bytes 887816 | tf_op jit(solution)/shard_map/ppermute | solution.py:544
  98.3 25.4 %collective-permute-start.16 = (bf16[136,1088]{1,0:T(8,128)(2,1)S(1)}, bf16[136,1088]{1,0:T(8,128)(2,1)S(1)}, u32[]{:S(2)}, u32[]{:S(2)}) collective-permute-start(bf16[136,1088]{1,0:T(8,128)(2,1)S(1)} %convert_bitcast_fusion), channel_id=1, source_target_pairs={{0,8},{4,12},{8,0},{12,4},{1,9},{5,13},{9,1},{13,5},{2,10},{6,14},... | collective-permute-start | bytes 887816 | tf_op jit(solution)/shard_map/ppermute | solution.py:544
  98.4 38.3 %copy-start.4 = (bf16[2,136,1088]{2,1,0:T(8,128)(2,1)}, bf16[2,136,1088]{2,1,0:T(8,128)(2,1)S(1)}, u32[]{:S(2)}) copy-start(bf16[2,136,1088]{2,1,0:T(8,128)(2,1)S(1)} %pad_maximum_fusion.12.refs_0_) | copy-start | bytes 1775620
  98.4 36.3 %collective-permute-start.11 = (bf16[2,136,1088]{2,1,0:T(8,128)(2,1)S(1)}, bf16[2,136,1088]{2,1,0:T(8,128)(2,1)S(1)}, u32[]{:S(2)}, u32[]{:S(2)}) collective-permute-start(bf16[2,136,1088]{2,1,0:T(8,128)(2,1)S(1)} %pad_maximum_fusion.12.refs_0_), channel_id=1, source_target_pairs={{0,2},{1,3},{2,0},{3,1},{4,6},{5,7},{6,4},{7,5},{8,10},{9,11},{10,... | collective-permute-start | bytes 1775624 | tf_op jit(solution)/shard_map/ppermute | solution.py:531
  100.1 39.5 %copy-start.6 = (bf16[2,136,1088]{2,1,0:T(8,128)(2,1)}, bf16[2,136,1088]{2,1,0:T(8,128)(2,1)S(1)}, u32[]{:S(2)}) copy-start(bf16[2,136,1088]{2,1,0:T(8,128)(2,1)S(1)} %pad_maximum_fusion.13.refs_2_) | copy-start | bytes 1775620
  106.4 28.3 %collective-permute-start.12 = (bf16[2,136,1088]{2,1,0:T(8,128)(2,1)S(1)}, bf16[2,136,1088]{2,1,0:T(8,128)(2,1)}, u32[]{:S(2)}, u32[]{:S(2)}) collective-permute-start(bf16[2,136,1088]{2,1,0:T(8,128)(2,1)S(1)} %pad_maximum_fusion.13.refs_2_), channel_id=1, source_target_pairs={{0,16},{16,0},{1,17},{17,1},{2,18},{18,2},{3,19},{19,3},{4,20},{20... | collective-permute-start | bytes 1775624 | tf_op jit(solution)/shard_map/ppermute | solution.py:539
  113.5 49.0 %collective-permute-start.15 = (bf16[2,136,1088]{2,1,0:T(8,128)(2,1)}, bf16[2,136,1088]{2,1,0:T(8,128)(2,1)}, u32[]{:S(2)}, u32[]{:S(2)}) collective-permute-start(bf16[2,136,1088]{2,1,0:T(8,128)(2,1)} %pad_maximum_fusion.14.refs_0_), channel_id=1, source_target_pairs={{0,2},{1,3},{2,0},{3,1},{4,6},{5,7},{6,4},{7,5},{8,10},{9,11},{10,... | collective-permute-start | bytes 1775624 | tf_op jit(solution)/shard_map/ppermute | solution.py:531
  125.5 5.5 collective-permute-start.7
  131.0 31.5 %collective-permute-start.18 = (bf16[2,136,1088]{2,1,0:T(8,128)(2,1)}, bf16[2,136,1088]{2,1,0:T(8,128)(2,1)}, u32[]{:S(2)}, u32[]{:S(2)}) collective-permute-start(bf16[2,136,1088]{2,1,0:T(8,128)(2,1)} %pad_maximum_fusion.15.refs_2_), channel_id=1, source_target_pairs={{0,16},{16,0},{1,17},{17,1},{2,18},{18,2},{3,19},{19,3},{4,20},{20... | collective-permute-start | bytes 1775624 | tf_op jit(solution)/shard_map/ppermute | solution.py:539
  138.1 58.1 %collective-permute-start.20 = (bf16[2,2,136,1088]{3,2,1,0:T(8,128)(2,1)}, bf16[2,2,136,1088]{3,2,1,0:T(8,128)(2,1)}, u32[]{:S(2)}, u32[]{:S(2)}) collective-permute-start(bf16[2,2,136,1088]{3,2,1,0:T(8,128)(2,1)} %pad_maximum_fusion.3), channel_id=1, source_target_pairs={{0,16},{16,0},{1,17},{17,1},{2,18},{18,2},{3,19},{19,3},{4,20},{20... | collective-permute-start | bytes 3551240 | tf_op jit(solution)/shard_map/ppermute | solution.py:539
  141.8 54.3 %collective-permute-start.21 = (bf16[2,2,136,1088]{3,2,1,0:T(8,128)(2,1)}, bf16[2,2,136,1088]{3,2,1,0:T(8,128)(2,1)}, u32[]{:S(2)}, u32[]{:S(2)}) collective-permute-start(bf16[2,2,136,1088]{3,2,1,0:T(8,128)(2,1)} %pad_maximum_fusion.4), channel_id=1, source_target_pairs={{0,2},{1,3},{2,0},{3,1},{4,6},{5,7},{6,4},{7,5},{8,10},{9,11},{10,... | collective-permute-start | bytes 3551240 | tf_op jit(solution)/shard_map/ppermute | solution.py:531
  165.1 13.5 %collective-permute-start.19 = (bf16[512,2304]{1,0:T(8,128)(2,1)}, bf16[512,2304]{1,0:T(8,128)(2,1)}, u32[]{:S(2)}, u32[]{:S(2)}) collective-permute-start(bf16[512,2304]{1,0:T(8,128)(2,1)} %slice.219), channel_id=1, source_target_pairs={{0,1},{2,3},{4,5},{6,7},{8,9},{10,11},{12,13},{14,15},{16,17},{18,... | collective-permute-start | bytes 7077896 | tf_op jit(solution)/shard_map/ppermute | solution.py:769
  170.8 60.6 %collective-permute-start.22 = (bf16[2,2,136,1088]{3,2,1,0:T(8,128)(2,1)}, bf16[2,2,136,1088]{3,2,1,0:T(8,128)(2,1)S(1)}, u32[]{:S(2)}, u32[]{:S(2)}) collective-permute-start(bf16[2,2,136,1088]{3,2,1,0:T(8,128)(2,1)} %pad_maximum_fusion.5), channel_id=1, source_target_pairs={{0,16},{16,0},{1,17},{17,1},{2,18},{18,2},{3,19},{19,3},{4,20},{20... | collective-permute-start | bytes 3551240 | tf_op jit(solution)/shard_map/ppermute | solution.py:539
  173.8 57.6 %collective-permute-start.23 = (bf16[2,2,136,1088]{3,2,1,0:T(8,128)(2,1)}, bf16[2,2,136,1088]{3,2,1,0:T(8,128)(2,1)S(1)}, u32[]{:S(2)}, u32[]{:S(2)}) collective-permute-start(bf16[2,2,136,1088]{3,2,1,0:T(8,128)(2,1)} %pad_maximum_fusion.6), channel_id=1, source_target_pairs={{0,2},{1,3},{2,0},{3,1},{4,6},{5,7},{6,4},{7,5},{8,10},{9,11},{10,... | collective-permute-start | bytes 3551240 | tf_op jit(solution)/shard_map/ppermute | solution.py:531
  220.3 31.4 %collective-permute-start.24 = (bf16[2,1088,1088]{2,1,0:T(8,128)(2,1)}, bf16[2,1088,1088]{2,1,0:T(8,128)(2,1)}, u32[]{:S(2)}, u32[]{:S(2)}) collective-permute-start(bf16[2,1088,1088]{2,1,0:T(8,128)(2,1)} %bitcast.53), channel_id=1, source_target_pairs={{0,1},{1,0},{2,3},{3,2},{4,5},{5,4},{6,7},{7,6},{8,9},{9,8},{10,11... | collective-permute-start | bytes 14204936 | tf_op jit(solution)/shard_map/ppermute | solution.py:531
  241.4 29.6 %collective-permute-start.25 = (bf16[2,1088,1088]{2,1,0:T(8,128)(2,1)}, bf16[2,1088,1088]{2,1,0:T(8,128)(2,1)}, u32[]{:S(2)}, u32[]{:S(2)}) collective-permute-start(bf16[2,1088,1088]{2,1,0:T(8,128)(2,1)} %bitcast.55), channel_id=1, source_target_pairs={{0,1},{1,0},{2,3},{3,2},{4,5},{5,4},{6,7},{7,6},{8,9},{9,8},{10,11... | collective-permute-start | bytes 14204936 | tf_op jit(solution)/shard_map/ppermute | solution.py:531
  245.7 25.8 %copy-start.59 = (bf16[512,1088]{1,0:T(8,128)(2,1)}, bf16[512,1088]{1,0:T(8,128)(2,1)S(1)}, u32[]{:S(2)}) copy-start(bf16[512,1088]{1,0:T(8,128)(2,1)S(1)} %multiply_convert_fusion.3.refs_1_) | copy-start | bytes 3342340
  271.0 41.4 %collective-permute-start.26 = (bf16[2,1088,1088]{2,1,0:T(8,128)(2,1)}, bf16[2,1088,1088]{2,1,0:T(8,128)(2,1)}, u32[]{:S(2)}, u32[]{:S(2)}) collective-permute-start(bf16[2,1088,1088]{2,1,0:T(8,128)(2,1)} %block_grads.6), channel_id=1, source_target_pairs={{0,1},{1,0},{2,3},{3,2},{4,5},{5,4},{6,7},{7,6},{8,9},{9,8},{10,11... | collective-permute-start | bytes 14204936 | tf_op jit(solution)/shard_map/ppermute | solution.py:531
  334.9 44.7 %collective-permute-start.27 = (bf16[2,1088,1088]{2,1,0:T(8,128)(2,1)}, bf16[2,1088,1088]{2,1,0:T(8,128)(2,1)}, u32[]{:S(2)}, u32[]{:S(2)}) collective-permute-start(bf16[2,1088,1088]{2,1,0:T(8,128)(2,1)} %block_grads.8), channel_id=1, source_target_pairs={{0,1},{1,0},{2,3},{3,2},{4,5},{5,4},{6,7},{7,6},{8,9},{9,8},{10,11... | collective-permute-start | bytes 14204936 | tf_op jit(solution)/shard_map/ppermute | solution.py:531
  346.5 29.9 %collective-permute-start.28 = (bf16[2,272,1088]{2,1,0:T(8,128)(2,1)}, bf16[2,272,1088]{2,1,0:T(8,128)(2,1)}, u32[]{:S(2)}, u32[]{:S(2)}) collective-permute-start(bf16[2,272,1088]{2,1,0:T(8,128)(2,1)} %get-tuple-element.156), channel_id=1, source_target_pairs={{0,16},{16,0},{1,17},{17,1},{2,18},{18,2},{3,19},{19,3},{4,20},{20... | collective-permute-start | bytes 3551240 | tf_op jit(solution)/shard_map/ppermute | solution.py:539
  347.9 30.1 %collective-permute-start.29 = (bf16[2,272,1088]{2,1,0:T(8,128)(2,1)}, bf16[2,272,1088]{2,1,0:T(8,128)(2,1)}, u32[]{:S(2)}, u32[]{:S(2)}) collective-permute-start(bf16[2,272,1088]{2,1,0:T(8,128)(2,1)} %get-tuple-element.158), channel_id=1, source_target_pairs={{0,2},{1,3},{2,0},{3,1},{4,6},{5,7},{6,4},{7,5},{8,10},{9,11},{10,... | collective-permute-start | bytes 3551240 | tf_op jit(solution)/shard_map/ppermute | solution.py:531
  389.2 27.8 %collective-permute-start.31 = (bf16[272,1088]{1,0:T(8,128)(2,1)S(1)}, bf16[272,1088]{1,0:T(8,128)(2,1)}, u32[]{:S(2)}, u32[]{:S(2)}) collective-permute-start(bf16[272,1088]{1,0:T(8,128)(2,1)S(1)} %dynamic-slice_bitcast_fusion.2), channel_id=1, source_target_pairs={{0,16},{16,0},{1,17},{17,1},{2,18},{18,2},{3,19},{19,3},{4,20},{20... | collective-permute-start | bytes 1775624 | tf_op jit(solution)/shard_map/ppermute | solution.py:539
  391.5 25.3 %collective-permute-start.30 = (bf16[272,1088]{1,0:T(8,128)(2,1)}, bf16[272,1088]{1,0:T(8,128)(2,1)S(1)}, u32[]{:S(2)}, u32[]{:S(2)}) collective-permute-start(bf16[272,1088]{1,0:T(8,128)(2,1)} %slice_bitcast_fusion.15), channel_id=1, source_target_pairs={{0,2},{1,3},{2,0},{3,1},{4,6},{5,7},{6,4},{7,5},{8,10},{9,11},{10,... | collective-permute-start | bytes 1775624 | tf_op jit(solution)/shard_map/ppermute | solution.py:531
  393.0 38.5 %collective-permute-start.32 = (bf16[2,272,1088]{2,1,0:T(8,128)(2,1)}, bf16[2,272,1088]{2,1,0:T(8,128)(2,1)}, u32[]{:S(2)}, u32[]{:S(2)}) collective-permute-start(bf16[2,272,1088]{2,1,0:T(8,128)(2,1)} %get-tuple-element.167), channel_id=1, source_target_pairs={{0,16},{16,0},{1,17},{17,1},{2,18},{18,2},{3,19},{19,3},{4,20},{20... | collective-permute-start | bytes 3551240 | tf_op jit(solution)/shard_map/ppermute | solution.py:539
  393.7 40.0 %collective-permute-start.33 = (bf16[2,272,1088]{2,1,0:T(8,128)(2,1)}, bf16[2,272,1088]{2,1,0:T(8,128)(2,1)}, u32[]{:S(2)}, u32[]{:S(2)}) collective-permute-start(bf16[2,272,1088]{2,1,0:T(8,128)(2,1)} %get-tuple-element.169), channel_id=1, source_target_pairs={{0,2},{1,3},{2,0},{3,1},{4,6},{5,7},{6,4},{7,5},{8,10},{9,11},{10,... | collective-permute-start | bytes 3551240 | tf_op jit(solution)/shard_map/ppermute | solution.py:531
  415.4 19.9 %collective-permute-start.34 = (bf16[512,2304]{1,0:T(8,128)(2,1)S(1)}, bf16[512,2304]{1,0:T(8,128)(2,1)S(1)}, u32[]{:S(2)}, u32[]{:S(2)}) collective-permute-start(bf16[512,2304]{1,0:T(8,128)(2,1)S(1)} %pad_maximum_fusion), channel_id=1, source_target_pairs={{1,0},{3,2},{5,4},{7,6},{9,8},{11,10},{13,12},{15,14},{17,16},{19,... | collective-permute-start | bytes 7077896 | tf_op jit(solution)/shard_map/ppermute | solution.py:879
  441.9 30.4 %copy-start.12 = (bf16[2,512,896]{2,1,0:T(8,128)(2,1)}, bf16[2,512,896]{2,1,0:T(8,128)(2,1)S(1)}, u32[]{:S(2)}) copy-start(bf16[2,512,896]{2,1,0:T(8,128)(2,1)S(1)} %get-tuple-element.175.refs_2_) | copy-start | bytes 5505028
  449.9 34.5 %collective-permute-start.36 = (bf16[2,1088,1152]{2,1,0:T(8,128)(2,1)}, bf16[2,1088,1152]{2,1,0:T(8,128)(2,1)}, u32[]{:S(2)}, u32[]{:S(2)}) collective-permute-start(bf16[2,1088,1152]{2,1,0:T(8,128)(2,1)} %block_grads.10), channel_id=1, source_target_pairs={{0,1},{1,0},{2,3},{3,2},{4,5},{5,4},{6,7},{7,6},{8,9},{9,8},{10,11... | collective-permute-start | bytes 15040520 | tf_op jit(solution)/shard_map/ppermute | solution.py:531
  450.0 16.6 %collective-permute-start.45 = (bf16[272,1088]{1,0:T(8,128)(2,1)S(1)}, bf16[272,1088]{1,0:T(8,128)(2,1)S(1)}, u32[]{:S(2)}, u32[]{:S(2)}) collective-permute-start(bf16[272,1088]{1,0:T(8,128)(2,1)S(1)} %dynamic-slice_bitcast_fusion), channel_id=1, source_target_pairs={{0,16},{16,0},{1,17},{17,1},{2,18},{18,2},{3,19},{19,3},{4,20},{20... | collective-permute-start | bytes 1775624 | tf_op jit(solution)/shard_map/ppermute | solution.py:539
  450.9 16.3 %collective-permute-start.44 = (bf16[272,1088]{1,0:T(8,128)(2,1)S(1)}, bf16[272,1088]{1,0:T(8,128)(2,1)S(1)}, u32[]{:S(2)}, u32[]{:S(2)}) collective-permute-start(bf16[272,1088]{1,0:T(8,128)(2,1)S(1)} %slice_bitcast_fusion.14), channel_id=1, source_target_pairs={{0,2},{1,3},{2,0},{3,1},{4,6},{5,7},{6,4},{7,5},{8,10},{9,11},{10,... | collective-permute-start | bytes 1775624 | tf_op jit(solution)/shard_map/ppermute | solution.py:531
  453.4 40.4 %collective-permute-start.51 = (bf16[136,1088]{1,0:T(8,128)(2,1)}, bf16[136,1088]{1,0:T(8,128)(2,1)}, u32[]{:S(2)}, u32[]{:S(2)}) collective-permute-start(bf16[136,1088]{1,0:T(8,128)(2,1)} %get-tuple-element.256), channel_id=1, source_target_pairs={{0,12},{4,0},{8,4},{12,8},{1,13},{5,1},{9,5},{13,9},{2,14},{6,2},{... | collective-permute-start | bytes 887816 | tf_op jit(solution)/shard_map/ppermute | solution.py:544
  454.4 40.0 %collective-permute-start.50 = (bf16[136,1088]{1,0:T(8,128)(2,1)}, bf16[136,1088]{1,0:T(8,128)(2,1)}, u32[]{:S(2)}, u32[]{:S(2)}) collective-permute-start(bf16[136,1088]{1,0:T(8,128)(2,1)} %get-tuple-element.257), channel_id=1, source_target_pairs={{0,8},{4,12},{8,0},{12,4},{1,9},{5,13},{9,1},{13,5},{2,10},{6,14},... | collective-permute-start | bytes 887816 | tf_op jit(solution)/shard_map/ppermute | solution.py:544
  466.5 29.4 %collective-permute-start.49 = (bf16[136,1088]{1,0:T(8,128)(2,1)S(1)}, bf16[136,1088]{1,0:T(8,128)(2,1)}, u32[]{:S(2)}, u32[]{:S(2)}) collective-permute-start(bf16[136,1088]{1,0:T(8,128)(2,1)S(1)} %get-tuple-element.255), channel_id=1, source_target_pairs={{0,4},{4,8},{8,12},{12,0},{1,5},{5,9},{9,13},{13,1},{2,6},{6,10},{... | collective-permute-start | bytes 887816 | tf_op jit(solution)/shard_map/ppermute | solution.py:544
  478.4 1.3 collective-permute-start.35
  479.7 20.0 %collective-permute-start.48 = (bf16[136,1088]{1,0:T(8,128)(2,1)S(1)}, bf16[136,1088]{1,0:T(8,128)(2,1)}, u32[]{:S(2)}, u32[]{:S(2)}) collective-permute-start(bf16[136,1088]{1,0:T(8,128)(2,1)S(1)} %get-tuple-element.259), channel_id=1, source_target_pairs={{0,12},{4,0},{8,4},{12,8},{1,13},{5,1},{9,5},{13,9},{2,14},{6,2},{... | collective-permute-start | bytes 887816 | tf_op jit(solution)/shard_map/ppermute | solution.py:544
  484.4 24.9 %collective-permute-start.47 = (bf16[136,1088]{1,0:T(8,128)(2,1)S(1)}, bf16[136,1088]{1,0:T(8,128)(2,1)}, u32[]{:S(2)}, u32[]{:S(2)}) collective-permute-start(bf16[136,1088]{1,0:T(8,128)(2,1)S(1)} %get-tuple-element.260), channel_id=1, source_target_pairs={{0,8},{4,12},{8,0},{12,4},{1,9},{5,13},{9,1},{13,5},{2,10},{6,14},... | collective-permute-start | bytes 887816 | tf_op jit(solution)/shard_map/ppermute | solution.py:544
  493.8 15.5 %collective-permute-start.46 = (bf16[136,1088]{1,0:T(8,128)(2,1)S(1)}, bf16[136,1088]{1,0:T(8,128)(2,1)S(1)}, u32[]{:S(2)}, u32[]{:S(2)}) collective-permute-start(bf16[136,1088]{1,0:T(8,128)(2,1)S(1)} %get-tuple-element.258), channel_id=1, source_target_pairs={{0,4},{4,8},{8,12},{12,0},{1,5},{5,9},{9,13},{13,1},{2,6},{6,10},{... | collective-permute-start | bytes 887816 | tf_op jit(solution)/shard_map/ppermute | solution.py:544
  494.4 29.3 %collective-permute-start.39 = (bf16[2,272,1152]{2,1,0:T(8,128)(2,1)}, bf16[2,272,1152]{2,1,0:T(8,128)(2,1)S(1)}, u32[]{:S(2)}, u32[]{:S(2)}) collective-permute-start(bf16[2,272,1152]{2,1,0:T(8,128)(2,1)} %get-tuple-element.181), channel_id=1, source_target_pairs={{0,2},{1,3},{2,0},{3,1},{4,6},{5,7},{6,4},{7,5},{8,10},{9,11},{10,... | collective-permute-start | bytes 3760136 | tf_op jit(solution)/shard_map/ppermute | solution.py:531
  498.9 24.9 %copy-start.58 = (bf16[2,272,1152]{2,1,0:T(8,128)(2,1)S(1)}, bf16[2,272,1152]{2,1,0:T(8,128)(2,1)}, u32[]{:S(2)}) copy-start(bf16[2,272,1152]{2,1,0:T(8,128)(2,1)} %get-tuple-element.180) | copy-start | bytes 3760132
  498.9 30.5 %collective-permute-start.37 = (bf16[2,272,1152]{2,1,0:T(8,128)(2,1)S(1)}, bf16[2,272,1152]{2,1,0:T(8,128)(2,1)S(1)}, u32[]{:S(2)}, u32[]{:S(2)}) collective-permute-start(bf16[2,272,1152]{2,1,0:T(8,128)(2,1)S(1)} %copy-done.86), channel_id=1, source_target_pairs={{0,16},{16,0},{1,17},{17,1},{2,18},{18,2},{3,19},{19,3},{4,20},{20... | collective-permute-start | bytes 3760136 | tf_op jit(solution)/shard_map/ppermute | solution.py:539
  524.1 17.0 %collective-permute-start.40 = (bf16[272,1152]{1,0:T(8,128)(2,1)S(1)}, bf16[272,1152]{1,0:T(8,128)(2,1)S(1)}, u32[]{:S(2)}, u32[]{:S(2)}) collective-permute-start(bf16[272,1152]{1,0:T(8,128)(2,1)S(1)} %dynamic-slice_bitcast_fusion.1), channel_id=1, source_target_pairs={{0,16},{16,0},{1,17},{17,1},{2,18},{18,2},{3,19},{19,3},{4,20},{20... | collective-permute-start | bytes 1880072 | tf_op jit(solution)/shard_map/ppermute | solution.py:539
  529.7 12.8 %collective-permute-start.38 = (bf16[272,1152]{1,0:T(8,128)(2,1)S(1)}, bf16[272,1152]{1,0:T(8,128)(2,1)S(1)}, u32[]{:S(2)}, u32[]{:S(2)}) collective-permute-start(bf16[272,1152]{1,0:T(8,128)(2,1)S(1)} %slice_bitcast_fusion.12), channel_id=1, source_target_pairs={{0,2},{1,3},{2,0},{3,1},{4,6},{5,7},{6,4},{7,5},{8,10},{9,11},{10,... | collective-permute-start | bytes 1880072 | tf_op jit(solution)/shard_map/ppermute | solution.py:531
  542.9 11.2 %collective-permute-start.43 = (bf16[136,1152]{1,0:T(8,128)(2,1)S(1)}, bf16[136,1152]{1,0:T(8,128)(2,1)S(1)}, u32[]{:S(2)}, u32[]{:S(2)}) collective-permute-start(bf16[136,1152]{1,0:T(8,128)(2,1)S(1)} %get-tuple-element.262), channel_id=1, source_target_pairs={{0,12},{4,0},{8,4},{12,8},{1,13},{5,1},{9,5},{13,9},{2,14},{6,2},{... | collective-permute-start | bytes 940040 | tf_op jit(solution)/shard_map/ppermute | solution.py:544
  546.2 25.1 %collective-permute-start.42 = (bf16[136,1152]{1,0:T(8,128)(2,1)S(1)}, bf16[136,1152]{1,0:T(8,128)(2,1)S(1)}, u32[]{:S(2)}, u32[]{:S(2)}) collective-permute-start(bf16[136,1152]{1,0:T(8,128)(2,1)S(1)} %get-tuple-element.263), channel_id=1, source_target_pairs={{0,8},{4,12},{8,0},{12,4},{1,9},{5,13},{9,1},{13,5},{2,10},{6,14},... | collective-permute-start | bytes 940040 | tf_op jit(solution)/shard_map/ppermute | solution.py:544
  546.8 24.6 %collective-permute-start.41 = (bf16[136,1152]{1,0:T(8,128)(2,1)S(1)}, bf16[136,1152]{1,0:T(8,128)(2,1)S(1)}, u32[]{:S(2)}, u32[]{:S(2)}) collective-permute-start(bf16[136,1152]{1,0:T(8,128)(2,1)S(1)} %get-tuple-element.261), channel_id=1, source_target_pairs={{0,4},{4,8},{8,12},{12,0},{1,5},{5,9},{9,13},{13,1},{2,6},{6,10},{... | collective-permute-start | bytes 940040 | tf_op jit(solution)/shard_map/ppermute | solution.py:544
  549.4 22.8 %copy-start.62 = (f32[272,136]{0,1:T(8,128)S(1)}, f32[272,136]{0,1:T(8,128)}, u32[]{:S(2)}) copy-start(f32[272,136]{0,1:T(8,128)} %param.31) | copy-start | bytes 443908
  (86 other events, 529.6 us)

commit v5 on v4

--- a/solution.py
+++ b/solution.py
@@ -243,9 +243,6 @@
             jax.ShapeDtypeStruct((pairs, 2, count), f32),
         ],
         compiler_params=pltpu.CompilerParams(vmem_limit_bytes=48 << 20),
-        cost_estimate=pl.CostEstimate(
-            flops=4 * work, bytes_accessed=6 * count * pairs * LANES * 2, transcendentals=0
-        ),
         name="attention_forward",
     )(later, *labels, projected, projected, projected, others, others)
 
@@ -266,9 +263,6 @@
         ),
         out_shape=[jax.ShapeDtypeStruct((count, pairs * LANES), bf16)] * 5,
         compiler_params=pltpu.CompilerParams(vmem_limit_bytes=48 << 20),
-        cost_estimate=pl.CostEstimate(
-            flops=10 * work, bytes_accessed=12 * count * pairs * LANES * 2, transcendentals=0
-        ),
         name="attention_backward",
     )(later, *labels, projected, projected, projected, others, others, grad, mixed, log_totals)
 
@@ -343,11 +337,6 @@
         ),
         out_shape=jax.ShapeDtypeStruct((count, out_lanes), bf16),
         compiler_params=pltpu.CompilerParams(vmem_limit_bytes=48 << 20),
-        cost_estimate=pl.CostEstimate(
-            flops=2 * count * depth * lanes * each * sources,
-            bytes_accessed=2 * (each * sources * depth * lanes + count * (depth + out_lanes)),
-            transcendentals=0,
-        ),
         name="multiply_and_place",
     )(places, *operands)
 
@@ -409,7 +398,6 @@
         ),
         out_shape=out_shapes,
         compiler_params=pltpu.CompilerParams(vmem_limit_bytes=48 << 20),
-        cost_estimate=pl.CostEstimate(flops=moved, bytes_accessed=moved, transcendentals=0),
         name=name,
     )(column, *operands)
 
@@ -421,47 +409,44 @@
     rights = [[refs.pop(0) for _ in range(count)] for count in counts]
     vec_part = refs.pop(0) if has_vec else None
     received = refs.pop(0) if has_received else None
-    total = refs.pop()
-
-    def product(left, right):
-        right = right[0] if len(right.shape) == 3 else right[...]
-        return jnp.dot(left[...], right, preferred_element_type=f32)
-
-    if counts[0] > 1:
-        for i, right in enumerate(rights[0]):
-
-            @pl.when(step == i)
-            def _(right=right):
-                total[...] = product(lefts[0], right)
-
-    else:
-        lanes_one = rights[0][0].shape[-1]
-        total[:, :lanes_one] = product(lefts[0], rights[0][0])
-        total[:, lanes_one:] = jnp.zeros_like(total[:, lanes_one:])
-    for left, right in zip(lefts[1:], rights[1:]):
-        total[:, -right[0].shape[-1] :] += product(left, right[0])
-    if has_vec:
-        total[:, -LANES:] += vec_part[0].astype(f32)
-    if has_received:
-        total[...] += received[0].astype(f32)
-    if not split:
-        refs[0][0] = total[...].astype(bf16)
-        return
-    first_keep, first_send, second_keep, second_send = refs
-    half = total.shape[0] // 2
-    quarter = half // 2
-
-    def rows(start):
-        return total[pl.ds(pl.multiple_of(start, 8), quarter)].astype(bf16)
-
-    first_keep[0] = rows(place[0] * half)
-    first_send[0] = rows((1 - place[0]) * half)
-    for i, second in enumerate((second_keep, second_send)):
+    width = lefts[0].shape[0]
+    quarter = width // 4
+
+    def value(start, which):
+        rows = pl.ds(start, quarter)
+        if counts[0] > 1:
+            whole = contract_last(lefts[0][rows], rights[0][which][...])
+        else:
+            one, two = [
+                jnp.dot(left[rows], right[0][0], preferred_element_type=f32)
+                for left, right in zip(lefts, rights)
+            ]
+            lead = one.shape[1] - LANES
+            whole = jnp.concatenate(
+                [one[:, :lead], one[:, lead:] + two[:, :LANES], two[:, LANES:]], 1
+            )
+        if has_vec:
+            more = whole[:, -LANES:] + vec_part[0, rows].astype(f32)
+            whole = jnp.concatenate([whole[:, :-LANES], more], 1)
+        if has_received:
+            whole = whole + received[0, rows].astype(f32)
+        return whole.astype(bf16)
+
+    for i in range(2):
 
         @pl.when(step == i)
-        def _(second=second):
+        def _(i=i):
+            if not split:
+                for k in range(4):
+                    refs[0][0, k * quarter : (k + 1) * quarter] = value(k * quarter, i)
+                return
+            first_keep, first_send, second_keep, second_send = refs
+            half = width // 2
+            first_keep[0] = value(pl.multiple_of(place[0] * half, 16), i)
+            first_send[0] = value(pl.multiple_of((1 - place[0]) * half, 16), i)
+            second = (second_keep, second_send)[i]
             for dp in range(2):
-                second[dp] = total[dp * half + quarter : (dp + 1) * half].astype(bf16)
+                second[dp] = value(dp * half + quarter, i)
 
 
 def block_grads(pairs, vec_part, received, split):
@@ -469,7 +454,7 @@
     rights = [r if isinstance(r, list) else [r] for r in rights]
     width, count = lefts[0].shape
     each = 2
-    lanes = rights[0][0].shape[-1] if len(pairs) == 1 else -(-width // LANES) * LANES
+    lanes = width if len(pairs) == 1 else -(-width // LANES) * LANES
     place = lax.axis_index("dp").reshape(1).astype(jnp.int32)
 
     def fixed(shape):
@@ -503,15 +488,9 @@
             grid=(each,),
             in_specs=in_specs,
             out_specs=out_specs,
-            scratch_shapes=[pltpu.VMEM((width, lanes), f32)],
         ),
         out_shape=out_shape,
-        compiler_params=pltpu.CompilerParams(vmem_limit_bytes=56 << 20),
-        cost_estimate=pl.CostEstimate(
-            flops=2 * each * count * width * lanes,
-            bytes_accessed=2 * each * width * lanes * 2,
-            transcendentals=0,
-        ),
+        compiler_params=pltpu.CompilerParams(vmem_limit_bytes=48 << 20),
         name="block_grads",
     )(place, *lefts, *flat, *more)
 
@@ -559,47 +538,51 @@
     return lax.axis_size("row") == 4 and lax.axis_size("dp") == 2 and lax.axis_size("col") == 4
 
 
-def assemble_kernel(ranges, targets, *refs):
-    sources, out = refs[:-1], refs[-1]
-    step = pl.program_id(0)
-    for (start, end), source in zip(ranges, sources):
-
-        @pl.when((step >= start) & (step < end))
-        def _(source=source):
-            out[...] = source[...]
+def assemble_kernel(place, *refs):
+    sources, (out, held, sems_in, sems_out) = refs[:-4], refs[-4:]
+    dp, row = place[0], place[1]
+    order = (
+        [(0, 0, 0), (0, 0, 1), (1, 0, 0), (1, 0, 1), (0, 0, 2), (0, 0, 3), (0, 1, 2), (0, 1, 3)]
+        + [(0, 1, 0), (0, 1, 1), (1, 1, 0), (1, 1, 1)]
+        + [(1, 0, 2), (1, 0, 3), (1, 1, 2), (1, 1, 3)]
+    )
+    blocks = [source.at[i] for source in sources for i in range(source.shape[0])]
+    copies_in, copies_out = [], []
+    for k, (block, (over_x, over_y, behind)) in enumerate(zip(blocks, order)):
+        target = over_x * 8 + (1 - dp if over_y else dp) * 4 + lax.rem(row + 4 - behind, 4)
+        copies_in.append(pltpu.make_async_copy(block, held.at[k], sems_in.at[k]))
+        copies_out.append(pltpu.make_async_copy(held.at[k], out.at[target], sems_out.at[k]))
+    for copy in copies_in:
+        copy.start()
+    for copy_in, copy_out in zip(copies_in, copies_out):
+        copy_in.wait()
+        copy_out.start()
+    for copy in copies_out:
+        copy.wait()
 
 
 def assemble(pieces):
     rows, lanes = pieces[0].shape[-2:]
     pieces = [p.reshape(-1, rows, lanes) for p in pieces]
-    starts = [sum(p.shape[0] for p in pieces[:k]) for k in range(len(pieces))]
-    ends = [start + p.shape[0] for start, p in zip(starts, pieces)]
-    over_x = jnp.array([0, 0, 1, 1, 0, 0, 0, 0, 0, 0, 1, 1, 1, 1, 1, 1], jnp.int32)
-    over_y = jnp.array([0, 0, 0, 0, 0, 0, 1, 1, 1, 1, 1, 1, 0, 0, 1, 1], jnp.int32)
-    behind = jnp.array([0, 1, 0, 1, 2, 3, 2, 3, 0, 1, 0, 1, 2, 3, 2, 3], jnp.int32)
-    dp, row = lax.axis_index("dp"), lax.axis_index("row")
-    targets = (over_x * 8 + (dp ^ over_y) * 4 + (row + 4 - behind) % 4).astype(jnp.int32)
-
-    def from_piece(start, end):
-        return pl.BlockSpec(
-            (1, rows, lanes), lambda i, targets: (jnp.clip(i - start, 0, end - start - 1), 0, 0)
-        )
-
+    place = jnp.stack([lax.axis_index("dp"), lax.axis_index("row")]).astype(jnp.int32)
+    anywhere = pl.BlockSpec(memory_space=pl.ANY)
     out = pl.pallas_call(
-        functools.partial(assemble_kernel, tuple(zip(starts, ends))),
+        assemble_kernel,
         grid_spec=pltpu.PrefetchScalarGridSpec(
             num_scalar_prefetch=1,
-            grid=(ends[-1],),
-            in_specs=[from_piece(start, end) for start, end in zip(starts, ends)],
-            out_specs=pl.BlockSpec((1, rows, lanes), lambda i, targets: (targets[i], 0, 0)),
+            grid=(1,),
+            in_specs=[anywhere] * len(pieces),
+            out_specs=anywhere,
+            scratch_shapes=[
+                pltpu.VMEM((16, rows, lanes), bf16),
+                pltpu.SemaphoreType.DMA((16,)),
+                pltpu.SemaphoreType.DMA((16,)),
+            ],
         ),
-        out_shape=jax.ShapeDtypeStruct((ends[-1], rows, lanes), bf16),
-        compiler_params=pltpu.CompilerParams(vmem_limit_bytes=32 << 20),
-        cost_estimate=pl.CostEstimate(
-            flops=0, bytes_accessed=64 * rows * lanes, transcendentals=0
-        ),
+        out_shape=jax.ShapeDtypeStruct((16, rows, lanes), bf16),
+        compiler_params=pltpu.CompilerParams(vmem_limit_bytes=48 << 20),
         name="assemble",
-    )(targets, *pieces)
+    )(place, *pieces)
     return out.reshape(2, -1, lanes)
 
 
@@ -722,13 +705,14 @@
     up_block, down_block = up_weight.astype(bf16), down_weight.T.astype(bf16)
     staged = short_rows()
     if staged:
-        attn_one = spread_one(spread_rows(attn_block))
-        up_block, attn_one = together(up_block, attn_one)
+        attn_rows = spread_rows(attn_block)
+        up_block, attn_rows = together(up_block, attn_rows)
+        attn_one = spread_one(attn_rows)
         up_rows = spread_rows(up_block)
         down_block, up_rows = together(down_block, up_rows)
         down_rows = spread_rows(down_block)
         attn_own = assemble(spread_two(attn_one))
-        up_one, down_one = spread_one(up_rows), spread_one(down_rows)
+        up_one = spread_one(up_rows)
     else:
         attn_own, up_own, down_own = [
             gather_groups(b) for b in (attn_block, up_block, down_block)
@@ -758,11 +742,13 @@
     spans = tuple((part * piece, part * padded) for part in range(3))
     projected = None
     for places, weights in ((places_own, attn_own), (places_oth, attn_oth)):
+        if staged and projected is not None:
+            projected, down_rows = together(projected, down_rows)
         projected = multiply_and_place(
             places, normed_low, [weights], lanes_qkv, 0, spans, piece, 3 * padded, bias, projected
         )
     if staged:
-        projected, down_one = together(projected, down_one)
+        projected, down_one = together(projected, spread_one(down_rows))
         down_two = spread_two(down_one)
     ahead = [(c, c + 1) for c in range(cols - 1) if c % halves + 1 < halves]
     behind = [(b, a) for a, b in ahead]
@@ -821,15 +807,19 @@
             branch = branch + contract_last(lows[i], downs[i])
         return lows, pullbacks, branch
 
+    left_down, left_up = cotangent.T, normed_two_low.T
+
+    def turned(rights):
+        return [r.T for r in rights]
+
+    lows_oth, pull_oth, branch = forward_part(linear_oth, down_oth, branch)
+    sent_down = block_grads([(left_down, turned(lows_oth))], None, None, False)
+    linear_own, sent_down = together(linear_own, sent_down)
+    received_down = partner(sent_down)
     lows_own, pull_own, branch = forward_part(linear_own, down_own, branch)
-    lows_oth, pull_oth, branch = forward_part(linear_oth, down_oth, branch)
+    total_down = block_grads([(left_down, turned(lows_own))], None, received_down, staged)
     layer_out = (residual + branch + vec[7]).astype(bf16)
-
-    left_down, left_up = cotangent.T, normed_two_low.T
-    sent_down = block_grads([(left_down, lows_oth)], None, None, False)
-    down_oth, sent_down = together(down_oth, sent_down)
-    received_down = partner(sent_down)
-
+    down_oth, total_down = together(down_oth, total_down)
     grad_normed_two = jnp.zeros((here, width), f32)
 
     def backward_part(ups, downs, pullbacks, grad_normed_two):
@@ -845,12 +835,11 @@
     dups_oth, dbias_oth, grad_normed_two = backward_part(
         up_oth, down_oth, pull_oth, grad_normed_two
     )
-    lows_own, dups_oth = together(lows_own, dups_oth)
-    total_down = block_grads([(left_down, lows_own)], None, received_down, staged)
-    sent_up = block_grads([(left_up, dups_oth)], None, None, False)
-    down_own, total_down, sent_up = together(down_own, total_down, sent_up)
+    one_down = scatter_one(total_down)
+    sent_up = block_grads([(left_up, turned(dups_oth))], None, None, False)
+    down_own, one_down, sent_up = together(down_own, one_down, sent_up)
     received_up = partner(sent_up)
-    one_down = scatter_one(total_down)
+    two_down = scatter_two(one_down)
     dups_own, dbias_own, grad_normed_two = backward_part(
         up_own, down_own, pull_own, grad_normed_two
     )
@@ -871,15 +860,14 @@
         None,
         None,
     )
-    total_up = block_grads([(left_up, dups_own)], None, received_up, staged)
-    grad_mixed, total_up, one_down = together(grad_mixed, total_up, one_down)
+    total_up = block_grads([(left_up, turned(dups_own))], None, received_up, staged)
+    grad_mixed, total_up, two_down = together(grad_mixed, total_up, two_down)
     dq, dk_own, dv_own, dk_oth, dv_oth = attend_back(
         later, labels, projected, others, grad_mixed, mixed, log_totals
     )
     back = lax.ppermute(jnp.concatenate([dk_oth, dv_oth], 1), "col", behind)
-    two_down = scatter_two(one_down)
     one_up = scatter_one(total_up)
-    dq, dk_own, dv_own, two_down, one_up = together(dq, dk_own, dv_own, two_down, one_up)
+    dq, dk_own, dv_own, one_up = together(dq, dk_own, dv_own, one_up)
     grads_shape = jax.ShapeDtypeStruct((each, here, lanes_qkv), bf16)
     grads_own, grads_oth, grad_sums = split_call(
         functools.partial(split_grads_kernel, piece, cols),

time: 583 us -> 543 us (0.931)
  Pallas kernels: 148 us -> 117 us
  waiting for transfers between devices: 180 us -> 156 us
  starting transfers between devices: 61.5 us -> 84.9 us
  matrix products: 82.4 us -> 70.3 us
  other arithmetic: 58.2 us -> 68.2 us
  local copies, waits for them, and re-layouts: 45.1 us -> 38.1 us
    ppermute x12, waiting for transfers between devices: 85.4 us -> 59.9 us  [flip_dp(): return lax.ppermute(block, 'dp', [(0, 1), (1, 0)])]
    ppermute x20, waiting for transfers between devices: 17.3 us -> 41.7 us  [flip_col(): lax.ppermute(block, 'col', [(c, c ^ bit) for c in range(lax.axis_size('co...]
    ppermute x18, waiting for transfers between devices: 76.9 us -> 54 us  [shift_row(): lax.ppermute(block, 'row', [(i, (i + by) % count) for i in range(count)])]
    pallas_call x3, Pallas kernels: 31.3 us -> 13.5 us  [assemble(): pl.pallas_call(assemble_kernel, grid_spec=pltpu.PrefetchScalarGridSpec(nu...]
    ppermute x18, starting transfers between devices: 24.1 us -> 39.2 us  [shift_row(): lax.ppermute(block, 'row', [(i, (i + by) % count) for i in range(count)])]
    pallas_call x6, Pallas kernels: 51.8 us -> 37.3 us  [block_grads(): pl.pallas_call(functools.partial(block_grads_kernel, [len(r) for r in rig...]
    ppermute x20, starting transfers between devices: 20.4 us -> 28.6 us  [flip_col(): lax.ppermute(block, 'col', [(c, c ^ bit) for c in range(lax.axis_size('co...]
    dot_general x4, matrix products: 23 us -> 15.7 us  [backward_part(): grad_active = jnp.dot(cotangent, downs[i], preferred_element_type=f32)]
  transfers between devices with their start and end apart: 52 -> 52, of which waited for: 22 -> 21; matrix products, arithmetic and copies ran while one was open for 26% -> 26% of each run, Pallas kernels for 20% -> 17%
where the time goes in v5:
time: 543 us; the launch traced here: 537 us
  waiting for transfers between devices  156 us (29%)
  Pallas kernels  117 us (22%)
  starting transfers between devices  84.9 us (16%)
  matrix products  70.3 us (13%)
  other arithmetic  68.2 us (13%)
  local copies, waits for them, and re-layouts  38.1 us (7%)
    ppermute x12, waiting for transfers between devices, flip_dp(): return lax.ppermute(block, 'dp', [(0, 1), (1, 0)])  59.9 us
    ppermute x18, waiting for transfers between devices, shift_row(): lax.ppermute(block, 'row', [(i, (i + by) % count) for i in range(count)])  54 us
    ppermute x20, waiting for transfers between devices, flip_col(): lax.ppermute(block, 'col', [(c, c ^ bit) for c in range(lax.axis_size('co...  41.7 us
    ppermute x18, starting transfers between devices, shift_row(): lax.ppermute(block, 'row', [(i, (i + by) % count) for i in range(count)])  39.2 us
    dot_general x16, matrix products, contract(): lax.dot_general(left, right, (((left_dim,), (right_dim,)), ((), ())), pre...  37.8 us
    pallas_call x6, Pallas kernels, block_grads(): pl.pallas_call(functools.partial(block_grads_kernel, [len(r) for r in rig...  37.3 us
    ppermute x20, starting transfers between devices, flip_col(): lax.ppermute(block, 'col', [(c, c ^ bit) for c in range(lax.axis_size('co...  28.6 us
    pallas_call x3, Pallas kernels, multiply_and_place(): pl.pallas_call(functools.partial(place_kernel, spans, piece, sources, bia...  22.2 us
  transfers between devices with their start and end apart: 52, of which 21 were waited for; matrix products, arithmetic and copies ran while one was open for 26% of the time, Pallas kernels for 17%

profile of v5, /device:TPU:0, one launch (start us, length us, event | category | flops | bytes accessed | tf_op | source)
XLA Modules:
  0.0 536.8 jit_solution(15549335348182627023)
XLA Ops:
  2.7 3.1 collective-permute-start
  9.8 6.4 %collective-permute-done = bf16[136,1152]{1,0:T(8,128)(2,1)S(1)} collective-permute-done((bf16[136,1152]{1,0:T(8,128)(2,1)S(1)}, bf16[136,1152]{1,0:T(8,128)(2,1)S(1)}, u32[]{:S(2)}, u32[]{:S(2)}) %collective-permute-start) | collective-permute-done | bytes 313376 | tf_op jit(solution)/shard_map/ppermute | solution.py:523
  16.2 12.6 %collective-permute-done.1 = bf16[136,1152]{1,0:T(8,128)(2,1)S(1)} collective-permute-done((bf16[136,1152]{1,0:T(8,128)(2,1)S(1)}, bf16[136,1152]{1,0:T(8,128)(2,1)S(1)}, u32[]{:S(2)}, u32[]{:S(2)}) %collective-permute-start.1) | collective-permute-done | bytes 313376 | tf_op jit(solution)/shard_map/ppermute | solution.py:523
  33.4 11.5 %collective-permute-done.3.refs_1_ = bf16[2,136,1152]{2,1,0:T(8,128)(2,1)S(1)} collective-permute-done((bf16[2,136,1152]{2,1,0:T(8,128)(2,1)S(1)}, bf16[2,136,1152]{2,1,0:T(8,128)(2,1)S(1)}, u32[]{:S(2)}, u32[]{:S(2)}) %collective-permute-start.3) | collective-permute-done | bytes 626720 | tf_op jit(solution)/shard_map/ppermute | solution.py:510
  49.8 7.3 %collective-permute-start.8 = (bf16[136,1088]{1,0:T(8,128)(2,1)S(1)}, bf16[136,1088]{1,0:T(8,128)(2,1)}, u32[]{:S(2)}, u32[]{:S(2)}) collective-permute-start(bf16[136,1088]{1,0:T(8,128)(2,1)S(1)} %convert_element_type.313), channel_id=1, source_target_pairs={{0,4},{4,8},{8,12},{12,0},{1,5},{5,9},{9,13},{13,1},{2,6},{6,10},{... | collective-permute-start | bytes 887816 | tf_op jit(solution)/shard_map/ppermute | solution.py:523
  59.5 14.4 %collective-permute-done.5 = bf16[2,2,136,1152]{3,2,1,0:T(8,128)(2,1)S(1)} collective-permute-done((bf16[2,2,136,1152]{3,2,1,0:T(8,128)(2,1)S(1)}, bf16[2,2,136,1152]{3,2,1,0:T(8,128)(2,1)S(1)}, u32[]{:S(2)}, u32[]{:S(2)}) %collective-permute-start.5) | collective-permute-done | bytes 1253408 | tf_op jit(solution)/shard_map/ppermute | solution.py:518
  75.4 4.4 assemble.3
  82.8 7.4 %collective-permute-start.14 = (bf16[136,1088]{1,0:T(8,128)(2,1)}, bf16[136,1088]{1,0:T(8,128)(2,1)}, u32[]{:S(2)}, u32[]{:S(2)}) collective-permute-start(bf16[136,1088]{1,0:T(8,128)(2,1)} %convert_bitcast_fusion.2), channel_id=1, source_target_pairs={{0,4},{4,8},{8,12},{12,0},{1,5},{5,9},{9,13},{13,1},{2,6},{6,10},{... | collective-permute-start | bytes 887816 | tf_op jit(solution)/shard_map/ppermute | solution.py:523
  94.6 5.1 fusion.172
  102.6 5.0 collective-permute-done.11.refs_1_
  107.6 2.6 collective-permute-start.16
  111.4 5.3 collective-permute-done.12.refs_3_
  118.8 7.2 %multiply_and_place.3.refs_2_ = bf16[512,3456]{1,0:T(8,128)(2,1)S(1)} custom-call(s32[2]{0:T(128)S(1)} %copy-done.37, bf16[512,1088]{1,0:T(8,128)(2,1)S(1)} %copy.66.x, bf16[2,1088,1152]{2,1,0:T(8,128)(2,1)} %bitcast.352, f32[1,3456]{1,0:T(1,128)S(1)} %reshape.256.refs_1_), custom_call_target="tpu_custom_call" | custom-call | tf_op jit(solution)/shard_map/multiply_and_place/pallas_call | solution.py:327
  126.1 2.6 pad_maximum_fusion.14.refs_0_
  141.2 8.5 %multiply_and_place.4.q.k_own.v_own = bf16[512,3456]{1,0:T(8,128)(2,1)S(1)} custom-call(s32[2]{0:T(128)S(1)} %copy-done.36, bf16[512,1088]{1,0:T(8,128)(2,1)S(1)} %copy-done.6, bf16[2,1088,1152]{2,1,0:T(8,128)(2,1)} %collective-permute-done.13.refs_0_.refs_1_, f32[1,3456]{1,0:T(1,128)S(1)} %copy-done.35, bf16[512,3456]{1,0:T(8,128)(2,1)} %copy-done.4), custom_call_target="tpu_custom_call" | custom-call | tf_op jit(solution)/shard_map/multiply_and_place/pallas_call | solution.py:327
  152.1 2.9 collective-permute-start.19
  162.5 4.3 slice_bitcast_fusion.7
  166.9 17.6 %attention_forward.1 = (bf16[512,1152]{1,0:T(8,128)(2,1)S(1)}, f32[9,2,512]{2,1,0:T(2,128)S(1)}) custom-call(s32[1]{0:T(128)} %bitcast.17.later, s32[1,512]{1,0:T(1,128)S(1)} %bitcast.348, s32[512,1]{1,0:T(8,128)S(1)} %copy-done.22, s32[512,1]{1,0:T(8,128)S(1)} %copy-done.24, bf16[512,3456]{1,0:T(8,128)(2,1)} %copy-done, bf16[512,3456]{1,0:T(8,128)(2,1)} %copy-done, ...), custom_call_target="tpu_custom_call" | custom-call | tf_op jit(solution)/shard_map/attention_forward/pallas_call | solution.py:232
  184.6 4.9 assemble.4
  189.5 3.2 collective-permute-start.22
  202.3 3.0 convolution_add_fusion.11
  205.3 3.0 convolution_add_fusion.10
  208.3 4.3 assemble.5
  213.8 5.4 %fusion.81 = (bf16[1088,512]{1,0:T(8,128)(2,1)S(1)}, f32[512,1088]{0,1:T(8,128)}) fusion(f32[1088]{0:T(1024)S(1)} %get-tuple-element.225, bf16[512,1088]{0,1:T(8,128)(2,1)S(1)} %add_convert_fusion.6, bf16[2,1088,1088]{2,1,0:T(8,128)(2,1)} %collective-permute-done.22), kind=kOutput, calls=%fused_computation.132 | convolution fusion | flops 1217724416 | bytes 6967552 | tf_op jit(solution)/shard_map/dot_general | solution.py:788
  219.2 5.3 fusion.78
  224.5 5.0 block_grads.6
  233.9 3.5 fusion.13
  240.7 3.6 fusion.4
  244.2 2.9 fusion.6
  247.1 7.0 %block_grads.7 = (bf16[2,272,1088]{2,1,0:T(8,128)(2,1)S(1)}, bf16[2,272,1088]{2,1,0:T(8,128)(2,1)S(1)}, bf16[2,272,1088]{2,1,0:T(8,128)(2,1)}, bf16[2,272,1088]{2,1,0:T(8,128)(2,1)}) custom-call(s32[1]{0:T(128)} %bitcast.place, bf16[1088,512]{1,0:T(8,128)(2,1)S(1)} %bitcast.336, bf16[1088,512]{1,0:T(8,128)(2,1)S(1)} %fusion.157.refs_1_, ...), custom_call_target="tpu_custom_call" | custom-call | tf_op jit(solution)/shard_map/block_grads/pallas_call | solution.py:478
  254.2 5.4 %fusion.50 = (bf16[1088,512]{1,0:T(8,128)(2,1)S(1)}, f32[1088,512]{1,0:T(8,128)S(1)}) fusion(f32[512,1088]{0,1:T(8,128)} %get-tuple-element.279, bf16[512,1088]{0,1:T(8,128)(2,1)S(1)} %copy-done.3, bf16[2,1088,1088]{2,1,0:T(8,128)(2,1)} %collective-permute-done.25), kind=kOutput, calls=%fused_computation.93 | convolution fusion | flops 1223294976 | bytes 9191424 | tf_op jit(solution)/shard_map/dot_general | solution.py:828
  259.6 4.7 fusion.57
  266.0 4.1 fusion.165
  270.1 5.3 block_grads.8
  275.5 3.6 fusion.86
  279.1 14.7 %collective-permute-done.27 = bf16[2,272,1088]{2,1,0:T(8,128)(2,1)S(1)} collective-permute-done((bf16[2,272,1088]{2,1,0:T(8,128)(2,1)S(1)}, bf16[2,272,1088]{2,1,0:T(8,128)(2,1)S(1)}, u32[]{:S(2)}, u32[]{:S(2)}) %collective-permute-start.27) | collective-permute-done | bytes 1183776 | tf_op jit(solution)/shard_map/ppermute | solution.py:518
  296.6 2.8 fusion.63
  299.5 2.8 fusion.69
  309.9 3.6 fusion.1
  313.5 2.9 multiply_reduce_fusion
  316.4 2.8 fusion.169
  322.2 6.5 %multiply_and_place.5.grad = bf16[512,1152]{1,0:T(8,128)(2,1)S(1)} custom-call(s32[4]{0:T(128)S(1)} %pad_add_fusion.1.places, bf16[512,1088]{1,0:T(8,128)(2,1)S(1)} %copy.69.x, bf16[2,1088,1152]{2,1,0:T(8,128)(2,1)} %bitcast.353, bf16[2,1088,1152]{2,1,0:T(8,128)(2,1)} %collective-permute-done.13.refs_0_.refs_1_), custom_call_target="tpu_custom_call" | custom-call | tf_op jit(solution)/shard_map/multiply_and_place/pallas_call | solution.py:327
  333.2 7.1 %block_grads.9 = (bf16[2,272,1088]{2,1,0:T(8,128)(2,1)S(1)}, bf16[2,272,1088]{2,1,0:T(8,128)(2,1)}, bf16[2,272,1088]{2,1,0:T(8,128)(2,1)}, bf16[2,272,1088]{2,1,0:T(8,128)(2,1)}) custom-call(s32[1]{0:T(128)} %bitcast.place, bf16[1088,512]{1,0:T(8,128)(2,1)S(1)} %fusion.193.refs_0_, bf16[1088,512]{1,0:T(8,128)(2,1)S(1)} %copy-done.13, ...), custom_call_target="tpu_custom_call" | custom-call | tf_op jit(solution)/shard_map/block_grads/pallas_call | solution.py:478
  341.3 19.7 %attention_backward.1 = (bf16[512,1152]{1,0:T(8,128)(2,1)S(1)}, bf16[512,1152]{1,0:T(8,128)(2,1)S(1)}, bf16[512,1152]{1,0:T(8,128)(2,1)S(1)}, bf16[512,1152]{1,0:T(8,128)(2,1)S(1)}, bf16[512,1152]{1,0:T(8,128)(2,1)}) custom-call(s32[1]{0:T(128)} %bitcast.17.later, s32[1,512]{1,0:T(1,128)S(1)} %bitcast.349, s32[512,1]{1,0:T(8,128)S(1)} %copy-done.23, ...), custom_call_target="tpu_custom_call" | custom-call | tf_op jit(solution)/shard_map/attention_backward/pallas_call | solution.py:255
  361.0 3.9 pad_maximum_fusion
  371.8 14.8 %collective-permute-done.33 = bf16[2,272,1088]{2,1,0:T(8,128)(2,1)S(1)} collective-permute-done((bf16[2,272,1088]{2,1,0:T(8,128)(2,1)}, bf16[2,272,1088]{2,1,0:T(8,128)(2,1)S(1)}, u32[]{:S(2)}, u32[]{:S(2)}) %collective-permute-start.33) | collective-permute-done | bytes 1183776 | tf_op jit(solution)/shard_map/ppermute | solution.py:510
  387.0 5.4 split_grads.1
  394.5 5.3 block_grads.10
  399.8 10.5 %collective-permute-start.36 = (bf16[2,1088,1152]{2,1,0:T(8,128)(2,1)}, bf16[2,1088,1152]{2,1,0:T(8,128)(2,1)}, u32[]{:S(2)}, u32[]{:S(2)}) collective-permute-start(bf16[2,1088,1152]{2,1,0:T(8,128)(2,1)} %block_grads.10), channel_id=1, source_target_pairs={{0,1},{1,0},{2,3},{3,2},{4,5},{5,4},{6,7},{7,6},{8,9},{9,8},{10,11... | collective-permute-start | bytes 15040520 | tf_op jit(solution)/shard_map/ppermute | solution.py:510
  416.7 9.7 %collective-permute-done.45 = bf16[272,1088]{1,0:T(8,128)(2,1)S(1)} collective-permute-done((bf16[272,1088]{1,0:T(8,128)(2,1)S(1)}, bf16[272,1088]{1,0:T(8,128)(2,1)S(1)}, u32[]{:S(2)}, u32[]{:S(2)}) %collective-permute-start.45) | collective-permute-done | bytes 591904 | tf_op jit(solution)/shard_map/ppermute | solution.py:518
  434.9 3.5 fusion.30
  440.4 3.4 collective-permute-start.48
  445.2 7.5 %block_grads.11 = (bf16[2,272,1152]{2,1,0:T(8,128)(2,1)S(1)}, bf16[2,272,1152]{2,1,0:T(8,128)(2,1)S(1)}, bf16[2,272,1152]{2,1,0:T(8,128)(2,1)}, bf16[2,272,1152]{2,1,0:T(8,128)(2,1)}) custom-call(s32[1]{0:T(128)} %bitcast.place, bf16[1088,512]{1,0:T(8,128)(2,1)S(1)} %bitcast.334, bf16[1088,512]{1,0:T(8,128)(2,1)S(1)} %convert_bitcast_fusion.4.refs_1_, ...), custom_call_target="tpu_custom_call" | custom-call | tf_op jit(solution)/shard_map/block_grads/pallas_call | solution.py:478
  454.2 3.0 multiply_subtract_fusion
  458.1 14.8 %collective-permute-done.47 = bf16[136,1088]{1,0:T(8,128)(2,1)S(1)} collective-permute-done((bf16[136,1088]{1,0:T(8,128)(2,1)S(1)}, bf16[136,1088]{1,0:T(8,128)(2,1)S(1)}, u32[]{:S(2)}, u32[]{:S(2)}) %collective-permute-start.47) | collective-permute-done | bytes 295968 | tf_op jit(solution)/shard_map/ppermute | solution.py:523
  472.9 2.7 multiply_subtract_fusion.1
  475.6 6.8 %collective-permute-done.39 = bf16[2,272,1152]{2,1,0:T(8,128)(2,1)S(1)} collective-permute-done((bf16[2,272,1152]{2,1,0:T(8,128)(2,1)}, bf16[2,272,1152]{2,1,0:T(8,128)(2,1)S(1)}, u32[]{:S(2)}, u32[]{:S(2)}) %collective-permute-start.39) | collective-permute-done | bytes 1253408 | tf_op jit(solution)/shard_map/ppermute | solution.py:510
  483.9 3.7 collective-permute-done.37
  488.5 11.2 %collective-permute-done.40 = bf16[272,1152]{1,0:T(8,128)(2,1)S(1)} collective-permute-done((bf16[272,1152]{1,0:T(8,128)(2,1)S(1)}, bf16[272,1152]{1,0:T(8,128)(2,1)S(1)}, u32[]{:S(2)}, u32[]{:S(2)}) %collective-permute-start.40) | collective-permute-done | bytes 626720 | tf_op jit(solution)/shard_map/ppermute | solution.py:518
  501.9 3.5 collective-permute-start.43
  506.1 3.7 fusion.29
  509.8 3.5 collective-permute-done.43
  513.3 16.7 %collective-permute-done.42 = bf16[136,1152]{1,0:T(8,128)(2,1)S(1)} collective-permute-done((bf16[136,1152]{1,0:T(8,128)(2,1)S(1)}, bf16[136,1152]{1,0:T(8,128)(2,1)S(1)}, u32[]{:S(2)}, u32[]{:S(2)}) %collective-permute-start.42) | collective-permute-done | bytes 313376 | tf_op jit(solution)/shard_map/ppermute | solution.py:523
  533.0 2.7 multiply_subtract_fusion.2
  (469 shorter events, 131.9 us)
Async XLA Ops:
  2.7 30.2 %copy-start.107 = (s32[2,1024]{1,0:T(2,128)S(1)}, s32[2,1024]{1,0:T(2,128)}, u32[]{:S(2)}) copy-start(s32[2,1024]{1,0:T(2,128)} %param.20) | copy-start | bytes 24580
  2.7 13.5 %collective-permute-start = (bf16[136,1152]{1,0:T(8,128)(2,1)S(1)}, bf16[136,1152]{1,0:T(8,128)(2,1)S(1)}, u32[]{:S(2)}, u32[]{:S(2)}) collective-permute-start(bf16[136,1152]{1,0:T(8,128)(2,1)S(1)} %concatenate.26), channel_id=1, source_target_pairs={{0,4},{4,8},{8,12},{12,0},{1,5},{5,9},{9,13},{13,1},{2,6},{6,10},{... | collective-permute-start | bytes 940040 | tf_op jit(solution)/shard_map/ppermute | solution.py:523
  5.8 23.0 %collective-permute-start.1 = (bf16[136,1152]{1,0:T(8,128)(2,1)S(1)}, bf16[136,1152]{1,0:T(8,128)(2,1)S(1)}, u32[]{:S(2)}, u32[]{:S(2)}) collective-permute-start(bf16[136,1152]{1,0:T(8,128)(2,1)S(1)} %concatenate.26), channel_id=1, source_target_pairs={{0,8},{4,12},{8,0},{12,4},{1,9},{5,13},{9,1},{13,5},{2,10},{6,14},... | collective-permute-start | bytes 940040 | tf_op jit(solution)/shard_map/ppermute | solution.py:523
  8.4 20.4 %collective-permute-start.2 = (bf16[136,1152]{1,0:T(8,128)(2,1)S(1)}, bf16[136,1152]{1,0:T(8,128)(2,1)S(1)}, u32[]{:S(2)}, u32[]{:S(2)}) collective-permute-start(bf16[136,1152]{1,0:T(8,128)(2,1)S(1)} %concatenate.26), channel_id=1, source_target_pairs={{0,12},{4,0},{8,4},{12,8},{1,13},{5,1},{9,5},{13,9},{2,14},{6,2},{... | collective-permute-start | bytes 940040 | tf_op jit(solution)/shard_map/ppermute | solution.py:523
  28.9 16.0 %collective-permute-start.3 = (bf16[2,136,1152]{2,1,0:T(8,128)(2,1)S(1)}, bf16[2,136,1152]{2,1,0:T(8,128)(2,1)S(1)}, u32[]{:S(2)}, u32[]{:S(2)}) collective-permute-start(bf16[2,136,1152]{2,1,0:T(8,128)(2,1)S(1)} %get-tuple-element.273.refs_0_), channel_id=1, source_target_pairs={{0,2},{1,3},{2,0},{3,1},{4,6},{5,7},{6,4},{7,5},{8,10},{9,11},{10,... | collective-permute-start | bytes 1880072 | tf_op jit(solution)/shard_map/ppermute | solution.py:510
  31.4 15.9 %collective-permute-start.4 = (bf16[2,136,1152]{2,1,0:T(8,128)(2,1)S(1)}, bf16[2,136,1152]{2,1,0:T(8,128)(2,1)S(1)}, u32[]{:S(2)}, u32[]{:S(2)}) collective-permute-start(bf16[2,136,1152]{2,1,0:T(8,128)(2,1)S(1)} %get-tuple-element.271.refs_2_), channel_id=1, source_target_pairs={{0,16},{16,0},{1,17},{17,1},{2,18},{18,2},{3,19},{19,3},{4,20},{20... | collective-permute-start | bytes 1880072 | tf_op jit(solution)/shard_map/ppermute | solution.py:518
  45.0 28.9 %collective-permute-start.5 = (bf16[2,2,136,1152]{3,2,1,0:T(8,128)(2,1)S(1)}, bf16[2,2,136,1152]{3,2,1,0:T(8,128)(2,1)S(1)}, u32[]{:S(2)}, u32[]{:S(2)}) collective-permute-start(bf16[2,2,136,1152]{3,2,1,0:T(8,128)(2,1)S(1)} %pad_maximum_fusion.1), channel_id=1, source_target_pairs={{0,16},{16,0},{1,17},{17,1},{2,18},{18,2},{3,19},{19,3},{4,20},{20... | collective-permute-start | bytes 3760136 | tf_op jit(solution)/shard_map/ppermute | solution.py:518
  47.4 28.1 %collective-permute-start.6 = (bf16[2,2,136,1152]{3,2,1,0:T(8,128)(2,1)S(1)}, bf16[2,2,136,1152]{3,2,1,0:T(8,128)(2,1)S(1)}, u32[]{:S(2)}, u32[]{:S(2)}) collective-permute-start(bf16[2,2,136,1152]{3,2,1,0:T(8,128)(2,1)S(1)} %pad_maximum_fusion.2), channel_id=1, source_target_pairs={{0,2},{1,3},{2,0},{3,1},{4,6},{5,7},{6,4},{7,5},{8,10},{9,11},{10,... | collective-permute-start | bytes 3760136 | tf_op jit(solution)/shard_map/ppermute | solution.py:510
  48.7 31.1 %copy-start.98 = (f32[512]{0:T(512)}, f32[512]{0:T(512)S(1)}, u32[]{:S(2)}) copy-start(f32[512]{0:T(512)S(1)} %broadcast_multiply_fusion.5) | copy-start | bytes 6148
  49.8 32.9 %collective-permute-start.8 = (bf16[136,1088]{1,0:T(8,128)(2,1)S(1)}, bf16[136,1088]{1,0:T(8,128)(2,1)}, u32[]{:S(2)}, u32[]{:S(2)}) collective-permute-start(bf16[136,1088]{1,0:T(8,128)(2,1)S(1)} %convert_element_type.313), channel_id=1, source_target_pairs={{0,4},{4,8},{8,12},{12,0},{1,5},{5,9},{9,13},{13,1},{2,6},{6,10},{... | collective-permute-start | bytes 887816 | tf_op jit(solution)/shard_map/ppermute | solution.py:523
  57.1 25.6 %collective-permute-start.9 = (bf16[136,1088]{1,0:T(8,128)(2,1)S(1)}, bf16[136,1088]{1,0:T(8,128)(2,1)S(1)}, u32[]{:S(2)}, u32[]{:S(2)}) collective-permute-start(bf16[136,1088]{1,0:T(8,128)(2,1)S(1)} %convert_element_type.313), channel_id=1, source_target_pairs={{0,8},{4,12},{8,0},{12,4},{1,9},{5,13},{9,1},{13,5},{2,10},{6,14},... | collective-permute-start | bytes 887816 | tf_op jit(solution)/shard_map/ppermute | solution.py:523
  57.9 24.8 %collective-permute-start.10 = (bf16[136,1088]{1,0:T(8,128)(2,1)S(1)}, bf16[136,1088]{1,0:T(8,128)(2,1)}, u32[]{:S(2)}, u32[]{:S(2)}) collective-permute-start(bf16[136,1088]{1,0:T(8,128)(2,1)S(1)} %convert_element_type.313), channel_id=1, source_target_pairs={{0,12},{4,0},{8,4},{12,8},{1,13},{5,1},{9,5},{13,9},{2,14},{6,2},{... | collective-permute-start | bytes 887816 | tf_op jit(solution)/shard_map/ppermute | solution.py:523
  79.8 58.7 %collective-permute-start.13 = (bf16[2,1088,1152]{2,1,0:T(8,128)(2,1)}, bf16[2,1088,1152]{2,1,0:T(8,128)(2,1)}, u32[]{:S(2)}, u32[]{:S(2)}) collective-permute-start(bf16[2,1088,1152]{2,1,0:T(8,128)(2,1)} %bitcast.350), channel_id=1, source_target_pairs={{0,1},{1,0},{2,3},{3,2},{4,5},{5,4},{6,7},{7,6},{8,9},{9,8},{10,11... | collective-permute-start | bytes 15040520 | tf_op jit(solution)/shard_map/ppermute | solution.py:510
  82.8 43.3 %collective-permute-start.14 = (bf16[136,1088]{1,0:T(8,128)(2,1)}, bf16[136,1088]{1,0:T(8,128)(2,1)}, u32[]{:S(2)}, u32[]{:S(2)}) collective-permute-start(bf16[136,1088]{1,0:T(8,128)(2,1)} %convert_bitcast_fusion.2), channel_id=1, source_target_pairs={{0,4},{4,8},{8,12},{12,0},{1,5},{5,9},{9,13},{13,1},{2,6},{6,10},{... | collective-permute-start | bytes 887816 | tf_op jit(solution)/shard_map/ppermute | solution.py:523
  90.2 35.9 %collective-permute-start.15 = (bf16[136,1088]{1,0:T(8,128)(2,1)}, bf16[136,1088]{1,0:T(8,128)(2,1)}, u32[]{:S(2)}, u32[]{:S(2)}) collective-permute-start(bf16[136,1088]{1,0:T(8,128)(2,1)} %convert_bitcast_fusion.2), channel_id=1, source_target_pairs={{0,8},{4,12},{8,0},{12,4},{1,9},{5,13},{9,1},{13,5},{2,10},{6,14},... | collective-permute-start | bytes 887816 | tf_op jit(solution)/shard_map/ppermute | solution.py:523
  91.3 41.8 %copy-start.7 = (bf16[2,136,1088]{2,1,0:T(8,128)(2,1)}, bf16[2,136,1088]{2,1,0:T(8,128)(2,1)S(1)}, u32[]{:S(2)}) copy-start(bf16[2,136,1088]{2,1,0:T(8,128)(2,1)S(1)} %pad_maximum_fusion.12.refs_0_) | copy-start | bytes 1775620
  91.3 16.3 %collective-permute-start.11 = (bf16[2,136,1088]{2,1,0:T(8,128)(2,1)S(1)}, bf16[2,136,1088]{2,1,0:T(8,128)(2,1)S(1)}, u32[]{:S(2)}, u32[]{:S(2)}) collective-permute-start(bf16[2,136,1088]{2,1,0:T(8,128)(2,1)S(1)} %pad_maximum_fusion.12.refs_0_), channel_id=1, source_target_pairs={{0,2},{1,3},{2,0},{3,1},{4,6},{5,7},{6,4},{7,5},{8,10},{9,11},{10,... | collective-permute-start | bytes 1775624 | tf_op jit(solution)/shard_map/ppermute | solution.py:510
  93.6 41.2 %copy-start.9 = (bf16[2,136,1088]{2,1,0:T(8,128)(2,1)}, bf16[2,136,1088]{2,1,0:T(8,128)(2,1)S(1)}, u32[]{:S(2)}) copy-start(bf16[2,136,1088]{2,1,0:T(8,128)(2,1)S(1)} %pad_maximum_fusion.13.refs_2_) | copy-start | bytes 1775620
  94.5 5.5 %collective-permute-start.7 = (bf16[2,8,7,64]{3,2,1,0:T(8,128)(2,1)S(1)}, bf16[2,8,7,64]{3,2,1,0:T(8,128)(2,1)S(1)}, u32[]{:S(2)}, u32[]{:S(2)}) collective-permute-start(bf16[2,8,7,64]{3,2,1,0:T(8,128)(2,1)S(1)} %slice.275), channel_id=1, source_target_pairs={{0,1},{1,0},{2,3},{3,2},{4,5},{5,4},{6,7},{7,6},{8,9},{9,8},{10,11... | collective-permute-start | bytes 43016 | tf_op jit(solution)/shard_map/ppermute | solution.py:510
  100.0 16.6 %collective-permute-start.12 = (bf16[2,136,1088]{2,1,0:T(8,128)(2,1)S(1)}, bf16[2,136,1088]{2,1,0:T(8,128)(2,1)}, u32[]{:S(2)}, u32[]{:S(2)}) collective-permute-start(bf16[2,136,1088]{2,1,0:T(8,128)(2,1)S(1)} %pad_maximum_fusion.13.refs_2_), channel_id=1, source_target_pairs={{0,16},{16,0},{1,17},{17,1},{2,18},{18,2},{3,19},{19,3},{4,20},{20... | collective-permute-start | bytes 1775624 | tf_op jit(solution)/shard_map/ppermute | solution.py:518
  107.6 18.5 %collective-permute-start.16 = (bf16[136,1088]{1,0:T(8,128)(2,1)}, bf16[136,1088]{1,0:T(8,128)(2,1)}, u32[]{:S(2)}, u32[]{:S(2)}) collective-permute-start(bf16[136,1088]{1,0:T(8,128)(2,1)} %convert_bitcast_fusion.2), channel_id=1, source_target_pairs={{0,12},{4,0},{8,4},{12,8},{1,13},{5,1},{9,5},{13,9},{2,14},{6,2},{... | collective-permute-start | bytes 887816 | tf_op jit(solution)/shard_map/ppermute | solution.py:523
  128.7 21.0 %collective-permute-start.17 = (bf16[2,136,1088]{2,1,0:T(8,128)(2,1)}, bf16[2,136,1088]{2,1,0:T(8,128)(2,1)}, u32[]{:S(2)}, u32[]{:S(2)}) collective-permute-start(bf16[2,136,1088]{2,1,0:T(8,128)(2,1)} %pad_maximum_fusion.14.refs_0_), channel_id=1, source_target_pairs={{0,2},{1,3},{2,0},{3,1},{4,6},{5,7},{6,4},{7,5},{8,10},{9,11},{10,... | collective-permute-start | bytes 1775624 | tf_op jit(solution)/shard_map/ppermute | solution.py:510
  131.6 18.1 %collective-permute-start.18 = (bf16[2,136,1088]{2,1,0:T(8,128)(2,1)}, bf16[2,136,1088]{2,1,0:T(8,128)(2,1)}, u32[]{:S(2)}, u32[]{:S(2)}) collective-permute-start(bf16[2,136,1088]{2,1,0:T(8,128)(2,1)} %pad_maximum_fusion.15.refs_2_), channel_id=1, source_target_pairs={{0,16},{16,0},{1,17},{17,1},{2,18},{18,2},{3,19},{19,3},{4,20},{20... | collective-permute-start | bytes 1775624 | tf_op jit(solution)/shard_map/ppermute | solution.py:518
  134.3 50.3 %collective-permute-start.20 = (bf16[2,2,136,1088]{3,2,1,0:T(8,128)(2,1)}, bf16[2,2,136,1088]{3,2,1,0:T(8,128)(2,1)}, u32[]{:S(2)}, u32[]{:S(2)}) collective-permute-start(bf16[2,2,136,1088]{3,2,1,0:T(8,128)(2,1)} %pad_maximum_fusion.3), channel_id=1, source_target_pairs={{0,16},{16,0},{1,17},{17,1},{2,18},{18,2},{3,19},{19,3},{4,20},{20... | collective-permute-start | bytes 3551240 | tf_op jit(solution)/shard_map/ppermute | solution.py:518
  137.1 47.5 %collective-permute-start.21 = (bf16[2,2,136,1088]{3,2,1,0:T(8,128)(2,1)}, bf16[2,2,136,1088]{3,2,1,0:T(8,128)(2,1)}, u32[]{:S(2)}, u32[]{:S(2)}) collective-permute-start(bf16[2,2,136,1088]{3,2,1,0:T(8,128)(2,1)} %pad_maximum_fusion.4), channel_id=1, source_target_pairs={{0,2},{1,3},{2,0},{3,1},{4,6},{5,7},{6,4},{7,5},{8,10},{9,11},{10,... | collective-permute-start | bytes 3551240 | tf_op jit(solution)/shard_map/ppermute | solution.py:510
  152.1 14.7 %collective-permute-start.19 = (bf16[512,2304]{1,0:T(8,128)(2,1)}, bf16[512,2304]{1,0:T(8,128)(2,1)}, u32[]{:S(2)}, u32[]{:S(2)}) collective-permute-start(bf16[512,2304]{1,0:T(8,128)(2,1)} %slice.219), channel_id=1, source_target_pairs={{0,1},{2,3},{4,5},{6,7},{8,9},{10,11},{12,13},{14,15},{16,17},{18,... | collective-permute-start | bytes 7077896 | tf_op jit(solution)/shard_map/ppermute | solution.py:755
  157.7 50.7 %collective-permute-start.23 = (bf16[2,2,136,1088]{3,2,1,0:T(8,128)(2,1)}, bf16[2,2,136,1088]{3,2,1,0:T(8,128)(2,1)S(1)}, u32[]{:S(2)}, u32[]{:S(2)}) collective-permute-start(bf16[2,2,136,1088]{3,2,1,0:T(8,128)(2,1)} %pad_maximum_fusion.5), channel_id=1, source_target_pairs={{0,16},{16,0},{1,17},{17,1},{2,18},{18,2},{3,19},{19,3},{4,20},{20... | collective-permute-start | bytes 3551240 | tf_op jit(solution)/shard_map/ppermute | solution.py:518
  161.0 47.3 %collective-permute-start.24 = (bf16[2,2,136,1088]{3,2,1,0:T(8,128)(2,1)}, bf16[2,2,136,1088]{3,2,1,0:T(8,128)(2,1)S(1)}, u32[]{:S(2)}, u32[]{:S(2)}) collective-permute-start(bf16[2,2,136,1088]{3,2,1,0:T(8,128)(2,1)} %pad_maximum_fusion.6), channel_id=1, source_target_pairs={{0,2},{1,3},{2,0},{3,1},{4,6},{5,7},{6,4},{7,5},{8,10},{9,11},{10,... | collective-permute-start | bytes 3551240 | tf_op jit(solution)/shard_map/ppermute | solution.py:510
  166.9 26.8 %copy-start.56 = (bf16[1088,1152]{1,0:T(8,128)(2,1)}, bf16[1088,1152]{1,0:T(8,128)(2,1)S(1)}, u32[]{:S(2)}) copy-start(bf16[1088,1152]{1,0:T(8,128)(2,1)S(1)} %get-tuple-element.254) | copy-start | bytes 7520260
  189.5 24.2 %collective-permute-start.22 = (bf16[2,1088,1088]{2,1,0:T(8,128)(2,1)}, bf16[2,1088,1088]{2,1,0:T(8,128)(2,1)}, u32[]{:S(2)}, u32[]{:S(2)}) collective-permute-start(bf16[2,1088,1088]{2,1,0:T(8,128)(2,1)} %bitcast.359), channel_id=1, source_target_pairs={{0,1},{1,0},{2,3},{3,2},{4,5},{5,4},{6,7},{7,6},{8,9},{9,8},{10,11... | collective-permute-start | bytes 14204936 | tf_op jit(solution)/shard_map/ppermute | solution.py:510
  200.5 29.5 %copy-start.91 = (f32[512]{0:T(512)}, f32[512]{0:T(512)S(1)}, u32[]{:S(2)}) copy-start(f32[512]{0:T(512)S(1)} %broadcast_multiply_fusion.4) | copy-start | bytes 6148
  201.0 29.1 %copy-start.95 = (f32[512]{0:T(512)}, f32[512]{0:T(512)S(1)}, u32[]{:S(2)}) copy-start(f32[512]{0:T(512)S(1)} %add_rsqrt_fusion) | copy-start | bytes 6148
  212.6 21.3 %collective-permute-start.25 = (bf16[2,1088,1088]{2,1,0:T(8,128)(2,1)}, bf16[2,1088,1088]{2,1,0:T(8,128)(2,1)}, u32[]{:S(2)}, u32[]{:S(2)}) collective-permute-start(bf16[2,1088,1088]{2,1,0:T(8,128)(2,1)} %bitcast.354), channel_id=1, source_target_pairs={{0,1},{1,0},{2,3},{3,2},{4,5},{5,4},{6,7},{7,6},{8,9},{9,8},{10,11... | collective-permute-start | bytes 14204936 | tf_op jit(solution)/shard_map/ppermute | solution.py:510
  229.5 17.6 %collective-permute-start.26 = (bf16[2,1088,1088]{2,1,0:T(8,128)(2,1)}, bf16[2,1088,1088]{2,1,0:T(8,128)(2,1)}, u32[]{:S(2)}, u32[]{:S(2)}) collective-permute-start(bf16[2,1088,1088]{2,1,0:T(8,128)(2,1)} %block_grads.6), channel_id=1, source_target_pairs={{0,1},{1,0},{2,3},{3,2},{4,5},{5,4},{6,7},{7,6},{8,9},{9,8},{10,11... | collective-permute-start | bytes 14204936 | tf_op jit(solution)/shard_map/ppermute | solution.py:510
  264.3 29.5 %collective-permute-start.27 = (bf16[2,272,1088]{2,1,0:T(8,128)(2,1)S(1)}, bf16[2,272,1088]{2,1,0:T(8,128)(2,1)S(1)}, u32[]{:S(2)}, u32[]{:S(2)}) collective-permute-start(bf16[2,272,1088]{2,1,0:T(8,128)(2,1)S(1)} %get-tuple-element.156), channel_id=1, source_target_pairs={{0,16},{16,0},{1,17},{17,1},{2,18},{18,2},{3,19},{19,3},{4,20},{20... | collective-permute-start | bytes 3551240 | tf_op jit(solution)/shard_map/ppermute | solution.py:518
  264.9 29.5 %collective-permute-start.28 = (bf16[2,272,1088]{2,1,0:T(8,128)(2,1)}, bf16[2,272,1088]{2,1,0:T(8,128)(2,1)}, u32[]{:S(2)}, u32[]{:S(2)}) collective-permute-start(bf16[2,272,1088]{2,1,0:T(8,128)(2,1)} %get-tuple-element.158), channel_id=1, source_target_pairs={{0,2},{1,3},{2,0},{3,1},{4,6},{5,7},{6,4},{7,5},{8,10},{9,11},{10,... | collective-permute-start | bytes 3551240 | tf_op jit(solution)/shard_map/ppermute | solution.py:510
  302.3 30.9 %collective-permute-start.29 = (bf16[2,1088,1088]{2,1,0:T(8,128)(2,1)}, bf16[2,1088,1088]{2,1,0:T(8,128)(2,1)}, u32[]{:S(2)}, u32[]{:S(2)}) collective-permute-start(bf16[2,1088,1088]{2,1,0:T(8,128)(2,1)} %block_grads.8), channel_id=1, source_target_pairs={{0,1},{1,0},{2,3},{3,2},{4,5},{5,4},{6,7},{7,6},{8,9},{9,8},{10,11... | collective-permute-start | bytes 14204936 | tf_op jit(solution)/shard_map/ppermute | solution.py:510
  303.3 25.5 %collective-permute-start.31 = (bf16[272,1088]{1,0:T(8,128)(2,1)}, bf16[272,1088]{1,0:T(8,128)(2,1)}, u32[]{:S(2)}, u32[]{:S(2)}) collective-permute-start(bf16[272,1088]{1,0:T(8,128)(2,1)} %dynamic-slice_bitcast_fusion.2), channel_id=1, source_target_pairs={{0,16},{16,0},{1,17},{17,1},{2,18},{18,2},{3,19},{19,3},{4,20},{20... | collective-permute-start | bytes 1775624 | tf_op jit(solution)/shard_map/ppermute | solution.py:518
  305.0 25.5 %collective-permute-start.30 = (bf16[272,1088]{1,0:T(8,128)(2,1)}, bf16[272,1088]{1,0:T(8,128)(2,1)}, u32[]{:S(2)}, u32[]{:S(2)}) collective-permute-start(bf16[272,1088]{1,0:T(8,128)(2,1)} %slice_bitcast_fusion.15), channel_id=1, source_target_pairs={{0,2},{1,3},{2,0},{3,1},{4,6},{5,7},{6,4},{7,5},{8,10},{9,11},{10,... | collective-permute-start | bytes 1775624 | tf_op jit(solution)/shard_map/ppermute | solution.py:510
  340.4 29.7 %collective-permute-start.32 = (bf16[2,272,1088]{2,1,0:T(8,128)(2,1)}, bf16[2,272,1088]{2,1,0:T(8,128)(2,1)}, u32[]{:S(2)}, u32[]{:S(2)}) collective-permute-start(bf16[2,272,1088]{2,1,0:T(8,128)(2,1)} %get-tuple-element.173), channel_id=1, source_target_pairs={{0,16},{16,0},{1,17},{17,1},{2,18},{18,2},{3,19},{19,3},{4,20},{20... | collective-permute-start | bytes 3551240 | tf_op jit(solution)/shard_map/ppermute | solution.py:518
  364.9 22.1 %collective-permute-start.34 = (bf16[512,2304]{1,0:T(8,128)(2,1)}, bf16[512,2304]{1,0:T(8,128)(2,1)}, u32[]{:S(2)}, u32[]{:S(2)}) collective-permute-start(bf16[512,2304]{1,0:T(8,128)(2,1)} %pad_maximum_fusion), channel_id=1, source_target_pairs={{1,0},{3,2},{5,4},{7,6},{9,8},{11,10},{13,12},{15,14},{17,16},{19,... | collective-permute-start | bytes 7077896 | tf_op jit(solution)/shard_map/ppermute | solution.py:868
  366.6 20.1 %collective-permute-start.33 = (bf16[2,272,1088]{2,1,0:T(8,128)(2,1)}, bf16[2,272,1088]{2,1,0:T(8,128)(2,1)S(1)}, u32[]{:S(2)}, u32[]{:S(2)}) collective-permute-start(bf16[2,272,1088]{2,1,0:T(8,128)(2,1)} %get-tuple-element.175), channel_id=1, source_target_pairs={{0,2},{1,3},{2,0},{3,1},{4,6},{5,7},{6,4},{7,5},{8,10},{9,11},{10,... | collective-permute-start | bytes 3551240 | tf_op jit(solution)/shard_map/ppermute | solution.py:510
  392.4 40.2 %copy-start.27 = (bf16[2,512,896]{2,1,0:T(8,128)(2,1)}, bf16[2,512,896]{2,1,0:T(8,128)(2,1)S(1)}, u32[]{:S(2)}) copy-start(bf16[2,512,896]{2,1,0:T(8,128)(2,1)S(1)} %get-tuple-element.181.refs_2_) | copy-start | bytes 5505028
  399.8 44.1 %collective-permute-start.36 = (bf16[2,1088,1152]{2,1,0:T(8,128)(2,1)}, bf16[2,1088,1152]{2,1,0:T(8,128)(2,1)}, u32[]{:S(2)}, u32[]{:S(2)}) collective-permute-start(bf16[2,1088,1152]{2,1,0:T(8,128)(2,1)} %block_grads.10), channel_id=1, source_target_pairs={{0,1},{1,0},{2,3},{3,2},{4,5},{5,4},{6,7},{7,6},{8,9},{9,8},{10,11... | collective-permute-start | bytes 15040520 | tf_op jit(solution)/shard_map/ppermute | solution.py:510
  410.3 16.1 %collective-permute-start.45 = (bf16[272,1088]{1,0:T(8,128)(2,1)S(1)}, bf16[272,1088]{1,0:T(8,128)(2,1)S(1)}, u32[]{:S(2)}, u32[]{:S(2)}) collective-permute-start(bf16[272,1088]{1,0:T(8,128)(2,1)S(1)} %dynamic-slice_bitcast_fusion), channel_id=1, source_target_pairs={{0,16},{16,0},{1,17},{17,1},{2,18},{18,2},{3,19},{19,3},{4,20},{20... | collective-permute-start | bytes 1775624 | tf_op jit(solution)/shard_map/ppermute | solution.py:518
  411.6 15.8 %collective-permute-start.44 = (bf16[272,1088]{1,0:T(8,128)(2,1)S(1)}, bf16[272,1088]{1,0:T(8,128)(2,1)S(1)}, u32[]{:S(2)}, u32[]{:S(2)}) collective-permute-start(bf16[272,1088]{1,0:T(8,128)(2,1)S(1)} %slice_bitcast_fusion.14), channel_id=1, source_target_pairs={{0,2},{1,3},{2,0},{3,1},{4,6},{5,7},{6,4},{7,5},{8,10},{9,11},{10,... | collective-permute-start | bytes 1775624 | tf_op jit(solution)/shard_map/ppermute | solution.py:510
  413.7 38.9 %collective-permute-start.51 = (bf16[136,1088]{1,0:T(8,128)(2,1)}, bf16[136,1088]{1,0:T(8,128)(2,1)}, u32[]{:S(2)}, u32[]{:S(2)}) collective-permute-start(bf16[136,1088]{1,0:T(8,128)(2,1)} %get-tuple-element.262), channel_id=1, source_target_pairs={{0,12},{4,0},{8,4},{12,8},{1,13},{5,1},{9,5},{13,9},{2,14},{6,2},{... | collective-permute-start | bytes 887816 | tf_op jit(solution)/shard_map/ppermute | solution.py:523
  416.2 36.5 %collective-permute-start.50 = (bf16[136,1088]{1,0:T(8,128)(2,1)}, bf16[136,1088]{1,0:T(8,128)(2,1)}, u32[]{:S(2)}, u32[]{:S(2)}) collective-permute-start(bf16[136,1088]{1,0:T(8,128)(2,1)} %get-tuple-element.263), channel_id=1, source_target_pairs={{0,8},{4,12},{8,0},{12,4},{1,9},{5,13},{9,1},{13,5},{2,10},{6,14},... | collective-permute-start | bytes 887816 | tf_op jit(solution)/shard_map/ppermute | solution.py:523
  426.4 27.8 %collective-permute-start.49 = (bf16[136,1088]{1,0:T(8,128)(2,1)S(1)}, bf16[136,1088]{1,0:T(8,128)(2,1)}, u32[]{:S(2)}, u32[]{:S(2)}) collective-permute-start(bf16[136,1088]{1,0:T(8,128)(2,1)S(1)} %get-tuple-element.261), channel_id=1, source_target_pairs={{0,4},{4,8},{8,12},{12,0},{1,5},{5,9},{9,13},{13,1},{2,6},{6,10},{... | collective-permute-start | bytes 887816 | tf_op jit(solution)/shard_map/ppermute | solution.py:523
  439.1 1.3 collective-permute-start.35
  440.4 17.7 %collective-permute-start.48 = (bf16[136,1088]{1,0:T(8,128)(2,1)S(1)}, bf16[136,1088]{1,0:T(8,128)(2,1)S(1)}, u32[]{:S(2)}, u32[]{:S(2)}) collective-permute-start(bf16[136,1088]{1,0:T(8,128)(2,1)S(1)} %get-tuple-element.265), channel_id=1, source_target_pairs={{0,12},{4,0},{8,4},{12,8},{1,13},{5,1},{9,5},{13,9},{2,14},{6,2},{... | collective-permute-start | bytes 887816 | tf_op jit(solution)/shard_map/ppermute | solution.py:523
  443.9 29.0 %collective-permute-start.47 = (bf16[136,1088]{1,0:T(8,128)(2,1)S(1)}, bf16[136,1088]{1,0:T(8,128)(2,1)S(1)}, u32[]{:S(2)}, u32[]{:S(2)}) collective-permute-start(bf16[136,1088]{1,0:T(8,128)(2,1)S(1)} %get-tuple-element.266), channel_id=1, source_target_pairs={{0,8},{4,12},{8,0},{12,4},{1,9},{5,13},{9,1},{13,5},{2,10},{6,14},... | collective-permute-start | bytes 887816 | tf_op jit(solution)/shard_map/ppermute | solution.py:523
  452.7 20.2 %collective-permute-start.46 = (bf16[136,1088]{1,0:T(8,128)(2,1)S(1)}, bf16[136,1088]{1,0:T(8,128)(2,1)S(1)}, u32[]{:S(2)}, u32[]{:S(2)}) collective-permute-start(bf16[136,1088]{1,0:T(8,128)(2,1)S(1)} %get-tuple-element.264), channel_id=1, source_target_pairs={{0,4},{4,8},{8,12},{12,0},{1,5},{5,9},{9,13},{13,1},{2,6},{6,10},{... | collective-permute-start | bytes 887816 | tf_op jit(solution)/shard_map/ppermute | solution.py:523
  452.7 20.2 %copy-start.63 = (f32[136,1088]{1,0:T(8,128)S(1)}, f32[136,1088]{1,0:T(8,128)}, u32[]{:S(2)}) copy-start(f32[136,1088]{1,0:T(8,128)} %param.23) | copy-start | bytes 1775620
  452.7 20.2 %copy-start.82 = (f32[136,1088]{1,0:T(8,128)S(1)}, f32[136,1088]{1,0:T(8,128)}, u32[]{:S(2)}) copy-start(f32[136,1088]{1,0:T(8,128)} %param.33) | copy-start | bytes 1775620
  452.7 29.7 %collective-permute-start.39 = (bf16[2,272,1152]{2,1,0:T(8,128)(2,1)}, bf16[2,272,1152]{2,1,0:T(8,128)(2,1)S(1)}, u32[]{:S(2)}, u32[]{:S(2)}) collective-permute-start(bf16[2,272,1152]{2,1,0:T(8,128)(2,1)} %get-tuple-element.187), channel_id=1, source_target_pairs={{0,2},{1,3},{2,0},{3,1},{4,6},{5,7},{6,4},{7,5},{8,10},{9,11},{10,... | collective-permute-start | bytes 3760136 | tf_op jit(solution)/shard_map/ppermute | solution.py:510
  457.2 25.2 %copy-start.75 = (bf16[2,272,1152]{2,1,0:T(8,128)(2,1)S(1)}, bf16[2,272,1152]{2,1,0:T(8,128)(2,1)}, u32[]{:S(2)}) copy-start(bf16[2,272,1152]{2,1,0:T(8,128)(2,1)} %get-tuple-element.186) | copy-start | bytes 3760132
  457.2 30.5 %collective-permute-start.37 = (bf16[2,272,1152]{2,1,0:T(8,128)(2,1)S(1)}, bf16[2,272,1152]{2,1,0:T(8,128)(2,1)S(1)}, u32[]{:S(2)}, u32[]{:S(2)}) collective-permute-start(bf16[2,272,1152]{2,1,0:T(8,128)(2,1)S(1)} %get-tuple-element.185), channel_id=1, source_target_pairs={{0,16},{16,0},{1,17},{17,1},{2,18},{18,2},{3,19},{19,3},{4,20},{20... | collective-permute-start | bytes 3760136 | tf_op jit(solution)/shard_map/ppermute | solution.py:518
  482.8 16.9 %collective-permute-start.40 = (bf16[272,1152]{1,0:T(8,128)(2,1)S(1)}, bf16[272,1152]{1,0:T(8,128)(2,1)S(1)}, u32[]{:S(2)}, u32[]{:S(2)}) collective-permute-start(bf16[272,1152]{1,0:T(8,128)(2,1)S(1)} %dynamic-slice_bitcast_fusion.1), channel_id=1, source_target_pairs={{0,16},{16,0},{1,17},{17,1},{2,18},{18,2},{3,19},{19,3},{4,20},{20... | collective-permute-start | bytes 1880072 | tf_op jit(solution)/shard_map/ppermute | solution.py:518
  488.0 13.5 %collective-permute-start.38 = (bf16[272,1152]{1,0:T(8,128)(2,1)S(1)}, bf16[272,1152]{1,0:T(8,128)(2,1)S(1)}, u32[]{:S(2)}, u32[]{:S(2)}) collective-permute-start(bf16[272,1152]{1,0:T(8,128)(2,1)S(1)} %slice_bitcast_fusion.12), channel_id=1, source_target_pairs={{0,2},{1,3},{2,0},{3,1},{4,6},{5,7},{6,4},{7,5},{8,10},{9,11},{10,... | collective-permute-start | bytes 1880072 | tf_op jit(solution)/shard_map/ppermute | solution.py:510
  501.9 11.4 %collective-permute-start.43 = (bf16[136,1152]{1,0:T(8,128)(2,1)S(1)}, bf16[136,1152]{1,0:T(8,128)(2,1)S(1)}, u32[]{:S(2)}, u32[]{:S(2)}) collective-permute-start(bf16[136,1152]{1,0:T(8,128)(2,1)S(1)} %get-tuple-element.268), channel_id=1, source_target_pairs={{0,12},{4,0},{8,4},{12,8},{1,13},{5,1},{9,5},{13,9},{2,14},{6,2},{... | collective-permute-start | bytes 940040 | tf_op jit(solution)/shard_map/ppermute | solution.py:523
  505.4 24.6 %collective-permute-start.42 = (bf16[136,1152]{1,0:T(8,128)(2,1)S(1)}, bf16[136,1152]{1,0:T(8,128)(2,1)S(1)}, u32[]{:S(2)}, u32[]{:S(2)}) collective-permute-start(bf16[136,1152]{1,0:T(8,128)(2,1)S(1)} %get-tuple-element.269), channel_id=1, source_target_pairs={{0,8},{4,12},{8,0},{12,4},{1,9},{5,13},{9,1},{13,5},{2,10},{6,14},... | collective-permute-start | bytes 940040 | tf_op jit(solution)/shard_map/ppermute | solution.py:523
  505.4 24.6 %collective-permute-start.41 = (bf16[136,1152]{1,0:T(8,128)(2,1)S(1)}, bf16[136,1152]{1,0:T(8,128)(2,1)S(1)}, u32[]{:S(2)}, u32[]{:S(2)}) collective-permute-start(bf16[136,1152]{1,0:T(8,128)(2,1)S(1)} %get-tuple-element.267), channel_id=1, source_target_pairs={{0,4},{4,8},{8,12},{12,0},{1,5},{5,9},{9,13},{13,1},{2,6},{6,10},{... | collective-permute-start | bytes 940040 | tf_op jit(solution)/shard_map/ppermute | solution.py:523
  509.8 21.1 %copy-start.79 = (f32[272,136]{0,1:T(8,128)S(1)}, f32[272,136]{0,1:T(8,128)}, u32[]{:S(2)}) copy-start(f32[272,136]{0,1:T(8,128)} %param.22) | copy-start | bytes 443908
  (103 other events, 604.9 us)

commit v6 on v5

--- a/solution.py
+++ b/solution.py
@@ -412,10 +412,10 @@
     width = lefts[0].shape[0]
     quarter = width // 4
 
-    def value(start, which):
+    def value(start):
         rows = pl.ds(start, quarter)
-        if counts[0] > 1:
-            whole = contract_last(lefts[0][rows], rights[0][which][...])
+        if len(counts) == 1:
+            whole = jnp.dot(lefts[0][rows], rights[0][0][0], preferred_element_type=f32)
         else:
             one, two = [
                 jnp.dot(left[rows], right[0][0], preferred_element_type=f32)
@@ -438,15 +438,15 @@
         def _(i=i):
             if not split:
                 for k in range(4):
-                    refs[0][0, k * quarter : (k + 1) * quarter] = value(k * quarter, i)
+                    refs[0][0, k * quarter : (k + 1) * quarter] = value(k * quarter)
                 return
             first_keep, first_send, second_keep, second_send = refs
             half = width // 2
-            first_keep[0] = value(pl.multiple_of(place[0] * half, 16), i)
-            first_send[0] = value(pl.multiple_of((1 - place[0]) * half, 16), i)
+            first_keep[0] = value(pl.multiple_of(place[0] * half, 16))
+            first_send[0] = value(pl.multiple_of((1 - place[0]) * half, 16))
             second = (second_keep, second_send)[i]
             for dp in range(2):
-                second[dp] = value(dp * half + quarter, i)
+                second[dp] = value(dp * half + quarter)
 
 
 def block_grads(pairs, vec_part, received, split):
@@ -493,6 +493,79 @@
         compiler_params=pltpu.CompilerParams(vmem_limit_bytes=48 << 20),
         name="block_grads",
     )(place, *lefts, *flat, *more)
+
+
+def gelu_parts(values):
+    scale = (2.0 / jnp.pi) ** 0.5
+    square = values * values
+    return jnp.tanh(scale * values * (1.0 + 0.044715 * square)), scale * (
+        1.0 + (3.0 * 0.044715) * square
+    )
+
+
+def feed_forward_kernel(continued, x, up, bias, down, *refs):
+    before, refs = (refs[0], refs[1:]) if continued else (None, refs)
+    linear, active, branch = refs
+    count = x.shape[0]
+
+    @pl.when(pl.program_id(0) == 0)
+    def _():
+        branch[...] = before[...] if continued else jnp.zeros_like(branch)
+
+    for k in range(2):
+        rows = slice(k * count // 2, (k + 1) * count // 2)
+        values = jnp.dot(x[rows], up[0], preferred_element_type=f32) + bias[0]
+        linear[0, rows] = values
+        low = (0.5 * values * (1.0 + gelu_parts(values)[0])).astype(bf16)
+        active[0, rows] = low
+        branch[rows] += contract_last(low, down[0])
+
+
+def feed_backward_kernel(continued, grad, up, down, linear, *refs):
+    before, refs = (refs[0], refs[1:]) if continued else (None, refs)
+    lows, sums, grad_in = refs
+    count = grad.shape[0]
+
+    @pl.when(pl.program_id(0) == 0)
+    def _():
+        grad_in[...] = before[...] if continued else jnp.zeros_like(grad_in)
+
+    sums[...] = jnp.zeros_like(sums)
+    for k in range(2):
+        rows = slice(k * count // 2, (k + 1) * count // 2)
+        values = linear[0, rows]
+        tanh, slope = gelu_parts(values)
+        derivative = 0.5 * (1.0 + tanh) + 0.5 * values * (1.0 - tanh * tanh) * slope
+        grads = jnp.dot(grad[rows], down[0], preferred_element_type=f32) * derivative
+        sums[0] += jnp.sum(grads, 0, keepdims=True)
+        low = grads.astype(bf16)
+        lows[0, rows] = low
+        grad_in[rows] += contract_last(low, up[0])
+
+
+def feed_call(kernel, fixed, stepped, before, out_stepped, out_fixed, name):
+    each = stepped[0].shape[0]
+
+    def whole(x):
+        return pl.BlockSpec(x.shape, lambda i: (0,) * len(x.shape))
+
+    def step(x):
+        return pl.BlockSpec((1, *x.shape[1:]), lambda i: (i, 0, 0))
+
+    operands = [fixed, *stepped]
+    in_specs = [whole(fixed)] + [step(x) for x in stepped]
+    if before is not None:
+        operands.append(before)
+        in_specs.append(whole(before))
+    return pl.pallas_call(
+        functools.partial(kernel, before is not None),
+        grid=(each,),
+        in_specs=in_specs,
+        out_specs=[step(x) for x in out_stepped] + [whole(out_fixed)],
+        out_shape=[*out_stepped, out_fixed],
+        compiler_params=pltpu.CompilerParams(vmem_limit_bytes=56 << 20),
+        name=name,
+    )(*operands)
 
 
 AXES = ("col", "dp", "row")
@@ -783,71 +856,63 @@
     bias_up = by_place(vec[8:])
     bias_own, bias_oth = bias_up[0::2], bias_up[1::2]
 
-    def up_part(ups, biases):
-        return [
-            jnp.dot(normed_two_low, ups[i], preferred_element_type=f32) + biases[i]
-            for i in range(each)
-        ]
-
-    linear_own = up_part(up_own, bias_own)
     if staged:
-        linear_own, down_two = together(linear_own, down_two)
+        normed_two_low, down_two = together(normed_two_low, down_two)
         down_own = assemble(down_two)
     down_oth = partner(down_own)
-    linear_oth = up_part(up_oth, bias_oth)
-
-    branch = jnp.zeros((here, width), f32)
-
-    def forward_part(linears, downs, branch):
-        lows, pullbacks = [], []
-        for i in range(each):
-            active, pullback = jax.vjp(gelu_tanh, linears[i])
-            lows.append(active.astype(bf16))
-            pullbacks.append(pullback)
-            branch = branch + contract_last(lows[i], downs[i])
-        return lows, pullbacks, branch
+    unit = up_own.shape[2]
+    wide_shape = jax.ShapeDtypeStruct((each, here, unit), f32)
+    low_shape = jax.ShapeDtypeStruct((each, here, unit), bf16)
+    sums_shape = jax.ShapeDtypeStruct((each, 1, unit), f32)
+    sum_shape = jax.ShapeDtypeStruct((here, width), f32)
+
+    def forward_part(ups, biases, downs, before):
+        return feed_call(
+            feed_forward_kernel,
+            normed_two_low,
+            [ups, biases.reshape(each, 1, unit), downs],
+            before,
+            [wide_shape, low_shape],
+            sum_shape,
+            "feed_forward",
+        )
+
+    def backward_part(ups, downs, linears, before):
+        return feed_call(
+            feed_backward_kernel,
+            cotangent,
+            [ups, downs, linears],
+            before,
+            [low_shape, sums_shape],
+            sum_shape,
+            "feed_backward",
+        )
 
     left_down, left_up = cotangent.T, normed_two_low.T
-
-    def turned(rights):
-        return [r.T for r in rights]
-
-    lows_oth, pull_oth, branch = forward_part(linear_oth, down_oth, branch)
-    sent_down = block_grads([(left_down, turned(lows_oth))], None, None, False)
-    linear_own, sent_down = together(linear_own, sent_down)
+    linear_own, lows_own, branch = forward_part(up_own, bias_own, down_own, None)
+    linear_oth, lows_oth, branch = forward_part(up_oth, bias_oth, down_oth, branch)
+    layer_out = (residual + branch + vec[7]).astype(bf16)
+    sent_down = block_grads([(left_down, lows_oth)], None, None, False)
+    linear_oth, sent_down = together(linear_oth, sent_down)
     received_down = partner(sent_down)
-    lows_own, pull_own, branch = forward_part(linear_own, down_own, branch)
-    total_down = block_grads([(left_down, turned(lows_own))], None, received_down, staged)
-    layer_out = (residual + branch + vec[7]).astype(bf16)
-    down_oth, total_down = together(down_oth, total_down)
-    grad_normed_two = jnp.zeros((here, width), f32)
-
-    def backward_part(ups, downs, pullbacks, grad_normed_two):
-        lows, sums = [], []
-        for i in range(each):
-            grad_active = jnp.dot(cotangent, downs[i], preferred_element_type=f32)
-            grad_linear = pullbacks[i](grad_active)[0]
-            lows.append(grad_linear.astype(bf16))
-            sums.append(jnp.sum(grad_linear, 0))
-            grad_normed_two = grad_normed_two + contract_last(lows[i], ups[i])
-        return lows, sums, grad_normed_two
-
-    dups_oth, dbias_oth, grad_normed_two = backward_part(
-        up_oth, down_oth, pull_oth, grad_normed_two
+    dups_oth, dbias_oth, grad_normed_two = backward_part(up_oth, down_oth, linear_oth, None)
+    sent_up = block_grads([(left_up, dups_oth)], None, None, False)
+    lows_own, sent_up = together(lows_own, sent_up)
+    received_up = partner(sent_up)
+    total_down = block_grads([(left_down, lows_own)], None, received_down, staged)
+    linear_own, total_down = together(linear_own, total_down)
+    dups_own, dbias_own, grad_normed_two = backward_part(
+        up_own, down_own, linear_own, grad_normed_two
     )
     one_down = scatter_one(total_down)
-    sent_up = block_grads([(left_up, turned(dups_oth))], None, None, False)
-    down_own, one_down, sent_up = together(down_own, one_down, sent_up)
-    received_up = partner(sent_up)
-    two_down = scatter_two(one_down)
-    dups_own, dbias_own, grad_normed_two = backward_part(
-        up_own, down_own, pull_own, grad_normed_two
-    )
 
     grad_residual = cotangent.astype(f32) + norm_back(
         grad_normed_two, scaled_two, inverse_two, vec[5]
     )
+    total_up = block_grads([(left_up, dups_own)], None, received_up, staged)
     grad_residual_low = grad_residual.astype(bf16)
+    grad_residual_low, total_up, one_down = together(grad_residual_low, total_up, one_down)
+    two_down = scatter_two(one_down)
     grad_mixed = multiply_and_place(
         jnp.concatenate([places_own, places_oth]),
         grad_residual_low,
@@ -860,14 +925,14 @@
         None,
         None,
     )
-    total_up = block_grads([(left_up, turned(dups_own))], None, received_up, staged)
-    grad_mixed, total_up, two_down = together(grad_mixed, total_up, two_down)
     dq, dk_own, dv_own, dk_oth, dv_oth = attend_back(
         later, labels, projected, others, grad_mixed, mixed, log_totals
     )
+    one_up = scatter_one(total_up)
+    dq, dk_own, dv_own, dk_oth, dv_oth, one_up, two_down = together(
+        dq, dk_own, dv_own, dk_oth, dv_oth, one_up, two_down
+    )
     back = lax.ppermute(jnp.concatenate([dk_oth, dv_oth], 1), "col", behind)
-    one_up = scatter_one(total_up)
-    dq, dk_own, dv_own, one_up = together(dq, dk_own, dv_own, one_up)
     grads_shape = jax.ShapeDtypeStruct((each, here, lanes_qkv), bf16)
     grads_own, grads_oth, grad_sums = split_call(
         functools.partial(split_grads_kernel, piece, cols),
@@ -887,7 +952,7 @@
             grad_normed_one = grad_normed_one + contract_last(blocks[i], weights[i][:, :lanes_qkv])
     input_grad = grad_residual + norm_back(grad_normed_one, scaled_one, inverse_one, vec[0])
 
-    dbias = jnp.stack([jnp.stack(dbias_own), jnp.stack(dbias_oth)], 1).reshape(cols, width)
+    dbias = jnp.stack([dbias_own, dbias_oth], 1).reshape(cols, width)
     grad_vector = jnp.concatenate(
         [
             jnp.stack(

time: 543 us -> 589 us (1.085)
  waiting for transfers between devices: 156 us -> 217 us
  matrix products: 70.3 us -> 15.8 us
  Pallas kernels: 117 us -> 169 us
  starting transfers between devices: 84.9 us -> 63.2 us
  local copies, waits for them, and re-layouts: 38.1 us -> 58.4 us
  other arithmetic: 68.2 us -> 57.1 us
    pallas_call x0 -> x4, Pallas kernels: none -> 54.9 us  [feed_call(): pl.pallas_call(functools.partial(kernel, before is not None), grid=(each,...]
    ppermute x18, waiting for transfers between devices: 54 us -> 88.1 us  [shift_row(): lax.ppermute(block, 'row', [(i, (i + by) % count) for i in range(count)])]
    ppermute x20, waiting for transfers between devices: 41.7 us -> 74.5 us  [flip_col(): lax.ppermute(block, 'col', [(c, c ^ bit) for c in range(lax.axis_size('co...]
    dot_general x8 -> x0, matrix products: 32.5 us -> none  [the longest x4 16.7 us: up_part(): jnp.dot(normed_two_low, ups[i], preferred_element_type=f32) + biases[i]]
    dot_general x16 -> x8, matrix products: 37.8 us -> 15.8 us  [contract(): lax.dot_general(left, right, (((left_dim,), (right_dim,)), ((), ())), pre...]
    ppermute x20, starting transfers between devices: 28.6 us -> 15.8 us  [flip_col(): lax.ppermute(block, 'col', [(c, c ^ bit) for c in range(lax.axis_size('co...]
    ppermute x12, waiting for transfers between devices: 59.9 us -> 47.8 us  [flip_dp(): return lax.ppermute(block, 'dp', [(0, 1), (1, 0)])]
    unnamed x229 -> x220, local copies, waits for them, and re-layouts: 12.5 us -> 24.1 us
  transfers between devices with their start and end apart: 52 -> 52, of which waited for: 21 -> 26; matrix products, arithmetic and copies ran while one was open for 26% -> 16% of each run, Pallas kernels for 17% -> 23%
where the time goes in v6:
time: 589 us; the launch traced here: 583 us
  waiting for transfers between devices  217 us (37%)
  Pallas kernels  169 us (29%)
  starting transfers between devices  63.2 us (11%)
  local copies, waits for them, and re-layouts  58.4 us (10%)
  other arithmetic  57.1 us (10%)
  matrix products  15.8 us (3%)
    ppermute x18, waiting for transfers between devices, shift_row(): lax.ppermute(block, 'row', [(i, (i + by) % count) for i in range(count)])  88.1 us
    ppermute x20, waiting for transfers between devices, flip_col(): lax.ppermute(block, 'col', [(c, c ^ bit) for c in range(lax.axis_size('co...  74.5 us
    pallas_call x4, Pallas kernels, feed_call(): pl.pallas_call(functools.partial(kernel, before is not None), grid=(each,...  54.9 us
    ppermute x12, waiting for transfers between devices, flip_dp(): return lax.ppermute(block, 'dp', [(0, 1), (1, 0)])  47.8 us
    pallas_call x6, Pallas kernels, block_grads(): pl.pallas_call(functools.partial(block_grads_kernel, [len(r) for r in rig...  34.3 us
    ppermute x18, starting transfers between devices, shift_row(): lax.ppermute(block, 'row', [(i, (i + by) % count) for i in range(count)])  28.9 us
    unnamed x220, local copies, waits for them, and re-layouts  24.1 us
    pallas_call x3, Pallas kernels, multiply_and_place(): pl.pallas_call(functools.partial(place_kernel, spans, piece, sources, bia...  22.4 us
  transfers between devices with their start and end apart: 52, of which 26 were waited for; matrix products, arithmetic and copies ran while one was open for 16% of the time, Pallas kernels for 23%

profile of v6, /device:TPU:0, one launch (start us, length us, event | category | flops | bytes accessed | tf_op | source)
XLA Modules:
  0.0 583.1 jit_solution(3830422898273159328)
XLA Ops:
  4.3 5.1 collective-permute-start.2
  10.4 6.8 %collective-permute-done.2 = bf16[136,1152]{1,0:T(8,128)(2,1)S(1)} collective-permute-done((bf16[136,1152]{1,0:T(8,128)(2,1)S(1)}, bf16[136,1152]{1,0:T(8,128)(2,1)S(1)}, u32[]{:S(2)}, u32[]{:S(2)}) %collective-permute-start.2) | collective-permute-done | bytes 313376 | tf_op jit(solution)/shard_map/ppermute | solution.py:596
  17.2 18.8 %collective-permute-done.1 = bf16[136,1152]{1,0:T(8,128)(2,1)S(1)} collective-permute-done((bf16[136,1152]{1,0:T(8,128)(2,1)S(1)}, bf16[136,1152]{1,0:T(8,128)(2,1)S(1)}, u32[]{:S(2)}, u32[]{:S(2)}) %collective-permute-start.1) | collective-permute-done | bytes 313376 | tf_op jit(solution)/shard_map/ppermute | solution.py:596
  39.4 11.8 %collective-permute-done.4.refs_3_ = bf16[2,136,1152]{2,1,0:T(8,128)(2,1)S(1)} collective-permute-done((bf16[2,136,1152]{2,1,0:T(8,128)(2,1)S(1)}, bf16[2,136,1152]{2,1,0:T(8,128)(2,1)S(1)}, u32[]{:S(2)}, u32[]{:S(2)}) %collective-permute-start.4) | collective-permute-done | bytes 626720 | tf_op jit(solution)/shard_map/ppermute | solution.py:591
  60.5 19.7 %collective-permute-done.6 = bf16[2,2,136,1152]{3,2,1,0:T(8,128)(2,1)} collective-permute-done((bf16[2,2,136,1152]{3,2,1,0:T(8,128)(2,1)}, bf16[2,2,136,1152]{3,2,1,0:T(8,128)(2,1)}, u32[]{:S(2)}, u32[]{:S(2)}) %collective-permute-start.6) | collective-permute-done | bytes 1253408 | tf_op jit(solution)/shard_map/ppermute | solution.py:583
  80.2 2.4 collective-permute-done.5
  82.6 5.1 assemble.3
  88.9 3.4 collective-permute-start.9
  94.9 3.8 collective-permute-done.10
  98.7 21.8 %collective-permute-done.9 = bf16[136,1088]{1,0:T(8,128)(2,1)S(1)} collective-permute-done((bf16[136,1088]{1,0:T(8,128)(2,1)S(1)}, bf16[136,1088]{1,0:T(8,128)(2,1)S(1)}, u32[]{:S(2)}, u32[]{:S(2)}) %collective-permute-start.9) | collective-permute-done | bytes 295968 | tf_op jit(solution)/shard_map/ppermute | solution.py:596
  127.0 9.5 %collective-permute-done.12.refs_3_ = bf16[2,136,1088]{2,1,0:T(8,128)(2,1)S(1)} collective-permute-done((bf16[2,136,1088]{2,1,0:T(8,128)(2,1)S(1)}, bf16[2,136,1088]{2,1,0:T(8,128)(2,1)S(1)}, u32[]{:S(2)}, u32[]{:S(2)}) %collective-permute-start.12) | collective-permute-done | bytes 591904 | tf_op jit(solution)/shard_map/ppermute | solution.py:591
  142.5 7.2 %multiply_and_place.3.refs_2_ = bf16[512,3456]{1,0:T(8,128)(2,1)S(1)} custom-call(s32[2]{0:T(128)S(1)} %copy-done.47, bf16[512,1088]{1,0:T(8,128)(2,1)S(1)} %copy.110.x, bf16[2,1088,1152]{2,1,0:T(8,128)(2,1)} %bitcast.230, f32[1,3456]{1,0:T(1,128)S(1)} %copy-done.45), custom_call_target="tpu_custom_call" | custom-call | tf_op jit(solution)/shard_map/multiply_and_place/pallas_call | solution.py:327
  154.6 5.1 fusion.71
  161.5 8.5 %multiply_and_place.4.q.k_own.v_own = bf16[512,3456]{1,0:T(8,128)(2,1)S(1)} custom-call(s32[2]{0:T(128)S(1)} %copy-done.49, bf16[512,1088]{1,0:T(8,128)(2,1)S(1)} %copy-done.7, bf16[2,1088,1152]{2,1,0:T(8,128)(2,1)} %collective-permute-done.13.refs_0_.refs_1_, f32[1,3456]{1,0:T(1,128)S(1)} %copy-done.46, bf16[512,3456]{1,0:T(8,128)(2,1)} %copy-done.5), custom_call_target="tpu_custom_call" | custom-call | tf_op jit(solution)/shard_map/multiply_and_place/pallas_call | solution.py:327
  181.0 5.2 slice_bitcast_fusion.1
  186.2 17.7 %attention_forward.1 = (bf16[512,1152]{1,0:T(8,128)(2,1)S(1)}, f32[9,2,512]{2,1,0:T(2,128)S(1)}) custom-call(s32[1]{0:T(128)} %bitcast.17.later, s32[1,512]{1,0:T(1,128)S(1)} %bitcast.226, s32[512,1]{1,0:T(8,128)S(1)} %copy-done.25, s32[512,1]{1,0:T(8,128)S(1)} %copy-done.23, bf16[512,3456]{1,0:T(8,128)(2,1)} %copy-done, bf16[512,3456]{1,0:T(8,128)(2,1)} %copy-done, ...), custom_call_target="tpu_custom_call" | custom-call | tf_op jit(solution)/shard_map/attention_forward/pallas_call | solution.py:232
  206.5 2.5 convolution_add_fusion.2
  216.0 4.9 collective-permute-done.22
  220.9 9.2 %collective-permute-done.23 = bf16[2,2,136,1088]{3,2,1,0:T(8,128)(2,1)S(1)} collective-permute-done((bf16[2,2,136,1088]{3,2,1,0:T(8,128)(2,1)}, bf16[2,2,136,1088]{3,2,1,0:T(8,128)(2,1)S(1)}, u32[]{:S(2)}, u32[]{:S(2)}) %collective-permute-start.23) | collective-permute-done | bytes 1183776 | tf_op jit(solution)/shard_map/ppermute | solution.py:583
  230.1 4.5 assemble.5
  234.7 4.3 assemble.4
  242.7 12.8 %feed_forward.2 = (f32[2,512,1088]{2,1,0:T(8,128)}, bf16[2,512,1088]{2,1,0:T(8,128)(2,1)}, f32[512,1088]{1,0:T(8,128)}) custom-call(bf16[512,1088]{1,0:T(8,128)(2,1)} %copy.115.x, bf16[2,1088,1088]{2,1,0:T(8,128)(2,1)} %bitcast.236, f32[2,1,1088]{2,1,0:T(1,128)} %copy.114.bias, bf16[2,1088,1088]{2,1,0:T(8,128)(2,1)} %bitcast.233), custom_call_target="tpu_custom_call" | custom-call | tf_op jit(solution)/shard_map/feed_forward/pallas_call | solution.py:560
  255.6 12.9 %feed_forward.3 = (f32[2,512,1088]{2,1,0:T(8,128)}, bf16[2,512,1088]{2,1,0:T(8,128)(2,1)}, f32[512,1088]{1,0:T(8,128)}) custom-call(bf16[512,1088]{1,0:T(8,128)(2,1)} %copy.115.x, bf16[2,1088,1088]{2,1,0:T(8,128)(2,1)} %collective-permute-done.24.up, f32[2,1,1088]{2,1,0:T(1,128)} %reshape.260.bias, bf16[2,1088,1088]{2,1,0:T(8,128)(2,1)} %collective-permute-done.25.down, ...), custom_call_target="tpu_custom_call" | custom-call | tf_op jit(solution)/shard_map/feed_forward/pallas_call | solution.py:560
  270.2 4.7 block_grads.6
  276.3 14.2 %feed_backward.2 = (bf16[2,512,1088]{2,1,0:T(8,128)(2,1)}, f32[2,1,1088]{2,1,0:T(1,128)}, f32[512,1088]{1,0:T(8,128)}) custom-call(bf16[512,1088]{1,0:T(8,128)(2,1)} %copy.118.grad, bf16[2,1088,1088]{2,1,0:T(8,128)(2,1)} %collective-permute-done.24.up, bf16[2,1088,1088]{2,1,0:T(8,128)(2,1)} %collective-permute-done.25.down, ...), custom_call_target="tpu_custom_call" | custom-call | tf_op jit(solution)/shard_map/feed_backward/pallas_call | solution.py:560
  292.2 4.8 block_grads.7
  297.5 6.6 %block_grads.8 = (bf16[2,272,1088]{2,1,0:T(8,128)(2,1)S(1)}, bf16[2,272,1088]{2,1,0:T(8,128)(2,1)}, bf16[2,272,1088]{2,1,0:T(8,128)(2,1)S(1)}, bf16[2,272,1088]{2,1,0:T(8,128)(2,1)}) custom-call(s32[1]{0:T(128)} %bitcast.place, bf16[1088,512]{1,0:T(8,128)(2,1)S(1)} %bitcast.203, bf16[2,512,1088]{2,1,0:T(8,128)(2,1)} %get-tuple-element.166.refs_1_, ...), custom_call_target="tpu_custom_call" | custom-call | tf_op jit(solution)/shard_map/block_grads/pallas_call | solution.py:478
  306.9 3.1 copy.116
  309.9 15.0 %feed_backward.3 = (bf16[2,512,1088]{2,1,0:T(8,128)(2,1)}, f32[2,1,1088]{2,1,0:T(1,128)}, f32[512,1088]{1,0:T(8,128)}) custom-call(bf16[512,1088]{1,0:T(8,128)(2,1)} %copy.118.grad, bf16[2,1088,1088]{2,1,0:T(8,128)(2,1)} %bitcast.237, bf16[2,1088,1088]{2,1,0:T(8,128)(2,1)} %bitcast.234, f32[2,512,1088]{2,1,0:T(8,128)} %get-tuple-element.172.linear, ...), custom_call_target="tpu_custom_call" | custom-call | tf_op jit(solution)/shard_map/feed_backward/pallas_call | solution.py:560
  324.9 3.0 copy.119
  329.5 3.1 multiply_reduce_fusion
  332.6 3.9 fusion.70
  337.8 5.5 block_grads.9
  344.4 2.6 add_convert_fusion.5
  347.0 10.4 %collective-permute-done.29 = bf16[2,272,1088]{2,1,0:T(8,128)(2,1)S(1)} collective-permute-done((bf16[2,272,1088]{2,1,0:T(8,128)(2,1)}, bf16[2,272,1088]{2,1,0:T(8,128)(2,1)S(1)}, u32[]{:S(2)}, u32[]{:S(2)}) %collective-permute-start.29) | collective-permute-done | bytes 1183776 | tf_op jit(solution)/shard_map/ppermute | solution.py:583
  368.4 6.7 %multiply_and_place.5.grad = bf16[512,1152]{1,0:T(8,128)(2,1)S(1)} custom-call(s32[4]{0:T(128)S(1)} %pad_add_fusion.1.places, bf16[512,1088]{1,0:T(8,128)(2,1)S(1)} %copy-done.14, bf16[2,1088,1152]{2,1,0:T(8,128)(2,1)} %bitcast.231, bf16[2,1088,1152]{2,1,0:T(8,128)(2,1)} %collective-permute-done.13.refs_0_.refs_1_), custom_call_target="tpu_custom_call" | custom-call | tf_op jit(solution)/shard_map/multiply_and_place/pallas_call | solution.py:327
  376.1 19.8 %attention_backward.1 = (bf16[512,1152]{1,0:T(8,128)(2,1)S(1)}, bf16[512,1152]{1,0:T(8,128)(2,1)S(1)}, bf16[512,1152]{1,0:T(8,128)(2,1)S(1)}, bf16[512,1152]{1,0:T(8,128)(2,1)S(1)}, bf16[512,1152]{1,0:T(8,128)(2,1)}) custom-call(s32[1]{0:T(128)} %bitcast.17.later, s32[1,512]{1,0:T(1,128)S(1)} %bitcast.227, s32[512,1]{1,0:T(8,128)S(1)} %copy-done.26, ...), custom_call_target="tpu_custom_call" | custom-call | tf_op jit(solution)/shard_map/attention_backward/pallas_call | solution.py:255
  401.1 3.6 collective-permute-done.30
  413.2 6.4 %collective-permute-done.34.back = bf16[512,2304]{1,0:T(8,128)(2,1)} collective-permute-done((bf16[512,2304]{1,0:T(8,128)(2,1)}, bf16[512,2304]{1,0:T(8,128)(2,1)}, u32[]{:S(2)}, u32[]{:S(2)}) %collective-permute-start.34) | collective-permute-done | bytes 2359328 | tf_op jit(solution)/shard_map/ppermute | solution.py:935
  423.3 5.4 split_grads.1
  428.8 2.2 copy-done.29
  430.9 5.3 block_grads.10
  442.3 2.5 collective-permute-start.51
  444.8 8.1 %collective-permute-done.45 = bf16[272,1088]{1,0:T(8,128)(2,1)S(1)} collective-permute-done((bf16[272,1088]{1,0:T(8,128)(2,1)S(1)}, bf16[272,1088]{1,0:T(8,128)(2,1)S(1)}, u32[]{:S(2)}, u32[]{:S(2)}) %collective-permute-start.45) | collective-permute-done | bytes 591904 | tf_op jit(solution)/shard_map/ppermute | solution.py:591
  452.8 2.9 collective-permute-start.50
  463.5 3.5 fusion.14
  468.9 2.1 collective-permute-start.46
  471.1 2.1 collective-permute-start.48
  473.2 7.5 %block_grads.11 = (bf16[2,272,1152]{2,1,0:T(8,128)(2,1)S(1)}, bf16[2,272,1152]{2,1,0:T(8,128)(2,1)S(1)}, bf16[2,272,1152]{2,1,0:T(8,128)(2,1)}, bf16[2,272,1152]{2,1,0:T(8,128)(2,1)}) custom-call(s32[1]{0:T(128)} %bitcast.place, bf16[1088,512]{1,0:T(8,128)(2,1)S(1)} %bitcast.207, bf16[1088,512]{1,0:T(8,128)(2,1)S(1)} %bitcast.209, ...), custom_call_target="tpu_custom_call" | custom-call | tf_op jit(solution)/shard_map/block_grads/pallas_call | solution.py:478
  482.2 3.0 multiply_subtract_fusion
  485.2 2.1 collective-permute-done.48
  487.3 13.4 %collective-permute-done.47 = bf16[136,1088]{1,0:T(8,128)(2,1)S(1)} collective-permute-done((bf16[136,1088]{1,0:T(8,128)(2,1)S(1)}, bf16[136,1088]{1,0:T(8,128)(2,1)S(1)}, u32[]{:S(2)}, u32[]{:S(2)}) %collective-permute-start.47) | collective-permute-done | bytes 295968 | tf_op jit(solution)/shard_map/ppermute | solution.py:596
  500.7 2.7 multiply_subtract_fusion.1
  504.8 5.4 collective-permute-done.37
  512.1 21.6 %collective-permute-done.39 = bf16[2,272,1152]{2,1,0:T(8,128)(2,1)S(1)} collective-permute-done((bf16[2,272,1152]{2,1,0:T(8,128)(2,1)S(1)}, bf16[2,272,1152]{2,1,0:T(8,128)(2,1)S(1)}, u32[]{:S(2)}, u32[]{:S(2)}) %collective-permute-start.39) | collective-permute-done | bytes 1253408 | tf_op jit(solution)/shard_map/ppermute | solution.py:583
  535.6 10.7 %collective-permute-done.38 = bf16[272,1152]{1,0:T(8,128)(2,1)S(1)} collective-permute-done((bf16[272,1152]{1,0:T(8,128)(2,1)S(1)}, bf16[272,1152]{1,0:T(8,128)(2,1)S(1)}, u32[]{:S(2)}, u32[]{:S(2)}) %collective-permute-start.38) | collective-permute-done | bytes 626720 | tf_op jit(solution)/shard_map/ppermute | solution.py:583
  546.5 2.1 collective-permute-done.40
  549.0 3.8 collective-permute-start.43
  552.9 2.1 fusion.13
  555.0 6.3 %collective-permute-done.41 = bf16[136,1152]{1,0:T(8,128)(2,1)S(1)} collective-permute-done((bf16[136,1152]{1,0:T(8,128)(2,1)S(1)}, bf16[136,1152]{1,0:T(8,128)(2,1)S(1)}, u32[]{:S(2)}, u32[]{:S(2)}) %collective-permute-start.41) | collective-permute-done | bytes 313376 | tf_op jit(solution)/shard_map/ppermute | solution.py:596
  561.2 2.4 collective-permute-done.43
  563.7 12.7 %collective-permute-done.42 = bf16[136,1152]{1,0:T(8,128)(2,1)S(1)} collective-permute-done((bf16[136,1152]{1,0:T(8,128)(2,1)S(1)}, bf16[136,1152]{1,0:T(8,128)(2,1)S(1)}, u32[]{:S(2)}, u32[]{:S(2)}) %collective-permute-start.42) | collective-permute-done | bytes 313376 | tf_op jit(solution)/shard_map/ppermute | solution.py:596
  577.3 2.1 multiply_subtract_fusion.3
  580.0 2.6 multiply_subtract_fusion.2
  (434 shorter events, 129.8 us)
Async XLA Ops:
  4.3 13.0 %collective-permute-start.2 = (bf16[136,1152]{1,0:T(8,128)(2,1)S(1)}, bf16[136,1152]{1,0:T(8,128)(2,1)S(1)}, u32[]{:S(2)}, u32[]{:S(2)}) collective-permute-start(bf16[136,1152]{1,0:T(8,128)(2,1)S(1)} %concatenate.26), channel_id=1, source_target_pairs={{0,12},{4,0},{8,4},{12,8},{1,13},{5,1},{9,5},{13,9},{2,14},{6,2},{... | collective-permute-start | bytes 940040 | tf_op jit(solution)/shard_map/ppermute | solution.py:596
  9.4 26.7 %collective-permute-start.1 = (bf16[136,1152]{1,0:T(8,128)(2,1)S(1)}, bf16[136,1152]{1,0:T(8,128)(2,1)S(1)}, u32[]{:S(2)}, u32[]{:S(2)}) collective-permute-start(bf16[136,1152]{1,0:T(8,128)(2,1)S(1)} %concatenate.26), channel_id=1, source_target_pairs={{0,8},{4,12},{8,0},{12,4},{1,9},{5,13},{9,1},{13,5},{2,10},{6,14},... | collective-permute-start | bytes 940040 | tf_op jit(solution)/shard_map/ppermute | solution.py:596
  9.4 26.7 %collective-permute-start = (bf16[136,1152]{1,0:T(8,128)(2,1)S(1)}, bf16[136,1152]{1,0:T(8,128)(2,1)S(1)}, u32[]{:S(2)}, u32[]{:S(2)}) collective-permute-start(bf16[136,1152]{1,0:T(8,128)(2,1)S(1)} %concatenate.26), channel_id=1, source_target_pairs={{0,4},{4,8},{8,12},{12,0},{1,5},{5,9},{9,13},{13,1},{2,6},{6,10},{... | collective-permute-start | bytes 940040 | tf_op jit(solution)/shard_map/ppermute | solution.py:596
  36.2 15.1 %collective-permute-start.4 = (bf16[2,136,1152]{2,1,0:T(8,128)(2,1)S(1)}, bf16[2,136,1152]{2,1,0:T(8,128)(2,1)S(1)}, u32[]{:S(2)}, u32[]{:S(2)}) collective-permute-start(bf16[2,136,1152]{2,1,0:T(8,128)(2,1)S(1)} %get-tuple-element.296.refs_2_), channel_id=1, source_target_pairs={{0,16},{16,0},{1,17},{17,1},{2,18},{18,2},{3,19},{19,3},{4,20},{20... | collective-permute-start | bytes 1880072 | tf_op jit(solution)/shard_map/ppermute | solution.py:591
  37.9 16.1 %collective-permute-start.3 = (bf16[2,136,1152]{2,1,0:T(8,128)(2,1)S(1)}, bf16[2,136,1152]{2,1,0:T(8,128)(2,1)S(1)}, u32[]{:S(2)}, u32[]{:S(2)}) collective-permute-start(bf16[2,136,1152]{2,1,0:T(8,128)(2,1)S(1)} %get-tuple-element.298.refs_0_), channel_id=1, source_target_pairs={{0,2},{1,3},{2,0},{3,1},{4,6},{5,7},{6,4},{7,5},{8,10},{9,11},{10,... | collective-permute-start | bytes 1880072 | tf_op jit(solution)/shard_map/ppermute | solution.py:583
  52.4 27.8 %collective-permute-start.6 = (bf16[2,2,136,1152]{3,2,1,0:T(8,128)(2,1)}, bf16[2,2,136,1152]{3,2,1,0:T(8,128)(2,1)}, u32[]{:S(2)}, u32[]{:S(2)}) collective-permute-start(bf16[2,2,136,1152]{3,2,1,0:T(8,128)(2,1)} %pad_maximum_fusion.2), channel_id=1, source_target_pairs={{0,2},{1,3},{2,0},{3,1},{4,6},{5,7},{6,4},{7,5},{8,10},{9,11},{10,... | collective-permute-start | bytes 3760136 | tf_op jit(solution)/shard_map/ppermute | solution.py:583
  55.1 27.5 %collective-permute-start.5 = (bf16[2,2,136,1152]{3,2,1,0:T(8,128)(2,1)}, bf16[2,2,136,1152]{3,2,1,0:T(8,128)(2,1)}, u32[]{:S(2)}, u32[]{:S(2)}) collective-permute-start(bf16[2,2,136,1152]{3,2,1,0:T(8,128)(2,1)} %pad_maximum_fusion.1), channel_id=1, source_target_pairs={{0,16},{16,0},{1,17},{17,1},{2,18},{18,2},{3,19},{19,3},{4,20},{20... | collective-permute-start | bytes 3760136 | tf_op jit(solution)/shard_map/ppermute | solution.py:591
  60.5 27.3 %copy-start.99 = (f32[512]{0:T(512)}, f32[512]{0:T(512)S(1)}, u32[]{:S(2)}) copy-start(f32[512]{0:T(512)S(1)} %broadcast_multiply_fusion.5) | copy-start | bytes 6148
  87.7 73.8 %collective-permute-start.13 = (bf16[2,1088,1152]{2,1,0:T(8,128)(2,1)}, bf16[2,1088,1152]{2,1,0:T(8,128)(2,1)}, u32[]{:S(2)}, u32[]{:S(2)}) collective-permute-start(bf16[2,1088,1152]{2,1,0:T(8,128)(2,1)} %bitcast.228), channel_id=1, source_target_pairs={{0,1},{1,0},{2,3},{3,2},{4,5},{5,4},{6,7},{7,6},{8,9},{9,8},{10,11... | collective-permute-start | bytes 15040520 | tf_op jit(solution)/shard_map/ppermute | solution.py:583
  88.1 50.4 %copy-start.100 = (f32[512]{0:T(512)S(1)}, f32[512]{0:T(512)}, u32[]{:S(2)}) copy-start(f32[512]{0:T(512)} %copy-done.99) | copy-start | bytes 6148
  88.9 9.8 %collective-permute-start.10 = (bf16[136,1088]{1,0:T(8,128)(2,1)S(1)}, bf16[136,1088]{1,0:T(8,128)(2,1)S(1)}, u32[]{:S(2)}, u32[]{:S(2)}) collective-permute-start(bf16[136,1088]{1,0:T(8,128)(2,1)S(1)} %convert_element_type.277), channel_id=1, source_target_pairs={{0,12},{4,0},{8,4},{12,8},{1,13},{5,1},{9,5},{13,9},{2,14},{6,2},{... | collective-permute-start | bytes 887816 | tf_op jit(solution)/shard_map/ppermute | solution.py:596
  88.9 31.5 %collective-permute-start.9 = (bf16[136,1088]{1,0:T(8,128)(2,1)S(1)}, bf16[136,1088]{1,0:T(8,128)(2,1)S(1)}, u32[]{:S(2)}, u32[]{:S(2)}) collective-permute-start(bf16[136,1088]{1,0:T(8,128)(2,1)S(1)} %convert_element_type.277), channel_id=1, source_target_pairs={{0,8},{4,12},{8,0},{12,4},{1,9},{5,13},{9,1},{13,5},{2,10},{6,14},... | collective-permute-start | bytes 887816 | tf_op jit(solution)/shard_map/ppermute | solution.py:596
  92.3 28.2 %collective-permute-start.8 = (bf16[136,1088]{1,0:T(8,128)(2,1)S(1)}, bf16[136,1088]{1,0:T(8,128)(2,1)S(1)}, u32[]{:S(2)}, u32[]{:S(2)}) collective-permute-start(bf16[136,1088]{1,0:T(8,128)(2,1)S(1)} %convert_element_type.277), channel_id=1, source_target_pairs={{0,4},{4,8},{8,12},{12,0},{1,5},{5,9},{9,13},{13,1},{2,6},{6,10},{... | collective-permute-start | bytes 887816 | tf_op jit(solution)/shard_map/ppermute | solution.py:596
  94.9 45.4 %copy-start.102 = (f32[512]{0:T(512)}, f32[512]{0:T(512)S(1)}, u32[]{:S(2)}) copy-start(f32[512]{0:T(512)S(1)} %add_rsqrt_fusion.1) | copy-start | bytes 6148
  120.5 29.3 %collective-permute-start.16 = (bf16[136,1088]{1,0:T(8,128)(2,1)}, bf16[136,1088]{1,0:T(8,128)(2,1)}, u32[]{:S(2)}, u32[]{:S(2)}) collective-permute-start(bf16[136,1088]{1,0:T(8,128)(2,1)} %convert_bitcast_fusion), channel_id=1, source_target_pairs={{0,12},{4,0},{8,4},{12,8},{1,13},{5,1},{9,5},{13,9},{2,14},{6,2},{... | collective-permute-start | bytes 887816 | tf_op jit(solution)/shard_map/ppermute | solution.py:596
  120.5 29.3 %collective-permute-start.15 = (bf16[136,1088]{1,0:T(8,128)(2,1)}, bf16[136,1088]{1,0:T(8,128)(2,1)}, u32[]{:S(2)}, u32[]{:S(2)}) collective-permute-start(bf16[136,1088]{1,0:T(8,128)(2,1)} %convert_bitcast_fusion), channel_id=1, source_target_pairs={{0,8},{4,12},{8,0},{12,4},{1,9},{5,13},{9,1},{13,5},{2,10},{6,14},... | collective-permute-start | bytes 887816 | tf_op jit(solution)/shard_map/ppermute | solution.py:596
  120.6 16.0 %collective-permute-start.12 = (bf16[2,136,1088]{2,1,0:T(8,128)(2,1)S(1)}, bf16[2,136,1088]{2,1,0:T(8,128)(2,1)S(1)}, u32[]{:S(2)}, u32[]{:S(2)}) collective-permute-start(bf16[2,136,1088]{2,1,0:T(8,128)(2,1)S(1)} %pad_maximum_fusion.13.refs_2_), channel_id=1, source_target_pairs={{0,16},{16,0},{1,17},{17,1},{2,18},{18,2},{3,19},{19,3},{4,20},{20... | collective-permute-start | bytes 1775624 | tf_op jit(solution)/shard_map/ppermute | solution.py:591
  123.0 1.3 collective-permute-start.7
  123.2 36.5 %copy-start.10 = (bf16[2,136,1088]{2,1,0:T(8,128)(2,1)}, bf16[2,136,1088]{2,1,0:T(8,128)(2,1)S(1)}, u32[]{:S(2)}) copy-start(bf16[2,136,1088]{2,1,0:T(8,128)(2,1)S(1)} %pad_maximum_fusion.12.refs_0_) | copy-start | bytes 1775620
  124.3 16.2 %collective-permute-start.11 = (bf16[2,136,1088]{2,1,0:T(8,128)(2,1)S(1)}, bf16[2,136,1088]{2,1,0:T(8,128)(2,1)S(1)}, u32[]{:S(2)}, u32[]{:S(2)}) collective-permute-start(bf16[2,136,1088]{2,1,0:T(8,128)(2,1)S(1)} %pad_maximum_fusion.12.refs_0_), channel_id=1, source_target_pairs={{0,2},{1,3},{2,0},{3,1},{4,6},{5,7},{6,4},{7,5},{8,10},{9,11},{10,... | collective-permute-start | bytes 1775624 | tf_op jit(solution)/shard_map/ppermute | solution.py:583
  136.6 13.2 %collective-permute-start.14 = (bf16[136,1088]{1,0:T(8,128)(2,1)}, bf16[136,1088]{1,0:T(8,128)(2,1)}, u32[]{:S(2)}, u32[]{:S(2)}) collective-permute-start(bf16[136,1088]{1,0:T(8,128)(2,1)} %convert_bitcast_fusion), channel_id=1, source_target_pairs={{0,4},{4,8},{8,12},{12,0},{1,5},{5,9},{9,13},{13,1},{2,6},{6,10},{... | collective-permute-start | bytes 887816 | tf_op jit(solution)/shard_map/ppermute | solution.py:596
  151.4 18.7 %collective-permute-start.18 = (bf16[2,136,1088]{2,1,0:T(8,128)(2,1)S(1)}, bf16[2,136,1088]{2,1,0:T(8,128)(2,1)S(1)}, u32[]{:S(2)}, u32[]{:S(2)}) collective-permute-start(bf16[2,136,1088]{2,1,0:T(8,128)(2,1)S(1)} %pad_maximum_fusion.15.refs_2_), channel_id=1, source_target_pairs={{0,16},{16,0},{1,17},{17,1},{2,18},{18,2},{3,19},{19,3},{4,20},{20... | collective-permute-start | bytes 1775624 | tf_op jit(solution)/shard_map/ppermute | solution.py:591
  154.0 16.1 %collective-permute-start.17 = (bf16[2,136,1088]{2,1,0:T(8,128)(2,1)S(1)}, bf16[2,136,1088]{2,1,0:T(8,128)(2,1)S(1)}, u32[]{:S(2)}, u32[]{:S(2)}) collective-permute-start(bf16[2,136,1088]{2,1,0:T(8,128)(2,1)S(1)} %pad_maximum_fusion.14.refs_0_), channel_id=1, source_target_pairs={{0,2},{1,3},{2,0},{3,1},{4,6},{5,7},{6,4},{7,5},{8,10},{9,11},{10,... | collective-permute-start | bytes 1775624 | tf_op jit(solution)/shard_map/ppermute | solution.py:583
  160.9 43.1 %collective-permute-start.20 = (bf16[2,2,136,1088]{3,2,1,0:T(8,128)(2,1)}, bf16[2,2,136,1088]{3,2,1,0:T(8,128)(2,1)S(1)}, u32[]{:S(2)}, u32[]{:S(2)}) collective-permute-start(bf16[2,2,136,1088]{3,2,1,0:T(8,128)(2,1)} %pad_maximum_fusion.3), channel_id=1, source_target_pairs={{0,16},{16,0},{1,17},{17,1},{2,18},{18,2},{3,19},{19,3},{4,20},{20... | collective-permute-start | bytes 3551240 | tf_op jit(solution)/shard_map/ppermute | solution.py:591
  171.9 14.3 %collective-permute-start.19 = (bf16[512,2304]{1,0:T(8,128)(2,1)S(1)}, bf16[512,2304]{1,0:T(8,128)(2,1)S(1)}, u32[]{:S(2)}, u32[]{:S(2)}) collective-permute-start(bf16[512,2304]{1,0:T(8,128)(2,1)S(1)} %slice.163), channel_id=1, source_target_pairs={{0,1},{2,3},{4,5},{6,7},{8,9},{10,11},{12,13},{14,15},{16,17},{18,... | collective-permute-start | bytes 7077896 | tf_op jit(solution)/shard_map/ppermute | solution.py:828
  175.1 30.7 %collective-permute-start.21 = (bf16[2,2,136,1088]{3,2,1,0:T(8,128)(2,1)}, bf16[2,2,136,1088]{3,2,1,0:T(8,128)(2,1)S(1)}, u32[]{:S(2)}, u32[]{:S(2)}) collective-permute-start(bf16[2,2,136,1088]{3,2,1,0:T(8,128)(2,1)} %pad_maximum_fusion.4), channel_id=1, source_target_pairs={{0,2},{1,3},{2,0},{3,1},{4,6},{5,7},{6,4},{7,5},{8,10},{9,11},{10,... | collective-permute-start | bytes 3551240 | tf_op jit(solution)/shard_map/ppermute | solution.py:583
  177.8 43.0 %collective-permute-start.22 = (bf16[2,2,136,1088]{3,2,1,0:T(8,128)(2,1)}, bf16[2,2,136,1088]{3,2,1,0:T(8,128)(2,1)S(1)}, u32[]{:S(2)}, u32[]{:S(2)}) collective-permute-start(bf16[2,2,136,1088]{3,2,1,0:T(8,128)(2,1)} %pad_maximum_fusion.5), channel_id=1, source_target_pairs={{0,16},{16,0},{1,17},{17,1},{2,18},{18,2},{3,19},{19,3},{4,20},{20... | collective-permute-start | bytes 3551240 | tf_op jit(solution)/shard_map/ppermute | solution.py:591
  180.4 49.7 %collective-permute-start.23 = (bf16[2,2,136,1088]{3,2,1,0:T(8,128)(2,1)}, bf16[2,2,136,1088]{3,2,1,0:T(8,128)(2,1)S(1)}, u32[]{:S(2)}, u32[]{:S(2)}) collective-permute-start(bf16[2,2,136,1088]{3,2,1,0:T(8,128)(2,1)} %pad_maximum_fusion.6), channel_id=1, source_target_pairs={{0,2},{1,3},{2,0},{3,1},{4,6},{5,7},{6,4},{7,5},{8,10},{9,11},{10,... | collective-permute-start | bytes 3551240 | tf_op jit(solution)/shard_map/ppermute | solution.py:583
  186.2 20.3 %copy-start.56 = (bf16[512,1088]{0,1:T(8,128)(2,1)S(1)}, bf16[512,1088]{0,1:T(8,128)(2,1)}, u32[]{:S(2)}) copy-start(bf16[512,1088]{0,1:T(8,128)(2,1)} %param.18) | copy-start | bytes 3342340
  186.2 20.3 %copy-start.97 = (f32[1088]{0:T(1024)S(1)}, f32[1088]{0:T(1024)}, u32[]{:S(2)}) copy-start(f32[1088]{0:T(1024)} %get-tuple-element.263) | copy-start | bytes 13060
  234.6 20.9 %collective-permute-start.25 = (bf16[2,1088,1088]{2,1,0:T(8,128)(2,1)}, bf16[2,1088,1088]{2,1,0:T(8,128)(2,1)}, u32[]{:S(2)}, u32[]{:S(2)}) collective-permute-start(bf16[2,1088,1088]{2,1,0:T(8,128)(2,1)} %bitcast.232), channel_id=1, source_target_pairs={{0,1},{1,0},{2,3},{3,2},{4,5},{5,4},{6,7},{7,6},{8,9},{9,8},{10,11... | collective-permute-start | bytes 14204936 | tf_op jit(solution)/shard_map/ppermute | solution.py:583
  239.1 16.4 %collective-permute-start.24 = (bf16[2,1088,1088]{2,1,0:T(8,128)(2,1)}, bf16[2,1088,1088]{2,1,0:T(8,128)(2,1)}, u32[]{:S(2)}, u32[]{:S(2)}) collective-permute-start(bf16[2,1088,1088]{2,1,0:T(8,128)(2,1)} %bitcast.235), channel_id=1, source_target_pairs={{0,1},{1,0},{2,3},{3,2},{4,5},{5,4},{6,7},{7,6},{8,9},{9,8},{10,11... | collective-permute-start | bytes 14204936 | tf_op jit(solution)/shard_map/ppermute | solution.py:583
  274.9 22.6 %collective-permute-start.26 = (bf16[2,1088,1088]{2,1,0:T(8,128)(2,1)}, bf16[2,1088,1088]{2,1,0:T(8,128)(2,1)}, u32[]{:S(2)}, u32[]{:S(2)}) collective-permute-start(bf16[2,1088,1088]{2,1,0:T(8,128)(2,1)} %block_grads.6), channel_id=1, source_target_pairs={{0,1},{1,0},{2,3},{3,2},{4,5},{5,4},{6,7},{7,6},{8,9},{9,8},{10,11... | collective-permute-start | bytes 14204936 | tf_op jit(solution)/shard_map/ppermute | solution.py:583
  297.0 39.6 %collective-permute-start.27 = (bf16[2,1088,1088]{2,1,0:T(8,128)(2,1)}, bf16[2,1088,1088]{2,1,0:T(8,128)(2,1)}, u32[]{:S(2)}, u32[]{:S(2)}) collective-permute-start(bf16[2,1088,1088]{2,1,0:T(8,128)(2,1)} %block_grads.7), channel_id=1, source_target_pairs={{0,1},{1,0},{2,3},{3,2},{4,5},{5,4},{6,7},{7,6},{8,9},{9,8},{10,11... | collective-permute-start | bytes 14204936 | tf_op jit(solution)/shard_map/ppermute | solution.py:583
  306.2 38.2 %collective-permute-start.28 = (bf16[2,272,1088]{2,1,0:T(8,128)(2,1)}, bf16[2,272,1088]{2,1,0:T(8,128)(2,1)}, u32[]{:S(2)}, u32[]{:S(2)}) collective-permute-start(bf16[2,272,1088]{2,1,0:T(8,128)(2,1)} %get-tuple-element.182), channel_id=1, source_target_pairs={{0,16},{16,0},{1,17},{17,1},{2,18},{18,2},{3,19},{19,3},{4,20},{20... | collective-permute-start | bytes 3551240 | tf_op jit(solution)/shard_map/ppermute | solution.py:591
  327.9 29.5 %collective-permute-start.29 = (bf16[2,272,1088]{2,1,0:T(8,128)(2,1)}, bf16[2,272,1088]{2,1,0:T(8,128)(2,1)S(1)}, u32[]{:S(2)}, u32[]{:S(2)}) collective-permute-start(bf16[2,272,1088]{2,1,0:T(8,128)(2,1)} %get-tuple-element.184), channel_id=1, source_target_pairs={{0,2},{1,3},{2,0},{3,1},{4,6},{5,7},{6,4},{7,5},{8,10},{9,11},{10,... | collective-permute-start | bytes 3551240 | tf_op jit(solution)/shard_map/ppermute | solution.py:583
  359.6 36.4 %collective-permute-start.32 = (bf16[272,1088]{1,0:T(8,128)(2,1)}, bf16[272,1088]{1,0:T(8,128)(2,1)}, u32[]{:S(2)}, u32[]{:S(2)}) collective-permute-start(bf16[272,1088]{1,0:T(8,128)(2,1)} %slice_bitcast_fusion.5), channel_id=1, source_target_pairs={{0,2},{1,3},{2,0},{3,1},{4,6},{5,7},{6,4},{7,5},{8,10},{9,11},{10,... | collective-permute-start | bytes 1775624 | tf_op jit(solution)/shard_map/ppermute | solution.py:583
  363.1 34.8 %collective-permute-start.33 = (bf16[272,1088]{1,0:T(8,128)(2,1)}, bf16[272,1088]{1,0:T(8,128)(2,1)}, u32[]{:S(2)}, u32[]{:S(2)}) collective-permute-start(bf16[272,1088]{1,0:T(8,128)(2,1)} %dynamic-slice_bitcast_fusion.2), channel_id=1, source_target_pairs={{0,16},{16,0},{1,17},{17,1},{2,18},{18,2},{3,19},{19,3},{4,20},{20... | collective-permute-start | bytes 1775624 | tf_op jit(solution)/shard_map/ppermute | solution.py:591
  365.9 38.9 %collective-permute-start.30 = (bf16[2,272,1088]{2,1,0:T(8,128)(2,1)}, bf16[2,272,1088]{2,1,0:T(8,128)(2,1)S(1)}, u32[]{:S(2)}, u32[]{:S(2)}) collective-permute-start(bf16[2,272,1088]{2,1,0:T(8,128)(2,1)} %copy-done.52), channel_id=1, source_target_pairs={{0,16},{16,0},{1,17},{17,1},{2,18},{18,2},{3,19},{19,3},{4,20},{20... | collective-permute-start | bytes 3551240 | tf_op jit(solution)/shard_map/ppermute | solution.py:591
  366.6 39.5 %collective-permute-start.31 = (bf16[2,272,1088]{2,1,0:T(8,128)(2,1)}, bf16[2,272,1088]{2,1,0:T(8,128)(2,1)S(1)}, u32[]{:S(2)}, u32[]{:S(2)}) collective-permute-start(bf16[2,272,1088]{2,1,0:T(8,128)(2,1)} %copy-done.51), channel_id=1, source_target_pairs={{0,2},{1,3},{2,0},{3,1},{4,6},{5,7},{6,4},{7,5},{8,10},{9,11},{10,... | collective-permute-start | bytes 3551240 | tf_op jit(solution)/shard_map/ppermute | solution.py:583
  409.1 10.4 %collective-permute-start.34 = (bf16[512,2304]{1,0:T(8,128)(2,1)}, bf16[512,2304]{1,0:T(8,128)(2,1)}, u32[]{:S(2)}, u32[]{:S(2)}) collective-permute-start(bf16[512,2304]{1,0:T(8,128)(2,1)} %pad_maximum_fusion), channel_id=1, source_target_pairs={{1,0},{3,2},{5,4},{7,6},{9,8},{11,10},{13,12},{15,14},{17,16},{19,... | collective-permute-start | bytes 7077896 | tf_op jit(solution)/shard_map/ppermute | solution.py:935
  428.7 32.4 %copy-start.30 = (bf16[2,512,896]{2,1,0:T(8,128)(2,1)}, bf16[2,512,896]{2,1,0:T(8,128)(2,1)S(1)}, u32[]{:S(2)}) copy-start(bf16[2,512,896]{2,1,0:T(8,128)(2,1)S(1)} %get-tuple-element.203.refs_2_) | copy-start | bytes 5505028
  436.2 34.9 %collective-permute-start.36 = (bf16[2,1088,1152]{2,1,0:T(8,128)(2,1)}, bf16[2,1088,1152]{2,1,0:T(8,128)(2,1)}, u32[]{:S(2)}, u32[]{:S(2)}) collective-permute-start(bf16[2,1088,1152]{2,1,0:T(8,128)(2,1)} %block_grads.10), channel_id=1, source_target_pairs={{0,1},{1,0},{2,3},{3,2},{4,5},{5,4},{6,7},{7,6},{8,9},{9,8},{10,11... | collective-permute-start | bytes 15040520 | tf_op jit(solution)/shard_map/ppermute | solution.py:583
  436.4 16.4 %collective-permute-start.45 = (bf16[272,1088]{1,0:T(8,128)(2,1)S(1)}, bf16[272,1088]{1,0:T(8,128)(2,1)S(1)}, u32[]{:S(2)}, u32[]{:S(2)}) collective-permute-start(bf16[272,1088]{1,0:T(8,128)(2,1)S(1)} %dynamic-slice_bitcast_fusion), channel_id=1, source_target_pairs={{0,16},{16,0},{1,17},{17,1},{2,18},{18,2},{3,19},{19,3},{4,20},{20... | collective-permute-start | bytes 1775624 | tf_op jit(solution)/shard_map/ppermute | solution.py:591
  437.9 18.0 %collective-permute-start.44 = (bf16[272,1088]{1,0:T(8,128)(2,1)S(1)}, bf16[272,1088]{1,0:T(8,128)(2,1)S(1)}, u32[]{:S(2)}, u32[]{:S(2)}) collective-permute-start(bf16[272,1088]{1,0:T(8,128)(2,1)S(1)} %slice_bitcast_fusion.4), channel_id=1, source_target_pairs={{0,2},{1,3},{2,0},{3,1},{4,6},{5,7},{6,4},{7,5},{8,10},{9,11},{10,... | collective-permute-start | bytes 1775624 | tf_op jit(solution)/shard_map/ppermute | solution.py:583
  440.4 40.4 %collective-permute-start.49 = (bf16[136,1088]{1,0:T(8,128)(2,1)}, bf16[136,1088]{1,0:T(8,128)(2,1)}, u32[]{:S(2)}, u32[]{:S(2)}) collective-permute-start(bf16[136,1088]{1,0:T(8,128)(2,1)} %get-tuple-element.286), channel_id=1, source_target_pairs={{0,4},{4,8},{8,12},{12,0},{1,5},{5,9},{9,13},{13,1},{2,6},{6,10},{... | collective-permute-start | bytes 887816 | tf_op jit(solution)/shard_map/ppermute | solution.py:596
  442.3 38.4 %collective-permute-start.51 = (bf16[136,1088]{1,0:T(8,128)(2,1)}, bf16[136,1088]{1,0:T(8,128)(2,1)}, u32[]{:S(2)}, u32[]{:S(2)}) collective-permute-start(bf16[136,1088]{1,0:T(8,128)(2,1)} %get-tuple-element.287), channel_id=1, source_target_pairs={{0,12},{4,0},{8,4},{12,8},{1,13},{5,1},{9,5},{13,9},{2,14},{6,2},{... | collective-permute-start | bytes 887816 | tf_op jit(solution)/shard_map/ppermute | solution.py:596
  452.8 29.4 %collective-permute-start.50 = (bf16[136,1088]{1,0:T(8,128)(2,1)}, bf16[136,1088]{1,0:T(8,128)(2,1)}, u32[]{:S(2)}, u32[]{:S(2)}) collective-permute-start(bf16[136,1088]{1,0:T(8,128)(2,1)} %get-tuple-element.288), channel_id=1, source_target_pairs={{0,8},{4,12},{8,0},{12,4},{1,9},{5,13},{9,1},{13,5},{2,10},{6,14},... | collective-permute-start | bytes 887816 | tf_op jit(solution)/shard_map/ppermute | solution.py:596
  467.5 1.3 collective-permute-start.35
  468.9 16.3 %collective-permute-start.46 = (bf16[136,1088]{1,0:T(8,128)(2,1)S(1)}, bf16[136,1088]{1,0:T(8,128)(2,1)S(1)}, u32[]{:S(2)}, u32[]{:S(2)}) collective-permute-start(bf16[136,1088]{1,0:T(8,128)(2,1)S(1)} %get-tuple-element.289), channel_id=1, source_target_pairs={{0,4},{4,8},{8,12},{12,0},{1,5},{5,9},{9,13},{13,1},{2,6},{6,10},{... | collective-permute-start | bytes 887816 | tf_op jit(solution)/shard_map/ppermute | solution.py:596
  471.1 16.2 %collective-permute-start.48 = (bf16[136,1088]{1,0:T(8,128)(2,1)S(1)}, bf16[136,1088]{1,0:T(8,128)(2,1)S(1)}, u32[]{:S(2)}, u32[]{:S(2)}) collective-permute-start(bf16[136,1088]{1,0:T(8,128)(2,1)S(1)} %get-tuple-element.290), channel_id=1, source_target_pairs={{0,12},{4,0},{8,4},{12,8},{1,13},{5,1},{9,5},{13,9},{2,14},{6,2},{... | collective-permute-start | bytes 887816 | tf_op jit(solution)/shard_map/ppermute | solution.py:596
  480.7 19.9 %collective-permute-start.47 = (bf16[136,1088]{1,0:T(8,128)(2,1)S(1)}, bf16[136,1088]{1,0:T(8,128)(2,1)S(1)}, u32[]{:S(2)}, u32[]{:S(2)}) collective-permute-start(bf16[136,1088]{1,0:T(8,128)(2,1)S(1)} %get-tuple-element.291), channel_id=1, source_target_pairs={{0,8},{4,12},{8,0},{12,4},{1,9},{5,13},{9,1},{13,5},{2,10},{6,14},... | collective-permute-start | bytes 887816 | tf_op jit(solution)/shard_map/ppermute | solution.py:596
  480.7 19.9 %copy-start.75 = (f32[136,1088]{1,0:T(8,128)S(1)}, f32[136,1088]{1,0:T(8,128)}, u32[]{:S(2)}) copy-start(f32[136,1088]{1,0:T(8,128)} %param.23) | copy-start | bytes 1775620
  480.7 19.9 %copy-start.83 = (f32[136,1088]{1,0:T(8,128)S(1)}, f32[136,1088]{1,0:T(8,128)}, u32[]{:S(2)}) copy-start(f32[136,1088]{1,0:T(8,128)} %param.33) | copy-start | bytes 1775620
  480.8 19.9 %copy-start.84 = (f32[136,1088]{1,0:T(8,128)S(1)}, f32[136,1088]{1,0:T(8,128)}, u32[]{:S(2)}) copy-start(f32[136,1088]{1,0:T(8,128)} %param.28) | copy-start | bytes 1775620
  480.8 29.4 %collective-permute-start.37 = (bf16[2,272,1152]{2,1,0:T(8,128)(2,1)S(1)}, bf16[2,272,1152]{2,1,0:T(8,128)(2,1)S(1)}, u32[]{:S(2)}, u32[]{:S(2)}) collective-permute-start(bf16[2,272,1152]{2,1,0:T(8,128)(2,1)S(1)} %get-tuple-element.209), channel_id=1, source_target_pairs={{0,16},{16,0},{1,17},{17,1},{2,18},{18,2},{3,19},{19,3},{4,20},{20... | collective-permute-start | bytes 3760136 | tf_op jit(solution)/shard_map/ppermute | solution.py:591
  503.3 30.4 %collective-permute-start.39 = (bf16[2,272,1152]{2,1,0:T(8,128)(2,1)S(1)}, bf16[2,272,1152]{2,1,0:T(8,128)(2,1)S(1)}, u32[]{:S(2)}, u32[]{:S(2)}) collective-permute-start(bf16[2,272,1152]{2,1,0:T(8,128)(2,1)S(1)} %copy-done.108), channel_id=1, source_target_pairs={{0,2},{1,3},{2,0},{3,1},{4,6},{5,7},{6,4},{7,5},{8,10},{9,11},{10,... | collective-permute-start | bytes 3760136 | tf_op jit(solution)/shard_map/ppermute | solution.py:583
  510.2 23.5 %copy-start.78 = (bf16[2,272,1152]{2,1,0:T(8,128)(2,1)S(1)}, bf16[2,272,1152]{2,1,0:T(8,128)(2,1)}, u32[]{:S(2)}) copy-start(bf16[2,272,1152]{2,1,0:T(8,128)(2,1)} %get-tuple-element.210) | copy-start | bytes 3760132
  510.6 35.7 %collective-permute-start.38 = (bf16[272,1152]{1,0:T(8,128)(2,1)S(1)}, bf16[272,1152]{1,0:T(8,128)(2,1)S(1)}, u32[]{:S(2)}, u32[]{:S(2)}) collective-permute-start(bf16[272,1152]{1,0:T(8,128)(2,1)S(1)} %slice_bitcast_fusion.2), channel_id=1, source_target_pairs={{0,2},{1,3},{2,0},{3,1},{4,6},{5,7},{6,4},{7,5},{8,10},{9,11},{10,... | collective-permute-start | bytes 1880072 | tf_op jit(solution)/shard_map/ppermute | solution.py:583
  534.1 14.4 %collective-permute-start.40 = (bf16[272,1152]{1,0:T(8,128)(2,1)S(1)}, bf16[272,1152]{1,0:T(8,128)(2,1)S(1)}, u32[]{:S(2)}, u32[]{:S(2)}) collective-permute-start(bf16[272,1152]{1,0:T(8,128)(2,1)S(1)} %dynamic-slice_bitcast_fusion.1), channel_id=1, source_target_pairs={{0,16},{16,0},{1,17},{17,1},{2,18},{18,2},{3,19},{19,3},{4,20},{20... | collective-permute-start | bytes 1880072 | tf_op jit(solution)/shard_map/ppermute | solution.py:591
  549.0 12.2 %collective-permute-start.41 = (bf16[136,1152]{1,0:T(8,128)(2,1)S(1)}, bf16[136,1152]{1,0:T(8,128)(2,1)S(1)}, u32[]{:S(2)}, u32[]{:S(2)}) collective-permute-start(bf16[136,1152]{1,0:T(8,128)(2,1)S(1)} %get-tuple-element.292), channel_id=1, source_target_pairs={{0,4},{4,8},{8,12},{12,0},{1,5},{5,9},{9,13},{13,1},{2,6},{6,10},{... | collective-permute-start | bytes 940040 | tf_op jit(solution)/shard_map/ppermute | solution.py:596
  549.0 14.6 %collective-permute-start.43 = (bf16[136,1152]{1,0:T(8,128)(2,1)S(1)}, bf16[136,1152]{1,0:T(8,128)(2,1)S(1)}, u32[]{:S(2)}, u32[]{:S(2)}) collective-permute-start(bf16[136,1152]{1,0:T(8,128)(2,1)S(1)} %get-tuple-element.293), channel_id=1, source_target_pairs={{0,12},{4,0},{8,4},{12,8},{1,13},{5,1},{9,5},{13,9},{2,14},{6,2},{... | collective-permute-start | bytes 940040 | tf_op jit(solution)/shard_map/ppermute | solution.py:596
  552.9 23.5 %collective-permute-start.42 = (bf16[136,1152]{1,0:T(8,128)(2,1)S(1)}, bf16[136,1152]{1,0:T(8,128)(2,1)S(1)}, u32[]{:S(2)}, u32[]{:S(2)}) collective-permute-start(bf16[136,1152]{1,0:T(8,128)(2,1)S(1)} %get-tuple-element.294), channel_id=1, source_target_pairs={{0,8},{4,12},{8,0},{12,4},{1,9},{5,13},{9,1},{13,5},{2,10},{6,14},... | collective-permute-start | bytes 940040 | tf_op jit(solution)/shard_map/ppermute | solution.py:596
  555.0 22.4 %copy-start.80 = (f32[272,136]{0,1:T(8,128)S(1)}, f32[272,136]{0,1:T(8,128)}, u32[]{:S(2)}) copy-start(f32[272,136]{0,1:T(8,128)} %param.22) | copy-start | bytes 443908
  (98 other events, 621.5 us)

commit v7 on v6

--- a/solution.py
+++ b/solution.py
@@ -339,6 +339,43 @@
         compiler_params=pltpu.CompilerParams(vmem_limit_bytes=48 << 20),
         name="multiply_and_place",
     )(places, *operands)
+
+
+def add_product_kernel(each, blocks_own, blocks_oth, own, oth, start, out):
+    step = pl.program_id(0)
+
+    @pl.when(step == 0)
+    def _():
+        out[...] = start[...]
+
+    for k, (blocks, weights) in enumerate(((blocks_own, own), (blocks_oth, oth))):
+
+        @pl.when(step // each == k)
+        def _(blocks=blocks, weights=weights):
+            out[...] += contract_last(blocks[0], weights[0])
+
+
+def add_products(start, blocks_own, blocks_oth, own, oth, lane_block):
+    each, count, lanes = blocks_own.shape
+    width = own.shape[1]
+
+    def stepped(shape, k, lane):
+        return pl.BlockSpec(
+            (1, *shape), lambda j: (jnp.clip(j - k * each, 0, each - 1), 0, lane)
+        )
+
+    whole = pl.BlockSpec((count, width), lambda j: (0, 0))
+    return pl.pallas_call(
+        functools.partial(add_product_kernel, each),
+        grid=(2 * each,),
+        in_specs=[stepped((count, lanes), k, 0) for k in range(2)]
+        + [stepped((width, lanes), k, lane_block) for k in range(2)]
+        + [whole],
+        out_specs=whole,
+        out_shape=jax.ShapeDtypeStruct((count, width), f32),
+        compiler_params=pltpu.CompilerParams(vmem_limit_bytes=48 << 20),
+        name="add_products",
+    )(blocks_own, blocks_oth, own, oth, start)
 
 
 def split_all(column, cols, write):
@@ -784,7 +821,8 @@
         up_rows = spread_rows(up_block)
         down_block, up_rows = together(down_block, up_rows)
         down_rows = spread_rows(down_block)
-        attn_own = assemble(spread_two(attn_one))
+        attn_two, up_rows = together(spread_two(attn_one), up_rows)
+        attn_own = assemble(attn_two)
         up_one = spread_one(up_rows)
     else:
         attn_own, up_own, down_own = [
@@ -846,10 +884,9 @@
         [mixed_shape] * 2,
         "split_mixed",
     )
-    residual = inputs + vec[4]
-    for blocks, weights in ((mixed_own, attn_own), (mixed_oth, attn_oth)):
-        for i in range(each):
-            residual = residual + contract_last(blocks[i], weights[i][:, lead_out:])
+    residual = add_products(
+        inputs + vec[4], mixed_own, mixed_oth, attn_own, attn_oth, lead_out // lanes_out
+    )
     normed_two, scaled_two, inverse_two = normalize(residual, vec[5], vec[6])
     normed_two_low = normed_two.astype(bf16)
 
@@ -905,13 +942,14 @@
         up_own, down_own, linear_own, grad_normed_two
     )
     one_down = scatter_one(total_down)
+    dups_own, grad_normed_two, one_down = together(dups_own, grad_normed_two, one_down)
 
     grad_residual = cotangent.astype(f32) + norm_back(
         grad_normed_two, scaled_two, inverse_two, vec[5]
     )
     total_up = block_grads([(left_up, dups_own)], None, received_up, staged)
     grad_residual_low = grad_residual.astype(bf16)
-    grad_residual_low, total_up, one_down = together(grad_residual_low, total_up, one_down)
+    grad_residual_low, total_up = together(grad_residual_low, total_up)
     two_down = scatter_two(one_down)
     grad_mixed = multiply_and_place(
         jnp.concatenate([places_own, places_oth]),
@@ -980,7 +1018,9 @@
     ).reshape(each, width, LANES)
     total_attn = block_grads(pairs_own, vec_here, received, staged)
     sum_down, sum_up = scatter_three(two_down), scatter_three(two_up)
-    sum_attn = scatter_three(scatter_two(scatter_one(total_attn)))
+    one_attn = scatter_one(total_attn)
+    sum_down, sum_up, one_attn = together(sum_down, sum_up, one_attn)
+    sum_attn = scatter_three(scatter_two(one_attn))
     sum_qkv = sum_attn[:, : 3 * piece].reshape(rows_own, 3, piece)
     sum_out = sum_attn[:, 3 * piece : width].T
     sum_vector = sum_attn[:vec_lines, width:].reshape(-1)[:vec_count].reshape(vec_shape)

time: 589 us -> 576 us (0.978)
  waiting for transfers between devices: 217 us -> 175 us
  starting transfers between devices: 63.2 us -> 82.7 us
  local copies, waits for them, and re-layouts: 58.4 us -> 69.2 us
  matrix products: 15.8 us -> 7.47 us
  Pallas kernels: 169 us -> 175 us
    ppermute x20, waiting for transfers between devices: 74.5 us -> 34 us  [flip_col(): lax.ppermute(block, 'col', [(c, c ^ bit) for c in range(lax.axis_size('co...]
    ppermute x12, waiting for transfers between devices: 47.8 us -> 64.7 us  [flip_dp(): return lax.ppermute(block, 'dp', [(0, 1), (1, 0)])]
    ppermute x18, waiting for transfers between devices: 88.1 us -> 75.2 us  [shift_row(): lax.ppermute(block, 'row', [(i, (i + by) % count) for i in range(count)])]
    ppermute x18, starting transfers between devices: 28.9 us -> 39.7 us  [shift_row(): lax.ppermute(block, 'row', [(i, (i + by) % count) for i in range(count)])]
    ppermute x20, starting transfers between devices: 15.8 us -> 25.3 us  [flip_col(): lax.ppermute(block, 'col', [(c, c ^ bit) for c in range(lax.axis_size('co...]
    dot_general x8 -> x4, matrix products: 15.8 us -> 7.47 us  [contract(): lax.dot_general(left, right, (((left_dim,), (right_dim,)), ((), ())), pre...]
    pallas_call x0 -> x1, Pallas kernels: none -> 6.19 us  [add_products(): pl.pallas_call(functools.partial(add_product_kernel, each), grid=(2 * eac...]
    unnamed x220 -> x249, local copies, waits for them, and re-layouts: 24.1 us -> 26 us
  transfers between devices with their start and end apart: 52 -> 52, of which waited for: 26 -> 24; matrix products, arithmetic and copies ran while one was open for 16% -> 18% of each run, Pallas kernels for 23% -> 24%
where the time goes in v7:
time: 576 us; the launch traced here: 571 us
  waiting for transfers between devices  175 us (30%)
  Pallas kernels  175 us (30%)
  starting transfers between devices  82.7 us (14%)
  local copies, waits for them, and re-layouts  69.2 us (12%)
  other arithmetic  59.2 us (10%)
  matrix products  7.47 us (1%)
    ppermute x18, waiting for transfers between devices, shift_row(): lax.ppermute(block, 'row', [(i, (i + by) % count) for i in range(count)])  75.2 us
    ppermute x12, waiting for transfers between devices, flip_dp(): return lax.ppermute(block, 'dp', [(0, 1), (1, 0)])  64.7 us
    pallas_call x4, Pallas kernels, feed_call(): pl.pallas_call(functools.partial(kernel, before is not None), grid=(each,...  54.2 us
    ppermute x18, starting transfers between devices, shift_row(): lax.ppermute(block, 'row', [(i, (i + by) % count) for i in range(count)])  39.7 us
    pallas_call x6, Pallas kernels, block_grads(): pl.pallas_call(functools.partial(block_grads_kernel, [len(r) for r in rig...  34.9 us
    ppermute x20, waiting for transfers between devices, flip_col(): lax.ppermute(block, 'col', [(c, c ^ bit) for c in range(lax.axis_size('co...  34 us
    unnamed x249, local copies, waits for them, and re-layouts  26 us
    ppermute x20, starting transfers between devices, flip_col(): lax.ppermute(block, 'col', [(c, c ^ bit) for c in range(lax.axis_size('co...  25.3 us
  transfers between devices with their start and end apart: 52, of which 24 were waited for; matrix products, arithmetic and copies ran while one was open for 18% of the time, Pallas kernels for 24%

profile of v7, /device:TPU:0, one launch (start us, length us, event | category | flops | bytes accessed | tf_op | source)
XLA Modules:
  0.0 571.0 jit_solution(1252360357707923254)
XLA Ops:
  2.7 3.1 collective-permute-start
  5.8 2.6 collective-permute-start.1
  9.8 6.4 %collective-permute-done = bf16[136,1152]{1,0:T(8,128)(2,1)S(1)} collective-permute-done((bf16[136,1152]{1,0:T(8,128)(2,1)S(1)}, bf16[136,1152]{1,0:T(8,128)(2,1)S(1)}, u32[]{:S(2)}, u32[]{:S(2)}) %collective-permute-start) | collective-permute-done | bytes 313376 | tf_op jit(solution)/shard_map/ppermute | solution.py:633
  16.2 12.6 %collective-permute-done.1 = bf16[136,1152]{1,0:T(8,128)(2,1)S(1)} collective-permute-done((bf16[136,1152]{1,0:T(8,128)(2,1)S(1)}, bf16[136,1152]{1,0:T(8,128)(2,1)S(1)}, u32[]{:S(2)}, u32[]{:S(2)}) %collective-permute-start.1) | collective-permute-done | bytes 313376 | tf_op jit(solution)/shard_map/ppermute | solution.py:633
  32.1 12.8 %collective-permute-done.3.refs_1_ = bf16[2,136,1152]{2,1,0:T(8,128)(2,1)S(1)} collective-permute-done((bf16[2,136,1152]{2,1,0:T(8,128)(2,1)S(1)}, bf16[2,136,1152]{2,1,0:T(8,128)(2,1)S(1)}, u32[]{:S(2)}, u32[]{:S(2)}) %collective-permute-start.3) | collective-permute-done | bytes 626720 | tf_op jit(solution)/shard_map/ppermute | solution.py:620
  50.2 7.3 %collective-permute-start.7 = (bf16[136,1088]{1,0:T(8,128)(2,1)S(1)}, bf16[136,1088]{1,0:T(8,128)(2,1)}, u32[]{:S(2)}, u32[]{:S(2)}) collective-permute-start(bf16[136,1088]{1,0:T(8,128)(2,1)S(1)} %convert_element_type.277), channel_id=1, source_target_pairs={{0,4},{4,8},{8,12},{12,0},{1,5},{5,9},{9,13},{13,1},{2,6},{6,10},{... | collective-permute-start | bytes 887816 | tf_op jit(solution)/shard_map/ppermute | solution.py:633
  60.0 6.0 %collective-permute-done.7 = bf16[136,1088]{1,0:T(8,128)(2,1)} collective-permute-done((bf16[136,1088]{1,0:T(8,128)(2,1)S(1)}, bf16[136,1088]{1,0:T(8,128)(2,1)}, u32[]{:S(2)}, u32[]{:S(2)}) %collective-permute-start.7) | collective-permute-done | bytes 295968 | tf_op jit(solution)/shard_map/ppermute | solution.py:633
  66.0 10.2 %collective-permute-done.8 = bf16[136,1088]{1,0:T(8,128)(2,1)} collective-permute-done((bf16[136,1088]{1,0:T(8,128)(2,1)S(1)}, bf16[136,1088]{1,0:T(8,128)(2,1)}, u32[]{:S(2)}, u32[]{:S(2)}) %collective-permute-start.8) | collective-permute-done | bytes 295968 | tf_op jit(solution)/shard_map/ppermute | solution.py:633
  77.3 5.1 assemble.3
  85.6 7.4 %collective-permute-start.14 = (bf16[136,1088]{1,0:T(8,128)(2,1)S(1)}, bf16[136,1088]{1,0:T(8,128)(2,1)}, u32[]{:S(2)}, u32[]{:S(2)}) collective-permute-start(bf16[136,1088]{1,0:T(8,128)(2,1)S(1)} %convert_bitcast_fusion), channel_id=1, source_target_pairs={{0,4},{4,8},{8,12},{12,0},{1,5},{5,9},{9,13},{13,1},{2,6},{6,10},{... | collective-permute-start | bytes 887816 | tf_op jit(solution)/shard_map/ppermute | solution.py:633
  93.1 2.2 collective-permute-start.15
  102.5 13.5 %collective-permute-done.11.refs_1_ = bf16[2,136,1088]{2,1,0:T(8,128)(2,1)S(1)} collective-permute-done((bf16[2,136,1088]{2,1,0:T(8,128)(2,1)S(1)}, bf16[2,136,1088]{2,1,0:T(8,128)(2,1)S(1)}, u32[]{:S(2)}, u32[]{:S(2)}) %collective-permute-start.11) | collective-permute-done | bytes 591904 | tf_op jit(solution)/shard_map/ppermute | solution.py:620
  116.5 3.3 convert_add_fusion
  119.9 11.9 %collective-permute-done.12.refs_3_ = bf16[2,136,1088]{2,1,0:T(8,128)(2,1)S(1)} collective-permute-done((bf16[2,136,1088]{2,1,0:T(8,128)(2,1)S(1)}, bf16[2,136,1088]{2,1,0:T(8,128)(2,1)S(1)}, u32[]{:S(2)}, u32[]{:S(2)}) %collective-permute-start.12) | collective-permute-done | bytes 591904 | tf_op jit(solution)/shard_map/ppermute | solution.py:628
  133.3 7.2 %multiply_and_place.3.refs_2_ = bf16[512,3456]{1,0:T(8,128)(2,1)S(1)} custom-call(s32[2]{0:T(128)S(1)} %fusion.48.places, bf16[512,1088]{1,0:T(8,128)(2,1)S(1)} %copy.116.x, bf16[2,1088,1152]{2,1,0:T(8,128)(2,1)} %bitcast.198, f32[1,3456]{1,0:T(1,128)S(1)} %reshape.254.refs_1_), custom_call_target="tpu_custom_call" | custom-call | tf_op jit(solution)/shard_map/multiply_and_place/pallas_call | solution.py:327
  146.7 8.5 %multiply_and_place.4.q.k_own.v_own = bf16[512,3456]{1,0:T(8,128)(2,1)S(1)} custom-call(s32[2]{0:T(128)S(1)} %add_xor_fusion.places, bf16[512,1088]{1,0:T(8,128)(2,1)S(1)} %copy-done.9, bf16[2,1088,1152]{2,1,0:T(8,128)(2,1)} %collective-permute-done.13.refs_0_.oth.refs_1_, f32[1,3456]{1,0:T(1,128)S(1)} %reshape.254.refs_1_, bf16[512,3456]{1,0:T(8,128)(2,1)} %copy-done.7), custom_call_target="tpu_custom_call" | custom-call | tf_op jit(solution)/shard_map/multiply_and_place/pallas_call | solution.py:327
  155.3 3.5 collective-permute-done.17.refs_1_
  158.8 2.2 collective-permute-done.18.refs_3_
  162.6 3.0 collective-permute-start.19
  169.8 3.2 copy.119.start
  178.2 16.7 %attention_forward.1 = (bf16[512,1152]{1,0:T(8,128)(2,1)S(1)}, f32[9,2,512]{2,1,0:T(2,128)S(1)}) custom-call(s32[1]{0:T(128)} %bitcast.1.later, s32[1,512]{1,0:T(1,128)S(1)} %bitcast.194, s32[512,1]{1,0:T(8,128)S(1)} %copy.117.kseg_own, s32[512,1]{1,0:T(8,128)S(1)} %copy.118.kseg_oth, bf16[512,3456]{1,0:T(8,128)(2,1)} %copy-done, bf16[512,3456]{1,0:T(8,128)(2,1)} %copy-done, ...), custom_call_target="tpu_custom_call" | custom-call | tf_op jit(solution)/shard_map/attention_forward/pallas_call | solution.py:232
  194.9 2.6 collective-permute-done.20
  200.4 6.2 %add_products.1 = f32[512,1088]{1,0:T(8,128)S(1)} custom-call(bf16[2,512,384]{2,1,0:T(8,128)(2,1)S(1)} %get-tuple-element.165.blocks_own.refs_3_, bf16[2,512,384]{2,1,0:T(8,128)(2,1)S(1)} %get-tuple-element.166.blocks_oth.refs_3_, bf16[2,1088,1152]{2,1,0:T(8,128)(2,1)} %bitcast.199, bf16[2,1088,1152]{2,1,0:T(8,128)(2,1)} %collective-permute-done.13.refs_0_.oth.refs_1_, ...), custom_call_target="tpu_custom_call" | custom-call | tf_op jit(solution)/shard_map/add_products/pallas_call | solution.py:368
  210.5 2.0 multiply_reduce_fusion.2
  212.6 2.2 add_convert_fusion.7
  214.8 5.1 collective-permute-done.22
  221.5 4.7 assemble.4
  226.3 5.1 assemble.5
  232.0 3.0 rev.26
  239.0 12.9 %feed_forward.2 = (f32[2,512,1088]{2,1,0:T(8,128)}, bf16[2,512,1088]{2,1,0:T(8,128)(2,1)}, f32[512,1088]{1,0:T(8,128)}) custom-call(bf16[512,1088]{1,0:T(8,128)(2,1)} %copy.123.x, bf16[2,1088,1088]{2,1,0:T(8,128)(2,1)} %bitcast.202, f32[2,1,1088]{2,1,0:T(1,128)} %copy.122.bias, bf16[2,1088,1088]{2,1,0:T(8,128)(2,1)} %bitcast.205), custom_call_target="tpu_custom_call" | custom-call | tf_op jit(solution)/shard_map/feed_forward/pallas_call | solution.py:597
  252.0 13.0 %feed_forward.3 = (f32[2,512,1088]{2,1,0:T(8,128)}, bf16[2,512,1088]{2,1,0:T(8,128)(2,1)}, f32[512,1088]{1,0:T(8,128)}) custom-call(bf16[512,1088]{1,0:T(8,128)(2,1)} %copy.123.x, bf16[2,1088,1088]{2,1,0:T(8,128)(2,1)} %collective-permute-done.24.up, f32[2,1,1088]{2,1,0:T(1,128)} %reshape.260.bias, bf16[2,1088,1088]{2,1,0:T(8,128)(2,1)} %collective-permute-done.25.down, ...), custom_call_target="tpu_custom_call" | custom-call | tf_op jit(solution)/shard_map/feed_forward/pallas_call | solution.py:597
  266.6 4.9 block_grads.6
  274.1 13.9 %feed_backward.2 = (bf16[2,512,1088]{2,1,0:T(8,128)(2,1)}, f32[2,1,1088]{2,1,0:T(1,128)}, f32[512,1088]{1,0:T(8,128)}) custom-call(bf16[512,1088]{1,0:T(8,128)(2,1)} %copy.125.grad, bf16[2,1088,1088]{2,1,0:T(8,128)(2,1)} %collective-permute-done.24.up, bf16[2,1088,1088]{2,1,0:T(8,128)(2,1)} %collective-permute-done.25.down, ...), custom_call_target="tpu_custom_call" | custom-call | tf_op jit(solution)/shard_map/feed_backward/pallas_call | solution.py:597
  289.7 4.8 block_grads.7
  294.4 5.1 fusion.58
  299.5 6.6 %block_grads.8 = (bf16[2,272,1088]{2,1,0:T(8,128)(2,1)S(1)}, bf16[2,272,1088]{2,1,0:T(8,128)(2,1)S(1)}, bf16[2,272,1088]{2,1,0:T(8,128)(2,1)S(1)}, bf16[2,272,1088]{2,1,0:T(8,128)(2,1)}) custom-call(s32[1]{0:T(128)} %bitcast.5.place, bf16[1088,512]{1,0:T(8,128)(2,1)S(1)} %bitcast.174, bf16[2,512,1088]{2,1,0:T(8,128)(2,1)} %get-tuple-element.192.refs_1_, ...), custom_call_target="tpu_custom_call" | custom-call | tf_op jit(solution)/shard_map/block_grads/pallas_call | solution.py:515
  308.5 5.1 slice_bitcast_fusion.1
  313.7 14.5 %feed_backward.3 = (bf16[2,512,1088]{2,1,0:T(8,128)(2,1)}, f32[2,1,1088]{2,1,0:T(1,128)}, f32[512,1088]{1,0:T(8,128)}) custom-call(bf16[512,1088]{1,0:T(8,128)(2,1)} %copy.125.grad, bf16[2,1088,1088]{2,1,0:T(8,128)(2,1)} %bitcast.203, bf16[2,1088,1088]{2,1,0:T(8,128)(2,1)} %bitcast.206, f32[2,512,1088]{2,1,0:T(8,128)} %get-tuple-element.198.linear, ...), custom_call_target="tpu_custom_call" | custom-call | tf_op jit(solution)/shard_map/feed_backward/pallas_call | solution.py:597
  328.1 8.1 %collective-permute-done.27 = bf16[2,272,1088]{2,1,0:T(8,128)(2,1)} collective-permute-done((bf16[2,272,1088]{2,1,0:T(8,128)(2,1)S(1)}, bf16[2,272,1088]{2,1,0:T(8,128)(2,1)}, u32[]{:S(2)}, u32[]{:S(2)}) %collective-permute-start.27) | collective-permute-done | bytes 1183776 | tf_op jit(solution)/shard_map/ppermute | solution.py:628
  336.2 2.7 add_convert_fusion.5
  338.9 2.6 add_convert_fusion.4
  341.5 3.1 copy.126
  344.6 2.1 dynamic-slice_bitcast_fusion.2
  351.1 2.4 multiply_reduce_fusion
  356.6 5.8 %block_grads.9 = (bf16[2,272,1088]{2,1,0:T(8,128)(2,1)S(1)}, bf16[2,272,1088]{2,1,0:T(8,128)(2,1)S(1)}, bf16[2,272,1088]{2,1,0:T(8,128)(2,1)S(1)}, bf16[2,272,1088]{2,1,0:T(8,128)(2,1)S(1)}) custom-call(s32[1]{0:T(128)} %bitcast.5.place, bf16[1088,512]{1,0:T(8,128)(2,1)S(1)} %bitcast.176, bf16[2,512,1088]{2,1,0:T(8,128)(2,1)} %get-tuple-element.207.refs_1_, ...), custom_call_target="tpu_custom_call" | custom-call | tf_op jit(solution)/shard_map/block_grads/pallas_call | solution.py:515
  370.9 6.5 %multiply_and_place.5.grad = bf16[512,1152]{1,0:T(8,128)(2,1)S(1)} custom-call(s32[4]{0:T(128)S(1)} %pad_add_fusion.1.places, bf16[512,1088]{1,0:T(8,128)(2,1)S(1)} %copy-done.24, bf16[2,1088,1152]{2,1,0:T(8,128)(2,1)} %bitcast.200, bf16[2,1088,1152]{2,1,0:T(8,128)(2,1)} %collective-permute-done.13.refs_0_.oth.refs_1_), custom_call_target="tpu_custom_call" | custom-call | tf_op jit(solution)/shard_map/multiply_and_place/pallas_call | solution.py:327
  378.5 19.8 %attention_backward.1 = (bf16[512,1152]{1,0:T(8,128)(2,1)S(1)}, bf16[512,1152]{1,0:T(8,128)(2,1)S(1)}, bf16[512,1152]{1,0:T(8,128)(2,1)S(1)}, bf16[512,1152]{1,0:T(8,128)(2,1)S(1)}, bf16[512,1152]{1,0:T(8,128)(2,1)}) custom-call(s32[1]{0:T(128)} %bitcast.1.later, s32[1,512]{1,0:T(1,128)S(1)} %bitcast.195, s32[512,1]{1,0:T(8,128)S(1)} %copy-done.42, ...), custom_call_target="tpu_custom_call" | custom-call | tf_op jit(solution)/shard_map/attention_backward/pallas_call | solution.py:255
  410.6 2.6 copy.135
  415.2 2.3 collective-permute-start.37
  423.7 5.2 split_grads.1
  428.9 2.2 copy-done.47
  431.0 5.3 block_grads.10
  436.3 9.0 %collective-permute-start.44 = (bf16[2,1088,1152]{2,1,0:T(8,128)(2,1)}, bf16[2,1088,1152]{2,1,0:T(8,128)(2,1)}, u32[]{:S(2)}, u32[]{:S(2)}) collective-permute-start(bf16[2,1088,1152]{2,1,0:T(8,128)(2,1)} %block_grads.10), channel_id=1, source_target_pairs={{0,1},{1,0},{2,3},{3,2},{4,5},{5,4},{6,7},{7,6},{8,9},{9,8},{10,11... | collective-permute-start | bytes 15040520 | tf_op jit(solution)/shard_map/ppermute | solution.py:620
  448.8 3.5 collective-permute-start.42
  458.5 3.4 fusion.13
  462.6 17.6 %collective-permute-done.41 = bf16[136,1088]{1,0:T(8,128)(2,1)} collective-permute-done((bf16[136,1088]{1,0:T(8,128)(2,1)}, bf16[136,1088]{1,0:T(8,128)(2,1)}, u32[]{:S(2)}, u32[]{:S(2)}) %collective-permute-start.41) | collective-permute-done | bytes 295968 | tf_op jit(solution)/shard_map/ppermute | solution.py:633
  481.8 7.7 %block_grads.11 = (bf16[2,272,1152]{2,1,0:T(8,128)(2,1)S(1)}, bf16[2,272,1152]{2,1,0:T(8,128)(2,1)S(1)}, bf16[2,272,1152]{2,1,0:T(8,128)(2,1)}, bf16[2,272,1152]{2,1,0:T(8,128)(2,1)}) custom-call(s32[1]{0:T(128)} %bitcast.5.place, bf16[1088,512]{1,0:T(8,128)(2,1)S(1)} %bitcast.178, bf16[1088,512]{1,0:T(8,128)(2,1)S(1)} %bitcast.180, ...), custom_call_target="tpu_custom_call" | custom-call | tf_op jit(solution)/shard_map/block_grads/pallas_call | solution.py:515
  491.5 2.1 fusion.12
  493.7 24.5 %collective-permute-done.45 = bf16[2,272,1152]{2,1,0:T(8,128)(2,1)S(1)} collective-permute-done((bf16[2,272,1152]{2,1,0:T(8,128)(2,1)S(1)}, bf16[2,272,1152]{2,1,0:T(8,128)(2,1)S(1)}, u32[]{:S(2)}, u32[]{:S(2)}) %collective-permute-start.45) | collective-permute-done | bytes 1253408 | tf_op jit(solution)/shard_map/ppermute | solution.py:628
  523.6 10.1 %collective-permute-done.48 = bf16[272,1152]{1,0:T(8,128)(2,1)S(1)} collective-permute-done((bf16[272,1152]{1,0:T(8,128)(2,1)S(1)}, bf16[272,1152]{1,0:T(8,128)(2,1)S(1)}, u32[]{:S(2)}, u32[]{:S(2)}) %collective-permute-start.48) | collective-permute-done | bytes 626720 | tf_op jit(solution)/shard_map/ppermute | solution.py:628
  535.1 3.7 collective-permute-start.50
  543.7 20.8 %collective-permute-done.50 = bf16[136,1152]{1,0:T(8,128)(2,1)S(1)} collective-permute-done((bf16[136,1152]{1,0:T(8,128)(2,1)S(1)}, bf16[136,1152]{1,0:T(8,128)(2,1)S(1)}, u32[]{:S(2)}, u32[]{:S(2)}) %collective-permute-start.50) | collective-permute-done | bytes 313376 | tf_op jit(solution)/shard_map/ppermute | solution.py:633
  565.4 2.1 multiply_subtract_fusion.3
  567.5 2.7 multiply_subtract_fusion.2
  (465 shorter events, 130.0 us)
Async XLA Ops:
  2.7 13.5 %collective-permute-start = (bf16[136,1152]{1,0:T(8,128)(2,1)S(1)}, bf16[136,1152]{1,0:T(8,128)(2,1)S(1)}, u32[]{:S(2)}, u32[]{:S(2)}) collective-permute-start(bf16[136,1152]{1,0:T(8,128)(2,1)S(1)} %concatenate.26), channel_id=1, source_target_pairs={{0,4},{4,8},{8,12},{12,0},{1,5},{5,9},{9,13},{13,1},{2,6},{6,10},{... | collective-permute-start | bytes 940040 | tf_op jit(solution)/shard_map/ppermute | solution.py:633
  5.8 23.0 %collective-permute-start.1 = (bf16[136,1152]{1,0:T(8,128)(2,1)S(1)}, bf16[136,1152]{1,0:T(8,128)(2,1)S(1)}, u32[]{:S(2)}, u32[]{:S(2)}) collective-permute-start(bf16[136,1152]{1,0:T(8,128)(2,1)S(1)} %concatenate.26), channel_id=1, source_target_pairs={{0,8},{4,12},{8,0},{12,4},{1,9},{5,13},{9,1},{13,5},{2,10},{6,14},... | collective-permute-start | bytes 940040 | tf_op jit(solution)/shard_map/ppermute | solution.py:633
  8.4 20.4 %collective-permute-start.2 = (bf16[136,1152]{1,0:T(8,128)(2,1)S(1)}, bf16[136,1152]{1,0:T(8,128)(2,1)S(1)}, u32[]{:S(2)}, u32[]{:S(2)}) collective-permute-start(bf16[136,1152]{1,0:T(8,128)(2,1)S(1)} %concatenate.26), channel_id=1, source_target_pairs={{0,12},{4,0},{8,4},{12,8},{1,13},{5,1},{9,5},{13,9},{2,14},{6,2},{... | collective-permute-start | bytes 940040 | tf_op jit(solution)/shard_map/ppermute | solution.py:633
  28.9 16.0 %collective-permute-start.3 = (bf16[2,136,1152]{2,1,0:T(8,128)(2,1)S(1)}, bf16[2,136,1152]{2,1,0:T(8,128)(2,1)S(1)}, u32[]{:S(2)}, u32[]{:S(2)}) collective-permute-start(bf16[2,136,1152]{2,1,0:T(8,128)(2,1)S(1)} %get-tuple-element.141.refs_0_), channel_id=1, source_target_pairs={{0,2},{1,3},{2,0},{3,1},{4,6},{5,7},{6,4},{7,5},{8,10},{9,11},{10,... | collective-permute-start | bytes 1880072 | tf_op jit(solution)/shard_map/ppermute | solution.py:620
  30.5 17.0 %collective-permute-start.4 = (bf16[2,136,1152]{2,1,0:T(8,128)(2,1)S(1)}, bf16[2,136,1152]{2,1,0:T(8,128)(2,1)S(1)}, u32[]{:S(2)}, u32[]{:S(2)}) collective-permute-start(bf16[2,136,1152]{2,1,0:T(8,128)(2,1)S(1)} %get-tuple-element.143.refs_2_), channel_id=1, source_target_pairs={{0,16},{16,0},{1,17},{17,1},{2,18},{18,2},{3,19},{19,3},{4,20},{20... | collective-permute-start | bytes 1880072 | tf_op jit(solution)/shard_map/ppermute | solution.py:628
  46.1 30.4 %collective-permute-start.5 = (bf16[2,2,136,1152]{3,2,1,0:T(8,128)(2,1)}, bf16[2,2,136,1152]{3,2,1,0:T(8,128)(2,1)}, u32[]{:S(2)}, u32[]{:S(2)}) collective-permute-start(bf16[2,2,136,1152]{3,2,1,0:T(8,128)(2,1)} %pad_maximum_fusion.1), channel_id=1, source_target_pairs={{0,16},{16,0},{1,17},{17,1},{2,18},{18,2},{3,19},{19,3},{4,20},{20... | collective-permute-start | bytes 3760136 | tf_op jit(solution)/shard_map/ppermute | solution.py:628
  48.8 28.6 %collective-permute-start.6 = (bf16[2,2,136,1152]{3,2,1,0:T(8,128)(2,1)}, bf16[2,2,136,1152]{3,2,1,0:T(8,128)(2,1)}, u32[]{:S(2)}, u32[]{:S(2)}) collective-permute-start(bf16[2,2,136,1152]{3,2,1,0:T(8,128)(2,1)} %pad_maximum_fusion.2), channel_id=1, source_target_pairs={{0,2},{1,3},{2,0},{3,1},{4,6},{5,7},{6,4},{7,5},{8,10},{9,11},{10,... | collective-permute-start | bytes 3760136 | tf_op jit(solution)/shard_map/ppermute | solution.py:620
  50.2 15.8 %collective-permute-start.7 = (bf16[136,1088]{1,0:T(8,128)(2,1)S(1)}, bf16[136,1088]{1,0:T(8,128)(2,1)}, u32[]{:S(2)}, u32[]{:S(2)}) collective-permute-start(bf16[136,1088]{1,0:T(8,128)(2,1)S(1)} %convert_element_type.277), channel_id=1, source_target_pairs={{0,4},{4,8},{8,12},{12,0},{1,5},{5,9},{9,13},{13,1},{2,6},{6,10},{... | collective-permute-start | bytes 887816 | tf_op jit(solution)/shard_map/ppermute | solution.py:633
  57.5 18.6 %collective-permute-start.8 = (bf16[136,1088]{1,0:T(8,128)(2,1)S(1)}, bf16[136,1088]{1,0:T(8,128)(2,1)}, u32[]{:S(2)}, u32[]{:S(2)}) collective-permute-start(bf16[136,1088]{1,0:T(8,128)(2,1)S(1)} %convert_element_type.277), channel_id=1, source_target_pairs={{0,8},{4,12},{8,0},{12,4},{1,9},{5,13},{9,1},{13,5},{2,10},{6,14},... | collective-permute-start | bytes 887816 | tf_op jit(solution)/shard_map/ppermute | solution.py:633
  58.1 18.4 %collective-permute-start.9 = (bf16[136,1088]{1,0:T(8,128)(2,1)S(1)}, bf16[136,1088]{1,0:T(8,128)(2,1)}, u32[]{:S(2)}, u32[]{:S(2)}) collective-permute-start(bf16[136,1088]{1,0:T(8,128)(2,1)S(1)} %convert_element_type.277), channel_id=1, source_target_pairs={{0,12},{4,0},{8,4},{12,8},{1,13},{5,1},{9,5},{13,9},{2,14},{6,2},{... | collective-permute-start | bytes 887816 | tf_op jit(solution)/shard_map/ppermute | solution.py:633
  60.0 22.4 %copy-start.61 = (s32[2]{0:T(128)}, s32[2]{0:T(128)S(1)}, u32[]{:S(2)}) copy-start(s32[2]{0:T(128)S(1)} %pad_add_fusion.place) | copy-start | bytes 28
  82.4 64.3 %collective-permute-start.13 = (bf16[2,1088,1152]{2,1,0:T(8,128)(2,1)}, bf16[2,1088,1152]{2,1,0:T(8,128)(2,1)}, u32[]{:S(2)}, u32[]{:S(2)}) collective-permute-start(bf16[2,1088,1152]{2,1,0:T(8,128)(2,1)} %bitcast.196), channel_id=1, source_target_pairs={{0,1},{1,0},{2,3},{3,2},{4,5},{5,4},{6,7},{7,6},{8,9},{9,8},{10,11... | collective-permute-start | bytes 15040520 | tf_op jit(solution)/shard_map/ppermute | solution.py:620
  82.5 50.8 %copy-start.63 = (s32[2]{0:T(128)}, s32[2]{0:T(128)S(1)}, u32[]{:S(2)}) copy-start(s32[2]{0:T(128)S(1)} %fusion.48.places) | copy-start | bytes 28
  84.0 32.5 %copy-start.114 = (f32[512]{0:T(512)}, f32[512]{0:T(512)S(1)}, u32[]{:S(2)}) copy-start(f32[512]{0:T(512)S(1)} %broadcast_multiply_fusion.5) | copy-start | bytes 6148
  85.6 34.2 %copy-start.116 = (f32[512]{0:T(512)}, f32[512]{0:T(512)S(1)}, u32[]{:S(2)}) copy-start(f32[512]{0:T(512)S(1)} %add_rsqrt_fusion.1) | copy-start | bytes 6148
  85.6 56.7 %collective-permute-start.14 = (bf16[136,1088]{1,0:T(8,128)(2,1)S(1)}, bf16[136,1088]{1,0:T(8,128)(2,1)}, u32[]{:S(2)}, u32[]{:S(2)}) collective-permute-start(bf16[136,1088]{1,0:T(8,128)(2,1)S(1)} %convert_bitcast_fusion), channel_id=1, source_target_pairs={{0,4},{4,8},{8,12},{12,0},{1,5},{5,9},{9,13},{13,1},{2,6},{6,10},{... | collective-permute-start | bytes 887816 | tf_op jit(solution)/shard_map/ppermute | solution.py:633
  93.1 49.3 %collective-permute-start.15 = (bf16[136,1088]{1,0:T(8,128)(2,1)S(1)}, bf16[136,1088]{1,0:T(8,128)(2,1)}, u32[]{:S(2)}, u32[]{:S(2)}) collective-permute-start(bf16[136,1088]{1,0:T(8,128)(2,1)S(1)} %convert_bitcast_fusion), channel_id=1, source_target_pairs={{0,8},{4,12},{8,0},{12,4},{1,9},{5,13},{9,1},{13,5},{2,10},{6,14},... | collective-permute-start | bytes 887816 | tf_op jit(solution)/shard_map/ppermute | solution.py:633
  95.3 47.1 %collective-permute-start.16 = (bf16[136,1088]{1,0:T(8,128)(2,1)S(1)}, bf16[136,1088]{1,0:T(8,128)(2,1)}, u32[]{:S(2)}, u32[]{:S(2)}) collective-permute-start(bf16[136,1088]{1,0:T(8,128)(2,1)S(1)} %convert_bitcast_fusion), channel_id=1, source_target_pairs={{0,12},{4,0},{8,4},{12,8},{1,13},{5,1},{9,5},{13,9},{2,14},{6,2},{... | collective-permute-start | bytes 887816 | tf_op jit(solution)/shard_map/ppermute | solution.py:633
  96.5 2.8 collective-permute-start.10
  99.0 20.8 %copy-start.13 = (bf16[2,136,1088]{2,1,0:T(8,128)(2,1)}, bf16[2,136,1088]{2,1,0:T(8,128)(2,1)S(1)}, u32[]{:S(2)}) copy-start(bf16[2,136,1088]{2,1,0:T(8,128)(2,1)S(1)} %pad_maximum_fusion.13.refs_2_) | copy-start | bytes 1775620
  99.3 16.6 %collective-permute-start.11 = (bf16[2,136,1088]{2,1,0:T(8,128)(2,1)S(1)}, bf16[2,136,1088]{2,1,0:T(8,128)(2,1)S(1)}, u32[]{:S(2)}, u32[]{:S(2)}) collective-permute-start(bf16[2,136,1088]{2,1,0:T(8,128)(2,1)S(1)} %pad_maximum_fusion.12.refs_0_), channel_id=1, source_target_pairs={{0,2},{1,3},{2,0},{3,1},{4,6},{5,7},{6,4},{7,5},{8,10},{9,11},{10,... | collective-permute-start | bytes 1775624 | tf_op jit(solution)/shard_map/ppermute | solution.py:620
  102.5 110.2 %copy-start.103 = (f32[1088]{0:T(1024)}, f32[1088]{0:T(1024)S(1)}, u32[]{:S(2)}) copy-start(f32[1088]{0:T(1024)S(1)} %get-tuple-element.324) | copy-start | bytes 13060
  115.9 15.8 %collective-permute-start.12 = (bf16[2,136,1088]{2,1,0:T(8,128)(2,1)S(1)}, bf16[2,136,1088]{2,1,0:T(8,128)(2,1)S(1)}, u32[]{:S(2)}, u32[]{:S(2)}) collective-permute-start(bf16[2,136,1088]{2,1,0:T(8,128)(2,1)S(1)} %pad_maximum_fusion.13.refs_2_), channel_id=1, source_target_pairs={{0,16},{16,0},{1,17},{17,1},{2,18},{18,2},{3,19},{19,3},{4,20},{20... | collective-permute-start | bytes 1775624 | tf_op jit(solution)/shard_map/ppermute | solution.py:628
  119.8 20.7 %copy-start.5 = (bf16[512,1088]{0,1:T(8,128)(2,1)}, bf16[512,1088]{0,1:T(8,128)(2,1)S(1)}, u32[]{:S(2)}) copy-start(bf16[512,1088]{0,1:T(8,128)(2,1)S(1)} %get-tuple-element.151) | copy-start | bytes 3342340
  143.5 15.3 %collective-permute-start.17 = (bf16[2,136,1088]{2,1,0:T(8,128)(2,1)S(1)}, bf16[2,136,1088]{2,1,0:T(8,128)(2,1)S(1)}, u32[]{:S(2)}, u32[]{:S(2)}) collective-permute-start(bf16[2,136,1088]{2,1,0:T(8,128)(2,1)S(1)} %pad_maximum_fusion.14.refs_0_), channel_id=1, source_target_pairs={{0,2},{1,3},{2,0},{3,1},{4,6},{5,7},{6,4},{7,5},{8,10},{9,11},{10,... | collective-permute-start | bytes 1775624 | tf_op jit(solution)/shard_map/ppermute | solution.py:620
  146.1 14.9 %collective-permute-start.18 = (bf16[2,136,1088]{2,1,0:T(8,128)(2,1)S(1)}, bf16[2,136,1088]{2,1,0:T(8,128)(2,1)S(1)}, u32[]{:S(2)}, u32[]{:S(2)}) collective-permute-start(bf16[2,136,1088]{2,1,0:T(8,128)(2,1)S(1)} %pad_maximum_fusion.15.refs_2_), channel_id=1, source_target_pairs={{0,16},{16,0},{1,17},{17,1},{2,18},{18,2},{3,19},{19,3},{4,20},{20... | collective-permute-start | bytes 1775624 | tf_op jit(solution)/shard_map/ppermute | solution.py:628
  162.6 15.6 %collective-permute-start.19 = (bf16[512,2304]{1,0:T(8,128)(2,1)}, bf16[512,2304]{1,0:T(8,128)(2,1)}, u32[]{:S(2)}, u32[]{:S(2)}) collective-permute-start(bf16[512,2304]{1,0:T(8,128)(2,1)} %slice.134), channel_id=1, source_target_pairs={{0,1},{2,3},{4,5},{6,7},{8,9},{10,11},{12,13},{14,15},{16,17},{18,... | collective-permute-start | bytes 7077896 | tf_op jit(solution)/shard_map/ppermute | solution.py:866
  166.9 30.7 %collective-permute-start.20 = (bf16[2,2,136,1088]{3,2,1,0:T(8,128)(2,1)}, bf16[2,2,136,1088]{3,2,1,0:T(8,128)(2,1)S(1)}, u32[]{:S(2)}, u32[]{:S(2)}) collective-permute-start(bf16[2,2,136,1088]{3,2,1,0:T(8,128)(2,1)} %pad_maximum_fusion.3), channel_id=1, source_target_pairs={{0,16},{16,0},{1,17},{17,1},{2,18},{18,2},{3,19},{19,3},{4,20},{20... | collective-permute-start | bytes 3551240 | tf_op jit(solution)/shard_map/ppermute | solution.py:628
  168.6 30.8 %collective-permute-start.21 = (bf16[2,2,136,1088]{3,2,1,0:T(8,128)(2,1)}, bf16[2,2,136,1088]{3,2,1,0:T(8,128)(2,1)}, u32[]{:S(2)}, u32[]{:S(2)}) collective-permute-start(bf16[2,2,136,1088]{3,2,1,0:T(8,128)(2,1)} %pad_maximum_fusion.4), channel_id=1, source_target_pairs={{0,2},{1,3},{2,0},{3,1},{4,6},{5,7},{6,4},{7,5},{8,10},{9,11},{10,... | collective-permute-start | bytes 3551240 | tf_op jit(solution)/shard_map/ppermute | solution.py:620
  174.2 45.8 %collective-permute-start.22 = (bf16[2,2,136,1088]{3,2,1,0:T(8,128)(2,1)}, bf16[2,2,136,1088]{3,2,1,0:T(8,128)(2,1)}, u32[]{:S(2)}, u32[]{:S(2)}) collective-permute-start(bf16[2,2,136,1088]{3,2,1,0:T(8,128)(2,1)} %pad_maximum_fusion.5), channel_id=1, source_target_pairs={{0,16},{16,0},{1,17},{17,1},{2,18},{18,2},{3,19},{19,3},{4,20},{20... | collective-permute-start | bytes 3551240 | tf_op jit(solution)/shard_map/ppermute | solution.py:628
  176.9 44.5 %collective-permute-start.23 = (bf16[2,2,136,1088]{3,2,1,0:T(8,128)(2,1)}, bf16[2,2,136,1088]{3,2,1,0:T(8,128)(2,1)}, u32[]{:S(2)}, u32[]{:S(2)}) collective-permute-start(bf16[2,2,136,1088]{3,2,1,0:T(8,128)(2,1)} %pad_maximum_fusion.6), channel_id=1, source_target_pairs={{0,2},{1,3},{2,0},{3,1},{4,6},{5,7},{6,4},{7,5},{8,10},{9,11},{10,... | collective-permute-start | bytes 3551240 | tf_op jit(solution)/shard_map/ppermute | solution.py:620
  214.8 22.8 %copy-start.2 = (bf16[512,1088]{0,1:T(8,128)(2,1)}, bf16[512,1088]{0,1:T(8,128)(2,1)S(1)}, u32[]{:S(2)}) copy-start(bf16[512,1088]{0,1:T(8,128)(2,1)S(1)} %add_convert_fusion.7) | copy-start | bytes 3342340
  226.2 25.8 %collective-permute-start.24 = (bf16[2,1088,1088]{2,1,0:T(8,128)(2,1)}, bf16[2,1088,1088]{2,1,0:T(8,128)(2,1)}, u32[]{:S(2)}, u32[]{:S(2)}) collective-permute-start(bf16[2,1088,1088]{2,1,0:T(8,128)(2,1)} %bitcast.201), channel_id=1, source_target_pairs={{0,1},{1,0},{2,3},{3,2},{4,5},{5,4},{6,7},{7,6},{8,9},{9,8},{10,11... | collective-permute-start | bytes 14204936 | tf_op jit(solution)/shard_map/ppermute | solution.py:620
  231.4 20.6 %collective-permute-start.25 = (bf16[2,1088,1088]{2,1,0:T(8,128)(2,1)}, bf16[2,1088,1088]{2,1,0:T(8,128)(2,1)}, u32[]{:S(2)}, u32[]{:S(2)}) collective-permute-start(bf16[2,1088,1088]{2,1,0:T(8,128)(2,1)} %bitcast.204), channel_id=1, source_target_pairs={{0,1},{1,0},{2,3},{3,2},{4,5},{5,4},{6,7},{7,6},{8,9},{9,8},{10,11... | collective-permute-start | bytes 14204936 | tf_op jit(solution)/shard_map/ppermute | solution.py:620
  271.6 28.0 %collective-permute-start.26 = (bf16[2,1088,1088]{2,1,0:T(8,128)(2,1)}, bf16[2,1088,1088]{2,1,0:T(8,128)(2,1)}, u32[]{:S(2)}, u32[]{:S(2)}) collective-permute-start(bf16[2,1088,1088]{2,1,0:T(8,128)(2,1)} %block_grads.6), channel_id=1, source_target_pairs={{0,1},{1,0},{2,3},{3,2},{4,5},{5,4},{6,7},{7,6},{8,9},{9,8},{10,11... | collective-permute-start | bytes 14204936 | tf_op jit(solution)/shard_map/ppermute | solution.py:620
  294.4 61.4 %collective-permute-start.29 = (bf16[2,1088,1088]{2,1,0:T(8,128)(2,1)}, bf16[2,1088,1088]{2,1,0:T(8,128)(2,1)}, u32[]{:S(2)}, u32[]{:S(2)}) collective-permute-start(bf16[2,1088,1088]{2,1,0:T(8,128)(2,1)} %block_grads.7), channel_id=1, source_target_pairs={{0,1},{1,0},{2,3},{3,2},{4,5},{5,4},{6,7},{7,6},{8,9},{9,8},{10,11... | collective-permute-start | bytes 14204936 | tf_op jit(solution)/shard_map/ppermute | solution.py:620
  306.1 30.1 %collective-permute-start.27 = (bf16[2,272,1088]{2,1,0:T(8,128)(2,1)S(1)}, bf16[2,272,1088]{2,1,0:T(8,128)(2,1)}, u32[]{:S(2)}, u32[]{:S(2)}) collective-permute-start(bf16[2,272,1088]{2,1,0:T(8,128)(2,1)S(1)} %get-tuple-element.203), channel_id=1, source_target_pairs={{0,16},{16,0},{1,17},{17,1},{2,18},{18,2},{3,19},{19,3},{4,20},{20... | collective-permute-start | bytes 3551240 | tf_op jit(solution)/shard_map/ppermute | solution.py:628
  307.6 31.3 %collective-permute-start.28 = (bf16[2,272,1088]{2,1,0:T(8,128)(2,1)}, bf16[2,272,1088]{2,1,0:T(8,128)(2,1)}, u32[]{:S(2)}, u32[]{:S(2)}) collective-permute-start(bf16[2,272,1088]{2,1,0:T(8,128)(2,1)} %get-tuple-element.205), channel_id=1, source_target_pairs={{0,2},{1,3},{2,0},{3,1},{4,6},{5,7},{6,4},{7,5},{8,10},{9,11},{10,... | collective-permute-start | bytes 3551240 | tf_op jit(solution)/shard_map/ppermute | solution.py:620
  346.7 53.5 %collective-permute-start.33 = (bf16[272,1088]{1,0:T(8,128)(2,1)}, bf16[272,1088]{1,0:T(8,128)(2,1)}, u32[]{:S(2)}, u32[]{:S(2)}) collective-permute-start(bf16[272,1088]{1,0:T(8,128)(2,1)} %dynamic-slice_bitcast_fusion.2), channel_id=1, source_target_pairs={{0,16},{16,0},{1,17},{17,1},{2,18},{18,2},{3,19},{19,3},{4,20},{20... | collective-permute-start | bytes 1775624 | tf_op jit(solution)/shard_map/ppermute | solution.py:628
  350.2 48.1 %collective-permute-start.32 = (bf16[272,1088]{1,0:T(8,128)(2,1)}, bf16[272,1088]{1,0:T(8,128)(2,1)}, u32[]{:S(2)}, u32[]{:S(2)}) collective-permute-start(bf16[272,1088]{1,0:T(8,128)(2,1)} %slice_bitcast_fusion.4), channel_id=1, source_target_pairs={{0,2},{1,3},{2,0},{3,1},{4,6},{5,7},{6,4},{7,5},{8,10},{9,11},{10,... | collective-permute-start | bytes 1775624 | tf_op jit(solution)/shard_map/ppermute | solution.py:620
  367.9 35.6 %collective-permute-start.30 = (bf16[2,272,1088]{2,1,0:T(8,128)(2,1)}, bf16[2,272,1088]{2,1,0:T(8,128)(2,1)S(1)}, u32[]{:S(2)}, u32[]{:S(2)}) collective-permute-start(bf16[2,272,1088]{2,1,0:T(8,128)(2,1)} %copy-done.68), channel_id=1, source_target_pairs={{0,16},{16,0},{1,17},{17,1},{2,18},{18,2},{3,19},{19,3},{4,20},{20... | collective-permute-start | bytes 3551240 | tf_op jit(solution)/shard_map/ppermute | solution.py:628
  368.5 36.5 %collective-permute-start.31 = (bf16[2,272,1088]{2,1,0:T(8,128)(2,1)}, bf16[2,272,1088]{2,1,0:T(8,128)(2,1)S(1)}, u32[]{:S(2)}, u32[]{:S(2)}) collective-permute-start(bf16[2,272,1088]{2,1,0:T(8,128)(2,1)} %copy-done.67), channel_id=1, source_target_pairs={{0,2},{1,3},{2,0},{3,1},{4,6},{5,7},{6,4},{7,5},{8,10},{9,11},{10,... | collective-permute-start | bytes 3551240 | tf_op jit(solution)/shard_map/ppermute | solution.py:620
  407.8 14.9 %collective-permute-start.34 = (bf16[512,2304]{1,0:T(8,128)(2,1)}, bf16[512,2304]{1,0:T(8,128)(2,1)}, u32[]{:S(2)}, u32[]{:S(2)}) collective-permute-start(bf16[512,2304]{1,0:T(8,128)(2,1)} %pad_maximum_fusion), channel_id=1, source_target_pairs={{1,0},{3,2},{5,4},{7,6},{9,8},{11,10},{13,12},{15,14},{17,16},{19,... | collective-permute-start | bytes 7077896 | tf_op jit(solution)/shard_map/ppermute | solution.py:973
  415.2 21.1 %collective-permute-start.37 = (bf16[136,1088]{1,0:T(8,128)(2,1)S(1)}, bf16[136,1088]{1,0:T(8,128)(2,1)S(1)}, u32[]{:S(2)}, u32[]{:S(2)}) collective-permute-start(bf16[136,1088]{1,0:T(8,128)(2,1)S(1)} %get-tuple-element.358), channel_id=1, source_target_pairs={{0,12},{4,0},{8,4},{12,8},{1,13},{5,1},{9,5},{13,9},{2,14},{6,2},{... | collective-permute-start | bytes 887816 | tf_op jit(solution)/shard_map/ppermute | solution.py:633
  417.6 27.8 %collective-permute-start.36 = (bf16[136,1088]{1,0:T(8,128)(2,1)S(1)}, bf16[136,1088]{1,0:T(8,128)(2,1)S(1)}, u32[]{:S(2)}, u32[]{:S(2)}) collective-permute-start(bf16[136,1088]{1,0:T(8,128)(2,1)S(1)} %get-tuple-element.359), channel_id=1, source_target_pairs={{0,8},{4,12},{8,0},{12,4},{1,9},{5,13},{9,1},{13,5},{2,10},{6,14},... | collective-permute-start | bytes 887816 | tf_op jit(solution)/shard_map/ppermute | solution.py:633
  418.1 27.3 %collective-permute-start.35 = (bf16[136,1088]{1,0:T(8,128)(2,1)S(1)}, bf16[136,1088]{1,0:T(8,128)(2,1)S(1)}, u32[]{:S(2)}, u32[]{:S(2)}) collective-permute-start(bf16[136,1088]{1,0:T(8,128)(2,1)S(1)} %get-tuple-element.357), channel_id=1, source_target_pairs={{0,4},{4,8},{8,12},{12,0},{1,5},{5,9},{9,13},{13,1},{2,6},{6,10},{... | collective-permute-start | bytes 887816 | tf_op jit(solution)/shard_map/ppermute | solution.py:633
  419.3 28.0 %collective-permute-start.39 = (bf16[272,1088]{1,0:T(8,128)(2,1)S(1)}, bf16[272,1088]{1,0:T(8,128)(2,1)S(1)}, u32[]{:S(2)}, u32[]{:S(2)}) collective-permute-start(bf16[272,1088]{1,0:T(8,128)(2,1)S(1)} %dynamic-slice_bitcast_fusion.1), channel_id=1, source_target_pairs={{0,16},{16,0},{1,17},{17,1},{2,18},{18,2},{3,19},{19,3},{4,20},{20... | collective-permute-start | bytes 1775624 | tf_op jit(solution)/shard_map/ppermute | solution.py:628
  422.7 24.8 %collective-permute-start.38 = (bf16[272,1088]{1,0:T(8,128)(2,1)S(1)}, bf16[272,1088]{1,0:T(8,128)(2,1)S(1)}, u32[]{:S(2)}, u32[]{:S(2)}) collective-permute-start(bf16[272,1088]{1,0:T(8,128)(2,1)S(1)} %slice_bitcast_fusion.3), channel_id=1, source_target_pairs={{0,2},{1,3},{2,0},{3,1},{4,6},{5,7},{6,4},{7,5},{8,10},{9,11},{10,... | collective-permute-start | bytes 1775624 | tf_op jit(solution)/shard_map/ppermute | solution.py:620
  428.9 27.3 %copy-start.48 = (bf16[2,512,896]{2,1,0:T(8,128)(2,1)}, bf16[2,512,896]{2,1,0:T(8,128)(2,1)S(1)}, u32[]{:S(2)}) copy-start(bf16[2,512,896]{2,1,0:T(8,128)(2,1)S(1)} %get-tuple-element.231.refs_2_) | copy-start | bytes 5505028
  436.3 45.5 %collective-permute-start.44 = (bf16[2,1088,1152]{2,1,0:T(8,128)(2,1)}, bf16[2,1088,1152]{2,1,0:T(8,128)(2,1)}, u32[]{:S(2)}, u32[]{:S(2)}) collective-permute-start(bf16[2,1088,1152]{2,1,0:T(8,128)(2,1)} %block_grads.10), channel_id=1, source_target_pairs={{0,1},{1,0},{2,3},{3,2},{4,5},{5,4},{6,7},{7,6},{8,9},{9,8},{10,11... | collective-permute-start | bytes 15040520 | tf_op jit(solution)/shard_map/ppermute | solution.py:620
  448.8 13.9 %collective-permute-start.42 = (bf16[136,1088]{1,0:T(8,128)(2,1)}, bf16[136,1088]{1,0:T(8,128)(2,1)}, u32[]{:S(2)}, u32[]{:S(2)}) collective-permute-start(bf16[136,1088]{1,0:T(8,128)(2,1)} %get-tuple-element.355), channel_id=1, source_target_pairs={{0,12},{4,0},{8,4},{12,8},{1,13},{5,1},{9,5},{13,9},{2,14},{6,2},{... | collective-permute-start | bytes 887816 | tf_op jit(solution)/shard_map/ppermute | solution.py:633
  452.3 27.9 %collective-permute-start.41 = (bf16[136,1088]{1,0:T(8,128)(2,1)}, bf16[136,1088]{1,0:T(8,128)(2,1)}, u32[]{:S(2)}, u32[]{:S(2)}) collective-permute-start(bf16[136,1088]{1,0:T(8,128)(2,1)} %get-tuple-element.356), channel_id=1, source_target_pairs={{0,8},{4,12},{8,0},{12,4},{1,9},{5,13},{9,1},{13,5},{2,10},{6,14},... | collective-permute-start | bytes 887816 | tf_op jit(solution)/shard_map/ppermute | solution.py:633
  452.4 27.9 %collective-permute-start.40 = (bf16[136,1088]{1,0:T(8,128)(2,1)}, bf16[136,1088]{1,0:T(8,128)(2,1)}, u32[]{:S(2)}, u32[]{:S(2)}) collective-permute-start(bf16[136,1088]{1,0:T(8,128)(2,1)} %get-tuple-element.354), channel_id=1, source_target_pairs={{0,4},{4,8},{8,12},{12,0},{1,5},{5,9},{9,13},{13,1},{2,6},{6,10},{... | collective-permute-start | bytes 887816 | tf_op jit(solution)/shard_map/ppermute | solution.py:633
  461.9 19.8 %copy-start.28 = (bf16[2,512,384]{2,1,0:T(8,128)(2,1)S(1)}, bf16[2,512,384]{2,1,0:T(8,128)(2,1)}, u32[]{:S(2)}) copy-start(bf16[2,512,384]{2,1,0:T(8,128)(2,1)} %copy-done.27) | copy-start | bytes 2359300
  462.5 19.1 %collective-permute-start.43 = (bf16[2,8,7,64]{3,2,1,0:T(8,128)(2,1)S(1)}, bf16[2,8,7,64]{3,2,1,0:T(8,128)(2,1)S(1)}, u32[]{:S(2)}, u32[]{:S(2)}) collective-permute-start(bf16[2,8,7,64]{3,2,1,0:T(8,128)(2,1)S(1)} %slice.160), channel_id=1, source_target_pairs={{0,1},{1,0},{2,3},{3,2},{4,5},{5,4},{6,7},{7,6},{8,9},{9,8},{10,11... | collective-permute-start | bytes 43016 | tf_op jit(solution)/shard_map/ppermute | solution.py:620
  489.5 28.7 %collective-permute-start.45 = (bf16[2,272,1152]{2,1,0:T(8,128)(2,1)S(1)}, bf16[2,272,1152]{2,1,0:T(8,128)(2,1)S(1)}, u32[]{:S(2)}, u32[]{:S(2)}) collective-permute-start(bf16[2,272,1152]{2,1,0:T(8,128)(2,1)S(1)} %get-tuple-element.240), channel_id=1, source_target_pairs={{0,16},{16,0},{1,17},{17,1},{2,18},{18,2},{3,19},{19,3},{4,20},{20... | collective-permute-start | bytes 3760136 | tf_op jit(solution)/shard_map/ppermute | solution.py:628
  490.1 28.8 %collective-permute-start.46 = (bf16[2,272,1152]{2,1,0:T(8,128)(2,1)}, bf16[2,272,1152]{2,1,0:T(8,128)(2,1)S(1)}, u32[]{:S(2)}, u32[]{:S(2)}) collective-permute-start(bf16[2,272,1152]{2,1,0:T(8,128)(2,1)} %get-tuple-element.242), channel_id=1, source_target_pairs={{0,2},{1,3},{2,0},{3,1},{4,6},{5,7},{6,4},{7,5},{8,10},{9,11},{10,... | collective-permute-start | bytes 3760136 | tf_op jit(solution)/shard_map/ppermute | solution.py:620
  493.7 25.3 %copy-start.93 = (bf16[2,272,1152]{2,1,0:T(8,128)(2,1)S(1)}, bf16[2,272,1152]{2,1,0:T(8,128)(2,1)}, u32[]{:S(2)}) copy-start(bf16[2,272,1152]{2,1,0:T(8,128)(2,1)} %get-tuple-element.241) | copy-start | bytes 3760132
  519.4 14.3 %collective-permute-start.48 = (bf16[272,1152]{1,0:T(8,128)(2,1)S(1)}, bf16[272,1152]{1,0:T(8,128)(2,1)S(1)}, u32[]{:S(2)}, u32[]{:S(2)}) collective-permute-start(bf16[272,1152]{1,0:T(8,128)(2,1)S(1)} %dynamic-slice_bitcast_fusion), channel_id=1, source_target_pairs={{0,16},{16,0},{1,17},{17,1},{2,18},{18,2},{3,19},{19,3},{4,20},{20... | collective-permute-start | bytes 1880072 | tf_op jit(solution)/shard_map/ppermute | solution.py:628
  520.7 13.9 %collective-permute-start.47 = (bf16[272,1152]{1,0:T(8,128)(2,1)S(1)}, bf16[272,1152]{1,0:T(8,128)(2,1)S(1)}, u32[]{:S(2)}, u32[]{:S(2)}) collective-permute-start(bf16[272,1152]{1,0:T(8,128)(2,1)S(1)} %slice_bitcast_fusion.2), channel_id=1, source_target_pairs={{0,2},{1,3},{2,0},{3,1},{4,6},{5,7},{6,4},{7,5},{8,10},{9,11},{10,... | collective-permute-start | bytes 1880072 | tf_op jit(solution)/shard_map/ppermute | solution.py:620
  535.0 8.7 %collective-permute-start.51 = (bf16[136,1152]{1,0:T(8,128)(2,1)S(1)}, bf16[136,1152]{1,0:T(8,128)(2,1)S(1)}, u32[]{:S(2)}, u32[]{:S(2)}) collective-permute-start(bf16[136,1152]{1,0:T(8,128)(2,1)S(1)} %get-tuple-element.352), channel_id=1, source_target_pairs={{0,12},{4,0},{8,4},{12,8},{1,13},{5,1},{9,5},{13,9},{2,14},{6,2},{... | collective-permute-start | bytes 940040 | tf_op jit(solution)/shard_map/ppermute | solution.py:633
  535.1 29.4 %collective-permute-start.50 = (bf16[136,1152]{1,0:T(8,128)(2,1)S(1)}, bf16[136,1152]{1,0:T(8,128)(2,1)S(1)}, u32[]{:S(2)}, u32[]{:S(2)}) collective-permute-start(bf16[136,1152]{1,0:T(8,128)(2,1)S(1)} %get-tuple-element.353), channel_id=1, source_target_pairs={{0,8},{4,12},{8,0},{12,4},{1,9},{5,13},{9,1},{13,5},{2,10},{6,14},... | collective-permute-start | bytes 940040 | tf_op jit(solution)/shard_map/ppermute | solution.py:633
  538.8 25.7 %collective-permute-start.49 = (bf16[136,1152]{1,0:T(8,128)(2,1)S(1)}, bf16[136,1152]{1,0:T(8,128)(2,1)S(1)}, u32[]{:S(2)}, u32[]{:S(2)}) collective-permute-start(bf16[136,1152]{1,0:T(8,128)(2,1)S(1)} %get-tuple-element.351), channel_id=1, source_target_pairs={{0,4},{4,8},{8,12},{12,0},{1,5},{5,9},{9,13},{13,1},{2,6},{6,10},{... | collective-permute-start | bytes 940040 | tf_op jit(solution)/shard_map/ppermute | solution.py:633
  542.3 23.1 %copy-start.96 = (f32[272,136]{0,1:T(8,128)S(1)}, f32[272,136]{0,1:T(8,128)}, u32[]{:S(2)}) copy-start(f32[272,136]{0,1:T(8,128)} %param.22) | copy-start | bytes 443908
  (112 other events, 633.6 us)

commit v8 on v5

--- a/solution.py
+++ b/solution.py
@@ -837,9 +837,8 @@
     )
     one_down = scatter_one(total_down)
     sent_up = block_grads([(left_up, turned(dups_oth))], None, None, False)
-    down_own, one_down, sent_up = together(down_own, one_down, sent_up)
+    down_own, sent_up = together(down_own, sent_up)
     received_up = partner(sent_up)
-    two_down = scatter_two(one_down)
     dups_own, dbias_own, grad_normed_two = backward_part(
         up_own, down_own, pull_own, grad_normed_two
     )
@@ -861,13 +860,16 @@
         None,
     )
     total_up = block_grads([(left_up, turned(dups_own))], None, received_up, staged)
-    grad_mixed, total_up, two_down = together(grad_mixed, total_up, two_down)
+    grad_mixed, total_up, one_down = together(grad_mixed, total_up, one_down)
+    two_down = scatter_two(one_down)
     dq, dk_own, dv_own, dk_oth, dv_oth = attend_back(
         later, labels, projected, others, grad_mixed, mixed, log_totals
     )
+    one_up = scatter_one(total_up)
+    dq, dk_own, dv_own, dk_oth, dv_oth, one_up, two_down = together(
+        dq, dk_own, dv_own, dk_oth, dv_oth, one_up, two_down
+    )
     back = lax.ppermute(jnp.concatenate([dk_oth, dv_oth], 1), "col", behind)
-    one_up = scatter_one(total_up)
-    dq, dk_own, dv_own, one_up = together(dq, dk_own, dv_own, one_up)
     grads_shape = jax.ShapeDtypeStruct((each, here, lanes_qkv), bf16)
     grads_own, grads_oth, grad_sums = split_call(
         functools.partial(split_grads_kernel, piece, cols),

time: 543 us -> 524 us (0.965)
  waiting for transfers between devices: 156 us -> 136 us
  starting transfers between devices: 84.9 us -> 76.1 us
  matrix products: 70.3 us -> 78.5 us
    ppermute x20, waiting for transfers between devices: 41.7 us -> 26.5 us  [flip_col(): lax.ppermute(block, 'col', [(c, c ^ bit) for c in range(lax.axis_size('co...]
    ppermute x20, starting transfers between devices: 28.6 us -> 20.8 us  [flip_col(): lax.ppermute(block, 'col', [(c, c ^ bit) for c in range(lax.axis_size('co...]
    unnamed x229 -> x227, local copies, waits for them, and re-layouts: 12.5 us -> 15.1 us
  transfers between devices with their start and end apart: 52 -> 52, of which waited for: 21 -> 17; matrix products, arithmetic and copies ran while one was open for 26% -> 27% of each run, Pallas kernels for 17% -> 17%
where the time goes in v8:
time: 524 us; the launch traced here: 518 us
  waiting for transfers between devices  136 us (26%)
  Pallas kernels  117 us (22%)
  matrix products  78.5 us (15%)
  starting transfers between devices  76.1 us (15%)
  other arithmetic  65.2 us (12%)
  local copies, waits for them, and re-layouts  42.3 us (8%)
    ppermute x18, waiting for transfers between devices, shift_row(): lax.ppermute(block, 'row', [(i, (i + by) % count) for i in range(count)])  54.9 us
    ppermute x12, waiting for transfers between devices, flip_dp(): return lax.ppermute(block, 'dp', [(0, 1), (1, 0)])  54.5 us
    dot_general x16, matrix products, contract(): lax.dot_general(left, right, (((left_dim,), (right_dim,)), ((), ())), pre...  41.9 us
    ppermute x18, starting transfers between devices, shift_row(): lax.ppermute(block, 'row', [(i, (i + by) % count) for i in range(count)])  39.4 us
    pallas_call x6, Pallas kernels, block_grads(): pl.pallas_call(functools.partial(block_grads_kernel, [len(r) for r in rig...  37.1 us
    ppermute x20, waiting for transfers between devices, flip_col(): lax.ppermute(block, 'col', [(c, c ^ bit) for c in range(lax.axis_size('co...  26.5 us
    pallas_call x3, Pallas kernels, multiply_and_place(): pl.pallas_call(functools.partial(place_kernel, spans, piece, sources, bia...  22.9 us
    ppermute x20, starting transfers between devices, flip_col(): lax.ppermute(block, 'col', [(c, c ^ bit) for c in range(lax.axis_size('co...  20.8 us
  transfers between devices with their start and end apart: 52, of which 17 were waited for; matrix products, arithmetic and copies ran while one was open for 27% of the time, Pallas kernels for 17%

profile of v8, /device:TPU:0, one launch (start us, length us, event | category | flops | bytes accessed | tf_op | source)
XLA Modules:
  0.0 517.5 jit_solution(15475042257750084420)
XLA Ops:
  2.7 3.1 collective-permute-start
  5.8 2.6 collective-permute-start.1
  9.8 6.4 %collective-permute-done = bf16[136,1152]{1,0:T(8,128)(2,1)S(1)} collective-permute-done((bf16[136,1152]{1,0:T(8,128)(2,1)S(1)}, bf16[136,1152]{1,0:T(8,128)(2,1)S(1)}, u32[]{:S(2)}, u32[]{:S(2)}) %collective-permute-start) | collective-permute-done | bytes 313376 | tf_op jit(solution)/shard_map/ppermute | solution.py:523
  16.2 12.6 %collective-permute-done.1 = bf16[136,1152]{1,0:T(8,128)(2,1)S(1)} collective-permute-done((bf16[136,1152]{1,0:T(8,128)(2,1)S(1)}, bf16[136,1152]{1,0:T(8,128)(2,1)S(1)}, u32[]{:S(2)}, u32[]{:S(2)}) %collective-permute-start.1) | collective-permute-done | bytes 313376 | tf_op jit(solution)/shard_map/ppermute | solution.py:523
  33.4 11.5 %collective-permute-done.3.refs_1_ = bf16[2,136,1152]{2,1,0:T(8,128)(2,1)S(1)} collective-permute-done((bf16[2,136,1152]{2,1,0:T(8,128)(2,1)S(1)}, bf16[2,136,1152]{2,1,0:T(8,128)(2,1)S(1)}, u32[]{:S(2)}, u32[]{:S(2)}) %collective-permute-start.3) | collective-permute-done | bytes 626720 | tf_op jit(solution)/shard_map/ppermute | solution.py:510
  49.8 7.3 %collective-permute-start.8 = (bf16[136,1088]{1,0:T(8,128)(2,1)S(1)}, bf16[136,1088]{1,0:T(8,128)(2,1)}, u32[]{:S(2)}, u32[]{:S(2)}) collective-permute-start(bf16[136,1088]{1,0:T(8,128)(2,1)S(1)} %convert_element_type.313), channel_id=1, source_target_pairs={{0,4},{4,8},{8,12},{12,0},{1,5},{5,9},{9,13},{13,1},{2,6},{6,10},{... | collective-permute-start | bytes 887816 | tf_op jit(solution)/shard_map/ppermute | solution.py:523
  59.5 14.4 %collective-permute-done.5 = bf16[2,2,136,1152]{3,2,1,0:T(8,128)(2,1)S(1)} collective-permute-done((bf16[2,2,136,1152]{3,2,1,0:T(8,128)(2,1)S(1)}, bf16[2,2,136,1152]{3,2,1,0:T(8,128)(2,1)S(1)}, u32[]{:S(2)}, u32[]{:S(2)}) %collective-permute-start.5) | collective-permute-done | bytes 1253408 | tf_op jit(solution)/shard_map/ppermute | solution.py:518
  75.4 4.4 assemble.3
  82.8 7.4 %collective-permute-start.14 = (bf16[136,1088]{1,0:T(8,128)(2,1)}, bf16[136,1088]{1,0:T(8,128)(2,1)}, u32[]{:S(2)}, u32[]{:S(2)}) collective-permute-start(bf16[136,1088]{1,0:T(8,128)(2,1)} %convert_bitcast_fusion.2), channel_id=1, source_target_pairs={{0,4},{4,8},{8,12},{12,0},{1,5},{5,9},{9,13},{13,1},{2,6},{6,10},{... | collective-permute-start | bytes 887816 | tf_op jit(solution)/shard_map/ppermute | solution.py:523
  94.6 5.1 fusion.172
  102.6 5.0 collective-permute-done.11.refs_1_
  107.6 2.9 collective-permute-start.16
  111.7 5.0 collective-permute-done.12.refs_3_
  118.9 7.2 %multiply_and_place.3.refs_2_ = bf16[512,3456]{1,0:T(8,128)(2,1)S(1)} custom-call(s32[2]{0:T(128)S(1)} %copy-done.35, bf16[512,1088]{1,0:T(8,128)(2,1)S(1)} %copy.66.x, bf16[2,1088,1152]{2,1,0:T(8,128)(2,1)} %bitcast.352, f32[1,3456]{1,0:T(1,128)S(1)} %reshape.256.refs_1_), custom_call_target="tpu_custom_call" | custom-call | tf_op jit(solution)/shard_map/multiply_and_place/pallas_call | solution.py:327
  126.2 2.6 pad_maximum_fusion.14.refs_0_
  141.2 8.5 %multiply_and_place.4.q.k_own.v_own = bf16[512,3456]{1,0:T(8,128)(2,1)S(1)} custom-call(s32[2]{0:T(128)S(1)} %copy-done.34, bf16[512,1088]{1,0:T(8,128)(2,1)S(1)} %copy-done.6, bf16[2,1088,1152]{2,1,0:T(8,128)(2,1)} %collective-permute-done.13.refs_0_.refs_1_, f32[1,3456]{1,0:T(1,128)S(1)} %copy-done.33, bf16[512,3456]{1,0:T(8,128)(2,1)} %copy-done.4), custom_call_target="tpu_custom_call" | custom-call | tf_op jit(solution)/shard_map/multiply_and_place/pallas_call | solution.py:327
  152.2 2.9 collective-permute-start.19
  155.2 2.5 pad_maximum_fusion.5
  162.5 4.4 slice_bitcast_fusion.7
  166.9 17.6 %attention_forward.1 = (bf16[512,1152]{1,0:T(8,128)(2,1)S(1)}, f32[9,2,512]{2,1,0:T(2,128)S(1)}) custom-call(s32[1]{0:T(128)} %bitcast.17.later, s32[1,512]{1,0:T(1,128)S(1)} %bitcast.348, s32[512,1]{1,0:T(8,128)S(1)} %copy-done.20, s32[512,1]{1,0:T(8,128)S(1)} %copy-done.22, bf16[512,3456]{1,0:T(8,128)(2,1)} %copy-done, bf16[512,3456]{1,0:T(8,128)(2,1)} %copy-done, ...), custom_call_target="tpu_custom_call" | custom-call | tf_op jit(solution)/shard_map/attention_forward/pallas_call | solution.py:232
  184.7 4.9 assemble.4
  189.6 3.2 collective-permute-start.22
  193.6 2.5 convolution_add_fusion.2
  202.7 3.1 convolution_add_fusion.11
  205.8 3.0 convolution_add_fusion.10
  208.8 4.1 assemble.5
  213.0 5.2 %fusion.81 = (bf16[1088,512]{1,0:T(8,128)(2,1)S(1)}, f32[512,1088]{0,1:T(8,128)}) fusion(f32[1088]{0:T(1024)S(1)} %get-tuple-element.229, bf16[512,1088]{0,1:T(8,128)(2,1)S(1)} %add_convert_fusion.6, bf16[2,1088,1088]{2,1,0:T(8,128)(2,1)} %collective-permute-done.22), kind=kOutput, calls=%fused_computation.132 | convolution fusion | flops 1217724416 | bytes 6967552 | tf_op jit(solution)/shard_map/dot_general | solution.py:788
  218.3 5.3 %fusion.78 = (bf16[1088,512]{1,0:T(8,128)(2,1)S(1)}, f32[512,1088]{0,1:T(8,128)}) fusion(f32[1088]{0:T(1024)S(1)} %get-tuple-element.228, bf16[512,1088]{0,1:T(8,128)(2,1)S(1)} %add_convert_fusion.6, bf16[2,1088,1088]{2,1,0:T(8,128)(2,1)} %collective-permute-done.22), kind=kOutput, calls=%fused_computation.127 | convolution fusion | flops 1217724416 | bytes 6967552 | tf_op jit(solution)/shard_map/dot_general | solution.py:788
  223.6 5.3 %block_grads.6 = bf16[2,1088,1088]{2,1,0:T(8,128)(2,1)} custom-call(s32[1]{0:T(128)} %bitcast.place, bf16[1088,512]{1,0:T(8,128)(2,1)S(1)} %bitcast.335, bf16[1088,512]{1,0:T(8,128)(2,1)S(1)} %get-tuple-element.282.refs_1_, bf16[1088,512]{1,0:T(8,128)(2,1)S(1)} %get-tuple-element.284.refs_2_), custom_call_target="tpu_custom_call" | custom-call | tf_op jit(solution)/shard_map/block_grads/pallas_call | solution.py:478
  231.9 4.4 fusion.170
  236.4 3.1 fusion.158
  239.5 4.8 fusion.13
  246.6 7.2 %block_grads.7 = (bf16[2,272,1088]{2,1,0:T(8,128)(2,1)S(1)}, bf16[2,272,1088]{2,1,0:T(8,128)(2,1)}, bf16[2,272,1088]{2,1,0:T(8,128)(2,1)}, bf16[2,272,1088]{2,1,0:T(8,128)(2,1)}) custom-call(s32[1]{0:T(128)} %bitcast.place, bf16[1088,512]{1,0:T(8,128)(2,1)S(1)} %bitcast.336, bf16[1088,512]{1,0:T(8,128)(2,1)S(1)} %fusion.157.refs_1_, ...), custom_call_target="tpu_custom_call" | custom-call | tf_op jit(solution)/shard_map/block_grads/pallas_call | solution.py:478
  253.9 6.4 %fusion.57 = (bf16[1088,512]{1,0:T(8,128)(2,1)S(1)}, f32[1088,512]{1,0:T(8,128)}) fusion(f32[512,1088]{0,1:T(8,128)S(1)} %copy-done.76, bf16[512,1088]{0,1:T(8,128)(2,1)S(1)} %copy-done.3, bf16[2,1088,1088]{2,1,0:T(8,128)(2,1)} %collective-permute-done.25), kind=kOutput, calls=%fused_computation.100 | convolution fusion | flops 1223294976 | bytes 9191424 | tf_op jit(solution)/shard_map/dot_general | solution.py:828
  260.3 6.1 %fusion.50 = (bf16[1088,512]{1,0:T(8,128)(2,1)S(1)}, f32[1088,512]{1,0:T(8,128)}) fusion(f32[512,1088]{0,1:T(8,128)S(1)} %copy-done.71, bf16[512,1088]{0,1:T(8,128)(2,1)S(1)} %copy-done.3, bf16[2,1088,1088]{2,1,0:T(8,128)(2,1)} %collective-permute-done.25), kind=kOutput, calls=%fused_computation.93 | convolution fusion | flops 1223294976 | bytes 9191424 | tf_op jit(solution)/shard_map/dot_general | solution.py:828
  266.3 5.0 block_grads.8
  271.3 4.6 fusion.63
  280.4 3.5 fusion.165
  283.9 3.3 fusion.86
  287.2 3.5 fusion.1
  290.8 2.8 fusion.69
  300.7 7.2 %multiply_and_place.5.grad = bf16[512,1152]{1,0:T(8,128)(2,1)S(1)} custom-call(s32[4]{0:T(128)S(1)} %pad_add_fusion.1.places, bf16[512,1088]{1,0:T(8,128)(2,1)S(1)} %copy.69.x, bf16[2,1088,1152]{2,1,0:T(8,128)(2,1)} %bitcast.353, bf16[2,1088,1152]{2,1,0:T(8,128)(2,1)} %collective-permute-done.13.refs_0_.refs_1_), custom_call_target="tpu_custom_call" | custom-call | tf_op jit(solution)/shard_map/multiply_and_place/pallas_call | solution.py:327
  312.9 6.9 %block_grads.9 = (bf16[2,272,1088]{2,1,0:T(8,128)(2,1)S(1)}, bf16[2,272,1088]{2,1,0:T(8,128)(2,1)S(1)}, bf16[2,272,1088]{2,1,0:T(8,128)(2,1)}, bf16[2,272,1088]{2,1,0:T(8,128)(2,1)}) custom-call(s32[1]{0:T(128)} %bitcast.place, bf16[1088,512]{1,0:T(8,128)(2,1)S(1)} %fusion.193.refs_0_, bf16[1088,512]{1,0:T(8,128)(2,1)S(1)} %get-tuple-element.262.refs_1_, ...), custom_call_target="tpu_custom_call" | custom-call | tf_op jit(solution)/shard_map/block_grads/pallas_call | solution.py:478
  322.0 5.6 %fusion.4 = f32[512,1088]{0,1:T(8,128)} fusion(f32[512,1088]{0,1:T(8,128)S(1)} %copy-done.107, f32[512,1088]{0,1:T(8,128)} %fusion.13, bf16[2,1088,1088]{2,1,0:T(8,128)(2,1)} %collective-permute-done.25, f32[512,1088]{0,1:T(8,128)S(1)} %copy-done.73), kind=kOutput, calls=%fused_computation.13 | convolution fusion | flops 1218281472 | bytes 11419648 | tf_op jit(solution)/shard_map/dot_general | solution.py:30
  329.8 19.7 %attention_backward.1 = (bf16[512,1152]{1,0:T(8,128)(2,1)S(1)}, bf16[512,1152]{1,0:T(8,128)(2,1)S(1)}, bf16[512,1152]{1,0:T(8,128)(2,1)S(1)}, bf16[512,1152]{1,0:T(8,128)(2,1)S(1)}, bf16[512,1152]{1,0:T(8,128)(2,1)}) custom-call(s32[1]{0:T(128)} %bitcast.17.later, s32[1,512]{1,0:T(1,128)S(1)} %bitcast.349, s32[512,1]{1,0:T(8,128)S(1)} %copy-done.21, ...), custom_call_target="tpu_custom_call" | custom-call | tf_op jit(solution)/shard_map/attention_backward/pallas_call | solution.py:255
  352.5 10.4 %collective-permute-done.30 = bf16[2,272,1088]{2,1,0:T(8,128)(2,1)S(1)} collective-permute-done((bf16[2,272,1088]{2,1,0:T(8,128)(2,1)S(1)}, bf16[2,272,1088]{2,1,0:T(8,128)(2,1)S(1)}, u32[]{:S(2)}, u32[]{:S(2)}) %collective-permute-start.30) | collective-permute-done | bytes 1183776 | tf_op jit(solution)/shard_map/ppermute | solution.py:518
  369.1 2.8 fusion.6
  377.0 5.2 %split_grads.1 = (bf16[2,512,896]{2,1,0:T(8,128)(2,1)S(1)}, bf16[2,512,896]{2,1,0:T(8,128)(2,1)}, f32[8,1152]{1,0:T(8,128)S(1)}) custom-call(s32[1]{0:T(128)} %bitcast.16.column, bf16[512,1152]{1,0:T(8,128)(2,1)S(1)} %get-tuple-element.180.dq, bf16[512,1152]{1,0:T(8,128)(2,1)S(1)} %copy-done.29, bf16[512,1152]{1,0:T(8,128)(2,1)S(1)} %copy-done.31, ...), custom_call_target="tpu_custom_call" | custom-call | tf_op jit(solution)/shard_map/split_grads/pallas_call | solution.py:391
  384.3 5.3 %block_grads.10 = bf16[2,1088,1152]{2,1,0:T(8,128)(2,1)} custom-call(s32[1]{0:T(128)} %bitcast.place, bf16[1088,512]{1,0:T(8,128)(2,1)S(1)} %bitcast.333, bf16[1088,512]{1,0:T(8,128)(2,1)S(1)} %convert_bitcast_fusion.4.refs_1_, bf16[2,512,896]{2,1,0:T(8,128)(2,1)S(1)} %copy-done.24, bf16[2,512,384]{2,1,0:T(8,128)(2,1)S(1)} %copy-done.14), custom_call_target="tpu_custom_call" | custom-call | tf_op jit(solution)/shard_map/block_grads/pallas_call | solution.py:478
  397.6 10.5 %collective-permute-done.45 = bf16[272,1088]{1,0:T(8,128)(2,1)S(1)} collective-permute-done((bf16[272,1088]{1,0:T(8,128)(2,1)S(1)}, bf16[272,1088]{1,0:T(8,128)(2,1)S(1)}, u32[]{:S(2)}, u32[]{:S(2)}) %collective-permute-start.45) | collective-permute-done | bytes 591904 | tf_op jit(solution)/shard_map/ppermute | solution.py:518
  416.4 3.4 fusion.30
  421.8 3.5 collective-permute-start.48
  426.5 7.5 %block_grads.11 = (bf16[2,272,1152]{2,1,0:T(8,128)(2,1)S(1)}, bf16[2,272,1152]{2,1,0:T(8,128)(2,1)S(1)}, bf16[2,272,1152]{2,1,0:T(8,128)(2,1)}, bf16[2,272,1152]{2,1,0:T(8,128)(2,1)}) custom-call(s32[1]{0:T(128)} %bitcast.place, bf16[1088,512]{1,0:T(8,128)(2,1)S(1)} %bitcast.334, bf16[1088,512]{1,0:T(8,128)(2,1)S(1)} %convert_bitcast_fusion.4.refs_1_, ...), custom_call_target="tpu_custom_call" | custom-call | tf_op jit(solution)/shard_map/block_grads/pallas_call | solution.py:478
  434.7 3.0 multiply_subtract_fusion
  438.8 15.5 %collective-permute-done.47 = bf16[136,1088]{1,0:T(8,128)(2,1)S(1)} collective-permute-done((bf16[136,1088]{1,0:T(8,128)(2,1)S(1)}, bf16[136,1088]{1,0:T(8,128)(2,1)S(1)}, u32[]{:S(2)}, u32[]{:S(2)}) %collective-permute-start.47) | collective-permute-done | bytes 295968 | tf_op jit(solution)/shard_map/ppermute | solution.py:523
  454.3 2.7 multiply_subtract_fusion.1
  457.0 6.8 %collective-permute-done.39 = bf16[2,272,1152]{2,1,0:T(8,128)(2,1)S(1)} collective-permute-done((bf16[2,272,1152]{2,1,0:T(8,128)(2,1)}, bf16[2,272,1152]{2,1,0:T(8,128)(2,1)S(1)}, u32[]{:S(2)}, u32[]{:S(2)}) %collective-permute-start.39) | collective-permute-done | bytes 1253408 | tf_op jit(solution)/shard_map/ppermute | solution.py:510
  464.7 3.3 collective-permute-done.37
  470.1 10.3 %collective-permute-done.40 = bf16[272,1152]{1,0:T(8,128)(2,1)S(1)} collective-permute-done((bf16[272,1152]{1,0:T(8,128)(2,1)S(1)}, bf16[272,1152]{1,0:T(8,128)(2,1)S(1)}, u32[]{:S(2)}, u32[]{:S(2)}) %collective-permute-start.40) | collective-permute-done | bytes 626720 | tf_op jit(solution)/shard_map/ppermute | solution.py:518
  482.7 3.5 collective-permute-start.43
  486.9 3.7 fusion.29
  490.6 3.5 collective-permute-done.43
  494.1 16.9 %collective-permute-done.42 = bf16[136,1152]{1,0:T(8,128)(2,1)S(1)} collective-permute-done((bf16[136,1152]{1,0:T(8,128)(2,1)S(1)}, bf16[136,1152]{1,0:T(8,128)(2,1)S(1)}, u32[]{:S(2)}, u32[]{:S(2)}) %collective-permute-start.42) | collective-permute-done | bytes 313376 | tf_op jit(solution)/shard_map/ppermute | solution.py:523
  514.0 2.7 multiply_subtract_fusion.2
  (467 shorter events, 130.4 us)
Async XLA Ops:
  2.7 30.2 %copy-start.104 = (s32[2,1024]{1,0:T(2,128)S(1)}, s32[2,1024]{1,0:T(2,128)}, u32[]{:S(2)}) copy-start(s32[2,1024]{1,0:T(2,128)} %param.20) | copy-start | bytes 24580
  2.7 13.5 %collective-permute-start = (bf16[136,1152]{1,0:T(8,128)(2,1)S(1)}, bf16[136,1152]{1,0:T(8,128)(2,1)S(1)}, u32[]{:S(2)}, u32[]{:S(2)}) collective-permute-start(bf16[136,1152]{1,0:T(8,128)(2,1)S(1)} %concatenate.26), channel_id=1, source_target_pairs={{0,4},{4,8},{8,12},{12,0},{1,5},{5,9},{9,13},{13,1},{2,6},{6,10},{... | collective-permute-start | bytes 940040 | tf_op jit(solution)/shard_map/ppermute | solution.py:523
  5.8 23.0 %collective-permute-start.1 = (bf16[136,1152]{1,0:T(8,128)(2,1)S(1)}, bf16[136,1152]{1,0:T(8,128)(2,1)S(1)}, u32[]{:S(2)}, u32[]{:S(2)}) collective-permute-start(bf16[136,1152]{1,0:T(8,128)(2,1)S(1)} %concatenate.26), channel_id=1, source_target_pairs={{0,8},{4,12},{8,0},{12,4},{1,9},{5,13},{9,1},{13,5},{2,10},{6,14},... | collective-permute-start | bytes 940040 | tf_op jit(solution)/shard_map/ppermute | solution.py:523
  8.4 20.4 %collective-permute-start.2 = (bf16[136,1152]{1,0:T(8,128)(2,1)S(1)}, bf16[136,1152]{1,0:T(8,128)(2,1)S(1)}, u32[]{:S(2)}, u32[]{:S(2)}) collective-permute-start(bf16[136,1152]{1,0:T(8,128)(2,1)S(1)} %concatenate.26), channel_id=1, source_target_pairs={{0,12},{4,0},{8,4},{12,8},{1,13},{5,1},{9,5},{13,9},{2,14},{6,2},{... | collective-permute-start | bytes 940040 | tf_op jit(solution)/shard_map/ppermute | solution.py:523
  28.9 16.0 %collective-permute-start.3 = (bf16[2,136,1152]{2,1,0:T(8,128)(2,1)S(1)}, bf16[2,136,1152]{2,1,0:T(8,128)(2,1)S(1)}, u32[]{:S(2)}, u32[]{:S(2)}) collective-permute-start(bf16[2,136,1152]{2,1,0:T(8,128)(2,1)S(1)} %get-tuple-element.277.refs_0_), channel_id=1, source_target_pairs={{0,2},{1,3},{2,0},{3,1},{4,6},{5,7},{6,4},{7,5},{8,10},{9,11},{10,... | collective-permute-start | bytes 1880072 | tf_op jit(solution)/shard_map/ppermute | solution.py:510
  31.4 15.9 %collective-permute-start.4 = (bf16[2,136,1152]{2,1,0:T(8,128)(2,1)S(1)}, bf16[2,136,1152]{2,1,0:T(8,128)(2,1)S(1)}, u32[]{:S(2)}, u32[]{:S(2)}) collective-permute-start(bf16[2,136,1152]{2,1,0:T(8,128)(2,1)S(1)} %get-tuple-element.275.refs_2_), channel_id=1, source_target_pairs={{0,16},{16,0},{1,17},{17,1},{2,18},{18,2},{3,19},{19,3},{4,20},{20... | collective-permute-start | bytes 1880072 | tf_op jit(solution)/shard_map/ppermute | solution.py:518
  45.0 28.9 %collective-permute-start.5 = (bf16[2,2,136,1152]{3,2,1,0:T(8,128)(2,1)S(1)}, bf16[2,2,136,1152]{3,2,1,0:T(8,128)(2,1)S(1)}, u32[]{:S(2)}, u32[]{:S(2)}) collective-permute-start(bf16[2,2,136,1152]{3,2,1,0:T(8,128)(2,1)S(1)} %pad_maximum_fusion.1), channel_id=1, source_target_pairs={{0,16},{16,0},{1,17},{17,1},{2,18},{18,2},{3,19},{19,3},{4,20},{20... | collective-permute-start | bytes 3760136 | tf_op jit(solution)/shard_map/ppermute | solution.py:518
  47.4 28.1 %collective-permute-start.6 = (bf16[2,2,136,1152]{3,2,1,0:T(8,128)(2,1)S(1)}, bf16[2,2,136,1152]{3,2,1,0:T(8,128)(2,1)S(1)}, u32[]{:S(2)}, u32[]{:S(2)}) collective-permute-start(bf16[2,2,136,1152]{3,2,1,0:T(8,128)(2,1)S(1)} %pad_maximum_fusion.2), channel_id=1, source_target_pairs={{0,2},{1,3},{2,0},{3,1},{4,6},{5,7},{6,4},{7,5},{8,10},{9,11},{10,... | collective-permute-start | bytes 3760136 | tf_op jit(solution)/shard_map/ppermute | solution.py:510
  48.7 31.1 %copy-start.98 = (f32[512]{0:T(512)}, f32[512]{0:T(512)S(1)}, u32[]{:S(2)}) copy-start(f32[512]{0:T(512)S(1)} %broadcast_multiply_fusion.5) | copy-start | bytes 6148
  49.8 33.0 %collective-permute-start.8 = (bf16[136,1088]{1,0:T(8,128)(2,1)S(1)}, bf16[136,1088]{1,0:T(8,128)(2,1)}, u32[]{:S(2)}, u32[]{:S(2)}) collective-permute-start(bf16[136,1088]{1,0:T(8,128)(2,1)S(1)} %convert_element_type.313), channel_id=1, source_target_pairs={{0,4},{4,8},{8,12},{12,0},{1,5},{5,9},{9,13},{13,1},{2,6},{6,10},{... | collective-permute-start | bytes 887816 | tf_op jit(solution)/shard_map/ppermute | solution.py:523
  57.1 25.7 %collective-permute-start.9 = (bf16[136,1088]{1,0:T(8,128)(2,1)S(1)}, bf16[136,1088]{1,0:T(8,128)(2,1)S(1)}, u32[]{:S(2)}, u32[]{:S(2)}) collective-permute-start(bf16[136,1088]{1,0:T(8,128)(2,1)S(1)} %convert_element_type.313), channel_id=1, source_target_pairs={{0,8},{4,12},{8,0},{12,4},{1,9},{5,13},{9,1},{13,5},{2,10},{6,14},... | collective-permute-start | bytes 887816 | tf_op jit(solution)/shard_map/ppermute | solution.py:523
  57.9 24.9 %collective-permute-start.10 = (bf16[136,1088]{1,0:T(8,128)(2,1)S(1)}, bf16[136,1088]{1,0:T(8,128)(2,1)}, u32[]{:S(2)}, u32[]{:S(2)}) collective-permute-start(bf16[136,1088]{1,0:T(8,128)(2,1)S(1)} %convert_element_type.313), channel_id=1, source_target_pairs={{0,12},{4,0},{8,4},{12,8},{1,13},{5,1},{9,5},{13,9},{2,14},{6,2},{... | collective-permute-start | bytes 887816 | tf_op jit(solution)/shard_map/ppermute | solution.py:523
  79.8 58.8 %collective-permute-start.13 = (bf16[2,1088,1152]{2,1,0:T(8,128)(2,1)}, bf16[2,1088,1152]{2,1,0:T(8,128)(2,1)}, u32[]{:S(2)}, u32[]{:S(2)}) collective-permute-start(bf16[2,1088,1152]{2,1,0:T(8,128)(2,1)} %bitcast.350), channel_id=1, source_target_pairs={{0,1},{1,0},{2,3},{3,2},{4,5},{5,4},{6,7},{7,6},{8,9},{9,8},{10,11... | collective-permute-start | bytes 15040520 | tf_op jit(solution)/shard_map/ppermute | solution.py:510
  82.8 43.4 %collective-permute-start.14 = (bf16[136,1088]{1,0:T(8,128)(2,1)}, bf16[136,1088]{1,0:T(8,128)(2,1)}, u32[]{:S(2)}, u32[]{:S(2)}) collective-permute-start(bf16[136,1088]{1,0:T(8,128)(2,1)} %convert_bitcast_fusion.2), channel_id=1, source_target_pairs={{0,4},{4,8},{8,12},{12,0},{1,5},{5,9},{9,13},{13,1},{2,6},{6,10},{... | collective-permute-start | bytes 887816 | tf_op jit(solution)/shard_map/ppermute | solution.py:523
  90.2 36.0 %collective-permute-start.15 = (bf16[136,1088]{1,0:T(8,128)(2,1)}, bf16[136,1088]{1,0:T(8,128)(2,1)}, u32[]{:S(2)}, u32[]{:S(2)}) collective-permute-start(bf16[136,1088]{1,0:T(8,128)(2,1)} %convert_bitcast_fusion.2), channel_id=1, source_target_pairs={{0,8},{4,12},{8,0},{12,4},{1,9},{5,13},{9,1},{13,5},{2,10},{6,14},... | collective-permute-start | bytes 887816 | tf_op jit(solution)/shard_map/ppermute | solution.py:523
  91.3 41.9 %copy-start.7 = (bf16[2,136,1088]{2,1,0:T(8,128)(2,1)}, bf16[2,136,1088]{2,1,0:T(8,128)(2,1)S(1)}, u32[]{:S(2)}) copy-start(bf16[2,136,1088]{2,1,0:T(8,128)(2,1)S(1)} %pad_maximum_fusion.12.refs_0_) | copy-start | bytes 1775620
  91.3 16.3 %collective-permute-start.11 = (bf16[2,136,1088]{2,1,0:T(8,128)(2,1)S(1)}, bf16[2,136,1088]{2,1,0:T(8,128)(2,1)S(1)}, u32[]{:S(2)}, u32[]{:S(2)}) collective-permute-start(bf16[2,136,1088]{2,1,0:T(8,128)(2,1)S(1)} %pad_maximum_fusion.12.refs_0_), channel_id=1, source_target_pairs={{0,2},{1,3},{2,0},{3,1},{4,6},{5,7},{6,4},{7,5},{8,10},{9,11},{10,... | collective-permute-start | bytes 1775624 | tf_op jit(solution)/shard_map/ppermute | solution.py:510
  93.6 41.3 %copy-start.9 = (bf16[2,136,1088]{2,1,0:T(8,128)(2,1)}, bf16[2,136,1088]{2,1,0:T(8,128)(2,1)S(1)}, u32[]{:S(2)}) copy-start(bf16[2,136,1088]{2,1,0:T(8,128)(2,1)S(1)} %pad_maximum_fusion.13.refs_2_) | copy-start | bytes 1775620
  94.5 5.5 %collective-permute-start.7 = (bf16[2,8,7,64]{3,2,1,0:T(8,128)(2,1)S(1)}, bf16[2,8,7,64]{3,2,1,0:T(8,128)(2,1)S(1)}, u32[]{:S(2)}, u32[]{:S(2)}) collective-permute-start(bf16[2,8,7,64]{3,2,1,0:T(8,128)(2,1)S(1)} %slice.275), channel_id=1, source_target_pairs={{0,1},{1,0},{2,3},{3,2},{4,5},{5,4},{6,7},{7,6},{8,9},{9,8},{10,11... | collective-permute-start | bytes 43016 | tf_op jit(solution)/shard_map/ppermute | solution.py:510
  100.1 16.6 %collective-permute-start.12 = (bf16[2,136,1088]{2,1,0:T(8,128)(2,1)S(1)}, bf16[2,136,1088]{2,1,0:T(8,128)(2,1)}, u32[]{:S(2)}, u32[]{:S(2)}) collective-permute-start(bf16[2,136,1088]{2,1,0:T(8,128)(2,1)S(1)} %pad_maximum_fusion.13.refs_2_), channel_id=1, source_target_pairs={{0,16},{16,0},{1,17},{17,1},{2,18},{18,2},{3,19},{19,3},{4,20},{20... | collective-permute-start | bytes 1775624 | tf_op jit(solution)/shard_map/ppermute | solution.py:518
  107.6 18.6 %collective-permute-start.16 = (bf16[136,1088]{1,0:T(8,128)(2,1)}, bf16[136,1088]{1,0:T(8,128)(2,1)}, u32[]{:S(2)}, u32[]{:S(2)}) collective-permute-start(bf16[136,1088]{1,0:T(8,128)(2,1)} %convert_bitcast_fusion.2), channel_id=1, source_target_pairs={{0,12},{4,0},{8,4},{12,8},{1,13},{5,1},{9,5},{13,9},{2,14},{6,2},{... | collective-permute-start | bytes 887816 | tf_op jit(solution)/shard_map/ppermute | solution.py:523
  128.8 20.9 %collective-permute-start.17 = (bf16[2,136,1088]{2,1,0:T(8,128)(2,1)}, bf16[2,136,1088]{2,1,0:T(8,128)(2,1)}, u32[]{:S(2)}, u32[]{:S(2)}) collective-permute-start(bf16[2,136,1088]{2,1,0:T(8,128)(2,1)} %pad_maximum_fusion.14.refs_0_), channel_id=1, source_target_pairs={{0,2},{1,3},{2,0},{3,1},{4,6},{5,7},{6,4},{7,5},{8,10},{9,11},{10,... | collective-permute-start | bytes 1775624 | tf_op jit(solution)/shard_map/ppermute | solution.py:510
  131.7 18.1 %collective-permute-start.18 = (bf16[2,136,1088]{2,1,0:T(8,128)(2,1)}, bf16[2,136,1088]{2,1,0:T(8,128)(2,1)}, u32[]{:S(2)}, u32[]{:S(2)}) collective-permute-start(bf16[2,136,1088]{2,1,0:T(8,128)(2,1)} %pad_maximum_fusion.15.refs_2_), channel_id=1, source_target_pairs={{0,16},{16,0},{1,17},{17,1},{2,18},{18,2},{3,19},{19,3},{4,20},{20... | collective-permute-start | bytes 1775624 | tf_op jit(solution)/shard_map/ppermute | solution.py:518
  134.4 50.2 %collective-permute-start.20 = (bf16[2,2,136,1088]{3,2,1,0:T(8,128)(2,1)}, bf16[2,2,136,1088]{3,2,1,0:T(8,128)(2,1)}, u32[]{:S(2)}, u32[]{:S(2)}) collective-permute-start(bf16[2,2,136,1088]{3,2,1,0:T(8,128)(2,1)} %pad_maximum_fusion.3), channel_id=1, source_target_pairs={{0,16},{16,0},{1,17},{17,1},{2,18},{18,2},{3,19},{19,3},{4,20},{20... | collective-permute-start | bytes 3551240 | tf_op jit(solution)/shard_map/ppermute | solution.py:518
  137.2 47.5 %collective-permute-start.21 = (bf16[2,2,136,1088]{3,2,1,0:T(8,128)(2,1)}, bf16[2,2,136,1088]{3,2,1,0:T(8,128)(2,1)}, u32[]{:S(2)}, u32[]{:S(2)}) collective-permute-start(bf16[2,2,136,1088]{3,2,1,0:T(8,128)(2,1)} %pad_maximum_fusion.4), channel_id=1, source_target_pairs={{0,2},{1,3},{2,0},{3,1},{4,6},{5,7},{6,4},{7,5},{8,10},{9,11},{10,... | collective-permute-start | bytes 3551240 | tf_op jit(solution)/shard_map/ppermute | solution.py:510
  152.2 14.7 %collective-permute-start.19 = (bf16[512,2304]{1,0:T(8,128)(2,1)}, bf16[512,2304]{1,0:T(8,128)(2,1)}, u32[]{:S(2)}, u32[]{:S(2)}) collective-permute-start(bf16[512,2304]{1,0:T(8,128)(2,1)} %slice.219), channel_id=1, source_target_pairs={{0,1},{2,3},{4,5},{6,7},{8,9},{10,11},{12,13},{14,15},{16,17},{18,... | collective-permute-start | bytes 7077896 | tf_op jit(solution)/shard_map/ppermute | solution.py:755
  157.7 51.1 %collective-permute-start.23 = (bf16[2,2,136,1088]{3,2,1,0:T(8,128)(2,1)}, bf16[2,2,136,1088]{3,2,1,0:T(8,128)(2,1)S(1)}, u32[]{:S(2)}, u32[]{:S(2)}) collective-permute-start(bf16[2,2,136,1088]{3,2,1,0:T(8,128)(2,1)} %pad_maximum_fusion.5), channel_id=1, source_target_pairs={{0,16},{16,0},{1,17},{17,1},{2,18},{18,2},{3,19},{19,3},{4,20},{20... | collective-permute-start | bytes 3551240 | tf_op jit(solution)/shard_map/ppermute | solution.py:518
  161.0 47.8 %collective-permute-start.24 = (bf16[2,2,136,1088]{3,2,1,0:T(8,128)(2,1)}, bf16[2,2,136,1088]{3,2,1,0:T(8,128)(2,1)S(1)}, u32[]{:S(2)}, u32[]{:S(2)}) collective-permute-start(bf16[2,2,136,1088]{3,2,1,0:T(8,128)(2,1)} %pad_maximum_fusion.6), channel_id=1, source_target_pairs={{0,2},{1,3},{2,0},{3,1},{4,6},{5,7},{6,4},{7,5},{8,10},{9,11},{10,... | collective-permute-start | bytes 3551240 | tf_op jit(solution)/shard_map/ppermute | solution.py:510
  166.9 29.2 %copy-start.55 = (bf16[1088,1152]{1,0:T(8,128)(2,1)}, bf16[1088,1152]{1,0:T(8,128)(2,1)S(1)}, u32[]{:S(2)}) copy-start(bf16[1088,1152]{1,0:T(8,128)(2,1)S(1)} %get-tuple-element.258) | copy-start | bytes 7520260
  166.9 17.7 %copy-start.8 = (bf16[2,136,1088]{2,1,0:T(8,128)(2,1)S(1)}, bf16[2,136,1088]{2,1,0:T(8,128)(2,1)}, u32[]{:S(2)}) copy-start(bf16[2,136,1088]{2,1,0:T(8,128)(2,1)} %copy-done.7) | copy-start | bytes 1775620
  189.6 23.5 %collective-permute-start.22 = (bf16[2,1088,1088]{2,1,0:T(8,128)(2,1)}, bf16[2,1088,1088]{2,1,0:T(8,128)(2,1)}, u32[]{:S(2)}, u32[]{:S(2)}) collective-permute-start(bf16[2,1088,1088]{2,1,0:T(8,128)(2,1)} %bitcast.359), channel_id=1, source_target_pairs={{0,1},{1,0},{2,3},{3,2},{4,5},{5,4},{6,7},{7,6},{8,9},{9,8},{10,11... | collective-permute-start | bytes 14204936 | tf_op jit(solution)/shard_map/ppermute | solution.py:510
  212.9 26.6 %collective-permute-start.25 = (bf16[2,1088,1088]{2,1,0:T(8,128)(2,1)}, bf16[2,1088,1088]{2,1,0:T(8,128)(2,1)}, u32[]{:S(2)}, u32[]{:S(2)}) collective-permute-start(bf16[2,1088,1088]{2,1,0:T(8,128)(2,1)} %bitcast.354), channel_id=1, source_target_pairs={{0,1},{1,0},{2,3},{3,2},{4,5},{5,4},{6,7},{7,6},{8,9},{9,8},{10,11... | collective-permute-start | bytes 14204936 | tf_op jit(solution)/shard_map/ppermute | solution.py:510
  228.9 17.7 %collective-permute-start.26 = (bf16[2,1088,1088]{2,1,0:T(8,128)(2,1)}, bf16[2,1088,1088]{2,1,0:T(8,128)(2,1)}, u32[]{:S(2)}, u32[]{:S(2)}) collective-permute-start(bf16[2,1088,1088]{2,1,0:T(8,128)(2,1)} %block_grads.6), channel_id=1, source_target_pairs={{0,1},{1,0},{2,3},{3,2},{4,5},{5,4},{6,7},{7,6},{8,9},{9,8},{10,11... | collective-permute-start | bytes 14204936 | tf_op jit(solution)/shard_map/ppermute | solution.py:510
  277.6 35.3 %collective-permute-start.27 = (bf16[2,1088,1088]{2,1,0:T(8,128)(2,1)}, bf16[2,1088,1088]{2,1,0:T(8,128)(2,1)}, u32[]{:S(2)}, u32[]{:S(2)}) collective-permute-start(bf16[2,1088,1088]{2,1,0:T(8,128)(2,1)} %block_grads.8), channel_id=1, source_target_pairs={{0,1},{1,0},{2,3},{3,2},{4,5},{5,4},{6,7},{7,6},{8,9},{9,8},{10,11... | collective-permute-start | bytes 14204936 | tf_op jit(solution)/shard_map/ppermute | solution.py:510
  277.7 31.3 %collective-permute-start.28 = (bf16[2,272,1088]{2,1,0:T(8,128)(2,1)}, bf16[2,272,1088]{2,1,0:T(8,128)(2,1)}, u32[]{:S(2)}, u32[]{:S(2)}) collective-permute-start(bf16[2,272,1088]{2,1,0:T(8,128)(2,1)} %get-tuple-element.164), channel_id=1, source_target_pairs={{0,16},{16,0},{1,17},{17,1},{2,18},{18,2},{3,19},{19,3},{4,20},{20... | collective-permute-start | bytes 3551240 | tf_op jit(solution)/shard_map/ppermute | solution.py:518
  278.3 33.0 %collective-permute-start.29 = (bf16[2,272,1088]{2,1,0:T(8,128)(2,1)}, bf16[2,272,1088]{2,1,0:T(8,128)(2,1)}, u32[]{:S(2)}, u32[]{:S(2)}) collective-permute-start(bf16[2,272,1088]{2,1,0:T(8,128)(2,1)} %get-tuple-element.166), channel_id=1, source_target_pairs={{0,2},{1,3},{2,0},{3,1},{4,6},{5,7},{6,4},{7,5},{8,10},{9,11},{10,... | collective-permute-start | bytes 3551240 | tf_op jit(solution)/shard_map/ppermute | solution.py:510
  319.9 29.8 %collective-permute-start.33 = (bf16[272,1088]{1,0:T(8,128)(2,1)S(1)}, bf16[272,1088]{1,0:T(8,128)(2,1)}, u32[]{:S(2)}, u32[]{:S(2)}) collective-permute-start(bf16[272,1088]{1,0:T(8,128)(2,1)S(1)} %dynamic-slice_bitcast_fusion.2), channel_id=1, source_target_pairs={{0,16},{16,0},{1,17},{17,1},{2,18},{18,2},{3,19},{19,3},{4,20},{20... | collective-permute-start | bytes 1775624 | tf_op jit(solution)/shard_map/ppermute | solution.py:518
  320.6 28.9 %collective-permute-start.32 = (bf16[272,1088]{1,0:T(8,128)(2,1)S(1)}, bf16[272,1088]{1,0:T(8,128)(2,1)S(1)}, u32[]{:S(2)}, u32[]{:S(2)}) collective-permute-start(bf16[272,1088]{1,0:T(8,128)(2,1)S(1)} %slice_bitcast_fusion.15), channel_id=1, source_target_pairs={{0,2},{1,3},{2,0},{3,1},{4,6},{5,7},{6,4},{7,5},{8,10},{9,11},{10,... | collective-permute-start | bytes 1775624 | tf_op jit(solution)/shard_map/ppermute | solution.py:510
  327.5 35.3 %collective-permute-start.30 = (bf16[2,272,1088]{2,1,0:T(8,128)(2,1)S(1)}, bf16[2,272,1088]{2,1,0:T(8,128)(2,1)S(1)}, u32[]{:S(2)}, u32[]{:S(2)}) collective-permute-start(bf16[2,272,1088]{2,1,0:T(8,128)(2,1)S(1)} %get-tuple-element.175), channel_id=1, source_target_pairs={{0,16},{16,0},{1,17},{17,1},{2,18},{18,2},{3,19},{19,3},{4,20},{20... | collective-permute-start | bytes 3551240 | tf_op jit(solution)/shard_map/ppermute | solution.py:518
  328.5 35.8 %collective-permute-start.31 = (bf16[2,272,1088]{2,1,0:T(8,128)(2,1)}, bf16[2,272,1088]{2,1,0:T(8,128)(2,1)S(1)}, u32[]{:S(2)}, u32[]{:S(2)}) collective-permute-start(bf16[2,272,1088]{2,1,0:T(8,128)(2,1)} %get-tuple-element.177), channel_id=1, source_target_pairs={{0,2},{1,3},{2,0},{3,1},{4,6},{5,7},{6,4},{7,5},{8,10},{9,11},{10,... | collective-permute-start | bytes 3551240 | tf_op jit(solution)/shard_map/ppermute | solution.py:510
  367.2 7.1 %collective-permute-start.34 = (bf16[512,2304]{1,0:T(8,128)(2,1)}, bf16[512,2304]{1,0:T(8,128)(2,1)}, u32[]{:S(2)}, u32[]{:S(2)}) collective-permute-start(bf16[512,2304]{1,0:T(8,128)(2,1)} %pad_maximum_fusion), channel_id=1, source_target_pairs={{1,0},{3,2},{5,4},{7,6},{9,8},{11,10},{13,12},{15,14},{17,16},{19,... | collective-permute-start | bytes 7077896 | tf_op jit(solution)/shard_map/ppermute | solution.py:872
  382.2 31.9 %copy-start.25 = (bf16[2,512,896]{2,1,0:T(8,128)(2,1)}, bf16[2,512,896]{2,1,0:T(8,128)(2,1)S(1)}, u32[]{:S(2)}) copy-start(bf16[2,512,896]{2,1,0:T(8,128)(2,1)S(1)} %get-tuple-element.185.refs_2_) | copy-start | bytes 5505028
  389.6 35.8 %collective-permute-start.36 = (bf16[2,1088,1152]{2,1,0:T(8,128)(2,1)}, bf16[2,1088,1152]{2,1,0:T(8,128)(2,1)}, u32[]{:S(2)}, u32[]{:S(2)}) collective-permute-start(bf16[2,1088,1152]{2,1,0:T(8,128)(2,1)} %block_grads.10), channel_id=1, source_target_pairs={{0,1},{1,0},{2,3},{3,2},{4,5},{5,4},{6,7},{7,6},{8,9},{9,8},{10,11... | collective-permute-start | bytes 15040520 | tf_op jit(solution)/shard_map/ppermute | solution.py:510
  391.9 16.1 %collective-permute-start.45 = (bf16[272,1088]{1,0:T(8,128)(2,1)S(1)}, bf16[272,1088]{1,0:T(8,128)(2,1)S(1)}, u32[]{:S(2)}, u32[]{:S(2)}) collective-permute-start(bf16[272,1088]{1,0:T(8,128)(2,1)S(1)} %dynamic-slice_bitcast_fusion), channel_id=1, source_target_pairs={{0,16},{16,0},{1,17},{17,1},{2,18},{18,2},{3,19},{19,3},{4,20},{20... | collective-permute-start | bytes 1775624 | tf_op jit(solution)/shard_map/ppermute | solution.py:518
  392.6 16.2 %collective-permute-start.44 = (bf16[272,1088]{1,0:T(8,128)(2,1)S(1)}, bf16[272,1088]{1,0:T(8,128)(2,1)S(1)}, u32[]{:S(2)}, u32[]{:S(2)}) collective-permute-start(bf16[272,1088]{1,0:T(8,128)(2,1)S(1)} %slice_bitcast_fusion.14), channel_id=1, source_target_pairs={{0,2},{1,3},{2,0},{3,1},{4,6},{5,7},{6,4},{7,5},{8,10},{9,11},{10,... | collective-permute-start | bytes 1775624 | tf_op jit(solution)/shard_map/ppermute | solution.py:510
  394.7 39.3 %collective-permute-start.51 = (bf16[136,1088]{1,0:T(8,128)(2,1)}, bf16[136,1088]{1,0:T(8,128)(2,1)}, u32[]{:S(2)}, u32[]{:S(2)}) collective-permute-start(bf16[136,1088]{1,0:T(8,128)(2,1)} %get-tuple-element.266), channel_id=1, source_target_pairs={{0,12},{4,0},{8,4},{12,8},{1,13},{5,1},{9,5},{13,9},{2,14},{6,2},{... | collective-permute-start | bytes 887816 | tf_op jit(solution)/shard_map/ppermute | solution.py:523
  397.1 37.0 %collective-permute-start.50 = (bf16[136,1088]{1,0:T(8,128)(2,1)}, bf16[136,1088]{1,0:T(8,128)(2,1)}, u32[]{:S(2)}, u32[]{:S(2)}) collective-permute-start(bf16[136,1088]{1,0:T(8,128)(2,1)} %get-tuple-element.267), channel_id=1, source_target_pairs={{0,8},{4,12},{8,0},{12,4},{1,9},{5,13},{9,1},{13,5},{2,10},{6,14},... | collective-permute-start | bytes 887816 | tf_op jit(solution)/shard_map/ppermute | solution.py:523
  408.0 26.6 %collective-permute-start.49 = (bf16[136,1088]{1,0:T(8,128)(2,1)S(1)}, bf16[136,1088]{1,0:T(8,128)(2,1)}, u32[]{:S(2)}, u32[]{:S(2)}) collective-permute-start(bf16[136,1088]{1,0:T(8,128)(2,1)S(1)} %get-tuple-element.265), channel_id=1, source_target_pairs={{0,4},{4,8},{8,12},{12,0},{1,5},{5,9},{9,13},{13,1},{2,6},{6,10},{... | collective-permute-start | bytes 887816 | tf_op jit(solution)/shard_map/ppermute | solution.py:523
  420.4 1.3 collective-permute-start.35
  421.8 17.0 %collective-permute-start.48 = (bf16[136,1088]{1,0:T(8,128)(2,1)S(1)}, bf16[136,1088]{1,0:T(8,128)(2,1)S(1)}, u32[]{:S(2)}, u32[]{:S(2)}) collective-permute-start(bf16[136,1088]{1,0:T(8,128)(2,1)S(1)} %get-tuple-element.269), channel_id=1, source_target_pairs={{0,12},{4,0},{8,4},{12,8},{1,13},{5,1},{9,5},{13,9},{2,14},{6,2},{... | collective-permute-start | bytes 887816 | tf_op jit(solution)/shard_map/ppermute | solution.py:523
  425.4 28.9 %collective-permute-start.47 = (bf16[136,1088]{1,0:T(8,128)(2,1)S(1)}, bf16[136,1088]{1,0:T(8,128)(2,1)S(1)}, u32[]{:S(2)}, u32[]{:S(2)}) collective-permute-start(bf16[136,1088]{1,0:T(8,128)(2,1)S(1)} %get-tuple-element.270), channel_id=1, source_target_pairs={{0,8},{4,12},{8,0},{12,4},{1,9},{5,13},{9,1},{13,5},{2,10},{6,14},... | collective-permute-start | bytes 887816 | tf_op jit(solution)/shard_map/ppermute | solution.py:523
  434.0 20.3 %collective-permute-start.46 = (bf16[136,1088]{1,0:T(8,128)(2,1)S(1)}, bf16[136,1088]{1,0:T(8,128)(2,1)S(1)}, u32[]{:S(2)}, u32[]{:S(2)}) collective-permute-start(bf16[136,1088]{1,0:T(8,128)(2,1)S(1)} %get-tuple-element.268), channel_id=1, source_target_pairs={{0,4},{4,8},{8,12},{12,0},{1,5},{5,9},{9,13},{13,1},{2,6},{6,10},{... | collective-permute-start | bytes 887816 | tf_op jit(solution)/shard_map/ppermute | solution.py:523
  434.1 20.2 %copy-start.63 = (f32[136,1088]{1,0:T(8,128)S(1)}, f32[136,1088]{1,0:T(8,128)}, u32[]{:S(2)}) copy-start(f32[136,1088]{1,0:T(8,128)} %param.23) | copy-start | bytes 1775620
  434.1 20.2 %copy-start.88 = (f32[136,1088]{1,0:T(8,128)S(1)}, f32[136,1088]{1,0:T(8,128)}, u32[]{:S(2)}) copy-start(f32[136,1088]{1,0:T(8,128)} %param.33) | copy-start | bytes 1775620
  434.1 20.2 %copy-start.89 = (f32[136,1088]{1,0:T(8,128)S(1)}, f32[136,1088]{1,0:T(8,128)}, u32[]{:S(2)}) copy-start(f32[136,1088]{1,0:T(8,128)} %param.28) | copy-start | bytes 1775620
  434.1 29.6 %collective-permute-start.39 = (bf16[2,272,1152]{2,1,0:T(8,128)(2,1)}, bf16[2,272,1152]{2,1,0:T(8,128)(2,1)S(1)}, u32[]{:S(2)}, u32[]{:S(2)}) collective-permute-start(bf16[2,272,1152]{2,1,0:T(8,128)(2,1)} %get-tuple-element.191), channel_id=1, source_target_pairs={{0,2},{1,3},{2,0},{3,1},{4,6},{5,7},{6,4},{7,5},{8,10},{9,11},{10,... | collective-permute-start | bytes 3760136 | tf_op jit(solution)/shard_map/ppermute | solution.py:510
  437.7 26.1 %copy-start.82 = (bf16[2,272,1152]{2,1,0:T(8,128)(2,1)S(1)}, bf16[2,272,1152]{2,1,0:T(8,128)(2,1)}, u32[]{:S(2)}) copy-start(bf16[2,272,1152]{2,1,0:T(8,128)(2,1)} %get-tuple-element.190) | copy-start | bytes 3760132
  437.7 30.4 %collective-permute-start.37 = (bf16[2,272,1152]{2,1,0:T(8,128)(2,1)S(1)}, bf16[2,272,1152]{2,1,0:T(8,128)(2,1)S(1)}, u32[]{:S(2)}, u32[]{:S(2)}) collective-permute-start(bf16[2,272,1152]{2,1,0:T(8,128)(2,1)S(1)} %get-tuple-element.189), channel_id=1, source_target_pairs={{0,16},{16,0},{1,17},{17,1},{2,18},{18,2},{3,19},{19,3},{4,20},{20... | collective-permute-start | bytes 3760136 | tf_op jit(solution)/shard_map/ppermute | solution.py:518
  464.1 16.3 %collective-permute-start.40 = (bf16[272,1152]{1,0:T(8,128)(2,1)S(1)}, bf16[272,1152]{1,0:T(8,128)(2,1)S(1)}, u32[]{:S(2)}, u32[]{:S(2)}) collective-permute-start(bf16[272,1152]{1,0:T(8,128)(2,1)S(1)} %dynamic-slice_bitcast_fusion.1), channel_id=1, source_target_pairs={{0,16},{16,0},{1,17},{17,1},{2,18},{18,2},{3,19},{19,3},{4,20},{20... | collective-permute-start | bytes 1880072 | tf_op jit(solution)/shard_map/ppermute | solution.py:518
  468.4 13.9 %collective-permute-start.38 = (bf16[272,1152]{1,0:T(8,128)(2,1)S(1)}, bf16[272,1152]{1,0:T(8,128)(2,1)S(1)}, u32[]{:S(2)}, u32[]{:S(2)}) collective-permute-start(bf16[272,1152]{1,0:T(8,128)(2,1)S(1)} %slice_bitcast_fusion.12), channel_id=1, source_target_pairs={{0,2},{1,3},{2,0},{3,1},{4,6},{5,7},{6,4},{7,5},{8,10},{9,11},{10,... | collective-permute-start | bytes 1880072 | tf_op jit(solution)/shard_map/ppermute | solution.py:510
  482.7 11.4 %collective-permute-start.43 = (bf16[136,1152]{1,0:T(8,128)(2,1)S(1)}, bf16[136,1152]{1,0:T(8,128)(2,1)S(1)}, u32[]{:S(2)}, u32[]{:S(2)}) collective-permute-start(bf16[136,1152]{1,0:T(8,128)(2,1)S(1)} %get-tuple-element.272), channel_id=1, source_target_pairs={{0,12},{4,0},{8,4},{12,8},{1,13},{5,1},{9,5},{13,9},{2,14},{6,2},{... | collective-permute-start | bytes 940040 | tf_op jit(solution)/shard_map/ppermute | solution.py:523
  486.2 24.7 %collective-permute-start.42 = (bf16[136,1152]{1,0:T(8,128)(2,1)S(1)}, bf16[136,1152]{1,0:T(8,128)(2,1)S(1)}, u32[]{:S(2)}, u32[]{:S(2)}) collective-permute-start(bf16[136,1152]{1,0:T(8,128)(2,1)S(1)} %get-tuple-element.273), channel_id=1, source_target_pairs={{0,8},{4,12},{8,0},{12,4},{1,9},{5,13},{9,1},{13,5},{2,10},{6,14},... | collective-permute-start | bytes 940040 | tf_op jit(solution)/shard_map/ppermute | solution.py:523
  486.3 24.7 %collective-permute-start.41 = (bf16[136,1152]{1,0:T(8,128)(2,1)S(1)}, bf16[136,1152]{1,0:T(8,128)(2,1)S(1)}, u32[]{:S(2)}, u32[]{:S(2)}) collective-permute-start(bf16[136,1152]{1,0:T(8,128)(2,1)S(1)} %get-tuple-element.271), channel_id=1, source_target_pairs={{0,4},{4,8},{8,12},{12,0},{1,5},{5,9},{9,13},{13,1},{2,6},{6,10},{... | collective-permute-start | bytes 940040 | tf_op jit(solution)/shard_map/ppermute | solution.py:523
  490.6 21.3 %copy-start.85 = (f32[272,136]{0,1:T(8,128)S(1)}, f32[272,136]{0,1:T(8,128)}, u32[]{:S(2)}) copy-start(f32[272,136]{0,1:T(8,128)} %param.22) | copy-start | bytes 443908
  (102 other events, 523.7 us)
